TPU v7x, 32 devices: a whole 2x2x4 slice. The times are simulated.
32 devices in a mesh: dp: 8 (over z, y), seq: 4 (over x, core).
Axes of the slice: x: 2, y: 2, z: 4, core: 2. Of those that a mesh axis runs over, the one named last changes fastest.
Arguments:
- query: bfloat16 [8, 1536, 4096], P('dp', 'seq'), may hold values from -51 to 51
- caption: bfloat16 [8, 256, 4096], P('dp'), may hold values from -6 to 6
- key_weight: bfloat16 [4096, 4096], P('dp', 'seq'), may hold values from -0.09375 to 0.09375
- value_weight: bfloat16 [4096, 4096], P('dp', 'seq'), may hold values from -0.09375 to 0.09375
- key_gain: float32 [4096], replicated, may hold values from 0.2 to 4.5
- lengths: int32 [8], P('dp'), may hold values from 64 to 128, as said below
- out_grad: bfloat16 [8, 1536, 4096], P('dp', 'seq'), may hold values from -6 to 6
Outputs:
- query_grad: bfloat16 [8, 1536, 4096], P('dp', 'seq')
- key_weight_grad: float32 [4096, 4096], P('dp', 'seq')
- value_weight_grad: float32 [4096, 4096], P('dp', 'seq')
Inputs may be any that keep to these rules, and one draw needn't show every extreme that they name: `lengths`: valid caption tokens of each video, at most 128, a count that some video reaches.
All inputs are finite; a program needn't handle non-finite values.
Results may differ from a plain program's by a relative error of at most 0.008.
The roundings to bfloat16 on the way count: a program that leaves them out, or rounds other values in their place, can miss the bound.
Values may be sent and summed in bfloat16 or wider, within the bound.
No kernel may reach another device: no remote copies, remote signals or barrier semaphores. Data moves between devices by JAX's collectives and lax.ppermute only.
A program may use at most 192 MiB of HBM per device.

v0:
```python
import jax
import jax.numpy as jnp
from jax import lax
from jax.sharding import PartitionSpec as P

HEADS = 32
HD = 128
HID = 4096


def shards(query, caption, key_weight, value_weight, key_gain, lengths, out_grad):
    factor = HD ** (-0.5)
    live_rows = caption.shape[1]
    caption_rows = caption[0, :live_rows]
    head_cols = key_weight.shape[1]
    columns = caption_rows
    key_part = jnp.dot(
        columns,
        lax.all_gather(key_weight, "dp", axis=0, tiled=True),
        preferred_element_type=jnp.float32,
    )
    value_part = jnp.dot(
        columns,
        lax.all_gather(value_weight, "dp", axis=0, tiled=True),
        preferred_element_type=jnp.float32,
    )
    raw_keys, values = (
        lax.all_gather(key_part.astype(jnp.bfloat16), "seq", axis=1, tiled=True),
        lax.all_gather(value_part.astype(jnp.bfloat16), "seq", axis=1, tiled=True),
    )
    raw_wide = raw_keys.astype(jnp.float32)
    inv_rms = lax.rsqrt(jnp.mean(raw_wide * raw_wide, axis=-1, keepdims=True) + 1e-06)
    keys = (raw_wide * inv_rms * key_gain).astype(jnp.bfloat16)
    tokens = query.shape[1]
    query_heads = query[0].reshape(tokens, HEADS, HD)
    grad_heads = out_grad[0].reshape(tokens, HEADS, HD)
    key_heads = keys.reshape(live_rows, HEADS, HD)
    value_heads = values.reshape(live_rows, HEADS, HD)
    scores = (
        jnp.einsum("thd,lhd->htl", query_heads, key_heads, preferred_element_type=jnp.float32)
        * factor
    )
    valid_mask = jnp.arange(live_rows) < lengths[0]
    scores = jnp.where(valid_mask, scores, -jnp.inf)
    attend = jax.nn.softmax(scores, axis=-1)
    dattend = jnp.einsum(
        "thd,lhd->htl", grad_heads, value_heads, preferred_element_type=jnp.float32
    )
    row_delta = jnp.sum(attend * dattend, axis=-1, keepdims=True)
    dscores = (attend * (dattend - row_delta)).astype(jnp.bfloat16)
    attend_low = attend.astype(jnp.bfloat16)
    query_grad = (
        jnp.einsum("htl,lhd->thd", dscores, key_heads, preferred_element_type=jnp.float32) * factor
    )
    query_grad = query_grad.reshape(1, tokens, HID).astype(jnp.bfloat16)
    key_grad = (
        jnp.einsum("htl,thd->lhd", dscores, query_heads, preferred_element_type=jnp.float32)
        * factor
    ).reshape(live_rows, HID)
    value_grad = jnp.einsum(
        "htl,thd->lhd", attend_low, grad_heads, preferred_element_type=jnp.float32
    ).reshape(live_rows, HID)
    scaled_all = key_grad * key_gain
    inner_all = jnp.mean(scaled_all * raw_wide, axis=-1, keepdims=True)
    first_member = inv_rms * scaled_all - raw_wide * inv_rms**3 * inner_all
    raw_grad, value_sum = (
        lax.psum_scatter(first_member, "seq", scatter_dimension=1, tiled=True),
        lax.psum_scatter(value_grad, "seq", scatter_dimension=1, tiled=True),
    )
    grad_pair = jnp.concatenate(
        [raw_grad.astype(jnp.bfloat16), value_sum.astype(jnp.bfloat16)], axis=1
    )
    columns = caption_rows
    summed = lax.psum_scatter(
        jnp.einsum("lc,lw->cw", columns, grad_pair, preferred_element_type=jnp.float32),
        "dp",
        scatter_dimension=0,
        tiled=True,
    )
    return (query_grad, summed[:, :head_cols], summed[:, head_cols:])


def solution(mesh):
    placed = (
        P("dp", "seq", None),
        P("dp", None, None),
        P("dp", "seq"),
        P("dp", "seq"),
        P(),
        P("dp"),
        P("dp", "seq", None),
    )
    return jax.shard_map(
        shards,
        mesh=mesh,
        in_specs=placed,
        out_specs=(P("dp", "seq", None), P("dp", "seq"), P("dp", "seq")),
        check_vma=False,
    )
```

profile of v0, /device:TPU:0, one launch (start us, length us, event | category | flops | bytes accessed | tf_op | source)
XLA Modules:
  0.0 990.5 jit_solution(5670646604321436610)
XLA Ops:
  8.7 129.1 %all-gather.5.cloned.1.call-done = bf16[4096,1024]{1,0:T(8,128)(2,1)} async-done(((bf16[512,1024]{1,0:T(8,128)(2,1)}), bf16[4096,1024]{1,0:T(8,128)(2,1)}) %all-gather.5.cloned.1.call-update) | async-done | bytes 8388624 | tf_op jit(solution)/shard_map/all_gather | solution.py:19
  137.8 6.5 fusion.27
  145.0 4.9 copy.31
  149.9 4.7 copy.32
  154.6 108.5 %all-gather.9.cloned.1.call-done = bf16[4096,1024]{1,0:T(8,128)(2,1)} async-done(((bf16[512,1024]{1,0:T(8,128)(2,1)}), bf16[4096,1024]{1,0:T(8,128)(2,1)}) %all-gather.9.cloned.1.call-update) | async-done | bytes 8388624 | tf_op jit(solution)/shard_map/all_gather | solution.py:24
  263.1 6.5 fusion.30
  269.8 16.2 %all-gather.7.cloned.1.call-done = bf16[256,4096]{1,0:T(8,128)(2,1)} async-done(((bf16[256,1024]{1,0:T(8,128)(2,1)}), bf16[256,4096]{1,0:T(8,128)(2,1)}) %all-gather.7.cloned.1.call-update) | async-done | bytes 2097168 | tf_op jit(solution)/shard_map/all_gather | solution.py:28
  288.1 3.5 fusion.15
  291.7 4.1 copy.30
  295.8 12.3 %fusion.42 = (f32[32,384]{1,0:T(8,128)S(1)}, f32[32,384,256]{1,2,0:T(8,128)}) fusion(pred[256]{0:T(512)(128)(4,1)S(1)} %iota_compare_fusion, bf16[256,32,128]{0,2,1:T(8,128)(2,1)} %bitcast.72, bf16[384,32,128]{0,2,1:T(8,128)(2,1)} %bitcast.70), kind=kOutput, calls=%fused_computation.52 | convolution fusion | flops 817889536 | bytes 17875200 | tf_op jit(solution)/shard_map/sub | solution.py:45
  308.1 9.6 fusion.8
  317.7 5.6 copy.29
  323.6 8.6 fusion.1
  332.3 6.9 fusion.3
  339.1 8.4 convolution_multiply_fusion
  347.5 5.7 copy.28
  353.2 3.6 fusion.18
  361.3 7.0 reduce-scatter.6.cloned.1.call-done
  369.6 45.8 %reduce-scatter.4.cloned.1.call-done = f32[256,1024]{1,0:T(8,128)} async-done(((f32[256,4096]{1,0:T(8,128)}), f32[256,1024]{1,0:T(8,128)}) %reduce-scatter.4.cloned.1.call-update) | async-done | bytes 1048592 | tf_op jit(solution)/shard_map/reduce_scatter | solution.py:67
  416.6 13.3 %convolution_bitcast_fusion = f32[4096,2048]{0,1:T(8,128)} fusion(bf16[1,256,4096]{2,1,0:T(8,128)(2,1)S(1)} %copy-done, bf16[256,1024]{1,0:T(8,128)(2,1)S(1)} %convert_element_type.51, bf16[256,1024]{1,0:T(8,128)(2,1)S(1)} %convert_element_type.49), kind=kOutput, calls=%fused_computation.1 | convolution fusion | flops 4297064448 | bytes 36700160 | tf_op jit(solution)/shard_map/lc,lw->cw/dot_general | solution.py:75
  429.9 6.4 multiply_convert_fusion
  436.3 4.8 copy.22
  441.2 532.0 %reduce-scatter.8.cloned.1.call-done = f32[512,2048]{0,1:T(8,128)} async-done(((f32[4096,2048]{0,1:T(8,128)}), f32[512,2048]{0,1:T(8,128)}) %reduce-scatter.8.cloned.1.call-update) | async-done | bytes 4194320 | tf_op jit(solution)/shard_map/reduce_scatter | solution.py:74
  973.2 4.7 fusion.41
  (34 shorter events, 17.0 us)
Async XLA Ops:
  7.2 130.6 %copy-start = (bf16[1,256,4096]{2,1,0:T(8,128)(2,1)S(1)}, bf16[1,256,4096]{2,1,0:T(8,128)(2,1)}, u32[]{:S(2)}) copy-start(bf16[1,256,4096]{2,1,0:T(8,128)(2,1)} %param.8) | copy-start | bytes 6291460
  7.2 130.6 %all-gather.5.cloned.1.call-start = ((), (), s32[]{:S(2)}) async-start(), calls=%async_computation.3 | async-start | bytes 9437184 | tf_op jit(solution)/shard_map/all_gather | solution.py:19
  7.9 255.2 %all-gather.9.cloned.1.call-start = ((), (), s32[]{:S(2)}) async-start(), calls=%async_computation.5 | async-start | bytes 9437184 | tf_op jit(solution)/shard_map/all_gather | solution.py:24
  8.7 277.4 %all-gather.7.cloned.1.call-start = ((), (), s32[]{:S(2)}) async-start(), calls=%async_computation.4 | async-start | bytes 2621440 | tf_op jit(solution)/shard_map/all_gather | solution.py:28
  144.3 179.3 %all-gather.11.cloned.1.call-start = ((), (), s32[]{:S(2)}) async-start(), calls=%async_computation.6 | async-start | bytes 2621440 | tf_op jit(solution)/shard_map/all_gather | solution.py:29
  154.6 133.5 %copy-start.4 = (f32[4096]{0:T(1024)S(1)}, f32[4096]{0:T(1024)}, u32[]{:S(2)}) copy-start(f32[4096]{0:T(1024)} %param.11) | copy-start | bytes 49156
  269.6 98.7 %reduce-scatter.6.cloned.1.call-start = ((), (), s32[]{:S(2)}) async-start(), calls=%async_computation.8 | async-start | bytes 5242880 | tf_op jit(solution)/shard_map/reduce_scatter | solution.py:68
  323.3 92.0 %reduce-scatter.4.cloned.1.call-start = ((), (), s32[]{:S(2)}) async-start(), calls=%async_computation.7 | async-start | bytes 5242880 | tf_op jit(solution)/shard_map/reduce_scatter | solution.py:67
  339.1 8.4 copy-start.1
  353.2 4.0 copy-start.2
  353.2 4.8 copy-start.3
  361.2 612.0 %reduce-scatter.8.cloned.1.call-start = ((), (), s32[]{:S(2)}) async-start(), calls=%async_computation.9 | async-start | bytes 37748736 | tf_op jit(solution)/shard_map/reduce_scatter | solution.py:74
Sparse Core Ops, SparseCore 0:
  10.1 127.6 all-gather.4
  139.9 123.1 all-gather.8
  265.2 20.7 all-gather.6
  287.4 22.5 all-gather.10
  323.5 44.7 reduce-scatter.5
  370.8 44.4 reduce-scatter.3
  430.1 543.0 reduce-scatter.7
where the time goes:
time: 991 us
  waiting for transfers between devices  840 us (85%)
  matrix products  71.5 us (7%)
  local copies, waits for them, and re-layouts  41.5 us (4%)
  other arithmetic  21.9 us (2%)
  between operations  14.8 us (1%)
    reduce_scatter x1, waiting for transfers between devices, shards(): lax.psum_scatter(jnp.einsum('lc,lw->cw', columns, grad_pair, preferred_el...  532 us
    all_gather x1, waiting for transfers between devices, shards(): lax.all_gather(key_weight, 'dp', axis=0, tiled=True)  129 us
    all_gather x1, waiting for transfers between devices, shards(): lax.all_gather(value_weight, 'dp', axis=0, tiled=True)  108 us
    reduce_scatter x1, waiting for transfers between devices, shards(): lax.psum_scatter(first_member, 'seq', scatter_dimension=1, tiled=True)  45.8 us
  transfers between devices with their start and end apart: 7, of which 6 were waited for; matrix products, arithmetic and copies ran while one was open for 11% of the time, Pallas kernels for 0%

commit v1 on v0

v1 whole, which is shorter than its diff:
```python
import functools

import jax
import jax.numpy as jnp
from jax import lax
from jax.experimental import pallas as pl
from jax.experimental.pallas import tpu as pltpu
from jax.sharding import PartitionSpec as P

HD = 128
LIVE = 128


ROWS = (((1,), (1,)), ((), ()))
COLUMNS = (((0,), (0,)), ((), ()))
FACTOR = HD ** (-0.5)


def attend_kernel(parts, length_ref, raw_ref, inv_ref, gain_ref, *refs):
    query_refs, grad_refs = refs[:parts], refs[parts : 2 * parts]
    attend_refs = refs[2 * parts : 3 * parts]
    keys_ref, value_grad_ref = refs[3 * parts :]
    raw = raw_ref[...].astype(jnp.float32)
    keys = (raw * inv_ref[...] * gain_ref[...]).astype(jnp.bfloat16)
    keys_ref[...] = keys
    valid = lax.broadcasted_iota(jnp.int32, (LIVE, 1), 0) < length_ref[0]
    value_grad = jnp.zeros((LIVE, HD), jnp.float32)
    for query_ref, grad_ref, attend_ref in zip(query_refs, grad_refs, attend_refs):
        scores = lax.dot_general(keys, query_ref[...], ROWS, preferred_element_type=jnp.float32)
        scores = jnp.where(valid, scores * FACTOR, -jnp.inf)
        powers = jnp.exp(scores - jnp.max(scores, axis=0, keepdims=True))
        attend = powers * (1.0 / jnp.sum(powers, axis=0, keepdims=True))
        attend_ref[0] = attend
        value_grad += jnp.dot(
            attend.astype(jnp.bfloat16), grad_ref[...], preferred_element_type=jnp.float32
        )
    value_grad_ref[...] = value_grad.astype(jnp.bfloat16)


def gradient_kernel(parts, raw_ref, keys_ref, value_ref, gain_ref, *refs):
    query_refs, grad_refs = refs[:parts], refs[parts : 2 * parts]
    attend_refs, out_refs = refs[2 * parts : 3 * parts], refs[3 * parts : 4 * parts]
    scaled_ref, inner_ref = refs[4 * parts :]
    keys, values = keys_ref[...], value_ref[...]
    key_grad = jnp.zeros((LIVE, HD), jnp.float32)
    for query_ref, grad_ref, attend_ref, out_ref in zip(
        query_refs, grad_refs, attend_refs, out_refs
    ):
        attend = attend_ref[0]
        dattend = lax.dot_general(values, grad_ref[...], ROWS, preferred_element_type=jnp.float32)
        delta = jnp.sum(attend * dattend, axis=0, keepdims=True)
        dscores = (attend * (dattend - delta)).astype(jnp.bfloat16)
        out = lax.dot_general(dscores, keys, COLUMNS, preferred_element_type=jnp.float32)
        out_ref[...] = (out * FACTOR).astype(jnp.bfloat16)
        key_grad += jnp.dot(dscores, query_ref[...], preferred_element_type=jnp.float32)
    scaled = key_grad * FACTOR * gain_ref[...]
    scaled_ref[...] = scaled

    @pl.when(pl.program_id(0) == 0)
    def _():
        inner_ref[...] = jnp.zeros_like(inner_ref)

    inner_ref[...] += scaled * raw_ref[...].astype(jnp.float32)


def specs(tokens):
    head = pl.BlockSpec((LIVE, HD), lambda h: (0, h))
    block = pl.BlockSpec((tokens, HD), lambda h: (0, h))
    weights = pl.BlockSpec((1, LIVE, tokens), lambda h: (h, 0, 0))
    gain = pl.BlockSpec((1, HD), lambda h: (0, h))
    return head, block, weights, gain


def attend_call(length, raw, inv, gain, queries, grads):
    parts = len(queries)
    tokens, cols = queries[0].shape
    heads = cols // HD
    head, block, weights, gains = specs(tokens)
    outs = pl.pallas_call(
        functools.partial(attend_kernel, parts),
        grid=(heads,),
        in_specs=[
            pl.BlockSpec(memory_space=pltpu.SMEM),
            head,
            pl.BlockSpec((LIVE, 1), lambda h: (0, 0)),
            gains,
        ]
        + [block] * (2 * parts),
        out_specs=[weights] * parts + [head, head],
        out_shape=[jax.ShapeDtypeStruct((heads, LIVE, tokens), jnp.float32)] * parts
        + [jax.ShapeDtypeStruct((LIVE, cols), jnp.bfloat16)] * 2,
        compiler_params=pltpu.CompilerParams(vmem_limit_bytes=32 * 1024 * 1024),
        cost_estimate=pl.CostEstimate(
            flops=16 * parts * tokens * cols * LIVE,
            bytes_accessed=8 * parts * tokens * cols,
            transcendentals=parts * tokens * heads * LIVE,
        ),
    )(length, raw, inv, gain, *queries, *grads)
    return outs[:parts], outs[parts], outs[parts + 1]


def gradient_call(raw, keys, values, gain, queries, grads, attends):
    parts = len(queries)
    tokens, cols = queries[0].shape
    heads = cols // HD
    head, block, weights, gains = specs(tokens)
    outs = pl.pallas_call(
        functools.partial(gradient_kernel, parts),
        grid=(heads,),
        in_specs=[head, head, head, gains] + [block] * (2 * parts) + [weights] * parts,
        out_specs=[block] * parts + [head, pl.BlockSpec((LIVE, HD), lambda h: (0, 0))],
        out_shape=[jax.ShapeDtypeStruct((tokens, cols), jnp.bfloat16)] * parts
        + [
            jax.ShapeDtypeStruct((LIVE, cols), jnp.float32),
            jax.ShapeDtypeStruct((LIVE, HD), jnp.float32),
        ],
        compiler_params=pltpu.CompilerParams(vmem_limit_bytes=32 * 1024 * 1024),
        cost_estimate=pl.CostEstimate(
            flops=24 * parts * tokens * cols * LIVE,
            bytes_accessed=10 * parts * tokens * cols,
            transcendentals=0,
        ),
    )(raw, keys, values, gain, *queries, *grads, *attends)
    return outs[:parts], outs[parts], outs[parts + 1]


def after(x, *others):
    return lax.optimization_barrier((x, *others))[0]


def shards(n_dp, n_seq, query, caption, key_weight, value_weight, key_gain, lengths, out_grad):
    rows, cols = key_weight.shape
    hid = cols * n_seq
    lines = n_dp // 2
    me = lax.axis_index("dp")
    lane = lax.axis_index("seq")
    line, side = me // 2, me % 2

    def over_dp(x, step):
        return lax.ppermute(x, "dp", [(a, a ^ step) for a in range(n_dp)])

    def over_seq(x, step):
        return lax.ppermute(x, "seq", [(a, a ^ step) for a in range(n_seq)])

    def col_block(x, index, width):
        return lax.dynamic_slice(x, (0, index * width), (x.shape[0], width))

    captions = caption[0, :LIVE]
    key_partner = over_dp(key_weight, 1)
    value_partner = over_dp(after(value_weight, key_partner), 1)
    blocks = [col_block(captions, line, 2 * rows)] + [
        over_dp(col_block(captions, line ^ s, 2 * rows), 2 * s) for s in range(1, lines)
    ]
    own = [col_block(b, side, rows) for b in blocks]
    other = [col_block(b, 1 - side, rows) for b in blocks]

    moved = {}
    previous = ()
    for name, x in (("query", query[0]), ("grad", out_grad[0])):
        moved[name, 0] = col_block(x, lane, cols)
        for s in range(1, n_seq):
            part = col_block(x, lane ^ s, cols)
            if s > 1:
                part = after(part, *previous)
            moved[name, s] = over_seq(part, s)
            if s > 1:
                previous = (moved[name, s],)
    queries = [moved["query", s] for s in range(n_seq)]
    grads = [moved["grad", s] for s in range(n_seq)]
    half = (n_seq + 2) // 2

    def project(weight, partner, first, second):
        def product(chosen):
            a = jnp.concatenate([own[s] for s in chosen], axis=0)
            b = jnp.concatenate([other[s] for s in chosen], axis=0)
            return jnp.dot(a, weight, preferred_element_type=jnp.float32) + jnp.dot(
                b, partner, preferred_element_type=jnp.float32
            )

        odd = after(product([s for s in range(lines) if s & 1]), *first)
        total = product([s for s in range(lines) if not s & 1]) + over_dp(odd, 2)
        total = after(total, *second)
        chunks = lines // 2
        step = 2
        while chunks > 1:
            total = total.reshape(chunks // 2, 2, LIVE, cols)
            total = total[:, 0] + over_dp(total[:, 1], 2 * step)
            chunks //= 2
            step *= 2
        return lax.reduce_precision(total.reshape(LIVE, cols), 8, 7)

    raw_wide = project(key_weight, key_partner, queries[1:half], queries[half:])
    raw = raw_wide.astype(jnp.bfloat16)
    values = project(value_weight, value_partner, (), grads[1:half]).astype(jnp.bfloat16)

    def seq_sum(x):
        return functools.reduce(lambda a, b: a + b, [x] + [over_seq(x, s) for s in range(1, n_seq)])

    squares = seq_sum(jnp.sum(raw_wide * raw_wide, axis=-1, keepdims=True))
    inv_rms = lax.rsqrt(squares / hid + 1e-06)
    gain = lax.dynamic_slice(key_gain, (lane * cols,), (cols,)).reshape(1, cols)
    attends, keys, value_grad = attend_call(lengths, raw, inv_rms, gain, queries, grads)

    def gather(part):
        near = [part] + [over_dp(part, 2 * s) for s in range(1, lines)]
        return near + [over_dp(x, 1) for x in near]

    other_columns = over_dp(jnp.concatenate(other, axis=0), 1)
    columns = jnp.concatenate([*own, other_columns], axis=0)

    def weight_grad(parts):
        return lax.dot_general(
            columns,
            jnp.concatenate(parts, axis=0),
            COLUMNS,
            preferred_element_type=jnp.float32,
        )

    value_parts = gather(value_grad)
    outs, scaled, inner = gradient_call(raw, keys, values, gain, queries, grads, attends)
    inner_mean = seq_sum(jnp.sum(inner, axis=-1, keepdims=True)) / hid
    raw_grad = (inv_rms * scaled - raw_wide * inv_rms**3 * inner_mean).astype(jnp.bfloat16)
    key_parts = gather(raw_grad)

    placed = [outs[0]] + [over_seq(outs[s], s) for s in range(1, n_seq)]
    stacked = jnp.stack(placed)
    query_grad = jnp.concatenate(
        [lax.dynamic_index_in_dim(stacked, lane ^ h, 0, keepdims=False) for h in range(n_seq)],
        axis=1,
    )[None]
    return query_grad, weight_grad(key_parts), weight_grad(value_parts)


def solution(mesh):
    placed = (
        P("dp", "seq", None),
        P("dp", None, None),
        P("dp", "seq"),
        P("dp", "seq"),
        P(),
        P("dp"),
        P("dp", "seq", None),
    )
    return jax.shard_map(
        functools.partial(shards, mesh.shape["dp"], mesh.shape["seq"]),
        mesh=mesh,
        in_specs=placed,
        out_specs=(P("dp", "seq", None), P("dp", "seq"), P("dp", "seq")),
        check_vma=False,
    )
```

time: 991 us -> 257 us (0.26)
  waiting for transfers between devices: 840 us -> 133 us
  matrix products: 71.5 us -> 22.6 us
  starting transfers between devices: 0.68 us -> 41.8 us
  Pallas kernels: 0 us -> 22.5 us
  other arithmetic: 21.9 us -> 4.89 us
  between operations: 14.8 us -> 1.94 us
  local copies, waits for them, and re-layouts: 41.5 us -> 29.3 us
    reduce_scatter x3 -> x0, waiting for transfers between devices: 585 us -> none  [the longest x1 532 us: shards(): lax.psum_scatter(jnp.einsum('lc,lw->cw', columns, grad_pair, preferred_el...]
    all_gather x4 -> x0, waiting for transfers between devices: 254 us -> none  [the longest x1 129 us: shards(): lax.all_gather(key_weight, 'dp', axis=0, tiled=True)]
    ppermute x0 -> x39, waiting for transfers between devices: none -> 133 us  [the longest x24 101 us: over_dp(): return lax.ppermute(x, 'dp', [(a, a ^ step) for a in range(n_dp)])]
    ppermute x0 -> x39, starting transfers between devices: none -> 41.8 us  [the longest x24 31.8 us: over_dp(): return lax.ppermute(x, 'dp', [(a, a ^ step) for a in range(n_dp)])]
    dot_general x7 -> x10, matrix products: 59.3 us -> 22.6 us  [the longest x4 8.12 us: product(): jnp.dot(b, partner, preferred_element_type=jnp.float32)]
    pallas_call x0 -> x2, Pallas kernels: none -> 22.5 us  [the longest x1 11.7 us: gradient_call(): pl.pallas_call(functools.partial(gradient_kernel, parts), grid=(heads,),...]
    reshape x3 -> x0, local copies, waits for them, and re-layouts: 15.4 us -> none  [the longest x1 5.66 us: shards(): key_grad = (jnp.einsum('htl,thd->lhd', dscores, query_heads, preferred_el...]
    sub x1 -> x0, matrix products: 12.3 us -> none  [shards(): attend = jax.nn.softmax(scores, axis=-1)]
  transfers between devices with their start and end apart: 7 -> 39, of which waited for: 6 -> 19; matrix products, arithmetic and copies ran while one was open for 11% -> 19% of each run, Pallas kernels for 0% -> 5%
where the time goes in v1:
time: 257 us; the launch traced here: 256 us
  waiting for transfers between devices  133 us (52%)
  starting transfers between devices  41.8 us (16%)
  local copies, waits for them, and re-layouts  29.3 us (11%)
  matrix products  22.6 us (9%)
  Pallas kernels  22.5 us (9%)
  other arithmetic  4.89 us (2%)
    ppermute x24, waiting for transfers between devices, over_dp(): return lax.ppermute(x, 'dp', [(a, a ^ step) for a in range(n_dp)])  101 us
    ppermute x15, waiting for transfers between devices, over_seq(): return lax.ppermute(x, 'seq', [(a, a ^ step) for a in range(n_seq)])  31.8 us
    ppermute x24, starting transfers between devices, over_dp(): return lax.ppermute(x, 'dp', [(a, a ^ step) for a in range(n_dp)])  31.8 us
    unnamed x89, local copies, waits for them, and re-layouts  16.2 us
    pallas_call x1, Pallas kernels, gradient_call(): pl.pallas_call(functools.partial(gradient_kernel, parts), grid=(heads,),...  11.7 us
    pallas_call x1, Pallas kernels, attend_call(): pl.pallas_call(functools.partial(attend_kernel, parts), grid=(heads,), in...  10.8 us
    ppermute x15, starting transfers between devices, over_seq(): return lax.ppermute(x, 'seq', [(a, a ^ step) for a in range(n_seq)])  10 us
    dot_general x4, matrix products, product(): jnp.dot(b, partner, preferred_element_type=jnp.float32)  8.12 us
  transfers between devices with their start and end apart: 39, of which 19 were waited for; matrix products, arithmetic and copies ran while one was open for 19% of the time, Pallas kernels for 5%

profile of v1, /device:TPU:0, one launch (start us, length us, event | category | flops | bytes accessed | tf_op | source)
XLA Modules:
  0.0 256.2 jit_solution(3230219833680193479)
XLA Ops:
  0.6 3.0 %collective-permute-start.1 = (bf16[512,1024]{1,0:T(8,128)(2,1)}, bf16[512,1024]{1,0:T(8,128)(2,1)}, u32[]{:S(2)}, u32[]{:S(2)}) collective-permute-start(bf16[512,1024]{1,0:T(8,128)(2,1)} %param.9), channel_id=1, source_target_pairs={{0,4},{4,0},{8,12},{12,8},{16,20},{20,16},{24,28},{28,24},{1,5},{5... | collective-permute-start | bytes 3145736 | tf_op jit(solution)/shard_map/ppermute | solution.py:140
  5.9 2.6 %collective-permute-start = (bf16[128,1024]{1,0:T(8,128)(2,1)}, bf16[128,1024]{1,0:T(8,128)(2,1)}, u32[]{:S(2)}, u32[]{:S(2)}) collective-permute-start(bf16[128,1024]{1,0:T(8,128)(2,1)} %get-tuple-element.66), channel_id=1, source_target_pairs={{0,16},{4,20},{8,24},{12,28},{16,0},{20,4},{24,8},{28,12},{1,17},{... | collective-permute-start | bytes 786440 | tf_op jit(solution)/shard_map/ppermute | solution.py:140
  10.1 3.4 %dynamic-slice_bitcast_fusion.8 = (bf16[384,1024]{1,0:T(8,128)(2,1)S(1)}, bf16[384,1024]{1,0:T(8,128)(2,1)}, bf16[384,1024]{1,0:T(8,128)(2,1)}, bf16[384,1024]{1,0:T(8,128)(2,1)}) fusion(bf16[1,384,4096]{2,1,0:T(8,128)(2,1)} %param.7, s32[]{:T(128)S(6)} %select_n.85, s32[]{:T(128)S(6)} %select_n.83, s32[]{:T(128)S(6)} %select_n.82, s32[]{:T(128)S(6)} %select_n.84), kind=kLoop, calls=%fused_computation.16 | loop fusion | bytes 6291472 | tf_op jit(solution)/shard_map/dynamic_slice | solution.py:146
  17.6 9.5 %collective-permute-done.2 = bf16[128,1024]{1,0:T(8,128)(2,1)S(1)} collective-permute-done((bf16[128,1024]{1,0:T(8,128)(2,1)S(1)}, bf16[128,1024]{1,0:T(8,128)(2,1)S(1)}, u32[]{:S(2)}, u32[]{:S(2)}) %collective-permute-start.2) | collective-permute-done | bytes 262176 | tf_op jit(solution)/shard_map/ppermute | solution.py:140
  44.9 9.0 %collective-permute-done.21 = bf16[512,512]{1,0:T(8,128)(2,1)} collective-permute-done((bf16[512,512]{1,0:T(8,128)(2,1)}, bf16[512,512]{1,0:T(8,128)(2,1)}, u32[]{:S(2)}, u32[]{:S(2)}) %collective-permute-start.21) | collective-permute-done | bytes 524320 | tf_op jit(solution)/shard_map/ppermute | solution.py:140
  63.4 3.8 %collective-permute-start.8 = (f32[1,128,1024]{2,1,0:T(8,128)S(1)}, f32[1,128,1024]{2,1,0:T(8,128)S(1)}, u32[]{:S(2)}, u32[]{:S(2)}) collective-permute-start(f32[1,128,1024]{2,1,0:T(8,128)S(1)} %slice_bitcast_fusion.2), channel_id=1, source_target_pairs={{0,16},{4,20},{8,24},{12,28},{16,0},{20,4},{24,8},{28,12},{1,17},{... | collective-permute-start | bytes 1572872 | tf_op jit(solution)/shard_map/ppermute | solution.py:140
  67.2 7.9 %collective-permute-done.15 = bf16[512,1024]{1,0:T(8,128)(2,1)} collective-permute-done((bf16[512,1024]{1,0:T(8,128)(2,1)}, bf16[512,1024]{1,0:T(8,128)(2,1)}, u32[]{:S(2)}, u32[]{:S(2)}) %collective-permute-start.15) | collective-permute-done | bytes 1048608 | tf_op jit(solution)/shard_map/ppermute | solution.py:140
  76.8 2.6 %convolution_add_fusion = f32[256,1024]{1,0:T(8,128)} fusion(f32[256,1024]{1,0:T(8,128)S(1)} %fusion.9, bf16[512,1024]{1,0:T(8,128)(2,1)} %param.10, bf16[128,512]{1,0:T(8,128)(2,1)S(1)} %copy-done.33, bf16[128,512]{1,0:T(8,128)(2,1)S(1)} %copy-done.31), kind=kOutput, calls=%fused_computation.2 | convolution fusion | flops 269221888 | bytes 3407872 | tf_op jit(solution)/shard_map/dot_general | solution.py:176
  79.7 2.7 %fusion.11 = f32[256,1024]{1,0:T(8,128)} fusion(bf16[512,1024]{1,0:T(8,128)(2,1)} %collective-permute-done.15, bf16[128,512]{1,0:T(8,128)(2,1)S(1)} %get-tuple-element.69, bf16[128,512]{1,0:T(8,128)(2,1)S(1)} %dynamic-slice_bitcast_fusion.15), kind=kOutput, calls=%fused_computation.43 | convolution fusion | flops 268959744 | bytes 2359296 | tf_op jit(solution)/shard_map/dot_general | solution.py:176
  83.3 6.6 %collective-permute-done.8 = f32[1,128,1024]{2,1,0:T(8,128)S(1)} collective-permute-done((f32[1,128,1024]{2,1,0:T(8,128)S(1)}, f32[1,128,1024]{2,1,0:T(8,128)S(1)}, u32[]{:S(2)}, u32[]{:S(2)}) %collective-permute-start.8) | collective-permute-done | bytes 524320 | tf_op jit(solution)/shard_map/ppermute | solution.py:140
  93.7 11.0 %collective-permute-done.11 = f32[128,1]{1,0:T(8,128)S(1)} collective-permute-done((f32[128,1]{1,0:T(8,128)S(1)}, f32[128,1]{1,0:T(8,128)S(1)}, u32[]{:S(2)}, u32[]{:S(2)}) %collective-permute-start.11) | collective-permute-done | bytes 544 | tf_op jit(solution)/shard_map/ppermute | solution.py:143
  106.3 6.0 %collective-permute-done.16 = f32[256,1024]{1,0:T(8,128)} collective-permute-done((f32[256,1024]{1,0:T(8,128)}, f32[256,1024]{1,0:T(8,128)}, u32[]{:S(2)}, u32[]{:S(2)}) %collective-permute-start.16) | collective-permute-done | bytes 1048608 | tf_op jit(solution)/shard_map/ppermute | solution.py:140
  114.7 10.8 %shard_map.94 = (f32[8,128,384]{2,1,0:T(8,128)S(1)}, f32[8,128,384]{2,1,0:T(8,128)S(1)}, f32[8,128,384]{2,1,0:T(8,128)S(1)}, f32[8,128,384]{2,1,0:T(8,128)S(1)},...) custom-call(s32[1]{0:T(128)S(6)} %copy.51.length_ref, bf16[128,1024]{1,0:T(8,128)(2,1)S(1)} %fusion.22.raw_ref, ...), custom_call_target="tpu_custom_call" | custom-call | flops 3221225472 | bytes 12582912 | tf_op jit(solution)/shard_map/pallas_call | solution.py:79
  131.9 4.8 %collective-permute-done.34 = bf16[128,1024]{1,0:T(8,128)(2,1)S(1)} collective-permute-done((bf16[128,1024]{1,0:T(8,128)(2,1)S(1)}, bf16[128,1024]{1,0:T(8,128)(2,1)S(1)}, u32[]{:S(2)}, u32[]{:S(2)}) %collective-permute-start.34) | collective-permute-done | bytes 262176 | tf_op jit(solution)/shard_map/ppermute | solution.py:140
  137.2 24.7 %collective-permute-done.33 = bf16[128,1024]{1,0:T(8,128)(2,1)} collective-permute-done((bf16[128,1024]{1,0:T(8,128)(2,1)S(1)}, bf16[128,1024]{1,0:T(8,128)(2,1)}, u32[]{:S(2)}, u32[]{:S(2)}) %collective-permute-start.33) | collective-permute-done | bytes 262176 | tf_op jit(solution)/shard_map/ppermute | solution.py:140
  166.0 6.1 %collective-permute-done.17 = f32[1,128,1024]{2,1,0:T(8,128)S(1)} collective-permute-done((f32[1,128,1024]{2,1,0:T(8,128)S(1)}, f32[1,128,1024]{2,1,0:T(8,128)S(1)}, u32[]{:S(2)}, u32[]{:S(2)}) %collective-permute-start.17) | collective-permute-done | bytes 524320 | tf_op jit(solution)/shard_map/ppermute | solution.py:140
  172.2 11.7 %shard_map.95 = (bf16[384,1024]{1,0:T(8,128)(2,1)S(1)}, bf16[384,1024]{1,0:T(8,128)(2,1)S(1)}, bf16[384,1024]{1,0:T(8,128)(2,1)S(1)}, bf16[384,1024]{1,0:T(8,128...) custom-call(bf16[128,1024]{1,0:T(8,128)(2,1)S(1)} %fusion.22.raw_ref, ...), custom_call_target="tpu_custom_call" | custom-call | flops 4831838208 | bytes 15728640 | tf_op jit(solution)/shard_map/pallas_call | solution.py:107
  198.8 3.8 %fusion.25 = f32[512,1024]{1,0:T(8,128)} fusion(bf16[1024,512]{1,0:T(8,128)(2,1)} %constant_dynamic-update-slice_fusion, bf16[1024,1024]{1,0:T(8,128)(2,1)S(1)} %copy-done.24), kind=kOutput, calls=%fused_computation.90 | convolution fusion | flops 1073741824 | bytes 5242880 | tf_op jit(solution)/shard_map/dot_general | solution.py:212
  203.1 10.9 %collective-permute-done.25 = bf16[128,1024]{1,0:T(8,128)(2,1)S(1)} collective-permute-done((bf16[128,1024]{1,0:T(8,128)(2,1)S(1)}, bf16[128,1024]{1,0:T(8,128)(2,1)S(1)}, u32[]{:S(2)}, u32[]{:S(2)}) %collective-permute-start.25) | collective-permute-done | bytes 262176 | tf_op jit(solution)/shard_map/ppermute | solution.py:140
  215.0 3.6 %collective-permute-done.26 = bf16[128,1024]{1,0:T(8,128)(2,1)S(1)} collective-permute-done((bf16[128,1024]{1,0:T(8,128)(2,1)S(1)}, bf16[128,1024]{1,0:T(8,128)(2,1)S(1)}, u32[]{:S(2)}, u32[]{:S(2)}) %collective-permute-start.26) | collective-permute-done | bytes 262176 | tf_op jit(solution)/shard_map/ppermute | solution.py:140
  223.0 6.5 %collective-permute-done.30 = bf16[128,1024]{1,0:T(8,128)(2,1)S(1)} collective-permute-done((bf16[128,1024]{1,0:T(8,128)(2,1)S(1)}, bf16[128,1024]{1,0:T(8,128)(2,1)S(1)}, u32[]{:S(2)}, u32[]{:S(2)}) %collective-permute-start.30) | collective-permute-done | bytes 262176 | tf_op jit(solution)/shard_map/ppermute | solution.py:140
  229.5 4.0 %collective-permute-done.31 = bf16[128,1024]{1,0:T(8,128)(2,1)S(1)} collective-permute-done((bf16[128,1024]{1,0:T(8,128)(2,1)S(1)}, bf16[128,1024]{1,0:T(8,128)(2,1)S(1)}, u32[]{:S(2)}, u32[]{:S(2)}) %collective-permute-start.31) | collective-permute-done | bytes 262176 | tf_op jit(solution)/shard_map/ppermute | solution.py:140
  236.1 3.0 %collective-permute-done.19 = bf16[384,1024]{1,0:T(8,128)(2,1)S(1)} collective-permute-done((bf16[384,1024]{1,0:T(8,128)(2,1)S(1)}, bf16[384,1024]{1,0:T(8,128)(2,1)S(1)}, u32[]{:S(2)}, u32[]{:S(2)}) %collective-permute-start.19) | collective-permute-done | bytes 786464 | tf_op jit(solution)/shard_map/ppermute | solution.py:143
  239.1 14.6 %collective-permute-done.20 = bf16[384,1024]{1,0:T(8,128)(2,1)S(1)} collective-permute-done((bf16[384,1024]{1,0:T(8,128)(2,1)S(1)}, bf16[384,1024]{1,0:T(8,128)(2,1)S(1)}, u32[]{:S(2)}, u32[]{:S(2)}) %collective-permute-start.20) | collective-permute-done | bytes 786464 | tf_op jit(solution)/shard_map/ppermute | solution.py:143
  (181 shorter events, 81.9 us)
Async XLA Ops:
  0.6 31.0 %collective-permute-start.1 = (bf16[512,1024]{1,0:T(8,128)(2,1)}, bf16[512,1024]{1,0:T(8,128)(2,1)}, u32[]{:S(2)}, u32[]{:S(2)}) collective-permute-start(bf16[512,1024]{1,0:T(8,128)(2,1)} %param.9), channel_id=1, source_target_pairs={{0,4},{4,0},{8,12},{12,8},{16,20},{20,16},{24,28},{28,24},{1,5},{5... | collective-permute-start | bytes 3145736 | tf_op jit(solution)/shard_map/ppermute | solution.py:140
  5.9 23.0 %collective-permute-start = (bf16[128,1024]{1,0:T(8,128)(2,1)}, bf16[128,1024]{1,0:T(8,128)(2,1)}, u32[]{:S(2)}, u32[]{:S(2)}) collective-permute-start(bf16[128,1024]{1,0:T(8,128)(2,1)} %get-tuple-element.66), channel_id=1, source_target_pairs={{0,16},{4,20},{8,24},{12,28},{16,0},{20,4},{24,8},{28,12},{1,17},{... | collective-permute-start | bytes 786440 | tf_op jit(solution)/shard_map/ppermute | solution.py:140
  8.5 22.1 %collective-permute-start.3 = (bf16[128,1024]{1,0:T(8,128)(2,1)S(1)}, bf16[128,1024]{1,0:T(8,128)(2,1)}, u32[]{:S(2)}, u32[]{:S(2)}) collective-permute-start(bf16[128,1024]{1,0:T(8,128)(2,1)S(1)} %get-tuple-element.67), channel_id=1, source_target_pairs={{0,24},{4,28},{8,16},{12,20},{16,8},{20,12},{24,0},{28,4},{1,25},{... | collective-permute-start | bytes 786440 | tf_op jit(solution)/shard_map/ppermute | solution.py:140
  13.4 21.8 %collective-permute-start.5 = (bf16[384,1024]{1,0:T(8,128)(2,1)}, bf16[384,1024]{1,0:T(8,128)(2,1)S(1)}, u32[]{:S(2)}, u32[]{:S(2)}) collective-permute-start(bf16[384,1024]{1,0:T(8,128)(2,1)} %get-tuple-element.63), channel_id=1, source_target_pairs={{0,2},{1,3},{2,0},{3,1},{4,6},{5,7},{6,4},{7,5},{8,10},{9,11},{10,... | collective-permute-start | bytes 2359304 | tf_op jit(solution)/shard_map/ppermute | solution.py:143
  36.2 25.4 %collective-permute-start.6 = (f32[256,1024]{1,0:T(8,128)}, f32[256,1024]{1,0:T(8,128)}, u32[]{:S(2)}, u32[]{:S(2)}) collective-permute-start(f32[256,1024]{1,0:T(8,128)} %convolution_add_fusion.2), channel_id=1, source_target_pairs={{0,8},{4,12},{8,0},{12,4},{16,24},{20,28},{24,16},{28,20},{1,9},{5... | collective-permute-start | bytes 3145736 | tf_op jit(solution)/shard_map/ppermute | solution.py:140
  39.2 20.0 %collective-permute-start.7 = (bf16[384,1024]{1,0:T(8,128)(2,1)}, bf16[384,1024]{1,0:T(8,128)(2,1)S(1)}, u32[]{:S(2)}, u32[]{:S(2)}) collective-permute-start(bf16[384,1024]{1,0:T(8,128)(2,1)} %get-tuple-element.23), channel_id=1, source_target_pairs={{0,3},{1,2},{2,1},{3,0},{4,7},{5,6},{6,5},{7,4},{8,11},{9,10},{10,... | collective-permute-start | bytes 2359304 | tf_op jit(solution)/shard_map/ppermute | solution.py:143
  39.8 35.3 %collective-permute-start.15 = (bf16[512,1024]{1,0:T(8,128)(2,1)}, bf16[512,1024]{1,0:T(8,128)(2,1)}, u32[]{:S(2)}, u32[]{:S(2)}) collective-permute-start(bf16[512,1024]{1,0:T(8,128)(2,1)} %param.10), channel_id=1, source_target_pairs={{0,4},{4,0},{8,12},{12,8},{16,20},{20,16},{24,28},{28,24},{1,5},{5... | collective-permute-start | bytes 3145736 | tf_op jit(solution)/shard_map/ppermute | solution.py:140
  42.8 71.9 %collective-permute-start.12 = (bf16[384,1024]{1,0:T(8,128)(2,1)}, bf16[384,1024]{1,0:T(8,128)(2,1)}, u32[]{:S(2)}, u32[]{:S(2)}) collective-permute-start(bf16[384,1024]{1,0:T(8,128)(2,1)} %get-tuple-element.59), channel_id=1, source_target_pairs={{0,1},{1,0},{2,3},{3,2},{4,5},{5,4},{6,7},{7,6},{8,9},{9,8},{10,11... | collective-permute-start | bytes 2359304 | tf_op jit(solution)/shard_map/ppermute | solution.py:143
  59.2 23.1 %collective-permute-start.13 = (bf16[384,1024]{1,0:T(8,128)(2,1)S(1)}, bf16[384,1024]{1,0:T(8,128)(2,1)S(1)}, u32[]{:S(2)}, u32[]{:S(2)}) collective-permute-start(bf16[384,1024]{1,0:T(8,128)(2,1)S(1)} %copy-done.34), channel_id=1, source_target_pairs={{0,2},{1,3},{2,0},{3,1},{4,6},{5,7},{6,4},{7,5},{8,10},{9,11},{10,... | collective-permute-start | bytes 2359304 | tf_op jit(solution)/shard_map/ppermute | solution.py:143
  63.4 26.4 %collective-permute-start.8 = (f32[1,128,1024]{2,1,0:T(8,128)S(1)}, f32[1,128,1024]{2,1,0:T(8,128)S(1)}, u32[]{:S(2)}, u32[]{:S(2)}) collective-permute-start(f32[1,128,1024]{2,1,0:T(8,128)S(1)} %slice_bitcast_fusion.2), channel_id=1, source_target_pairs={{0,16},{4,20},{8,24},{12,28},{16,0},{20,4},{24,8},{28,12},{1,17},{... | collective-permute-start | bytes 1572872 | tf_op jit(solution)/shard_map/ppermute | solution.py:140
  79.4 32.9 %collective-permute-start.16 = (f32[256,1024]{1,0:T(8,128)}, f32[256,1024]{1,0:T(8,128)}, u32[]{:S(2)}, u32[]{:S(2)}) collective-permute-start(f32[256,1024]{1,0:T(8,128)} %convolution_add_fusion), channel_id=1, source_target_pairs={{0,8},{4,12},{8,0},{12,4},{16,24},{20,28},{24,16},{28,20},{1,9},{5... | collective-permute-start | bytes 3145736 | tf_op jit(solution)/shard_map/ppermute | solution.py:140
  83.3 31.4 %collective-permute-start.14 = (bf16[384,1024]{1,0:T(8,128)(2,1)}, bf16[384,1024]{1,0:T(8,128)(2,1)}, u32[]{:S(2)}, u32[]{:S(2)}) collective-permute-start(bf16[384,1024]{1,0:T(8,128)(2,1)} %get-tuple-element.26), channel_id=1, source_target_pairs={{0,3},{1,2},{2,1},{3,0},{4,7},{5,6},{6,5},{7,4},{8,11},{9,10},{10,... | collective-permute-start | bytes 2359304 | tf_op jit(solution)/shard_map/ppermute | solution.py:143
  127.9 34.1 %collective-permute-start.33 = (bf16[128,1024]{1,0:T(8,128)(2,1)S(1)}, bf16[128,1024]{1,0:T(8,128)(2,1)}, u32[]{:S(2)}, u32[]{:S(2)}) collective-permute-start(bf16[128,1024]{1,0:T(8,128)(2,1)S(1)} %get-tuple-element.40), channel_id=1, source_target_pairs={{0,16},{4,20},{8,24},{12,28},{16,0},{20,4},{24,8},{28,12},{1,17},{... | collective-permute-start | bytes 786440 | tf_op jit(solution)/shard_map/ppermute | solution.py:140
  127.9 34.6 %collective-permute-start.32 = (bf16[128,1024]{1,0:T(8,128)(2,1)S(1)}, bf16[128,1024]{1,0:T(8,128)(2,1)}, u32[]{:S(2)}, u32[]{:S(2)}) collective-permute-start(bf16[128,1024]{1,0:T(8,128)(2,1)S(1)} %get-tuple-element.40), channel_id=1, source_target_pairs={{0,8},{4,12},{8,0},{12,4},{16,24},{20,28},{24,16},{28,20},{1,9},{5... | collective-permute-start | bytes 786440 | tf_op jit(solution)/shard_map/ppermute | solution.py:140
  130.0 42.1 %collective-permute-start.17 = (f32[1,128,1024]{2,1,0:T(8,128)S(1)}, f32[1,128,1024]{2,1,0:T(8,128)S(1)}, u32[]{:S(2)}, u32[]{:S(2)}) collective-permute-start(f32[1,128,1024]{2,1,0:T(8,128)S(1)} %slice_bitcast_fusion), channel_id=1, source_target_pairs={{0,16},{4,20},{8,24},{12,28},{16,0},{20,4},{24,8},{28,12},{1,17},{... | collective-permute-start | bytes 1572872 | tf_op jit(solution)/shard_map/ppermute | solution.py:140
  130.9 35.0 %collective-permute-start.35 = (bf16[128,1024]{1,0:T(8,128)(2,1)S(1)}, bf16[128,1024]{1,0:T(8,128)(2,1)S(1)}, u32[]{:S(2)}, u32[]{:S(2)}) collective-permute-start(bf16[128,1024]{1,0:T(8,128)(2,1)S(1)} %get-tuple-element.40), channel_id=1, source_target_pairs={{0,4},{4,0},{8,12},{12,8},{16,20},{20,16},{24,28},{28,24},{1,5},{5... | collective-permute-start | bytes 786440 | tf_op jit(solution)/shard_map/ppermute | solution.py:140
  136.7 55.6 %collective-permute-start.38 = (bf16[128,1024]{1,0:T(8,128)(2,1)S(1)}, bf16[128,1024]{1,0:T(8,128)(2,1)}, u32[]{:S(2)}, u32[]{:S(2)}) collective-permute-start(bf16[128,1024]{1,0:T(8,128)(2,1)S(1)} %collective-permute-done.34), channel_id=1, source_target_pairs={{0,4},{4,0},{8,12},{12,8},{16,20},{20,16},{24,28},{28,24},{1,5},{5... | collective-permute-start | bytes 786440 | tf_op jit(solution)/shard_map/ppermute | solution.py:140
  161.9 28.5 %collective-permute-start.37 = (bf16[128,1024]{1,0:T(8,128)(2,1)}, bf16[128,1024]{1,0:T(8,128)(2,1)}, u32[]{:S(2)}, u32[]{:S(2)}) collective-permute-start(bf16[128,1024]{1,0:T(8,128)(2,1)} %collective-permute-done.33), channel_id=1, source_target_pairs={{0,4},{4,0},{8,12},{12,8},{16,20},{20,16},{24,28},{28,24},{1,5},{5... | collective-permute-start | bytes 786440 | tf_op jit(solution)/shard_map/ppermute | solution.py:140
  162.4 26.0 %collective-permute-start.36 = (bf16[128,1024]{1,0:T(8,128)(2,1)}, bf16[128,1024]{1,0:T(8,128)(2,1)}, u32[]{:S(2)}, u32[]{:S(2)}) collective-permute-start(bf16[128,1024]{1,0:T(8,128)(2,1)} %collective-permute-done.32), channel_id=1, source_target_pairs={{0,4},{4,0},{8,12},{12,8},{16,20},{20,16},{24,28},{28,24},{1,5},{5... | collective-permute-start | bytes 786440 | tf_op jit(solution)/shard_map/ppermute | solution.py:140
  190.4 45.7 %collective-permute-start.18 = (bf16[384,1024]{1,0:T(8,128)(2,1)}, bf16[384,1024]{1,0:T(8,128)(2,1)S(1)}, u32[]{:S(2)}, u32[]{:S(2)}) collective-permute-start(bf16[384,1024]{1,0:T(8,128)(2,1)} %copy-done.12), channel_id=1, source_target_pairs={{0,1},{1,0},{2,3},{3,2},{4,5},{5,4},{6,7},{7,6},{8,9},{9,8},{10,11... | collective-permute-start | bytes 2359304 | tf_op jit(solution)/shard_map/ppermute | solution.py:143
  194.3 25.8 %collective-permute-start.27 = (bf16[128,1024]{1,0:T(8,128)(2,1)S(1)}, bf16[128,1024]{1,0:T(8,128)(2,1)S(1)}, u32[]{:S(2)}, u32[]{:S(2)}) collective-permute-start(bf16[128,1024]{1,0:T(8,128)(2,1)S(1)} %get-tuple-element.44), channel_id=1, source_target_pairs={{0,24},{4,28},{8,16},{12,20},{16,8},{20,12},{24,0},{28,4},{1,25},{... | collective-permute-start | bytes 786440 | tf_op jit(solution)/shard_map/ppermute | solution.py:140
  196.7 22.0 %collective-permute-start.26 = (bf16[128,1024]{1,0:T(8,128)(2,1)S(1)}, bf16[128,1024]{1,0:T(8,128)(2,1)S(1)}, u32[]{:S(2)}, u32[]{:S(2)}) collective-permute-start(bf16[128,1024]{1,0:T(8,128)(2,1)S(1)} %get-tuple-element.44), channel_id=1, source_target_pairs={{0,16},{4,20},{8,24},{12,28},{16,0},{20,4},{24,8},{28,12},{1,17},{... | collective-permute-start | bytes 786440 | tf_op jit(solution)/shard_map/ppermute | solution.py:140
  218.6 20.5 %collective-permute-start.19 = (bf16[384,1024]{1,0:T(8,128)(2,1)S(1)}, bf16[384,1024]{1,0:T(8,128)(2,1)S(1)}, u32[]{:S(2)}, u32[]{:S(2)}) collective-permute-start(bf16[384,1024]{1,0:T(8,128)(2,1)S(1)} %copy-done.11), channel_id=1, source_target_pairs={{0,2},{1,3},{2,0},{3,1},{4,6},{5,7},{6,4},{7,5},{8,10},{9,11},{10,... | collective-permute-start | bytes 2359304 | tf_op jit(solution)/shard_map/ppermute | solution.py:143
  220.9 32.7 %collective-permute-start.20 = (bf16[384,1024]{1,0:T(8,128)(2,1)S(1)}, bf16[384,1024]{1,0:T(8,128)(2,1)S(1)}, u32[]{:S(2)}, u32[]{:S(2)}) collective-permute-start(bf16[384,1024]{1,0:T(8,128)(2,1)S(1)} %copy-done.9), channel_id=1, source_target_pairs={{0,3},{1,2},{2,1},{3,0},{4,7},{5,6},{6,5},{7,4},{8,11},{9,10},{10,... | collective-permute-start | bytes 2359304 | tf_op jit(solution)/shard_map/ppermute | solution.py:143
  (51 other events, 657.9 us)

commit v2 on v1

--- a/solution.py
+++ b/solution.py
@@ -90,11 +90,7 @@
         out_shape=[jax.ShapeDtypeStruct((heads, LIVE, tokens), jnp.float32)] * parts
         + [jax.ShapeDtypeStruct((LIVE, cols), jnp.bfloat16)] * 2,
         compiler_params=pltpu.CompilerParams(vmem_limit_bytes=32 * 1024 * 1024),
-        cost_estimate=pl.CostEstimate(
-            flops=16 * parts * tokens * cols * LIVE,
-            bytes_accessed=8 * parts * tokens * cols,
-            transcendentals=parts * tokens * heads * LIVE,
-        ),
+        cost_estimate=pl.CostEstimate(flops=1000, bytes_accessed=1000, transcendentals=0),
     )(length, raw, inv, gain, *queries, *grads)
     return outs[:parts], outs[parts], outs[parts + 1]
 
@@ -117,13 +113,43 @@
         compiler_params=pltpu.CompilerParams(vmem_limit_bytes=32 * 1024 * 1024),
         cost_estimate=pl.CostEstimate(
             flops=24 * parts * tokens * cols * LIVE,
-            bytes_accessed=10 * parts * tokens * cols,
+            bytes_accessed=16 * parts * tokens * cols,
             transcendentals=0,
         ),
     )(raw, keys, values, gain, *queries, *grads, *attends)
     return outs[:parts], outs[parts], outs[parts + 1]
 
 
+def product_kernel(videos, place_ref, *refs):
+    mine_refs, sibling_refs = refs[:videos], refs[videos : 2 * videos]
+    weight_refs, out_ref = refs[2 * videos : -1], refs[-1]
+    rows = weight_refs[0].shape[0]
+    total = None
+    for step, weight_ref in enumerate(weight_refs):
+        here = place_ref[step // 2] == 0
+        at = pl.ds(pl.multiple_of(place_ref[2 + step % 2] * rows, rows), rows)
+        block = jnp.concatenate(
+            [jnp.where(here, m[:, at], s[:, at]) for m, s in zip(mine_refs, sibling_refs)], axis=0
+        )
+        term = jnp.dot(block, weight_ref[...], preferred_element_type=jnp.float32)
+        total = term if total is None else total + term
+    out_ref[...] = total
+
+
+def product_call(place, mine, sibling, weights):
+    videos = len(mine)
+    width = weights[0].shape[1]
+    return pl.pallas_call(
+        functools.partial(product_kernel, videos),
+        in_specs=[pl.BlockSpec(memory_space=pltpu.SMEM)]
+        + [pl.BlockSpec(memory_space=pltpu.VMEM)] * (2 * videos + 4),
+        out_specs=pl.BlockSpec(memory_space=pltpu.VMEM),
+        out_shape=jax.ShapeDtypeStruct((videos * LIVE, width), jnp.float32),
+        compiler_params=pltpu.CompilerParams(vmem_limit_bytes=32 * 1024 * 1024),
+        cost_estimate=pl.CostEstimate(flops=1000, bytes_accessed=1000, transcendentals=0),
+    )(place, *mine, *sibling, *weights)
+
+
 def after(x, *others):
     return lax.optimization_barrier((x, *others))[0]
 
@@ -132,9 +158,11 @@
     rows, cols = key_weight.shape
     hid = cols * n_seq
     lines = n_dp // 2
+    half = cols // 2
     me = lax.axis_index("dp")
     lane = lax.axis_index("seq")
-    line, side = me // 2, me % 2
+    quad, low, side = me // 4, me // 2 % 2, me % 2
+    core = lane % 2
 
     def over_dp(x, step):
         return lax.ppermute(x, "dp", [(a, a ^ step) for a in range(n_dp)])
@@ -145,53 +173,57 @@
     def col_block(x, index, width):
         return lax.dynamic_slice(x, (0, index * width), (x.shape[0], width))
 
+    def spread(weight):
+        kept = col_block(weight, low, half)
+        near = over_dp(col_block(weight, 1 - low, half), 2)
+        return kept, over_dp(kept, 1), near, over_dp(near, 1)
+
+    key_quad = spread(key_weight)
+
     captions = caption[0, :LIVE]
-    key_partner = over_dp(key_weight, 1)
-    value_partner = over_dp(after(value_weight, key_partner), 1)
-    blocks = [col_block(captions, line, 2 * rows)] + [
-        over_dp(col_block(captions, line ^ s, 2 * rows), 2 * s) for s in range(1, lines)
+    mine, sibling = [col_block(captions, quad * 2 + core, 2 * rows)], [
+        col_block(captions, quad * 2 + 1 - core, 2 * rows)
     ]
-    own = [col_block(b, side, rows) for b in blocks]
-    other = [col_block(b, 1 - side, rows) for b in blocks]
+    for s in range(1, lines):
+        block = over_dp(col_block(captions, (quad ^ (s // 2)) * 2 + core, 2 * rows), 2 * s)
+        mine.append(block)
+        sibling.append(over_seq(block, 1))
+    value_quad = spread(value_weight)
 
     moved = {}
-    previous = ()
     for name, x in (("query", query[0]), ("grad", out_grad[0])):
         moved[name, 0] = col_block(x, lane, cols)
         for s in range(1, n_seq):
-            part = col_block(x, lane ^ s, cols)
-            if s > 1:
-                part = after(part, *previous)
-            moved[name, s] = over_seq(part, s)
-            if s > 1:
-                previous = (moved[name, s],)
+            moved[name, s] = over_seq(col_block(x, lane ^ s, cols), s)
     queries = [moved["query", s] for s in range(n_seq)]
     grads = [moved["grad", s] for s in range(n_seq)]
-    half = (n_seq + 2) // 2
-
-    def project(weight, partner, first, second):
+
+    place = jnp.stack([core ^ low, 1 - (core ^ low), side, 1 - side]).astype(jnp.int32)
+
+    def project(weights, first, second):
         def product(chosen):
-            a = jnp.concatenate([own[s] for s in chosen], axis=0)
-            b = jnp.concatenate([other[s] for s in chosen], axis=0)
-            return jnp.dot(a, weight, preferred_element_type=jnp.float32) + jnp.dot(
-                b, partner, preferred_element_type=jnp.float32
-            )
-
-        odd = after(product([s for s in range(lines) if s & 1]), *first)
-        total = product([s for s in range(lines) if not s & 1]) + over_dp(odd, 2)
+            return product_call(place, [mine[s] for s in chosen], [sibling[s] for s in chosen], weights)
+
+        sent = after(product([s for s in range(lines) if s & 2]), *first)
+        total = product([s for s in range(lines) if not s & 2]) + over_dp(sent, 4)
         total = after(total, *second)
-        chunks = lines // 2
-        step = 2
-        while chunks > 1:
-            total = total.reshape(chunks // 2, 2, LIVE, cols)
-            total = total[:, 0] + over_dp(total[:, 1], 2 * step)
-            chunks //= 2
+        step = 8
+        while step < n_dp:
+            count = total.shape[0] // 2
+            total = total[:count] + over_dp(total[count:], step)
             step *= 2
-        return lax.reduce_precision(total.reshape(LIVE, cols), 8, 7)
-
-    raw_wide = project(key_weight, key_partner, queries[1:half], queries[half:])
-    raw = raw_wide.astype(jnp.bfloat16)
-    values = project(value_weight, value_partner, (), grads[1:half]).astype(jnp.bfloat16)
+        total = lax.reduce_precision(total, 8, 7).astype(jnp.bfloat16)
+        kept, other = total[:LIVE], over_dp(total[LIVE:], 2)
+        return jnp.where(
+            low == 0,
+            jnp.concatenate([kept, other], axis=1),
+            jnp.concatenate([other, kept], axis=1),
+        )
+
+    middle = (n_seq + 2) // 2
+    raw = project(key_quad, (*value_quad[:2], *queries[1:middle]), queries[middle:])
+    values = project(value_quad, (), grads[1:middle])
+    raw_wide = raw.astype(jnp.float32)
 
     def seq_sum(x):
         return functools.reduce(lambda a, b: a + b, [x] + [over_seq(x, s) for s in range(1, n_seq)])
@@ -201,14 +233,16 @@
     gain = lax.dynamic_slice(key_gain, (lane * cols,), (cols,)).reshape(1, cols)
     attends, keys, value_grad = attend_call(lengths, raw, inv_rms, gain, queries, grads)
 
-    def gather(part):
+    def gather(part, before):
         near = [part] + [over_dp(part, 2 * s) for s in range(1, lines)]
-        return near + [over_dp(x, 1) for x in near]
-
-    other_columns = over_dp(jnp.concatenate(other, axis=0), 1)
-    columns = jnp.concatenate([*own, other_columns], axis=0)
-
-    def weight_grad(parts):
+        return near + [over_dp(part, 1)] + [over_dp(after(x, *before), 1) for x in near[1:]]
+
+    held = [jnp.where(core == low, m, s) for m, s in zip(mine, sibling)]
+    other_columns = over_dp(jnp.concatenate([col_block(x, 1 - side, rows) for x in held], axis=0), 1)
+    columns = jnp.concatenate([col_block(x, side, rows) for x in held] + [other_columns], axis=0)
+
+    def weight_grad(parts, before):
+        parts = lax.optimization_barrier((*parts, *before))[:n_dp]
         return lax.dot_general(
             columns,
             jnp.concatenate(parts, axis=0),
@@ -216,19 +250,19 @@
             preferred_element_type=jnp.float32,
         )
 
-    value_parts = gather(value_grad)
+    value_parts = gather(value_grad, ())
     outs, scaled, inner = gradient_call(raw, keys, values, gain, queries, grads, attends)
+    inner = after(inner, *value_parts[1:lines])
     inner_mean = seq_sum(jnp.sum(inner, axis=-1, keepdims=True)) / hid
     raw_grad = (inv_rms * scaled - raw_wide * inv_rms**3 * inner_mean).astype(jnp.bfloat16)
-    key_parts = gather(raw_grad)
-
-    placed = [outs[0]] + [over_seq(outs[s], s) for s in range(1, n_seq)]
+    placed = [outs[0]] + [over_seq(after(outs[s], inner_mean), s) for s in range(1, n_seq)]
+    key_parts = gather(raw_grad, placed[1:middle])
     stacked = jnp.stack(placed)
     query_grad = jnp.concatenate(
         [lax.dynamic_index_in_dim(stacked, lane ^ h, 0, keepdims=False) for h in range(n_seq)],
         axis=1,
     )[None]
-    return query_grad, weight_grad(key_parts), weight_grad(value_parts)
+    return query_grad, weight_grad(key_parts, placed[middle:]), weight_grad(value_parts, key_parts[1:lines])
 
 
 def solution(mesh):

time: 257 us -> 239 us (0.930)
  waiting for transfers between devices: 133 us -> 115 us
  matrix products: 22.6 us -> 5.18 us
  Pallas kernels: 22.5 us -> 29.7 us
  local copies, waits for them, and re-layouts: 29.3 us -> 34.1 us
  starting transfers between devices: 41.8 us -> 44.8 us
    dot_general x8 -> x0, matrix products: 16.2 us -> none  [the longest x4 8.12 us: product(): jnp.dot(b, partner, preferred_element_type=jnp.float32)]
    ppermute x24 -> x28, waiting for transfers between devices: 101 us -> 87.1 us  [over_dp(): return lax.ppermute(x, 'dp', [(a, a ^ step) for a in range(n_dp)])]
    pallas_call x0 -> x4, Pallas kernels: none -> 8 us  [product_call(): pl.pallas_call(functools.partial(product_kernel, videos), in_specs=[pl.Bl...]
    dynamic_slice x4 -> x9, local copies, waits for them, and re-layouts: 6.75 us -> 12.5 us  [col_block(): return lax.dynamic_slice(x, (0, index * width), (x.shape[0], width))]
    ppermute x15 -> x18, waiting for transfers between devices: 31.8 us -> 28.2 us  [over_seq(): return lax.ppermute(x, 'seq', [(a, a ^ step) for a in range(n_seq)])]
    ppermute x24 -> x28, starting transfers between devices: 31.8 us -> 35 us  [over_dp(): return lax.ppermute(x, 'dp', [(a, a ^ step) for a in range(n_dp)])]
    select_n x0 -> x5, other arithmetic: none -> 2.7 us  [the longest x4 1.91 us: shards(): held = [jnp.where(core == low, m, s) for m, s in zip(mine, sibling)]]
    unnamed x89 -> x100, local copies, waits for them, and re-layouts: 16.2 us -> 16.8 us
  transfers between devices with their start and end apart: 39 -> 46, of which waited for: 19 -> 20; matrix products, arithmetic and copies ran while one was open for 19% -> 12% of each run, Pallas kernels for 5% -> 12%
where the time goes in v2:
time: 239 us; the launch traced here: 238 us
  waiting for transfers between devices  115 us (48%)
  starting transfers between devices  44.8 us (19%)
  local copies, waits for them, and re-layouts  34.1 us (14%)
  Pallas kernels  29.7 us (12%)
  other arithmetic  7.45 us (3%)
  matrix products  5.18 us (2%)
    ppermute x28, waiting for transfers between devices, over_dp(): return lax.ppermute(x, 'dp', [(a, a ^ step) for a in range(n_dp)])  87.1 us
    ppermute x28, starting transfers between devices, over_dp(): return lax.ppermute(x, 'dp', [(a, a ^ step) for a in range(n_dp)])  35 us
    ppermute x18, waiting for transfers between devices, over_seq(): return lax.ppermute(x, 'seq', [(a, a ^ step) for a in range(n_seq)])  28.2 us
    unnamed x100, local copies, waits for them, and re-layouts  16.8 us
    dynamic_slice x9, local copies, waits for them, and re-layouts, col_block(): return lax.dynamic_slice(x, (0, index * width), (x.shape[0], width))  12.5 us
    pallas_call x1, Pallas kernels, gradient_call(): pl.pallas_call(functools.partial(gradient_kernel, parts), grid=(heads,),...  11.4 us
    pallas_call x1, Pallas kernels, attend_call(): pl.pallas_call(functools.partial(attend_kernel, parts), grid=(heads,), in...  10.3 us
    ppermute x18, starting transfers between devices, over_seq(): return lax.ppermute(x, 'seq', [(a, a ^ step) for a in range(n_seq)])  9.85 us
  transfers between devices with their start and end apart: 46, of which 20 were waited for; matrix products, arithmetic and copies ran while one was open for 12% of the time, Pallas kernels for 12%

profile of v2, /device:TPU:0, one launch (start us, length us, event | category | flops | bytes accessed | tf_op | source)
XLA Modules:
  0.0 238.4 jit_solution(7654143142618855797)
XLA Ops:
  2.7 5.0 %collective-permute-start.6 = (bf16[128,1024]{1,0:T(8,128)(2,1)}, bf16[128,1024]{1,0:T(8,128)(2,1)S(1)}, u32[]{:S(2)}, u32[]{:S(2)}) collective-permute-start(bf16[128,1024]{1,0:T(8,128)(2,1)} %dynamic-slice_bitcast_fusion.12), channel_id=1, source_target_pairs={{0,24},{4,28},{8,16},{12,20},{16,8},{20,12},{24,0},{28,4},{1,25},{... | collective-permute-start | bytes 786440 | tf_op jit(solution)/shard_map/ppermute | solution.py:168
  9.1 2.1 constant_dynamic-slice_fusion.6
  16.3 9.7 %collective-permute-done.refs_1_ = bf16[128,1024]{1,0:T(8,128)(2,1)S(1)} collective-permute-done((bf16[128,1024]{1,0:T(8,128)(2,1)S(1)}, bf16[128,1024]{1,0:T(8,128)(2,1)S(1)}, u32[]{:S(2)}, u32[]{:S(2)}) %collective-permute-start) | collective-permute-done | bytes 262176 | tf_op jit(solution)/shard_map/ppermute | solution.py:168
  26.5 3.9 %collective-permute-done.5.refs_0_ = bf16[128,1024]{1,0:T(8,128)(2,1)S(1)} collective-permute-done((bf16[128,1024]{1,0:T(8,128)(2,1)}, bf16[128,1024]{1,0:T(8,128)(2,1)S(1)}, u32[]{:S(2)}, u32[]{:S(2)}) %collective-permute-start.5) | collective-permute-done | bytes 262176 | tf_op jit(solution)/shard_map/ppermute | solution.py:168
  31.1 3.5 %dynamic-slice_bitcast_fusion.8 = (bf16[384,1024]{1,0:T(8,128)(2,1)S(1)}, bf16[384,1024]{1,0:T(8,128)(2,1)}, bf16[384,1024]{1,0:T(8,128)(2,1)}, bf16[384,1024]{1,0:T(8,128)(2,1)}) fusion(bf16[1,384,4096]{2,1,0:T(8,128)(2,1)} %param.7, s32[]{:T(128)S(6)} %select_n.128, s32[]{:T(128)S(6)} %select_n.125, s32[]{:T(128)S(6)} %select_n.124, s32[]{:T(128)S(6)} %select_n.126), kind=kLoop, calls=%fused_computation.10 | loop fusion | bytes 6291472 | tf_op jit(solution)/shard_map/dynamic_slice | solution.py:174
  43.1 6.2 %collective-permute-done.21.refs_6_ = bf16[512,512]{1,0:T(8,128)(2,1)} collective-permute-done((bf16[512,512]{1,0:T(8,128)(2,1)}, bf16[512,512]{1,0:T(8,128)(2,1)}, u32[]{:S(2)}, u32[]{:S(2)}) %collective-permute-start.21) | collective-permute-done | bytes 524320 | tf_op jit(solution)/shard_map/ppermute | solution.py:168
  55.6 2.1 shard_map.95
  57.8 5.6 %collective-permute-done.9.refs_5_ = bf16[512,512]{1,0:T(8,128)(2,1)} collective-permute-done((bf16[512,512]{1,0:T(8,128)(2,1)S(1)}, bf16[512,512]{1,0:T(8,128)(2,1)}, u32[]{:S(2)}, u32[]{:S(2)}) %collective-permute-start.9) | collective-permute-done | bytes 524320 | tf_op jit(solution)/shard_map/ppermute | solution.py:168
  68.3 5.6 %collective-permute-done.22.refs_7_ = bf16[512,512]{1,0:T(8,128)(2,1)S(1)} collective-permute-done((bf16[512,512]{1,0:T(8,128)(2,1)}, bf16[512,512]{1,0:T(8,128)(2,1)S(1)}, u32[]{:S(2)}, u32[]{:S(2)}) %collective-permute-start.22) | collective-permute-done | bytes 524320 | tf_op jit(solution)/shard_map/ppermute | solution.py:168
  75.8 3.1 %collective-permute-start.23 = (f32[256,512]{1,0:T(8,128)S(1)}, f32[256,512]{1,0:T(8,128)S(1)}, u32[]{:S(2)}, u32[]{:S(2)}) collective-permute-start(f32[256,512]{1,0:T(8,128)S(1)} %shard_map.98), channel_id=1, source_target_pairs={{0,16},{4,20},{8,24},{12,28},{16,0},{20,4},{24,8},{28,12},{1,17},{... | collective-permute-start | bytes 1572872 | tf_op jit(solution)/shard_map/ppermute | solution.py:168
  83.6 19.4 %collective-permute-done.12 = f32[256,512]{1,0:T(8,128)S(1)} collective-permute-done((f32[256,512]{1,0:T(8,128)S(1)}, f32[256,512]{1,0:T(8,128)S(1)}, u32[]{:S(2)}, u32[]{:S(2)}) %collective-permute-start.12) | collective-permute-done | bytes 524320 | tf_op jit(solution)/shard_map/ppermute | solution.py:168
  103.3 10.3 %collective-permute-done.23 = f32[256,512]{1,0:T(8,128)S(1)} collective-permute-done((f32[256,512]{1,0:T(8,128)S(1)}, f32[256,512]{1,0:T(8,128)S(1)}, u32[]{:S(2)}, u32[]{:S(2)}) %collective-permute-start.23) | collective-permute-done | bytes 524320 | tf_op jit(solution)/shard_map/ppermute | solution.py:168
  120.9 3.5 %collective-permute-done.17 = f32[128,1]{1,0:T(8,128)S(1)} collective-permute-done((f32[128,1]{1,0:T(8,128)S(1)}, f32[128,1]{1,0:T(8,128)S(1)}, u32[]{:S(2)}, u32[]{:S(2)}) %collective-permute-start.17) | collective-permute-done | bytes 544 | tf_op jit(solution)/shard_map/ppermute | solution.py:171
  126.8 10.3 %shard_map.96 = (f32[8,128,384]{2,1,0:T(8,128)S(1)}, f32[8,128,384]{2,1,0:T(8,128)S(1)}, f32[8,128,384]{2,1,0:T(8,128)S(1)}, f32[8,128,384]{2,1,0:T(8,128)S(1)},...) custom-call(s32[1]{0:T(128)S(6)} %copy.51.length_ref, bf16[128,1024]{1,0:T(8,128)(2,1)S(1)} %get-tuple-element.88.raw_ref, ...), custom_call_target="tpu_custom_call" | custom-call | flops 1000 | bytes 1000 | tf_op jit(solution)/shard_map/pallas_call | solution.py:79
  137.1 3.8 %collective-permute-start.27 = (bf16[128,1024]{1,0:T(8,128)(2,1)S(1)}, bf16[128,1024]{1,0:T(8,128)(2,1)S(1)}, u32[]{:S(2)}, u32[]{:S(2)}) collective-permute-start(bf16[128,1024]{1,0:T(8,128)(2,1)S(1)} %get-tuple-element.71), channel_id=1, source_target_pairs={{0,24},{4,28},{8,16},{12,20},{16,8},{20,12},{24,0},{28,4},{1,25},{... | collective-permute-start | bytes 786440 | tf_op jit(solution)/shard_map/ppermute | solution.py:168
  141.6 11.4 %shard_map.99 = (bf16[384,1024]{1,0:T(8,128)(2,1)S(1)}, bf16[384,1024]{1,0:T(8,128)(2,1)S(1)}, bf16[384,1024]{1,0:T(8,128)(2,1)S(1)}, bf16[384,1024]{1,0:T(8,128...) custom-call(bf16[128,1024]{1,0:T(8,128)(2,1)S(1)} %get-tuple-element.88.raw_ref, ...), custom_call_target="tpu_custom_call" | custom-call | flops 4831838208 | bytes 25165824 | tf_op jit(solution)/shard_map/pallas_call | solution.py:103
  156.5 6.1 %collective-permute-done.26 = bf16[128,1024]{1,0:T(8,128)(2,1)S(1)} collective-permute-done((bf16[128,1024]{1,0:T(8,128)(2,1)S(1)}, bf16[128,1024]{1,0:T(8,128)(2,1)S(1)}, u32[]{:S(2)}, u32[]{:S(2)}) %collective-permute-start.26) | collective-permute-done | bytes 262176 | tf_op jit(solution)/shard_map/ppermute | solution.py:168
  175.6 5.6 %collective-permute-done.45 = bf16[128,1024]{1,0:T(8,128)(2,1)S(1)} collective-permute-done((bf16[128,1024]{1,0:T(8,128)(2,1)}, bf16[128,1024]{1,0:T(8,128)(2,1)S(1)}, u32[]{:S(2)}, u32[]{:S(2)}) %collective-permute-start.45) | collective-permute-done | bytes 262176 | tf_op jit(solution)/shard_map/ppermute | solution.py:168
  183.2 3.7 %collective-permute-done.44 = bf16[128,1024]{1,0:T(8,128)(2,1)} collective-permute-done((bf16[128,1024]{1,0:T(8,128)(2,1)}, bf16[128,1024]{1,0:T(8,128)(2,1)}, u32[]{:S(2)}, u32[]{:S(2)}) %collective-permute-start.44) | collective-permute-done | bytes 262176 | tf_op jit(solution)/shard_map/ppermute | solution.py:168
  188.5 4.1 %collective-permute-done.43 = bf16[128,1024]{1,0:T(8,128)(2,1)} collective-permute-done((bf16[128,1024]{1,0:T(8,128)(2,1)}, bf16[128,1024]{1,0:T(8,128)(2,1)}, u32[]{:S(2)}, u32[]{:S(2)}) %collective-permute-start.43) | collective-permute-done | bytes 262176 | tf_op jit(solution)/shard_map/ppermute | solution.py:168
  198.9 2.6 %fusion.10 = f32[512,1024]{1,0:T(8,128)} fusion(bf16[1024,512]{1,0:T(8,128)(2,1)S(1)} %copy-done.28, bf16[1024,1024]{1,0:T(8,128)(2,1)S(1)} %constant_dynamic-update-slice_fusion.9), kind=kOutput, calls=%fused_computation.72 | convolution fusion | flops 1073741824 | bytes 5242880 | tf_op jit(solution)/shard_map/dot_general | solution.py:246
  201.5 11.4 %collective-permute-done.32 = bf16[384,1024]{1,0:T(8,128)(2,1)S(1)} collective-permute-done((bf16[384,1024]{1,0:T(8,128)(2,1)S(1)}, bf16[384,1024]{1,0:T(8,128)(2,1)S(1)}, u32[]{:S(2)}, u32[]{:S(2)}) %collective-permute-start.32) | collective-permute-done | bytes 786464 | tf_op jit(solution)/shard_map/ppermute | solution.py:171
  216.5 12.4 %collective-permute-done.33 = bf16[384,1024]{1,0:T(8,128)(2,1)S(1)} collective-permute-done((bf16[384,1024]{1,0:T(8,128)(2,1)S(1)}, bf16[384,1024]{1,0:T(8,128)(2,1)S(1)}, u32[]{:S(2)}, u32[]{:S(2)}) %collective-permute-start.33) | collective-permute-done | bytes 786464 | tf_op jit(solution)/shard_map/ppermute | solution.py:171
  235.8 2.6 %fusion.9 = f32[512,1024]{1,0:T(8,128)} fusion(bf16[1024,512]{1,0:T(8,128)(2,1)S(1)} %copy-done.28, bf16[1024,1024]{1,0:T(8,128)(2,1)S(1)} %constant_dynamic-update-slice_fusion.1), kind=kOutput, calls=%fused_computation.71 | convolution fusion | flops 1073741824 | bytes 5242880 | tf_op jit(solution)/shard_map/dot_general | solution.py:246
  (215 shorter events, 82.3 us)
Async XLA Ops:
  2.7 23.3 %collective-permute-start.6 = (bf16[128,1024]{1,0:T(8,128)(2,1)}, bf16[128,1024]{1,0:T(8,128)(2,1)S(1)}, u32[]{:S(2)}, u32[]{:S(2)}) collective-permute-start(bf16[128,1024]{1,0:T(8,128)(2,1)} %dynamic-slice_bitcast_fusion.12), channel_id=1, source_target_pairs={{0,24},{4,28},{8,16},{12,20},{16,8},{20,12},{24,0},{28,4},{1,25},{... | collective-permute-start | bytes 786440 | tf_op jit(solution)/shard_map/ppermute | solution.py:168
  7.7 22.6 %collective-permute-start.5 = (bf16[128,1024]{1,0:T(8,128)(2,1)}, bf16[128,1024]{1,0:T(8,128)(2,1)S(1)}, u32[]{:S(2)}, u32[]{:S(2)}) collective-permute-start(bf16[128,1024]{1,0:T(8,128)(2,1)} %dynamic-slice_bitcast_fusion.12), channel_id=1, source_target_pairs={{0,16},{4,20},{8,24},{12,28},{16,0},{20,4},{24,8},{28,12},{1,17},{... | collective-permute-start | bytes 786440 | tf_op jit(solution)/shard_map/ppermute | solution.py:168
  11.2 25.9 %collective-permute-start.3 = (bf16[512,512]{1,0:T(8,128)(2,1)}, bf16[512,512]{1,0:T(8,128)(2,1)}, u32[]{:S(2)}, u32[]{:S(2)}) collective-permute-start(bf16[512,512]{1,0:T(8,128)(2,1)} %get-tuple-element.103), channel_id=1, source_target_pairs={{0,8},{4,12},{8,0},{12,4},{16,24},{20,28},{24,16},{28,20},{1,9},{5... | collective-permute-start | bytes 1572872 | tf_op jit(solution)/shard_map/ppermute | solution.py:168
  12.7 27.4 %collective-permute-start.2 = (bf16[512,512]{1,0:T(8,128)(2,1)S(1)}, bf16[512,512]{1,0:T(8,128)(2,1)}, u32[]{:S(2)}, u32[]{:S(2)}) collective-permute-start(bf16[512,512]{1,0:T(8,128)(2,1)S(1)} %get-tuple-element.104.refs_4_), channel_id=1, source_target_pairs={{0,4},{4,0},{8,12},{12,8},{16,20},{20,16},{24,28},{28,24},{1,5},{5... | collective-permute-start | bytes 1572872 | tf_op jit(solution)/shard_map/ppermute | solution.py:168
  35.4 28.0 %collective-permute-start.11 = (bf16[384,1024]{1,0:T(8,128)(2,1)}, bf16[384,1024]{1,0:T(8,128)(2,1)}, u32[]{:S(2)}, u32[]{:S(2)}) collective-permute-start(bf16[384,1024]{1,0:T(8,128)(2,1)} %get-tuple-element.98), channel_id=1, source_target_pairs={{0,2},{1,3},{2,0},{3,1},{4,6},{5,7},{6,4},{7,5},{8,10},{9,11},{10,... | collective-permute-start | bytes 2359304 | tf_op jit(solution)/shard_map/ppermute | solution.py:171
  36.9 28.0 %collective-permute-start.10 = (bf16[384,1024]{1,0:T(8,128)(2,1)}, bf16[384,1024]{1,0:T(8,128)(2,1)}, u32[]{:S(2)}, u32[]{:S(2)}) collective-permute-start(bf16[384,1024]{1,0:T(8,128)(2,1)} %get-tuple-element.99), channel_id=1, source_target_pairs={{0,1},{1,0},{2,3},{3,2},{4,5},{5,4},{6,7},{7,6},{8,9},{9,8},{10,11... | collective-permute-start | bytes 2359304 | tf_op jit(solution)/shard_map/ppermute | solution.py:171
  40.1 23.3 %collective-permute-start.9 = (bf16[512,512]{1,0:T(8,128)(2,1)S(1)}, bf16[512,512]{1,0:T(8,128)(2,1)}, u32[]{:S(2)}, u32[]{:S(2)}) collective-permute-start(bf16[512,512]{1,0:T(8,128)(2,1)S(1)} %get-tuple-element.102.refs_4_), channel_id=1, source_target_pairs={{0,4},{4,0},{8,12},{12,8},{16,20},{20,16},{24,28},{28,24},{1,5},{5... | collective-permute-start | bytes 1572872 | tf_op jit(solution)/shard_map/ppermute | solution.py:168
  49.3 53.8 %collective-permute-start.13 = (bf16[384,1024]{1,0:T(8,128)(2,1)}, bf16[384,1024]{1,0:T(8,128)(2,1)S(1)}, u32[]{:S(2)}, u32[]{:S(2)}) collective-permute-start(bf16[384,1024]{1,0:T(8,128)(2,1)} %get-tuple-element.100), channel_id=1, source_target_pairs={{0,3},{1,2},{2,1},{3,0},{4,7},{5,6},{6,5},{7,4},{8,11},{9,10},{10,... | collective-permute-start | bytes 2359304 | tf_op jit(solution)/shard_map/ppermute | solution.py:171
  52.2 21.7 %collective-permute-start.22 = (bf16[512,512]{1,0:T(8,128)(2,1)}, bf16[512,512]{1,0:T(8,128)(2,1)S(1)}, u32[]{:S(2)}, u32[]{:S(2)}) collective-permute-start(bf16[512,512]{1,0:T(8,128)(2,1)} %collective-permute-done.21.refs_6_), channel_id=1, source_target_pairs={{0,4},{4,0},{8,12},{12,8},{16,20},{20,16},{24,28},{28,24},{1,5},{5... | collective-permute-start | bytes 1572872 | tf_op jit(solution)/shard_map/ppermute | solution.py:168
  63.4 50.2 %collective-permute-start.18 = (bf16[384,1024]{1,0:T(8,128)(2,1)S(1)}, bf16[384,1024]{1,0:T(8,128)(2,1)S(1)}, u32[]{:S(2)}, u32[]{:S(2)}) collective-permute-start(bf16[384,1024]{1,0:T(8,128)(2,1)S(1)} %copy-done.32), channel_id=1, source_target_pairs={{0,1},{1,0},{2,3},{3,2},{4,5},{5,4},{6,7},{7,6},{8,9},{9,8},{10,11... | collective-permute-start | bytes 2359304 | tf_op jit(solution)/shard_map/ppermute | solution.py:171
  63.4 50.3 %collective-permute-start.19 = (bf16[384,1024]{1,0:T(8,128)(2,1)S(1)}, bf16[384,1024]{1,0:T(8,128)(2,1)S(1)}, u32[]{:S(2)}, u32[]{:S(2)}) collective-permute-start(bf16[384,1024]{1,0:T(8,128)(2,1)S(1)} %copy-done.31), channel_id=1, source_target_pairs={{0,2},{1,3},{2,0},{3,1},{4,6},{5,7},{6,4},{7,5},{8,10},{9,11},{10,... | collective-permute-start | bytes 2359304 | tf_op jit(solution)/shard_map/ppermute | solution.py:171
  64.9 38.1 %collective-permute-start.12 = (f32[256,512]{1,0:T(8,128)S(1)}, f32[256,512]{1,0:T(8,128)S(1)}, u32[]{:S(2)}, u32[]{:S(2)}) collective-permute-start(f32[256,512]{1,0:T(8,128)S(1)} %shard_map.95), channel_id=1, source_target_pairs={{0,16},{4,20},{8,24},{12,28},{16,0},{20,4},{24,8},{28,12},{1,17},{... | collective-permute-start | bytes 1572872 | tf_op jit(solution)/shard_map/ppermute | solution.py:168
  75.8 37.8 %collective-permute-start.23 = (f32[256,512]{1,0:T(8,128)S(1)}, f32[256,512]{1,0:T(8,128)S(1)}, u32[]{:S(2)}, u32[]{:S(2)}) collective-permute-start(f32[256,512]{1,0:T(8,128)S(1)} %shard_map.98), channel_id=1, source_target_pairs={{0,16},{4,20},{8,24},{12,28},{16,0},{20,4},{24,8},{28,12},{1,17},{... | collective-permute-start | bytes 1572872 | tf_op jit(solution)/shard_map/ppermute | solution.py:168
  103.0 21.5 %collective-permute-start.20 = (bf16[384,1024]{1,0:T(8,128)(2,1)}, bf16[384,1024]{1,0:T(8,128)(2,1)}, u32[]{:S(2)}, u32[]{:S(2)}) collective-permute-start(bf16[384,1024]{1,0:T(8,128)(2,1)} %get-tuple-element.93), channel_id=1, source_target_pairs={{0,3},{1,2},{2,1},{3,0},{4,7},{5,6},{6,5},{7,4},{8,11},{9,10},{10,... | collective-permute-start | bytes 2359304 | tf_op jit(solution)/shard_map/ppermute | solution.py:171
  114.7 58.3 %collective-permute-start.34 = (bf16[512,512]{1,0:T(8,128)(2,1)}, bf16[512,512]{1,0:T(8,128)(2,1)}, u32[]{:S(2)}, u32[]{:S(2)}) collective-permute-start(bf16[512,512]{1,0:T(8,128)(2,1)} %pad_maximum_fusion.1), channel_id=1, source_target_pairs={{0,4},{4,0},{8,12},{12,8},{16,20},{20,16},{24,28},{28,24},{1,5},{5... | collective-permute-start | bytes 1572872 | tf_op jit(solution)/shard_map/ppermute | solution.py:168
  137.1 19.4 %collective-permute-start.27 = (bf16[128,1024]{1,0:T(8,128)(2,1)S(1)}, bf16[128,1024]{1,0:T(8,128)(2,1)S(1)}, u32[]{:S(2)}, u32[]{:S(2)}) collective-permute-start(bf16[128,1024]{1,0:T(8,128)(2,1)S(1)} %get-tuple-element.71), channel_id=1, source_target_pairs={{0,24},{4,28},{8,16},{12,20},{16,8},{20,12},{24,0},{28,4},{1,25},{... | collective-permute-start | bytes 786440 | tf_op jit(solution)/shard_map/ppermute | solution.py:168
  140.9 21.8 %collective-permute-start.26 = (bf16[128,1024]{1,0:T(8,128)(2,1)S(1)}, bf16[128,1024]{1,0:T(8,128)(2,1)S(1)}, u32[]{:S(2)}, u32[]{:S(2)}) collective-permute-start(bf16[128,1024]{1,0:T(8,128)(2,1)S(1)} %get-tuple-element.71), channel_id=1, source_target_pairs={{0,16},{4,20},{8,24},{12,28},{16,0},{20,4},{24,8},{28,12},{1,17},{... | collective-permute-start | bytes 786440 | tf_op jit(solution)/shard_map/ppermute | solution.py:168
  140.9 21.8 %collective-permute-start.25 = (bf16[128,1024]{1,0:T(8,128)(2,1)S(1)}, bf16[128,1024]{1,0:T(8,128)(2,1)S(1)}, u32[]{:S(2)}, u32[]{:S(2)}) collective-permute-start(bf16[128,1024]{1,0:T(8,128)(2,1)S(1)} %get-tuple-element.71), channel_id=1, source_target_pairs={{0,8},{4,12},{8,0},{12,4},{16,24},{20,28},{24,16},{28,20},{1,9},{5... | collective-permute-start | bytes 786440 | tf_op jit(solution)/shard_map/ppermute | solution.py:168
  171.4 21.2 %collective-permute-start.43 = (bf16[128,1024]{1,0:T(8,128)(2,1)}, bf16[128,1024]{1,0:T(8,128)(2,1)}, u32[]{:S(2)}, u32[]{:S(2)}) collective-permute-start(bf16[128,1024]{1,0:T(8,128)(2,1)} %copy-done.38), channel_id=1, source_target_pairs={{0,4},{4,0},{8,12},{12,8},{16,20},{20,16},{24,28},{28,24},{1,5},{5... | collective-permute-start | bytes 786440 | tf_op jit(solution)/shard_map/ppermute | solution.py:168
  173.0 19.6 %collective-permute-start.37 = (bf16[128,1024]{1,0:T(8,128)(2,1)}, bf16[128,1024]{1,0:T(8,128)(2,1)}, u32[]{:S(2)}, u32[]{:S(2)}) collective-permute-start(bf16[128,1024]{1,0:T(8,128)(2,1)} %fusion.3), channel_id=1, source_target_pairs={{0,24},{4,28},{8,16},{12,20},{16,8},{20,12},{24,0},{28,4},{1,25},{... | collective-permute-start | bytes 786440 | tf_op jit(solution)/shard_map/ppermute | solution.py:168
  175.6 20.2 %collective-permute-start.36 = (bf16[128,1024]{1,0:T(8,128)(2,1)}, bf16[128,1024]{1,0:T(8,128)(2,1)}, u32[]{:S(2)}, u32[]{:S(2)}) collective-permute-start(bf16[128,1024]{1,0:T(8,128)(2,1)} %fusion.3), channel_id=1, source_target_pairs={{0,16},{4,20},{8,24},{12,28},{16,0},{20,4},{24,8},{28,12},{1,17},{... | collective-permute-start | bytes 786440 | tf_op jit(solution)/shard_map/ppermute | solution.py:168
  186.9 44.5 %collective-permute-start.38 = (bf16[128,1024]{1,0:T(8,128)(2,1)}, bf16[128,1024]{1,0:T(8,128)(2,1)S(1)}, u32[]{:S(2)}, u32[]{:S(2)}) collective-permute-start(bf16[128,1024]{1,0:T(8,128)(2,1)} %fusion.3), channel_id=1, source_target_pairs={{0,4},{4,0},{8,12},{12,8},{16,20},{20,16},{24,28},{28,24},{1,5},{5... | collective-permute-start | bytes 786440 | tf_op jit(solution)/shard_map/ppermute | solution.py:168
  192.6 20.4 %collective-permute-start.32 = (bf16[384,1024]{1,0:T(8,128)(2,1)S(1)}, bf16[384,1024]{1,0:T(8,128)(2,1)S(1)}, u32[]{:S(2)}, u32[]{:S(2)}) collective-permute-start(bf16[384,1024]{1,0:T(8,128)(2,1)S(1)} %copy-done.26), channel_id=1, source_target_pairs={{0,2},{1,3},{2,0},{3,1},{4,6},{5,7},{6,4},{7,5},{8,10},{9,11},{10,... | collective-permute-start | bytes 2359304 | tf_op jit(solution)/shard_map/ppermute | solution.py:171
  195.8 33.1 %collective-permute-start.33 = (bf16[384,1024]{1,0:T(8,128)(2,1)S(1)}, bf16[384,1024]{1,0:T(8,128)(2,1)S(1)}, u32[]{:S(2)}, u32[]{:S(2)}) collective-permute-start(bf16[384,1024]{1,0:T(8,128)(2,1)S(1)} %copy-done.24), channel_id=1, source_target_pairs={{0,3},{1,2},{2,1},{3,0},{4,7},{5,6},{6,5},{7,4},{8,11},{9,10},{10,... | collective-permute-start | bytes 2359304 | tf_op jit(solution)/shard_map/ppermute | solution.py:171
  (65 other events, 724.6 us)

commit v3 on v2

--- a/solution.py
+++ b/solution.py
@@ -66,16 +66,17 @@
 def specs(tokens):
     head = pl.BlockSpec((LIVE, HD), lambda h: (0, h))
     block = pl.BlockSpec((tokens, HD), lambda h: (0, h))
+    lower = pl.BlockSpec((tokens, HD), lambda h: (1, h))
     weights = pl.BlockSpec((1, LIVE, tokens), lambda h: (h, 0, 0))
     gain = pl.BlockSpec((1, HD), lambda h: (0, h))
-    return head, block, weights, gain
-
-
-def attend_call(length, raw, inv, gain, queries, grads):
-    parts = len(queries)
-    tokens, cols = queries[0].shape
+    return head, block, lower, weights, gain
+
+
+def attend_call(length, raw, inv, gain, moved, tokens):
+    parts = len(moved)
+    cols = moved[0].shape[1]
     heads = cols // HD
-    head, block, weights, gains = specs(tokens)
+    head, block, lower, weights, gains = specs(tokens)
     outs = pl.pallas_call(
         functools.partial(attend_kernel, parts),
         grid=(heads,),
@@ -85,25 +86,30 @@
             pl.BlockSpec((LIVE, 1), lambda h: (0, 0)),
             gains,
         ]
-        + [block] * (2 * parts),
+        + [block] * parts
+        + [lower] * parts,
         out_specs=[weights] * parts + [head, head],
         out_shape=[jax.ShapeDtypeStruct((heads, LIVE, tokens), jnp.float32)] * parts
         + [jax.ShapeDtypeStruct((LIVE, cols), jnp.bfloat16)] * 2,
         compiler_params=pltpu.CompilerParams(vmem_limit_bytes=32 * 1024 * 1024),
-        cost_estimate=pl.CostEstimate(flops=1000, bytes_accessed=1000, transcendentals=0),
-    )(length, raw, inv, gain, *queries, *grads)
+        cost_estimate=pl.CostEstimate(
+            flops=16 * parts * tokens * cols * LIVE,
+            bytes_accessed=16 * parts * tokens * cols,
+            transcendentals=0,
+        ),
+    )(length, raw, inv, gain, *moved, *moved)
     return outs[:parts], outs[parts], outs[parts + 1]
 
 
-def gradient_call(raw, keys, values, gain, queries, grads, attends):
-    parts = len(queries)
-    tokens, cols = queries[0].shape
+def gradient_call(raw, keys, values, gain, moved, attends, tokens):
+    parts = len(moved)
+    cols = moved[0].shape[1]
     heads = cols // HD
-    head, block, weights, gains = specs(tokens)
+    head, block, lower, weights, gains = specs(tokens)
     outs = pl.pallas_call(
         functools.partial(gradient_kernel, parts),
         grid=(heads,),
-        in_specs=[head, head, head, gains] + [block] * (2 * parts) + [weights] * parts,
+        in_specs=[head, head, head, gains] + [block] * parts + [lower] * parts + [weights] * parts,
         out_specs=[block] * parts + [head, pl.BlockSpec((LIVE, HD), lambda h: (0, 0))],
         out_shape=[jax.ShapeDtypeStruct((tokens, cols), jnp.bfloat16)] * parts
         + [
@@ -116,8 +122,15 @@
             bytes_accessed=16 * parts * tokens * cols,
             transcendentals=0,
         ),
-    )(raw, keys, values, gain, *queries, *grads, *attends)
+    )(raw, keys, values, gain, *moved, *moved, *attends)
     return outs[:parts], outs[parts], outs[parts + 1]
+
+
+def rows_spec(part, width, tiled=False):
+    _, count, index = part
+    if tiled:
+        return pl.BlockSpec((count, width), lambda n: (index, n))
+    return pl.BlockSpec((count, width), lambda n: (index, 0))
 
 
 def product_kernel(videos, place_ref, *refs):
@@ -138,16 +151,47 @@
 
 def product_call(place, mine, sibling, weights):
     videos = len(mine)
-    width = weights[0].shape[1]
+    width = weights[0][0].shape[1]
+    parts = [*mine, *sibling, *weights]
     return pl.pallas_call(
         functools.partial(product_kernel, videos),
+        grid=(1,),
         in_specs=[pl.BlockSpec(memory_space=pltpu.SMEM)]
-        + [pl.BlockSpec(memory_space=pltpu.VMEM)] * (2 * videos + 4),
-        out_specs=pl.BlockSpec(memory_space=pltpu.VMEM),
+        + [rows_spec(part, part[0].shape[1]) for part in parts],
+        out_specs=pl.BlockSpec((videos * LIVE, width), lambda n: (0, 0)),
         out_shape=jax.ShapeDtypeStruct((videos * LIVE, width), jnp.float32),
         compiler_params=pltpu.CompilerParams(vmem_limit_bytes=32 * 1024 * 1024),
         cost_estimate=pl.CostEstimate(flops=1000, bytes_accessed=1000, transcendentals=0),
-    )(place, *mine, *sibling, *weights)
+    )(place, *[part[0] for part in parts])
+
+
+def weights_kernel(videos, columns_ref, *refs):
+    part_refs, out_refs = refs[:-2], refs[-2:]
+    for index, out_ref in enumerate(out_refs):
+        parts = [ref[...] for ref in part_refs[index * videos : (index + 1) * videos]]
+        out_ref[...] = jnp.dot(
+            columns_ref[...], jnp.concatenate(parts, axis=0), preferred_element_type=jnp.float32
+        )
+
+
+def weights_call(columns, parts):
+    rows, videos = columns.shape[0], len(parts) // 2
+    cols = parts[0][0].shape[1]
+    tile = min(cols, 512)
+    return pl.pallas_call(
+        functools.partial(weights_kernel, videos),
+        grid=(cols // tile,),
+        in_specs=[pl.BlockSpec(columns.shape, lambda n: (0, 0))]
+        + [rows_spec(part, tile, True) for part in parts],
+        out_specs=[pl.BlockSpec((rows, tile), lambda n: (0, n))] * 2,
+        out_shape=[jax.ShapeDtypeStruct((rows, cols), jnp.float32)] * 2,
+        compiler_params=pltpu.CompilerParams(vmem_limit_bytes=32 * 1024 * 1024),
+        cost_estimate=pl.CostEstimate(
+            flops=4 * rows * cols * videos * LIVE,
+            bytes_accessed=8 * rows * cols + 4 * videos * LIVE * cols,
+            transcendentals=0,
+        ),
+    )(columns, *[part[0] for part in parts])
 
 
 def after(x, *others):
@@ -173,96 +217,141 @@
     def col_block(x, index, width):
         return lax.dynamic_slice(x, (0, index * width), (x.shape[0], width))
 
-    def spread(weight):
-        kept = col_block(weight, low, half)
-        near = over_dp(col_block(weight, 1 - low, half), 2)
-        return kept, over_dp(kept, 1), near, over_dp(near, 1)
-
-    key_quad = spread(key_weight)
+    key_given = col_block(key_weight, 1 - low, half)
+    kept = jnp.concatenate(
+        [col_block(key_weight, low, half), col_block(value_weight, low, half)], axis=0
+    )
 
     captions = caption[0, :LIVE]
-    mine, sibling = [col_block(captions, quad * 2 + core, 2 * rows)], [
-        col_block(captions, quad * 2 + 1 - core, 2 * rows)
-    ]
-    for s in range(1, lines):
-        block = over_dp(col_block(captions, (quad ^ (s // 2)) * 2 + core, 2 * rows), 2 * s)
-        mine.append(block)
-        sibling.append(over_seq(block, 1))
-    value_quad = spread(value_weight)
-
-    moved = {}
-    for name, x in (("query", query[0]), ("grad", out_grad[0])):
-        moved[name, 0] = col_block(x, lane, cols)
-        for s in range(1, n_seq):
-            moved[name, s] = over_seq(col_block(x, lane ^ s, cols), s)
-    queries = [moved["query", s] for s in range(n_seq)]
-    grads = [moved["grad", s] for s in range(n_seq)]
+    given = [col_block(captions, (quad ^ (s // 2)) * 2 + core, 2 * rows) for s in range(lines)]
+    pieces = 2 * rows // half
+    near = over_dp(
+        jnp.concatenate(
+            [key_given] + [given[1][:, p * half : (p + 1) * half] for p in range(pieces)], axis=0
+        ),
+        2,
+    )
+    beside = over_dp(kept, 1)
+    arrived = [over_dp(given[s], 2 * s) for s in range(2, lines)]
+    near_columns = jnp.concatenate(
+        [near[rows + p * LIVE : rows + (p + 1) * LIVE] for p in range(pieces)], axis=1
+    )
+    mine = [given[0], near_columns, *arrived]
+    shared = over_seq(jnp.concatenate(mine[1:], axis=0), 1)
+    first = col_block(captions, quad * 2 + 1 - core, 2 * rows)
+    key_far = over_dp(near[:rows], 1)
+    value_given = col_block(value_weight, 1 - low, half)
+    value_near = over_dp(after(value_given, near, *arrived), 2)
+
+    tokens = query.shape[1]
+
+    def both(index):
+        return jnp.concatenate(
+            [col_block(query[0], index, cols), col_block(out_grad[0], index, cols)], axis=0
+        )
+
+    moved = [both(lane)] + [None] * (n_seq - 1)
+    previous = ()
+    for s in range(2, n_seq):
+        moved[s] = over_seq(after(both(lane ^ s), *previous), s)
+        previous = (moved[s],)
+    moved[1] = over_seq(after(both(lane ^ 1), beside), 1)
+
+    value_far = over_dp(after(value_near, moved[2 % n_seq]), 1)
+    key_quad = ((kept, rows, 0), (beside, rows, 0), (near, rows, 0), (key_far, rows, 0))
+    value_quad = ((kept, rows, 1), (beside, rows, 1), (value_near, rows, 0), (value_far, rows, 0))
 
     place = jnp.stack([core ^ low, 1 - (core ^ low), side, 1 - side]).astype(jnp.int32)
 
-    def project(weights, first, second):
-        def product(chosen):
-            return product_call(place, [mine[s] for s in chosen], [sibling[s] for s in chosen], weights)
-
-        sent = after(product([s for s in range(lines) if s & 2]), *first)
-        total = product([s for s in range(lines) if not s & 2]) + over_dp(sent, 4)
-        total = after(total, *second)
+    def product(weights, other):
+        chosen = [s for s in range(lines) if bool(s & 2) == other]
+        return product_call(
+            place,
+            [(mine[s], LIVE, 0) for s in chosen],
+            [(shared, LIVE, s - 1) if s else (first, LIVE, 0) for s in chosen],
+            weights,
+        )
+
+    def reduced(total):
         step = 8
         while step < n_dp:
             count = total.shape[0] // 2
             total = total[:count] + over_dp(total[count:], step)
             step *= 2
-        total = lax.reduce_precision(total, 8, 7).astype(jnp.bfloat16)
-        kept, other = total[:LIVE], over_dp(total[LIVE:], 2)
+        return lax.reduce_precision(total, 8, 7).astype(jnp.bfloat16)
+
+    def joined(total):
+        own, other = total[:LIVE], over_dp(total[LIVE:], 2)
         return jnp.where(
             low == 0,
-            jnp.concatenate([kept, other], axis=1),
-            jnp.concatenate([other, kept], axis=1),
-        )
-
-    middle = (n_seq + 2) // 2
-    raw = project(key_quad, (*value_quad[:2], *queries[1:middle]), queries[middle:])
-    values = project(value_quad, (), grads[1:middle])
+            jnp.concatenate([own, other], axis=1),
+            jnp.concatenate([other, own], axis=1),
+        )
+
+    def seq_sum(x):
+        step = 1
+        while step < n_seq:
+            x = x + over_seq(x, step)
+            step *= 2
+        return x
+
+    key_sent = over_dp(product(key_quad, True), 4)
+    value_sent = over_dp(product(value_quad, True), 4)
+    key_total = reduced(product(key_quad, False) + key_sent)
+    raw = joined(key_total)
     raw_wide = raw.astype(jnp.float32)
-
-    def seq_sum(x):
-        return functools.reduce(lambda a, b: a + b, [x] + [over_seq(x, s) for s in range(1, n_seq)])
-
     squares = seq_sum(jnp.sum(raw_wide * raw_wide, axis=-1, keepdims=True))
     inv_rms = lax.rsqrt(squares / hid + 1e-06)
     gain = lax.dynamic_slice(key_gain, (lane * cols,), (cols,)).reshape(1, cols)
-    attends, keys, value_grad = attend_call(lengths, raw, inv_rms, gain, queries, grads)
-
-    def gather(part, before):
-        near = [part] + [over_dp(part, 2 * s) for s in range(1, lines)]
-        return near + [over_dp(part, 1)] + [over_dp(after(x, *before), 1) for x in near[1:]]
-
-    held = [jnp.where(core == low, m, s) for m, s in zip(mine, sibling)]
-    other_columns = over_dp(jnp.concatenate([col_block(x, 1 - side, rows) for x in held], axis=0), 1)
-    columns = jnp.concatenate([col_block(x, side, rows) for x in held] + [other_columns], axis=0)
-
-    def weight_grad(parts, before):
-        parts = lax.optimization_barrier((*parts, *before))[:n_dp]
-        return lax.dot_general(
-            columns,
-            jnp.concatenate(parts, axis=0),
-            COLUMNS,
-            preferred_element_type=jnp.float32,
-        )
-
-    value_parts = gather(value_grad, ())
-    outs, scaled, inner = gradient_call(raw, keys, values, gain, queries, grads, attends)
-    inner = after(inner, *value_parts[1:lines])
+    attends, keys, value_grad = attend_call(lengths, raw, inv_rms, gain, moved, tokens)
+    values = joined(reduced(product(value_quad, False) + after(value_sent, value_grad)))
+
+    value_sent_grad = after(value_grad, values)
+    value_near_parts = [over_dp(value_sent_grad, 2 * s) for s in range(1, lines)]
+    value_first = over_dp(value_sent_grad, 1)
+    outs, scaled, inner = gradient_call(raw, keys, values, gain, moved, attends, tokens)
+    inner = after(inner, value_first, *value_near_parts)
     inner_mean = seq_sum(jnp.sum(inner, axis=-1, keepdims=True)) / hid
     raw_grad = (inv_rms * scaled - raw_wide * inv_rms**3 * inner_mean).astype(jnp.bfloat16)
-    placed = [outs[0]] + [over_seq(after(outs[s], inner_mean), s) for s in range(1, n_seq)]
-    key_parts = gather(raw_grad, placed[1:middle])
+    value_rest = over_dp(jnp.concatenate(value_near_parts, axis=0), 1)
+    key_near_parts = [over_dp(raw_grad, 2 * s) for s in range(1, lines)]
+    placed = [outs[0]] + [None] * (n_seq - 1)
+    previous = (inner_mean,)
+    for s in [*range(2, n_seq), 1]:
+        placed[s] = over_seq(after(outs[s], *previous), s)
+        previous = (placed[s], value_rest, *key_near_parts)
+    split = lines // 2
+    key_first = over_dp(
+        after(jnp.concatenate([raw_grad, *key_near_parts[: split - 1]], axis=0), value_rest), 1
+    )
+    key_rest = over_dp(
+        after(jnp.concatenate(key_near_parts[split - 1 :], axis=0), placed[2 % n_seq]), 1
+    )
+
+    held = [
+        jnp.where(core == low, mine[s], shared[(s - 1) * LIVE : s * LIVE] if s else first)
+        for s in range(lines)
+    ]
+    other_columns = over_dp(jnp.concatenate([col_block(x, 1 - side, rows) for x in held], axis=0), 1)
+    columns = jnp.concatenate([col_block(x, side, rows) for x in held] + [other_columns], axis=0).T
+    key_parts = (
+        [(x, LIVE, 0) for x in (raw_grad, *key_near_parts)]
+        + [(key_first, LIVE, s) for s in range(split)]
+        + [(key_rest, LIVE, s) for s in range(split)]
+    )
+    value_parts = (
+        [(x, LIVE, 0) for x in (value_grad, *value_near_parts)]
+        + [(value_first, LIVE, 0)]
+        + [(value_rest, LIVE, s) for s in range(lines - 1)]
+    )
+    key_weight_grad, value_weight_grad = weights_call(columns, key_parts + value_parts)
+
     stacked = jnp.stack(placed)
     query_grad = jnp.concatenate(
         [lax.dynamic_index_in_dim(stacked, lane ^ h, 0, keepdims=False) for h in range(n_seq)],
         axis=1,
     )[None]
-    return query_grad, weight_grad(key_parts, placed[middle:]), weight_grad(value_parts, key_parts[1:lines])
+    return query_grad, key_weight_grad, value_weight_grad
 
 
 def solution(mesh):

time: 239 us -> 255 us (1.067)
  other arithmetic: 7.45 us -> 25 us
  local copies, waits for them, and re-layouts: 34.1 us -> 42.5 us
  starting transfers between devices: 44.8 us -> 38.7 us
  Pallas kernels: 29.7 us -> 35.6 us
  matrix products: 5.18 us -> 0 us
  waiting for transfers between devices: 115 us -> 110 us
    concatenate x0 -> x10, other arithmetic: none -> 13.3 us  [the longest x4 6.65 us: both(): jnp.concatenate([col_block(query[0], index, cols), col_block(out_grad[0],...]
    ppermute x18 -> x11, waiting for transfers between devices: 28.2 us -> 15.4 us  [over_seq(): return lax.ppermute(x, 'seq', [(a, a ^ step) for a in range(n_seq)])]
    ppermute x0 -> x5, local copies, waits for them, and re-layouts: none -> 8.27 us  [the longest x4 6.87 us: over_dp(): return lax.ppermute(x, 'dp', [(a, a ^ step) for a in range(n_dp)])]
    ppermute x28 -> x22, waiting for transfers between devices: 87.1 us -> 95 us  [over_dp(): return lax.ppermute(x, 'dp', [(a, a ^ step) for a in range(n_dp)])]
    pallas_call x4 -> x5, Pallas kernels: 8 us -> 13.5 us  [the longest x4 8.78 us: product_call(): pl.pallas_call(functools.partial(product_kernel, videos), grid=(1,), in_s...]
    dot_general x2 -> x0, matrix products: 5.18 us -> none  [weight_grad(): lax.dot_general(columns, jnp.concatenate(parts, axis=0), COLUMNS, preferr...]
    ppermute x18 -> x11, starting transfers between devices: 9.85 us -> 5.78 us  [over_seq(): return lax.ppermute(x, 'seq', [(a, a ^ step) for a in range(n_seq)])]
    ppermute x28 -> x22, starting transfers between devices: 35 us -> 33 us  [over_dp(): return lax.ppermute(x, 'dp', [(a, a ^ step) for a in range(n_dp)])]
  transfers between devices with their start and end apart: 46 -> 33, of which waited for: 20 -> 15; matrix products, arithmetic and copies ran while one was open for 12% -> 17% of each run, Pallas kernels for 12% -> 14%
where the time goes in v3:
time: 255 us; the launch traced here: 254 us
  waiting for transfers between devices  110 us (43%)
  local copies, waits for them, and re-layouts  42.5 us (17%)
  starting transfers between devices  38.7 us (15%)
  Pallas kernels  35.6 us (14%)
  other arithmetic  25 us (10%)
    ppermute x22, waiting for transfers between devices, over_dp(): return lax.ppermute(x, 'dp', [(a, a ^ step) for a in range(n_dp)])  95 us
    ppermute x22, starting transfers between devices, over_dp(): return lax.ppermute(x, 'dp', [(a, a ^ step) for a in range(n_dp)])  33 us
    ppermute x11, waiting for transfers between devices, over_seq(): return lax.ppermute(x, 'seq', [(a, a ^ step) for a in range(n_seq)])  15.4 us
    unnamed x75, local copies, waits for them, and re-layouts  15.4 us
    dynamic_slice x11, local copies, waits for them, and re-layouts, col_block(): return lax.dynamic_slice(x, (0, index * width), (x.shape[0], width))  12 us
    pallas_call x1, Pallas kernels, gradient_call(): pl.pallas_call(functools.partial(gradient_kernel, parts), grid=(heads,),...  11.6 us
    pallas_call x1, Pallas kernels, attend_call(): pl.pallas_call(functools.partial(attend_kernel, parts), grid=(heads,), in...  10.5 us
    pallas_call x4, Pallas kernels, product_call(): pl.pallas_call(functools.partial(product_kernel, videos), grid=(1,), in_s...  8.78 us
  transfers between devices with their start and end apart: 33, of which 15 were waited for; matrix products, arithmetic and copies ran while one was open for 17% of the time, Pallas kernels for 14%

profile of v3, /device:TPU:0, one launch (start us, length us, event | category | flops | bytes accessed | tf_op | source)
XLA Modules:
  0.0 254.1 jit_solution(1469020670086203111)
XLA Ops:
  4.9 3.0 %collective-permute-start = (bf16[768,512]{0,1:T(8,128)(2,1)}, bf16[768,512]{0,1:T(8,128)(2,1)S(1)}, u32[]{:S(2)}, u32[]{:S(2)}) collective-permute-start(bf16[768,512]{0,1:T(8,128)(2,1)} %pad_maximum_fusion.6), channel_id=1, source_target_pairs={{0,8},{4,12},{8,0},{12,4},{16,24},{20,28},{24,16},{28,20},{1,9},{5... | collective-permute-start | bytes 2359304 | tf_op jit(solution)/shard_map/ppermute | solution.py:212
  8.8 2.5 collective-permute-start.2
  11.4 5.2 %dynamic-slice_bitcast_fusion.4 = (bf16[384,1024]{1,0:T(8,128)(2,1)}, bf16[384,1024]{1,0:T(8,128)(2,1)}, bf16[384,1024]{1,0:T(8,128)(2,1)}, bf16[384,1024]{1,0:T...) fusion(bf16[1,384,4096]{2,1,0:T(8,128)(2,1)} %param.13, ...), kind=kLoop, calls=%fused_computation.14 | loop fusion | bytes 12582928 | tf_op jit(solution)/shard_map/dynamic_slice | solution.py:218
  21.9 15.0 %collective-permute-done = bf16[768,512]{0,1:T(8,128)(2,1)S(1)} collective-permute-done((bf16[768,512]{0,1:T(8,128)(2,1)}, bf16[768,512]{0,1:T(8,128)(2,1)S(1)}, u32[]{:S(2)}, u32[]{:S(2)}) %collective-permute-start) | collective-permute-done | bytes 786464 | tf_op jit(solution)/shard_map/ppermute | solution.py:212
  42.2 2.6 %pad_maximum_fusion.4 = bf16[768,1024]{1,0:T(8,128)(2,1)} fusion(bf16[384,1024]{1,0:T(8,128)(2,1)} %get-tuple-element.70, bf16[384,1024]{1,0:T(8,128)(2,1)} %get-tuple-element.104), kind=kLoop, calls=%fused_computation.5 | loop fusion | flops 3145728 | bytes 3145728 | tf_op jit(solution)/shard_map/concatenate | solution.py:249
  51.8 4.0 %collective-permute-done.5 = bf16[512,512]{0,1:T(8,128)(2,1)} collective-permute-done((bf16[512,512]{0,1:T(8,128)(2,1)}, bf16[512,512]{0,1:T(8,128)(2,1)}, u32[]{:S(2)}, u32[]{:S(2)}) %collective-permute-start.5) | collective-permute-done | bytes 524320 | tf_op jit(solution)/shard_map/ppermute | solution.py:212
  63.3 2.7 %shard_map.95 = f32[256,512]{1,0:T(8,128)} custom-call(s32[4]{0:T(128)S(1)} %pad_add_fusion.place_ref, bf16[128,1024]{1,0:T(8,128)(2,1)S(1)} %copy-done.14, bf16[128,1024]{1,0:T(8,128)(2,1)S(1)} %copy-done.12, bf16[384,1024]{1,0:T(8,128)(2,1)S(1)} %copy.45.refs_3_.refs_2_, bf16[384,1024]{1,0:T(8,128)(2,1)S(1)} %copy.45.refs_3_.refs_2_, ...), custom_call_target="tpu_custom_call" | custom-call | flops 1000 | bytes 1000 | tf_op jit(solution)/shard_map/pallas_call | solution.py:156
  66.0 2.5 collective-permute-start.6
  83.1 8.8 %collective-permute-done.6 = f32[256,512]{1,0:T(8,128)} collective-permute-done((f32[256,512]{1,0:T(8,128)}, f32[256,512]{1,0:T(8,128)}, u32[]{:S(2)}, u32[]{:S(2)}) %collective-permute-start.6) | collective-permute-done | bytes 524320 | tf_op jit(solution)/shard_map/ppermute | solution.py:212
  93.9 5.1 %collective-permute-done.7 = bf16[128,512]{1,0:T(8,128)(2,1)} collective-permute-done((bf16[128,512]{1,0:T(8,128)(2,1)}, bf16[128,512]{1,0:T(8,128)(2,1)}, u32[]{:S(2)}, u32[]{:S(2)}) %collective-permute-start.7) | collective-permute-done | bytes 131104 | tf_op jit(solution)/shard_map/ppermute | solution.py:212
  108.5 2.5 %collective-permute-start.15 = (f32[256,512]{1,0:T(8,128)S(1)}, f32[256,512]{1,0:T(8,128)S(1)}, u32[]{:S(2)}, u32[]{:S(2)}) collective-permute-start(f32[256,512]{1,0:T(8,128)S(1)} %shard_map.98), channel_id=1, source_target_pairs={{0,16},{4,20},{8,24},{12,28},{16,0},{20,4},{24,8},{28,12},{1,17},{... | collective-permute-start | bytes 1572872 | tf_op jit(solution)/shard_map/ppermute | solution.py:212
  113.4 10.5 %shard_map.96 = (f32[8,128,384]{2,1,0:T(8,128)S(1)}, f32[8,128,384]{2,1,0:T(8,128)S(1)}, f32[8,128,384]{2,1,0:T(8,128)S(1)}, f32[8,128,384]{2,1,0:T(8,128)S(1)},...) custom-call(s32[1]{0:T(128)S(6)} %copy.73.length_ref, bf16[128,1024]{1,0:T(8,128)(2,1)S(1)} %copy-done.4, ...), custom_call_target="tpu_custom_call" | custom-call | flops 3221225472 | bytes 25165824 | tf_op jit(solution)/shard_map/pallas_call | solution.py:80
  123.8 10.6 %collective-permute-done.15 = f32[256,512]{1,0:T(8,128)S(1)} collective-permute-done((f32[256,512]{1,0:T(8,128)S(1)}, f32[256,512]{1,0:T(8,128)S(1)}, u32[]{:S(2)}, u32[]{:S(2)}) %collective-permute-start.15) | collective-permute-done | bytes 524320 | tf_op jit(solution)/shard_map/ppermute | solution.py:212
  135.2 4.4 %collective-permute-done.16 = bf16[128,512]{1,0:T(8,128)(2,1)S(1)} collective-permute-done((bf16[128,512]{1,0:T(8,128)(2,1)S(1)}, bf16[128,512]{1,0:T(8,128)(2,1)S(1)}, u32[]{:S(2)}, u32[]{:S(2)}) %collective-permute-start.16) | collective-permute-done | bytes 131104 | tf_op jit(solution)/shard_map/ppermute | solution.py:212
  139.7 3.9 %collective-permute-start.20 = (bf16[128,1024]{1,0:T(8,128)(2,1)S(1)}, bf16[128,1024]{1,0:T(8,128)(2,1)S(1)}, u32[]{:S(2)}, u32[]{:S(2)}) collective-permute-start(bf16[128,1024]{1,0:T(8,128)(2,1)S(1)} %get-tuple-element.45.refs_8_), channel_id=1, source_target_pairs={{0,24},{4,28},{8,16},{12,20},{16,8},{20,12},{24,0},{28,4},{1,25},{... | collective-permute-start | bytes 786440 | tf_op jit(solution)/shard_map/ppermute | solution.py:212
  145.7 11.6 %shard_map.99 = (bf16[384,1024]{1,0:T(8,128)(2,1)S(1)}, bf16[384,1024]{1,0:T(8,128)(2,1)}, bf16[384,1024]{1,0:T(8,128)(2,1)S(1)}, bf16[384,1024]{1,0:T(8,128)(2,...) custom-call(bf16[128,1024]{1,0:T(8,128)(2,1)S(1)} %copy-done.4, ...), custom_call_target="tpu_custom_call" | custom-call | flops 4831838208 | bytes 25165824 | tf_op jit(solution)/shard_map/pallas_call | solution.py:109
  160.0 5.3 %collective-permute-done.19.refs_10_ = bf16[128,1024]{1,0:T(8,128)(2,1)} collective-permute-done((bf16[128,1024]{1,0:T(8,128)(2,1)S(1)}, bf16[128,1024]{1,0:T(8,128)(2,1)}, u32[]{:S(2)}, u32[]{:S(2)}) %collective-permute-start.19) | collective-permute-done | bytes 262176 | tf_op jit(solution)/shard_map/ppermute | solution.py:212
  173.6 2.7 %collective-permute-start.27 = (bf16[128,1024]{1,0:T(8,128)(2,1)S(1)}, bf16[128,1024]{1,0:T(8,128)(2,1)S(1)}, u32[]{:S(2)}, u32[]{:S(2)}) collective-permute-start(bf16[128,1024]{1,0:T(8,128)(2,1)S(1)} %fusion.3.refs_0_), channel_id=1, source_target_pairs={{0,24},{4,28},{8,16},{12,20},{16,8},{20,12},{24,0},{28,4},{1,25},{... | collective-permute-start | bytes 786440 | tf_op jit(solution)/shard_map/ppermute | solution.py:212
  178.2 6.6 %collective-permute-done.27.refs_3_ = bf16[128,1024]{1,0:T(8,128)(2,1)S(1)} collective-permute-done((bf16[128,1024]{1,0:T(8,128)(2,1)S(1)}, bf16[128,1024]{1,0:T(8,128)(2,1)S(1)}, u32[]{:S(2)}, u32[]{:S(2)}) %collective-permute-start.27) | collective-permute-done | bytes 262176 | tf_op jit(solution)/shard_map/ppermute | solution.py:212
  184.8 12.4 %collective-permute-done.26.refs_2_ = bf16[128,1024]{1,0:T(8,128)(2,1)S(1)} collective-permute-done((bf16[128,1024]{1,0:T(8,128)(2,1)S(1)}, bf16[128,1024]{1,0:T(8,128)(2,1)S(1)}, u32[]{:S(2)}, u32[]{:S(2)}) %collective-permute-start.26) | collective-permute-done | bytes 262176 | tf_op jit(solution)/shard_map/ppermute | solution.py:212
  203.8 12.8 %collective-permute-done.28 = bf16[384,1024]{1,0:T(8,128)(2,1)} collective-permute-done((bf16[384,1024]{1,0:T(8,128)(2,1)}, bf16[384,1024]{1,0:T(8,128)(2,1)}, u32[]{:S(2)}, u32[]{:S(2)}) %collective-permute-start.28) | collective-permute-done | bytes 786464 | tf_op jit(solution)/shard_map/ppermute | solution.py:215
  220.6 11.9 %collective-permute-done.31.refs_4_.refs_5_ = bf16[256,1024]{1,0:T(8,128)(2,1)} collective-permute-done((bf16[256,1024]{1,0:T(8,128)(2,1)}, bf16[256,1024]{1,0:T(8,128)(2,1)}, u32[]{:S(2)}, u32[]{:S(2)}) %collective-permute-start.31) | collective-permute-done | bytes 524320 | tf_op jit(solution)/shard_map/ppermute | solution.py:212
  232.5 10.9 %collective-permute-done.32.refs_6_.refs_7_ = bf16[256,1024]{1,0:T(8,128)(2,1)} collective-permute-done((bf16[256,1024]{1,0:T(8,128)(2,1)}, bf16[256,1024]{1,0:T(8,128)(2,1)}, u32[]{:S(2)}, u32[]{:S(2)}) %collective-permute-start.32) | collective-permute-done | bytes 524320 | tf_op jit(solution)/shard_map/ppermute | solution.py:212
  245.4 4.8 %shard_map.100 = (f32[512,1024]{1,0:T(8,128)}, f32[512,1024]{1,0:T(8,128)}) custom-call(bf16[512,1024]{1,0:T(8,128)(2,1)S(1)} %bitcast.52, bf16[128,1024]{1,0:T(8,128)(2,1)S(1)} %fusion.3.refs_0_, bf16[128,1024]{1,0:T(8,128)(2,1)S(1)} %collective-permute-done.25.refs_1_, bf16[128,1024]{1,0:T(8,128)(2,1)S(1)} %collective-permute-done.26.refs_2_, ...), custom_call_target="tpu_custom_call" | custom-call | flops 2147483648 | bytes 8388608 | tf_op jit(solution)/shard_map/pallas_call | solution.py:181
  (179 shorter events, 90.0 us)
Async XLA Ops:
  4.9 32.0 %collective-permute-start = (bf16[768,512]{0,1:T(8,128)(2,1)}, bf16[768,512]{0,1:T(8,128)(2,1)S(1)}, u32[]{:S(2)}, u32[]{:S(2)}) collective-permute-start(bf16[768,512]{0,1:T(8,128)(2,1)} %pad_maximum_fusion.6), channel_id=1, source_target_pairs={{0,8},{4,12},{8,0},{12,4},{16,24},{20,28},{24,16},{28,20},{1,9},{5... | collective-permute-start | bytes 2359304 | tf_op jit(solution)/shard_map/ppermute | solution.py:212
  8.8 28.2 %collective-permute-start.2 = (bf16[128,1024]{0,1:T(8,128)(2,1)}, bf16[128,1024]{0,1:T(8,128)(2,1)}, u32[]{:S(2)}, u32[]{:S(2)}) collective-permute-start(bf16[128,1024]{0,1:T(8,128)(2,1)} %bitcast.8), channel_id=1, source_target_pairs={{0,24},{4,28},{8,16},{12,20},{16,8},{20,12},{24,0},{28,4},{1,25},{... | collective-permute-start | bytes 786440 | tf_op jit(solution)/shard_map/ppermute | solution.py:212
  11.3 25.7 %collective-permute-start.1 = (bf16[128,1024]{0,1:T(8,128)(2,1)}, bf16[128,1024]{0,1:T(8,128)(2,1)}, u32[]{:S(2)}, u32[]{:S(2)}) collective-permute-start(bf16[128,1024]{0,1:T(8,128)(2,1)} %bitcast.8), channel_id=1, source_target_pairs={{0,16},{4,20},{8,24},{12,28},{16,0},{20,4},{24,8},{28,12},{1,17},{... | collective-permute-start | bytes 786440 | tf_op jit(solution)/shard_map/ppermute | solution.py:212
  17.8 52.0 %collective-permute-start.11 = (bf16[768,1024]{1,0:T(8,128)(2,1)}, bf16[768,1024]{1,0:T(8,128)(2,1)S(1)}, u32[]{:S(2)}, u32[]{:S(2)}) collective-permute-start(bf16[768,1024]{1,0:T(8,128)(2,1)} %pad_maximum_fusion.3), channel_id=1, source_target_pairs={{0,2},{1,3},{2,0},{3,1},{4,6},{5,7},{6,4},{7,5},{8,10},{9,11},{10,... | collective-permute-start | bytes 4718600 | tf_op jit(solution)/shard_map/ppermute | solution.py:215
  20.3 38.9 %collective-permute-start.4 = (bf16[1024,512]{1,0:T(8,128)(2,1)S(1)}, bf16[1024,512]{1,0:T(8,128)(2,1)}, u32[]{:S(2)}, u32[]{:S(2)}) collective-permute-start(bf16[1024,512]{1,0:T(8,128)(2,1)S(1)} %pad_maximum_fusion.5.refs_4_), channel_id=1, source_target_pairs={{0,4},{4,0},{8,12},{12,8},{16,20},{20,16},{24,28},{28,24},{1,5},{5... | collective-permute-start | bytes 3145736 | tf_op jit(solution)/shard_map/ppermute | solution.py:212
  39.6 18.2 %collective-permute-start.3 = (bf16[384,1024]{0,1:T(8,128)(2,1)}, bf16[384,1024]{0,1:T(8,128)(2,1)}, u32[]{:S(2)}, u32[]{:S(2)}) collective-permute-start(bf16[384,1024]{0,1:T(8,128)(2,1)} %pad_maximum_fusion.7), channel_id=1, source_target_pairs={{0,1},{1,0},{2,3},{3,2},{4,5},{5,4},{6,7},{7,6},{8,9},{9,8},{10,11... | collective-permute-start | bytes 2359304 | tf_op jit(solution)/shard_map/ppermute | solution.py:215
  48.5 26.3 %collective-permute-start.13 = (bf16[512,512]{1,0:T(8,128)(2,1)}, bf16[512,512]{1,0:T(8,128)(2,1)}, u32[]{:S(2)}, u32[]{:S(2)}) collective-permute-start(bf16[512,512]{1,0:T(8,128)(2,1)} %get-tuple-element.32), channel_id=1, source_target_pairs={{0,8},{4,12},{8,0},{12,4},{16,24},{20,28},{24,16},{28,20},{1,9},{5... | collective-permute-start | bytes 1572872 | tf_op jit(solution)/shard_map/ppermute | solution.py:212
  66.0 25.8 %collective-permute-start.6 = (f32[256,512]{1,0:T(8,128)}, f32[256,512]{1,0:T(8,128)}, u32[]{:S(2)}, u32[]{:S(2)}) collective-permute-start(f32[256,512]{1,0:T(8,128)} %shard_map.95), channel_id=1, source_target_pairs={{0,16},{4,20},{8,24},{12,28},{16,0},{20,4},{24,8},{28,12},{1,17},{... | collective-permute-start | bytes 1572872 | tf_op jit(solution)/shard_map/ppermute | solution.py:212
  69.8 43.5 %collective-permute-start.10 = (bf16[768,1024]{1,0:T(8,128)(2,1)}, bf16[768,1024]{1,0:T(8,128)(2,1)}, u32[]{:S(2)}, u32[]{:S(2)}) collective-permute-start(bf16[768,1024]{1,0:T(8,128)(2,1)} %pad_maximum_fusion.2), channel_id=1, source_target_pairs={{0,1},{1,0},{2,3},{3,2},{4,5},{5,4},{6,7},{7,6},{8,9},{9,8},{10,11... | collective-permute-start | bytes 4718600 | tf_op jit(solution)/shard_map/ppermute | solution.py:215
  69.9 43.5 %collective-permute-start.12 = (bf16[768,1024]{1,0:T(8,128)(2,1)}, bf16[768,1024]{1,0:T(8,128)(2,1)}, u32[]{:S(2)}, u32[]{:S(2)}) collective-permute-start(bf16[768,1024]{1,0:T(8,128)(2,1)} %pad_maximum_fusion.4), channel_id=1, source_target_pairs={{0,3},{1,2},{2,1},{3,0},{4,7},{5,6},{6,5},{7,4},{8,11},{9,10},{10,... | collective-permute-start | bytes 4718600 | tf_op jit(solution)/shard_map/ppermute | solution.py:215
  74.8 31.5 %collective-permute-start.14 = (bf16[512,512]{1,0:T(8,128)(2,1)}, bf16[512,512]{1,0:T(8,128)(2,1)}, u32[]{:S(2)}, u32[]{:S(2)}) collective-permute-start(bf16[512,512]{1,0:T(8,128)(2,1)} %collective-permute-done.13.refs_6_), channel_id=1, source_target_pairs={{0,4},{4,0},{8,12},{12,8},{16,20},{20,16},{24,28},{28,24},{1,5},{5... | collective-permute-start | bytes 1572872 | tf_op jit(solution)/shard_map/ppermute | solution.py:212
  108.5 25.9 %collective-permute-start.15 = (f32[256,512]{1,0:T(8,128)S(1)}, f32[256,512]{1,0:T(8,128)S(1)}, u32[]{:S(2)}, u32[]{:S(2)}) collective-permute-start(f32[256,512]{1,0:T(8,128)S(1)} %shard_map.98), channel_id=1, source_target_pairs={{0,16},{4,20},{8,24},{12,28},{16,0},{20,4},{24,8},{28,12},{1,17},{... | collective-permute-start | bytes 1572872 | tf_op jit(solution)/shard_map/ppermute | solution.py:212
  139.7 20.3 %collective-permute-start.20 = (bf16[128,1024]{1,0:T(8,128)(2,1)S(1)}, bf16[128,1024]{1,0:T(8,128)(2,1)S(1)}, u32[]{:S(2)}, u32[]{:S(2)}) collective-permute-start(bf16[128,1024]{1,0:T(8,128)(2,1)S(1)} %get-tuple-element.45.refs_8_), channel_id=1, source_target_pairs={{0,24},{4,28},{8,16},{12,20},{16,8},{20,12},{24,0},{28,4},{1,25},{... | collective-permute-start | bytes 786440 | tf_op jit(solution)/shard_map/ppermute | solution.py:212
  143.6 21.7 %collective-permute-start.19 = (bf16[128,1024]{1,0:T(8,128)(2,1)S(1)}, bf16[128,1024]{1,0:T(8,128)(2,1)}, u32[]{:S(2)}, u32[]{:S(2)}) collective-permute-start(bf16[128,1024]{1,0:T(8,128)(2,1)S(1)} %get-tuple-element.45.refs_8_), channel_id=1, source_target_pairs={{0,16},{4,20},{8,24},{12,28},{16,0},{20,4},{24,8},{28,12},{1,17},{... | collective-permute-start | bytes 786440 | tf_op jit(solution)/shard_map/ppermute | solution.py:212
  143.6 21.7 %collective-permute-start.18 = (bf16[128,1024]{1,0:T(8,128)(2,1)S(1)}, bf16[128,1024]{1,0:T(8,128)(2,1)}, u32[]{:S(2)}, u32[]{:S(2)}) collective-permute-start(bf16[128,1024]{1,0:T(8,128)(2,1)S(1)} %get-tuple-element.45.refs_8_), channel_id=1, source_target_pairs={{0,8},{4,12},{8,0},{12,4},{16,24},{20,28},{24,16},{28,20},{1,9},{5... | collective-permute-start | bytes 786440 | tf_op jit(solution)/shard_map/ppermute | solution.py:212
  144.2 21.1 %collective-permute-start.17 = (bf16[128,1024]{1,0:T(8,128)(2,1)S(1)}, bf16[128,1024]{1,0:T(8,128)(2,1)S(1)}, u32[]{:S(2)}, u32[]{:S(2)}) collective-permute-start(bf16[128,1024]{1,0:T(8,128)(2,1)S(1)} %get-tuple-element.45.refs_8_), channel_id=1, source_target_pairs={{0,4},{4,0},{8,12},{12,8},{16,20},{20,16},{24,28},{28,24},{1,5},{5... | collective-permute-start | bytes 786440 | tf_op jit(solution)/shard_map/ppermute | solution.py:212
  170.3 26.9 %collective-permute-start.24 = (bf16[384,1024]{1,0:T(8,128)(2,1)}, bf16[384,1024]{1,0:T(8,128)(2,1)S(1)}, u32[]{:S(2)}, u32[]{:S(2)}) collective-permute-start(bf16[384,1024]{1,0:T(8,128)(2,1)} %pad_maximum_fusion.8), channel_id=1, source_target_pairs={{0,4},{4,0},{8,12},{12,8},{16,20},{20,16},{24,28},{28,24},{1,5},{5... | collective-permute-start | bytes 2359304 | tf_op jit(solution)/shard_map/ppermute | solution.py:212
  172.0 25.1 %collective-permute-start.23 = (bf16[384,1024]{1,0:T(8,128)(2,1)}, bf16[384,1024]{1,0:T(8,128)(2,1)}, u32[]{:S(2)}, u32[]{:S(2)}) collective-permute-start(bf16[384,1024]{1,0:T(8,128)(2,1)} %copy-done.25), channel_id=1, source_target_pairs={{0,2},{1,3},{2,0},{3,1},{4,6},{5,7},{6,4},{7,5},{8,10},{9,11},{10,... | collective-permute-start | bytes 2359304 | tf_op jit(solution)/shard_map/ppermute | solution.py:215
  176.3 20.9 %collective-permute-start.26 = (bf16[128,1024]{1,0:T(8,128)(2,1)S(1)}, bf16[128,1024]{1,0:T(8,128)(2,1)S(1)}, u32[]{:S(2)}, u32[]{:S(2)}) collective-permute-start(bf16[128,1024]{1,0:T(8,128)(2,1)S(1)} %fusion.3.refs_0_), channel_id=1, source_target_pairs={{0,16},{4,20},{8,24},{12,28},{16,0},{20,4},{24,8},{28,12},{1,17},{... | collective-permute-start | bytes 786440 | tf_op jit(solution)/shard_map/ppermute | solution.py:212
  176.3 20.9 %collective-permute-start.25 = (bf16[128,1024]{1,0:T(8,128)(2,1)S(1)}, bf16[128,1024]{1,0:T(8,128)(2,1)S(1)}, u32[]{:S(2)}, u32[]{:S(2)}) collective-permute-start(bf16[128,1024]{1,0:T(8,128)(2,1)S(1)} %fusion.3.refs_0_), channel_id=1, source_target_pairs={{0,8},{4,12},{8,0},{12,4},{16,24},{20,28},{24,16},{28,20},{1,9},{5... | collective-permute-start | bytes 786440 | tf_op jit(solution)/shard_map/ppermute | solution.py:212
  197.2 19.4 %collective-permute-start.28 = (bf16[384,1024]{1,0:T(8,128)(2,1)}, bf16[384,1024]{1,0:T(8,128)(2,1)}, u32[]{:S(2)}, u32[]{:S(2)}) collective-permute-start(bf16[384,1024]{1,0:T(8,128)(2,1)} %copy-done.24), channel_id=1, source_target_pairs={{0,3},{1,2},{2,1},{3,0},{4,7},{5,6},{6,5},{7,4},{8,11},{9,10},{10,... | collective-permute-start | bytes 2359304 | tf_op jit(solution)/shard_map/ppermute | solution.py:215
  202.5 17.0 %collective-permute-start.30 = (bf16[512,512]{0,1:T(8,128)(2,1)}, bf16[512,512]{0,1:T(8,128)(2,1)}, u32[]{:S(2)}, u32[]{:S(2)}) collective-permute-start(bf16[512,512]{0,1:T(8,128)(2,1)} %pad_maximum_fusion.9), channel_id=1, source_target_pairs={{0,4},{4,0},{8,12},{12,8},{16,20},{20,16},{24,28},{28,24},{1,5},{5... | collective-permute-start | bytes 1572872 | tf_op jit(solution)/shard_map/ppermute | solution.py:212
  216.6 33.6 %collective-permute-start.29 = (bf16[384,1024]{1,0:T(8,128)(2,1)}, bf16[384,1024]{1,0:T(8,128)(2,1)}, u32[]{:S(2)}, u32[]{:S(2)}) collective-permute-start(bf16[384,1024]{1,0:T(8,128)(2,1)} %get-tuple-element.50), channel_id=1, source_target_pairs={{0,1},{1,0},{2,3},{3,2},{4,5},{5,4},{6,7},{7,6},{8,9},{9,8},{10,11... | collective-permute-start | bytes 2359304 | tf_op jit(solution)/shard_map/ppermute | solution.py:215
  218.5 24.8 %collective-permute-start.32 = (bf16[256,1024]{1,0:T(8,128)(2,1)}, bf16[256,1024]{1,0:T(8,128)(2,1)}, u32[]{:S(2)}, u32[]{:S(2)}) collective-permute-start(bf16[256,1024]{1,0:T(8,128)(2,1)} %pad_maximum_fusion.11), channel_id=1, source_target_pairs={{0,4},{4,0},{8,12},{12,8},{16,20},{20,16},{24,28},{28,24},{1,5},{5... | collective-permute-start | bytes 1572872 | tf_op jit(solution)/shard_map/ppermute | solution.py:212
  (47 other events, 315.5 us)

commit v4 on v3

--- a/solution.py
+++ b/solution.py
@@ -9,6 +9,7 @@
 
 HD = 128
 LIVE = 128
+VMEM = 60 * 1024 * 1024
 
 
 ROWS = (((1,), (1,)), ((), ()))
@@ -91,7 +92,7 @@
         out_specs=[weights] * parts + [head, head],
         out_shape=[jax.ShapeDtypeStruct((heads, LIVE, tokens), jnp.float32)] * parts
         + [jax.ShapeDtypeStruct((LIVE, cols), jnp.bfloat16)] * 2,
-        compiler_params=pltpu.CompilerParams(vmem_limit_bytes=32 * 1024 * 1024),
+        compiler_params=pltpu.CompilerParams(vmem_limit_bytes=VMEM),
         cost_estimate=pl.CostEstimate(
             flops=16 * parts * tokens * cols * LIVE,
             bytes_accessed=16 * parts * tokens * cols,
@@ -116,7 +117,7 @@
             jax.ShapeDtypeStruct((LIVE, cols), jnp.float32),
             jax.ShapeDtypeStruct((LIVE, HD), jnp.float32),
         ],
-        compiler_params=pltpu.CompilerParams(vmem_limit_bytes=32 * 1024 * 1024),
+        compiler_params=pltpu.CompilerParams(vmem_limit_bytes=VMEM),
         cost_estimate=pl.CostEstimate(
             flops=24 * parts * tokens * cols * LIVE,
             bytes_accessed=16 * parts * tokens * cols,
@@ -160,7 +161,7 @@
         + [rows_spec(part, part[0].shape[1]) for part in parts],
         out_specs=pl.BlockSpec((videos * LIVE, width), lambda n: (0, 0)),
         out_shape=jax.ShapeDtypeStruct((videos * LIVE, width), jnp.float32),
-        compiler_params=pltpu.CompilerParams(vmem_limit_bytes=32 * 1024 * 1024),
+        compiler_params=pltpu.CompilerParams(vmem_limit_bytes=VMEM),
         cost_estimate=pl.CostEstimate(flops=1000, bytes_accessed=1000, transcendentals=0),
     )(place, *[part[0] for part in parts])
 
@@ -185,7 +186,7 @@
         + [rows_spec(part, tile, True) for part in parts],
         out_specs=[pl.BlockSpec((rows, tile), lambda n: (0, n))] * 2,
         out_shape=[jax.ShapeDtypeStruct((rows, cols), jnp.float32)] * 2,
-        compiler_params=pltpu.CompilerParams(vmem_limit_bytes=32 * 1024 * 1024),
+        compiler_params=pltpu.CompilerParams(vmem_limit_bytes=VMEM),
         cost_estimate=pl.CostEstimate(
             flops=4 * rows * cols * videos * LIVE,
             bytes_accessed=8 * rows * cols + 4 * videos * LIVE * cols,
@@ -198,11 +199,47 @@
     return lax.optimization_barrier((x, *others))[0]
 
 
+def pack_kernel(moves, inputs, place_ref, *refs):
+    ins, outs, sems = refs[:inputs], refs[inputs:-1], refs[-1]
+
+    def span(at, width):
+        if isinstance(at, int):
+            return pl.ds(at, width)
+        return pl.ds(pl.multiple_of(place_ref[at[0]] * width, width), width)
+
+    copies = []
+    for index, (source, row, col, count, width, target, to_row, to_col) in enumerate(moves):
+        copy = pltpu.make_async_copy(
+            ins[source].at[pl.ds(row, count), span(col, width)],
+            outs[target].at[pl.ds(to_row, count), span(to_col, width)],
+            sems.at[index],
+        )
+        copy.start()
+        copies.append(copy)
+    for copy in copies:
+        copy.wait()
+
+
+def pack_call(place, arrays, shapes, moves):
+    return pl.pallas_call(
+        functools.partial(pack_kernel, moves, len(arrays)),
+        in_specs=[pl.BlockSpec(memory_space=pltpu.SMEM)]
+        + [pl.BlockSpec(memory_space=pl.ANY)] * len(arrays),
+        out_specs=[pl.BlockSpec(memory_space=pl.ANY)] * len(shapes),
+        out_shape=[jax.ShapeDtypeStruct(shape, jnp.bfloat16) for shape in shapes],
+        scratch_shapes=[pltpu.SemaphoreType.DMA((len(moves),))],
+        compiler_params=pltpu.CompilerParams(vmem_limit_bytes=VMEM),
+        cost_estimate=pl.CostEstimate(flops=1000, bytes_accessed=1000, transcendentals=0),
+    )(place, *arrays)
+
+
 def shards(n_dp, n_seq, query, caption, key_weight, value_weight, key_gain, lengths, out_grad):
     rows, cols = key_weight.shape
     hid = cols * n_seq
     lines = n_dp // 2
     half = cols // 2
+    wide = 2 * rows
+    tokens = query.shape[1]
     me = lax.axis_index("dp")
     lane = lax.axis_index("seq")
     quad, low, side = me // 4, me // 2 % 2, me % 2
@@ -217,58 +254,76 @@
     def col_block(x, index, width):
         return lax.dynamic_slice(x, (0, index * width), (x.shape[0], width))
 
-    key_given = col_block(key_weight, 1 - low, half)
-    kept = jnp.concatenate(
-        [col_block(key_weight, low, half), col_block(value_weight, low, half)], axis=0
-    )
-
-    captions = caption[0, :LIVE]
-    given = [col_block(captions, (quad ^ (s // 2)) * 2 + core, 2 * rows) for s in range(lines)]
-    pieces = 2 * rows // half
-    near = over_dp(
-        jnp.concatenate(
-            [key_given] + [given[1][:, p * half : (p + 1) * half] for p in range(pieces)], axis=0
-        ),
-        2,
-    )
+    pieces = wide // half
+    quads = lines // 2
+    scalars = [low, 1 - low, quad * 2 + core, quad * 2 + 1 - core]
+    scalars += [(quad ^ (s // 2)) * 2 + core for s in range(2, lines)]
+    scalars += [(quad * 2 + core) * pieces + p for p in range(pieces)]
+    place = jnp.stack(scalars).astype(jnp.int32)
+    near_at = lines + 2
+    near_given, kept, mine_first, sibling_first, *given = pack_call(
+        place,
+        [key_weight, value_weight, caption[0]],
+        [(2 * rows + pieces * LIVE, half), (2 * rows, half)] + [(LIVE, wide)] * lines,
+        [
+            (0, 0, (1,), rows, half, 0, 0, 0),
+            (1, 0, (1,), rows, half, 0, rows, 0),
+        ]
+        + [
+            (2, 0, (near_at + p,), LIVE, half, 0, 2 * rows + p * LIVE, 0) for p in range(pieces)
+        ]
+        + [
+            (0, 0, (0,), rows, half, 1, 0, 0),
+            (1, 0, (0,), rows, half, 1, rows, 0),
+        ]
+        + [(2, 0, (2 + s,), LIVE, wide, 2 + s, 0, 0) for s in range(lines)],
+    )
+    near = over_dp(near_given, 2)
     beside = over_dp(kept, 1)
-    arrived = [over_dp(given[s], 2 * s) for s in range(2, lines)]
-    near_columns = jnp.concatenate(
-        [near[rows + p * LIVE : rows + (p + 1) * LIVE] for p in range(pieces)], axis=1
-    )
-    mine = [given[0], near_columns, *arrived]
-    shared = over_seq(jnp.concatenate(mine[1:], axis=0), 1)
-    first = col_block(captions, quad * 2 + 1 - core, 2 * rows)
-    key_far = over_dp(near[:rows], 1)
-    value_given = col_block(value_weight, 1 - low, half)
-    value_near = over_dp(after(value_given, near, *arrived), 2)
-
-    tokens = query.shape[1]
-
-    def both(index):
-        return jnp.concatenate(
-            [col_block(query[0], index, cols), col_block(out_grad[0], index, cols)], axis=0
-        )
-
-    moved = [both(lane)] + [None] * (n_seq - 1)
+    arrived = [over_dp(x, 2 * s) for s, x in enumerate(given, 2)]
+
+    lanes = jnp.stack([lane ^ s for s in range(n_seq)]).astype(jnp.int32)
+    packed = pack_call(
+        after(lanes, kept),
+        [query[0], out_grad[0]],
+        [(2 * tokens, cols)] * n_seq,
+        [
+            (source, 0, (s,), tokens, cols, s, source * tokens, 0)
+            for s in [*range(2, n_seq), 1, 0]
+            for source in range(2)
+        ],
+    )
+    moved = [packed[0]] + [None] * (n_seq - 1)
     previous = ()
     for s in range(2, n_seq):
-        moved[s] = over_seq(after(both(lane ^ s), *previous), s)
+        moved[s] = over_seq(after(packed[s], *previous), s)
         previous = (moved[s],)
-    moved[1] = over_seq(after(both(lane ^ 1), beside), 1)
-
-    value_far = over_dp(after(value_near, moved[2 % n_seq]), 1)
-    key_quad = ((kept, rows, 0), (beside, rows, 0), (near, rows, 0), (key_far, rows, 0))
+    moved[1] = over_seq(after(packed[1], beside), 1)
+
+    key_near, value_near, shared = pack_call(
+        place,
+        [near, *arrived],
+        [(rows, half), (rows, half), ((lines - 1) * LIVE, wide)],
+        [(0, 0, 0, rows, half, 0, 0, 0), (0, rows, 0, rows, half, 1, 0, 0)]
+        + [
+            (0, 2 * rows + p * LIVE, 0, LIVE, half, 2, 0, p * half) for p in range(pieces)
+        ]
+        + [(s - 1, 0, 0, LIVE, wide, 2, (s - 1) * LIVE, 0) for s in range(2, lines)],
+    )
+    key_far = over_dp(key_near, 1)
+    value_far = over_dp(value_near, 1)
+    sibling = over_seq(shared, 1)
+    key_quad = ((kept, rows, 0), (beside, rows, 0), (key_near, rows, 0), (key_far, rows, 0))
     value_quad = ((kept, rows, 1), (beside, rows, 1), (value_near, rows, 0), (value_far, rows, 0))
 
-    place = jnp.stack([core ^ low, 1 - (core ^ low), side, 1 - side]).astype(jnp.int32)
+    places = jnp.stack([core ^ low, 1 - (core ^ low), side, 1 - side]).astype(jnp.int32)
 
     def product(weights, other):
         chosen = [s for s in range(lines) if bool(s & 2) == other]
         return product_call(
-            place,
-            [(mine[s], LIVE, 0) for s in chosen],
-            [(shared, LIVE, s - 1) if s else (first, LIVE, 0) for s in chosen],
+            places,
+            [(shared, LIVE, s - 1) if s else (mine_first, LIVE, 0) for s in chosen],
+            [(sibling, LIVE, s - 1) if s else (sibling_first, LIVE, 0) for s in chosen],
             weights,
         )
 
@@ -295,20 +350,28 @@
             step *= 2
         return x
 
+    own = jnp.concatenate([mine_first, shared], axis=0)
+    other = jnp.concatenate([sibling_first, sibling], axis=0)
+    held = jnp.where(core == low, own, other)
+    other_columns = over_dp(col_block(held, 1 - side, rows), 1)
+    columns = jnp.concatenate([col_block(held, side, rows), other_columns], axis=0).T
+
     key_sent = over_dp(product(key_quad, True), 4)
     value_sent = over_dp(product(value_quad, True), 4)
-    key_total = reduced(product(key_quad, False) + key_sent)
+    key_total = reduced(product(key_quad, False) + after(key_sent, value_far))
     raw = joined(key_total)
     raw_wide = raw.astype(jnp.float32)
     squares = seq_sum(jnp.sum(raw_wide * raw_wide, axis=-1, keepdims=True))
     inv_rms = lax.rsqrt(squares / hid + 1e-06)
     gain = lax.dynamic_slice(key_gain, (lane * cols,), (cols,)).reshape(1, cols)
-    attends, keys, value_grad = attend_call(lengths, raw, inv_rms, gain, moved, tokens)
+    attends, keys, value_grad = attend_call(
+        lengths, after(raw, columns), inv_rms, gain, moved, tokens
+    )
     values = joined(reduced(product(value_quad, False) + after(value_sent, value_grad)))
 
-    value_sent_grad = after(value_grad, values)
-    value_near_parts = [over_dp(value_sent_grad, 2 * s) for s in range(1, lines)]
-    value_first = over_dp(value_sent_grad, 1)
+    value_given = after(value_grad, values)
+    value_near_parts = [over_dp(value_given, 2 * s) for s in range(1, lines)]
+    value_first = over_dp(value_given, 1)
     outs, scaled, inner = gradient_call(raw, keys, values, gain, moved, attends, tokens)
     inner = after(inner, value_first, *value_near_parts)
     inner_mean = seq_sum(jnp.sum(inner, axis=-1, keepdims=True)) / hid
@@ -317,23 +380,15 @@
     key_near_parts = [over_dp(raw_grad, 2 * s) for s in range(1, lines)]
     placed = [outs[0]] + [None] * (n_seq - 1)
     previous = (inner_mean,)
-    for s in [*range(2, n_seq), 1]:
+    for s in range(2, n_seq):
         placed[s] = over_seq(after(outs[s], *previous), s)
         previous = (placed[s], value_rest, *key_near_parts)
+    placed[1] = over_seq(after(outs[1], value_rest), 1)
     split = lines // 2
     key_first = over_dp(
         after(jnp.concatenate([raw_grad, *key_near_parts[: split - 1]], axis=0), value_rest), 1
     )
-    key_rest = over_dp(
-        after(jnp.concatenate(key_near_parts[split - 1 :], axis=0), placed[2 % n_seq]), 1
-    )
-
-    held = [
-        jnp.where(core == low, mine[s], shared[(s - 1) * LIVE : s * LIVE] if s else first)
-        for s in range(lines)
-    ]
-    other_columns = over_dp(jnp.concatenate([col_block(x, 1 - side, rows) for x in held], axis=0), 1)
-    columns = jnp.concatenate([col_block(x, side, rows) for x in held] + [other_columns], axis=0).T
+    key_rest = over_dp(jnp.concatenate(key_near_parts[split - 1 :], axis=0), 1)
     key_parts = (
         [(x, LIVE, 0) for x in (raw_grad, *key_near_parts)]
         + [(key_first, LIVE, s) for s in range(split)]
@@ -346,12 +401,13 @@
     )
     key_weight_grad, value_weight_grad = weights_call(columns, key_parts + value_parts)
 
-    stacked = jnp.stack(placed)
-    query_grad = jnp.concatenate(
-        [lax.dynamic_index_in_dim(stacked, lane ^ h, 0, keepdims=False) for h in range(n_seq)],
-        axis=1,
-    )[None]
-    return query_grad, key_weight_grad, value_weight_grad
+    (query_grad,) = pack_call(
+        lanes,
+        placed,
+        [(tokens, hid)],
+        [(s, 0, 0, tokens, cols, 0, 0, (s,)) for s in range(n_seq)],
+    )
+    return query_grad[None], key_weight_grad, value_weight_grad
 
 
 def solution(mesh):

time: 255 us -> 662 us (2.60)
  Pallas kernels: 35.6 us -> 495 us
  local copies, waits for them, and re-layouts: 42.5 us -> 14.7 us
  other arithmetic: 25 us -> 9.19 us
  waiting for transfers between devices: 110 us -> 103 us
    pallas_call x0 -> x4, Pallas kernels: none -> 452 us  [pack_call(): pl.pallas_call(functools.partial(pack_kernel, moves, len(arrays)), in_spe...]
    concatenate x9 -> x1, other arithmetic: 11.4 us -> 0.03 us  [shards(): key_rest = over_dp(jnp.concatenate(key_near_parts[split - 1:], axis=0), 1)]
    dynamic_slice x11 -> x1, local copies, waits for them, and re-layouts: 12 us -> 1.17 us  [col_block(): return lax.dynamic_slice(x, (0, index * width), (x.shape[0], width))]
    unnamed x75 -> x58, local copies, waits for them, and re-layouts: 15.4 us -> 4.71 us
    ppermute x11, waiting for transfers between devices: 15.4 us -> 7.09 us  [over_seq(): return lax.ppermute(x, 'seq', [(a, a ^ step) for a in range(n_seq)])]
    ppermute x4 -> x0, local copies, waits for them, and re-layouts: 6.87 us -> none  [over_dp(): return lax.ppermute(x, 'dp', [(a, a ^ step) for a in range(n_dp)])]
    ppermute x22 -> x21, starting transfers between devices: 33 us -> 31.3 us  [over_dp(): return lax.ppermute(x, 'dp', [(a, a ^ step) for a in range(n_dp)])]
    ppermute x22 -> x21, waiting for transfers between devices: 95 us -> 96.3 us  [over_dp(): return lax.ppermute(x, 'dp', [(a, a ^ step) for a in range(n_dp)])]
  transfers between devices with their start and end apart: 33 -> 32, of which waited for: 15 -> 14; matrix products, arithmetic and copies ran while one was open for 17% -> 3% of each run, Pallas kernels for 14% -> 44%
where the time goes in v4:
time: 662 us; the launch traced here: 661 us
  Pallas kernels  495 us (75%)
  waiting for transfers between devices  103 us (16%)
  starting transfers between devices  37.1 us (6%)
  local copies, waits for them, and re-layouts  14.7 us (2%)
  other arithmetic  9.19 us (1%)
    pallas_call x4, Pallas kernels, pack_call(): pl.pallas_call(functools.partial(pack_kernel, moves, len(arrays)), in_spe...  452 us
    ppermute x21, waiting for transfers between devices, over_dp(): return lax.ppermute(x, 'dp', [(a, a ^ step) for a in range(n_dp)])  96.3 us
    ppermute x21, starting transfers between devices, over_dp(): return lax.ppermute(x, 'dp', [(a, a ^ step) for a in range(n_dp)])  31.3 us
    pallas_call x4, Pallas kernels, product_call(): pl.pallas_call(functools.partial(product_kernel, videos), grid=(1,), in_s...  13.5 us
  transfers between devices with their start and end apart: 32, of which 14 were waited for; matrix products, arithmetic and copies ran while one was open for 3% of the time, Pallas kernels for 44%

profile of v4, /device:TPU:0, one launch (start us, length us, event | category | flops | bytes accessed | tf_op | source)
XLA Modules:
  0.0 661.3 jit_solution(2751172444405653525)
XLA Ops:
  1.3 105.1 %shard_map.94 = (bf16[1280,512]{1,0:T(8,128)(2,1)}, bf16[1024,512]{1,0:T(8,128)(2,1)}, bf16[128,1024]{1,0:T(8,128)(2,1)}, bf16[128,1024]{1,0:T(8,128)(2,1)}, bf1...) custom-call(s32[8]{0:T(128)} %stack.72.place_ref, bf16[512,1024]{1,0:T(8,128)(2,1)} %refs_0_.1, ...), custom_call_target="tpu_custom_call" | custom-call | flops 1000 | bytes 1000 | tf_op jit(solution)/shard_map/pallas_call | solution.py:224
  110.1 192.6 %shard_map.98 = (bf16[768,1024]{1,0:T(8,128)(2,1)}, bf16[768,1024]{1,0:T(8,128)(2,1)}, bf16[768,1024]{1,0:T(8,128)(2,1)}, bf16[768,1024]{1,0:T(8,128)(2,1)}) custom-call(s32[4]{0:T(128)} %pad_add_fusion.place_ref, bf16[384,4096]{1,0:T(8,128)(2,1)} %bitcast.24, bf16[384,4096]{1,0:T(8,128)(2,1)} %bitcast.25), custom_call_target="tpu_custom_call" | custom-call | flops 1000 | bytes 1000 | tf_op jit(solution)/shard_map/pallas_call | solution.py:224
  308.6 15.3 %collective-permute-done.1.refs_1_ = bf16[128,1024]{1,0:T(8,128)(2,1)S(1)} collective-permute-done((bf16[128,1024]{1,0:T(8,128)(2,1)S(1)}, bf16[128,1024]{1,0:T(8,128)(2,1)S(1)}, u32[]{:S(2)}, u32[]{:S(2)}) %collective-permute-start.1) | collective-permute-done | bytes 262176 | tf_op jit(solution)/shard_map/ppermute | solution.py:249
  324.6 57.4 %shard_map.95 = (bf16[512,512]{1,0:T(8,128)(2,1)}, bf16[512,512]{1,0:T(8,128)(2,1)}, bf16[384,1024]{1,0:T(8,128)(2,1)}) custom-call(s32[8]{0:T(128)} %stack.72.place_ref, bf16[1280,512]{1,0:T(8,128)(2,1)} %collective-permute-done.refs_0_, bf16[128,1024]{1,0:T(8,128)(2,1)} %copy-done.19, bf16[128,1024]{1,0:T(8,128)(2,1)} %copy-done.20), custom_call_target="tpu_custom_call" | custom-call | flops 1000 | bytes 1000 | tf_op jit(solution)/shard_map/pallas_call | solution.py:224
  389.4 9.9 %collective-permute-done.5.refs_7_ = bf16[512,512]{1,0:T(8,128)(2,1)} collective-permute-done((bf16[512,512]{1,0:T(8,128)(2,1)S(1)}, bf16[512,512]{1,0:T(8,128)(2,1)}, u32[]{:S(2)}, u32[]{:S(2)}) %collective-permute-start.5) | collective-permute-done | bytes 524320 | tf_op jit(solution)/shard_map/ppermute | solution.py:249
  399.3 3.3 shard_map.97
  402.7 7.1 %collective-permute-start.6 = (f32[256,512]{1,0:T(8,128)}, f32[256,512]{1,0:T(8,128)}, u32[]{:S(2)}, u32[]{:S(2)}) collective-permute-start(f32[256,512]{1,0:T(8,128)} %shard_map.97), channel_id=1, source_target_pairs={{0,16},{4,20},{8,24},{12,28},{16,0},{20,4},{24,8},{28,12},{1,17},{... | collective-permute-start | bytes 1572872 | tf_op jit(solution)/shard_map/ppermute | solution.py:249
  416.8 3.4 shard_map.96
  420.2 12.5 %collective-permute-done.6 = f32[256,512]{1,0:T(8,128)} collective-permute-done((f32[256,512]{1,0:T(8,128)}, f32[256,512]{1,0:T(8,128)}, u32[]{:S(2)}, u32[]{:S(2)}) %collective-permute-start.6) | collective-permute-done | bytes 524320 | tf_op jit(solution)/shard_map/ppermute | solution.py:249
  434.2 4.9 collective-permute-done.8
  442.0 3.3 shard_map.101
  445.3 3.4 shard_map.100
  455.1 11.4 %shard_map.99 = (f32[8,128,384]{2,1,0:T(8,128)}, f32[8,128,384]{2,1,0:T(8,128)}, f32[8,128,384]{2,1,0:T(8,128)}, f32[8,128,384]{2,1,0:T(8,128)}, bf16[128,1024]{1,0:T(8,128)(2,1)}, /*index=5*/bf16[128,1024]{1,0:T(8,128)(2,1)}) custom-call(s32[1]{0:T(128)S(6)} %copy.38.length_ref, bf16[128,1024]{1,0:T(8,128)(2,1)} %get-tuple-element.52.raw_ref, ...), custom_call_target="tpu_custom_call" | custom-call | flops 3221225472 | bytes 25165824 | tf_op jit(solution)/shard_map/pallas_call | solution.py:81
  466.5 4.9 collective-permute-done.15
  471.7 5.5 collective-permute-done.16
  483.8 12.6 %shard_map.102 = (bf16[384,1024]{1,0:T(8,128)(2,1)}, bf16[384,1024]{1,0:T(8,128)(2,1)}, bf16[384,1024]{1,0:T(8,128)(2,1)}, bf16[384,1024]{1,0:T(8,128)(2,1)}, f32[128,1024]{1,0:T(8,128)}, /*index=5*/f32[128,128]{1,0:T(8,128)}) custom-call(bf16[128,1024]{1,0:T(8,128)(2,1)} %get-tuple-element.52.raw_ref, bf16[128,1024]{1,0:T(8,128)(2,1)} %get-tuple-element.60.keys_ref, ...), custom_call_target="tpu_custom_call" | custom-call | flops 4831838208 | bytes 25165824 | tf_op jit(solution)/shard_map/pallas_call | solution.py:110
  496.4 7.0 %collective-permute-done.18.refs_10_ = bf16[128,1024]{1,0:T(8,128)(2,1)S(1)} collective-permute-done((bf16[128,1024]{1,0:T(8,128)(2,1)S(1)}, bf16[128,1024]{1,0:T(8,128)(2,1)S(1)}, u32[]{:S(2)}, u32[]{:S(2)}) %collective-permute-start.18) | collective-permute-done | bytes 262176 | tf_op jit(solution)/shard_map/ppermute | solution.py:249
  512.6 3.1 collective-permute-start.26
  515.7 6.8 %collective-permute-done.28.refs_3_ = bf16[128,1024]{1,0:T(8,128)(2,1)S(1)} collective-permute-done((bf16[128,1024]{1,0:T(8,128)(2,1)S(1)}, bf16[128,1024]{1,0:T(8,128)(2,1)S(1)}, u32[]{:S(2)}, u32[]{:S(2)}) %collective-permute-start.28) | collective-permute-done | bytes 262176 | tf_op jit(solution)/shard_map/ppermute | solution.py:249
  522.5 10.5 %collective-permute-done.27.refs_2_ = bf16[128,1024]{1,0:T(8,128)(2,1)S(1)} collective-permute-done((bf16[128,1024]{1,0:T(8,128)(2,1)S(1)}, bf16[128,1024]{1,0:T(8,128)(2,1)S(1)}, u32[]{:S(2)}, u32[]{:S(2)}) %collective-permute-start.27) | collective-permute-done | bytes 262176 | tf_op jit(solution)/shard_map/ppermute | solution.py:249
  536.9 11.0 %collective-permute-done.31.refs_6_.refs_7_ = bf16[256,1024]{1,0:T(8,128)(2,1)S(1)} collective-permute-done((bf16[256,1024]{1,0:T(8,128)(2,1)S(1)}, bf16[256,1024]{1,0:T(8,128)(2,1)S(1)}, u32[]{:S(2)}, u32[]{:S(2)}) %collective-permute-start.31) | collective-permute-done | bytes 524320 | tf_op jit(solution)/shard_map/ppermute | solution.py:249
  548.8 8.0 %collective-permute-done.30.refs_4_.refs_5_ = bf16[256,1024]{1,0:T(8,128)(2,1)S(1)} collective-permute-done((bf16[256,1024]{1,0:T(8,128)(2,1)S(1)}, bf16[256,1024]{1,0:T(8,128)(2,1)S(1)}, u32[]{:S(2)}, u32[]{:S(2)}) %collective-permute-start.30) | collective-permute-done | bytes 524320 | tf_op jit(solution)/shard_map/ppermute | solution.py:249
  557.5 5.5 shard_map.104
  564.2 97.1 %shard_map.103 = bf16[384,4096]{1,0:T(8,128)(2,1)} custom-call(s32[4]{0:T(128)} %pad_add_fusion.place_ref, bf16[384,1024]{1,0:T(8,128)(2,1)} %get-tuple-element.67.refs_0_, bf16[384,1024]{1,0:T(8,128)(2,1)} %copy-done.10, bf16[384,1024]{1,0:T(8,128)(2,1)} %copy-done.9, bf16[384,1024]{1,0:T(8,128)(2,1)} %copy-done.11), custom_call_target="tpu_custom_call" | custom-call | flops 1000 | bytes 1000 | tf_op jit(solution)/shard_map/pallas_call | solution.py:224
  (137 shorter events, 57.9 us)
Async XLA Ops:
  106.4 217.4 %collective-permute-start = (bf16[1280,512]{1,0:T(8,128)(2,1)}, bf16[1280,512]{1,0:T(8,128)(2,1)}, u32[]{:S(2)}, u32[]{:S(2)}) collective-permute-start(bf16[1280,512]{1,0:T(8,128)(2,1)} %get-tuple-element.43), channel_id=1, source_target_pairs={{0,8},{4,12},{8,0},{12,4},{16,24},{20,28},{24,16},{28,20},{1,9},{5... | collective-permute-start | bytes 3932168 | tf_op jit(solution)/shard_map/ppermute | solution.py:249
  302.7 107.1 %collective-permute-start.13 = (bf16[768,1024]{1,0:T(8,128)(2,1)}, bf16[768,1024]{1,0:T(8,128)(2,1)S(1)}, u32[]{:S(2)}, u32[]{:S(2)}) collective-permute-start(bf16[768,1024]{1,0:T(8,128)(2,1)} %get-tuple-element.57), channel_id=1, source_target_pairs={{0,2},{1,3},{2,0},{3,1},{4,6},{5,7},{6,4},{7,5},{8,10},{9,11},{10,... | collective-permute-start | bytes 4718600 | tf_op jit(solution)/shard_map/ppermute | solution.py:252
  304.2 19.6 %collective-permute-start.1 = (bf16[128,1024]{1,0:T(8,128)(2,1)S(1)}, bf16[128,1024]{1,0:T(8,128)(2,1)S(1)}, u32[]{:S(2)}, u32[]{:S(2)}) collective-permute-start(bf16[128,1024]{1,0:T(8,128)(2,1)S(1)} %copy-done.28), channel_id=1, source_target_pairs={{0,16},{4,20},{8,24},{12,28},{16,0},{20,4},{24,8},{28,12},{1,17},{... | collective-permute-start | bytes 786440 | tf_op jit(solution)/shard_map/ppermute | solution.py:249
  306.8 17.0 %collective-permute-start.2 = (bf16[128,1024]{1,0:T(8,128)(2,1)S(1)}, bf16[128,1024]{1,0:T(8,128)(2,1)S(1)}, u32[]{:S(2)}, u32[]{:S(2)}) collective-permute-start(bf16[128,1024]{1,0:T(8,128)(2,1)S(1)} %copy-done.27), channel_id=1, source_target_pairs={{0,24},{4,28},{8,16},{12,20},{16,8},{20,12},{24,0},{28,4},{1,25},{... | collective-permute-start | bytes 786440 | tf_op jit(solution)/shard_map/ppermute | solution.py:249
  307.1 82.4 %collective-permute-start.4 = (bf16[1024,512]{1,0:T(8,128)(2,1)S(1)}, bf16[1024,512]{1,0:T(8,128)(2,1)}, u32[]{:S(2)}, u32[]{:S(2)}) collective-permute-start(bf16[1024,512]{1,0:T(8,128)(2,1)S(1)} %copy-done.2), channel_id=1, source_target_pairs={{0,4},{4,0},{8,12},{12,8},{16,20},{20,16},{24,28},{28,24},{1,5},{5... | collective-permute-start | bytes 3145736 | tf_op jit(solution)/shard_map/ppermute | solution.py:249
  384.5 14.8 %collective-permute-start.5 = (bf16[512,512]{1,0:T(8,128)(2,1)S(1)}, bf16[512,512]{1,0:T(8,128)(2,1)}, u32[]{:S(2)}, u32[]{:S(2)}) collective-permute-start(bf16[512,512]{1,0:T(8,128)(2,1)S(1)} %copy-done.6), channel_id=1, source_target_pairs={{0,4},{4,0},{8,12},{12,8},{16,20},{20,16},{24,28},{28,24},{1,5},{5... | collective-permute-start | bytes 1572872 | tf_op jit(solution)/shard_map/ppermute | solution.py:249
  386.6 33.6 %collective-permute-start.7 = (bf16[512,512]{1,0:T(8,128)(2,1)}, bf16[512,512]{1,0:T(8,128)(2,1)}, u32[]{:S(2)}, u32[]{:S(2)}) collective-permute-start(bf16[512,512]{1,0:T(8,128)(2,1)} %get-tuple-element.50.refs_6_), channel_id=1, source_target_pairs={{0,4},{4,0},{8,12},{12,8},{16,20},{20,16},{24,28},{28,24},{1,5},{5... | collective-permute-start | bytes 1572872 | tf_op jit(solution)/shard_map/ppermute | solution.py:249
  402.7 30.1 %collective-permute-start.6 = (f32[256,512]{1,0:T(8,128)}, f32[256,512]{1,0:T(8,128)}, u32[]{:S(2)}, u32[]{:S(2)}) collective-permute-start(f32[256,512]{1,0:T(8,128)} %shard_map.97), channel_id=1, source_target_pairs={{0,16},{4,20},{8,24},{12,28},{16,0},{20,4},{24,8},{28,12},{1,17},{... | collective-permute-start | bytes 1572872 | tf_op jit(solution)/shard_map/ppermute | solution.py:249
  409.8 44.2 %collective-permute-start.12 = (bf16[768,1024]{1,0:T(8,128)(2,1)}, bf16[768,1024]{1,0:T(8,128)(2,1)S(1)}, u32[]{:S(2)}, u32[]{:S(2)}) collective-permute-start(bf16[768,1024]{1,0:T(8,128)(2,1)} %get-tuple-element.56), channel_id=1, source_target_pairs={{0,1},{1,0},{2,3},{3,2},{4,5},{5,4},{6,7},{7,6},{8,9},{9,8},{10,11... | collective-permute-start | bytes 4718600 | tf_op jit(solution)/shard_map/ppermute | solution.py:252
  409.8 44.2 %collective-permute-start.14 = (bf16[768,1024]{1,0:T(8,128)(2,1)}, bf16[768,1024]{1,0:T(8,128)(2,1)}, u32[]{:S(2)}, u32[]{:S(2)}) collective-permute-start(bf16[768,1024]{1,0:T(8,128)(2,1)} %get-tuple-element.59), channel_id=1, source_target_pairs={{0,3},{1,2},{2,1},{3,0},{4,7},{5,6},{6,5},{7,4},{8,11},{9,10},{10,... | collective-permute-start | bytes 4718600 | tf_op jit(solution)/shard_map/ppermute | solution.py:252
  415.3 34.1 %collective-permute-start.9 = (bf16[512,512]{0,1:T(8,128)(2,1)}, bf16[512,512]{0,1:T(8,128)(2,1)S(1)}, u32[]{:S(2)}, u32[]{:S(2)}) collective-permute-start(bf16[512,512]{0,1:T(8,128)(2,1)} %get-tuple-element.89), channel_id=1, source_target_pairs={{0,4},{4,0},{8,12},{12,8},{16,20},{20,16},{24,28},{28,24},{1,5},{5... | collective-permute-start | bytes 1572872 | tf_op jit(solution)/shard_map/ppermute | solution.py:249
  445.3 26.1 %collective-permute-start.15 = (f32[256,512]{1,0:T(8,128)}, f32[256,512]{1,0:T(8,128)S(1)}, u32[]{:S(2)}, u32[]{:S(2)}) collective-permute-start(f32[256,512]{1,0:T(8,128)} %shard_map.101), channel_id=1, source_target_pairs={{0,16},{4,20},{8,24},{12,28},{16,0},{20,4},{24,8},{28,12},{1,17},{... | collective-permute-start | bytes 1572872 | tf_op jit(solution)/shard_map/ppermute | solution.py:249
  477.9 18.5 %collective-permute-start.22 = (bf16[128,1024]{1,0:T(8,128)(2,1)S(1)}, bf16[128,1024]{1,0:T(8,128)(2,1)S(1)}, u32[]{:S(2)}, u32[]{:S(2)}) collective-permute-start(bf16[128,1024]{1,0:T(8,128)(2,1)S(1)} %copy-done.25), channel_id=1, source_target_pairs={{0,4},{4,0},{8,12},{12,8},{16,20},{20,16},{24,28},{28,24},{1,5},{5... | collective-permute-start | bytes 786440 | tf_op jit(solution)/shard_map/ppermute | solution.py:249
  479.4 17.0 %collective-permute-start.19 = (bf16[128,1024]{1,0:T(8,128)(2,1)S(1)}, bf16[128,1024]{1,0:T(8,128)(2,1)S(1)}, u32[]{:S(2)}, u32[]{:S(2)}) collective-permute-start(bf16[128,1024]{1,0:T(8,128)(2,1)S(1)} %copy-done.25), channel_id=1, source_target_pairs={{0,24},{4,28},{8,16},{12,20},{16,8},{20,12},{24,0},{28,4},{1,25},{... | collective-permute-start | bytes 786440 | tf_op jit(solution)/shard_map/ppermute | solution.py:249
  480.9 22.6 %collective-permute-start.18 = (bf16[128,1024]{1,0:T(8,128)(2,1)S(1)}, bf16[128,1024]{1,0:T(8,128)(2,1)S(1)}, u32[]{:S(2)}, u32[]{:S(2)}) collective-permute-start(bf16[128,1024]{1,0:T(8,128)(2,1)S(1)} %copy-done.25), channel_id=1, source_target_pairs={{0,16},{4,20},{8,24},{12,28},{16,0},{20,4},{24,8},{28,12},{1,17},{... | collective-permute-start | bytes 786440 | tf_op jit(solution)/shard_map/ppermute | solution.py:249
  481.2 22.3 %collective-permute-start.17 = (bf16[128,1024]{1,0:T(8,128)(2,1)S(1)}, bf16[128,1024]{1,0:T(8,128)(2,1)S(1)}, u32[]{:S(2)}, u32[]{:S(2)}) collective-permute-start(bf16[128,1024]{1,0:T(8,128)(2,1)S(1)} %copy-done.25), channel_id=1, source_target_pairs={{0,8},{4,12},{8,0},{12,4},{16,24},{20,28},{24,16},{28,20},{1,9},{5... | collective-permute-start | bytes 786440 | tf_op jit(solution)/shard_map/ppermute | solution.py:249
  506.6 26.9 %collective-permute-start.20 = (bf16[384,1024]{1,0:T(8,128)(2,1)S(1)}, bf16[384,1024]{1,0:T(8,128)(2,1)S(1)}, u32[]{:S(2)}, u32[]{:S(2)}) collective-permute-start(bf16[384,1024]{1,0:T(8,128)(2,1)S(1)} %pad_maximum_fusion), channel_id=1, source_target_pairs={{0,4},{4,0},{8,12},{12,8},{16,20},{20,16},{24,28},{28,24},{1,5},{5... | collective-permute-start | bytes 2359304 | tf_op jit(solution)/shard_map/ppermute | solution.py:249
  510.4 23.2 %collective-permute-start.25 = (bf16[384,1024]{1,0:T(8,128)(2,1)S(1)}, bf16[384,1024]{1,0:T(8,128)(2,1)S(1)}, u32[]{:S(2)}, u32[]{:S(2)}) collective-permute-start(bf16[384,1024]{1,0:T(8,128)(2,1)S(1)} %copy-done.21), channel_id=1, source_target_pairs={{0,2},{1,3},{2,0},{3,1},{4,6},{5,7},{6,4},{7,5},{8,10},{9,11},{10,... | collective-permute-start | bytes 2359304 | tf_op jit(solution)/shard_map/ppermute | solution.py:252
  512.6 20.4 %collective-permute-start.27 = (bf16[128,1024]{1,0:T(8,128)(2,1)S(1)}, bf16[128,1024]{1,0:T(8,128)(2,1)S(1)}, u32[]{:S(2)}, u32[]{:S(2)}) collective-permute-start(bf16[128,1024]{1,0:T(8,128)(2,1)S(1)} %fusion.3.refs_0_), channel_id=1, source_target_pairs={{0,16},{4,20},{8,24},{12,28},{16,0},{20,4},{24,8},{28,12},{1,17},{... | collective-permute-start | bytes 786440 | tf_op jit(solution)/shard_map/ppermute | solution.py:249
  512.6 21.0 %collective-permute-start.26 = (bf16[128,1024]{1,0:T(8,128)(2,1)S(1)}, bf16[128,1024]{1,0:T(8,128)(2,1)S(1)}, u32[]{:S(2)}, u32[]{:S(2)}) collective-permute-start(bf16[128,1024]{1,0:T(8,128)(2,1)S(1)} %fusion.3.refs_0_), channel_id=1, source_target_pairs={{0,8},{4,12},{8,0},{12,4},{16,24},{20,28},{24,16},{28,20},{1,9},{5... | collective-permute-start | bytes 786440 | tf_op jit(solution)/shard_map/ppermute | solution.py:249
  533.0 14.9 %collective-permute-start.31 = (bf16[256,1024]{1,0:T(8,128)(2,1)S(1)}, bf16[256,1024]{1,0:T(8,128)(2,1)S(1)}, u32[]{:S(2)}, u32[]{:S(2)}) collective-permute-start(bf16[256,1024]{1,0:T(8,128)(2,1)S(1)} %pad_maximum_fusion.2), channel_id=1, source_target_pairs={{0,4},{4,0},{8,12},{12,8},{16,20},{20,16},{24,28},{28,24},{1,5},{5... | collective-permute-start | bytes 1572872 | tf_op jit(solution)/shard_map/ppermute | solution.py:249
  533.6 29.5 %collective-permute-start.21 = (bf16[384,1024]{1,0:T(8,128)(2,1)}, bf16[384,1024]{1,0:T(8,128)(2,1)S(1)}, u32[]{:S(2)}, u32[]{:S(2)}) collective-permute-start(bf16[384,1024]{1,0:T(8,128)(2,1)} %get-tuple-element.70), channel_id=1, source_target_pairs={{0,1},{1,0},{2,3},{3,2},{4,5},{5,4},{6,7},{7,6},{8,9},{9,8},{10,11... | collective-permute-start | bytes 2359304 | tf_op jit(solution)/shard_map/ppermute | solution.py:252
  533.6 29.5 %collective-permute-start.29 = (bf16[384,1024]{1,0:T(8,128)(2,1)}, bf16[384,1024]{1,0:T(8,128)(2,1)S(1)}, u32[]{:S(2)}, u32[]{:S(2)}) collective-permute-start(bf16[384,1024]{1,0:T(8,128)(2,1)} %get-tuple-element.77), channel_id=1, source_target_pairs={{0,3},{1,2},{2,1},{3,0},{4,7},{5,6},{6,5},{7,4},{8,11},{9,10},{10,... | collective-permute-start | bytes 2359304 | tf_op jit(solution)/shard_map/ppermute | solution.py:252
  535.3 21.4 %collective-permute-start.30 = (bf16[256,1024]{1,0:T(8,128)(2,1)S(1)}, bf16[256,1024]{1,0:T(8,128)(2,1)S(1)}, u32[]{:S(2)}, u32[]{:S(2)}) collective-permute-start(bf16[256,1024]{1,0:T(8,128)(2,1)S(1)} %pad_maximum_fusion.1), channel_id=1, source_target_pairs={{0,4},{4,0},{8,12},{12,8},{16,20},{20,16},{24,28},{28,24},{1,5},{5... | collective-permute-start | bytes 1572872 | tf_op jit(solution)/shard_map/ppermute | solution.py:249
  (37 other events, 996.6 us)

commit v5 on v4

--- a/solution.py
+++ b/solution.py
@@ -134,6 +134,30 @@
     return pl.BlockSpec((count, width), lambda n: (index, 0))
 
 
+def pick_kernel(place_ref, first_ref, mine_ref, sibling_first_ref, sibling_ref, *out_refs):
+    here = place_ref[0] == 0
+    rows = out_refs[0].shape[1]
+    for index, out_ref in enumerate(out_refs):
+        at = pl.ds(pl.multiple_of(place_ref[2 + index] * rows, rows), rows)
+        out_ref[:LIVE] = jnp.where(here, first_ref[:, at], sibling_first_ref[:, at])
+        out_ref[LIVE:] = jnp.where(here, mine_ref[:, at], sibling_ref[:, at])
+
+
+def pick_call(place, first, mine, sibling_first, sibling, rows):
+    arrays = (first, mine, sibling_first, sibling)
+    shape = (LIVE + mine.shape[0], rows)
+    return pl.pallas_call(
+        pick_kernel,
+        grid=(1,),
+        in_specs=[pl.BlockSpec(memory_space=pltpu.SMEM)]
+        + [pl.BlockSpec(x.shape, lambda n: (0, 0)) for x in arrays],
+        out_specs=[pl.BlockSpec(shape, lambda n: (0, 0))] * 2,
+        out_shape=[jax.ShapeDtypeStruct(shape, jnp.bfloat16)] * 2,
+        compiler_params=pltpu.CompilerParams(vmem_limit_bytes=VMEM),
+        cost_estimate=pl.CostEstimate(flops=1000, bytes_accessed=1000, transcendentals=0),
+    )(place, *arrays)
+
+
 def product_kernel(videos, place_ref, *refs):
     mine_refs, sibling_refs = refs[:videos], refs[videos : 2 * videos]
     weight_refs, out_ref = refs[2 * videos : -1], refs[-1]
@@ -200,36 +224,30 @@
 
 
 def pack_kernel(moves, inputs, place_ref, *refs):
-    ins, outs, sems = refs[:inputs], refs[inputs:-1], refs[-1]
+    ins, outs = refs[:inputs], refs[inputs:]
 
     def span(at, width):
         if isinstance(at, int):
             return pl.ds(at, width)
         return pl.ds(pl.multiple_of(place_ref[at[0]] * width, width), width)
 
-    copies = []
-    for index, (source, row, col, count, width, target, to_row, to_col) in enumerate(moves):
-        copy = pltpu.make_async_copy(
-            ins[source].at[pl.ds(row, count), span(col, width)],
-            outs[target].at[pl.ds(to_row, count), span(to_col, width)],
-            sems.at[index],
-        )
-        copy.start()
-        copies.append(copy)
-    for copy in copies:
-        copy.wait()
-
-
-def pack_call(place, arrays, shapes, moves):
+    for source, row, col, count, width, target, to_row, to_col in moves:
+        block = ins[source][pl.ds(row, count), span(col, width)]
+        outs[target][pl.ds(to_row, count), span(to_col, width)] = block
+
+
+def pack_call(place, arrays, shapes, moves, tiles=1, size=1000):
+    def spec(shape):
+        return pl.BlockSpec((shape[0] // tiles, shape[1]), lambda n: (n, 0))
+
     return pl.pallas_call(
         functools.partial(pack_kernel, moves, len(arrays)),
-        in_specs=[pl.BlockSpec(memory_space=pltpu.SMEM)]
-        + [pl.BlockSpec(memory_space=pl.ANY)] * len(arrays),
-        out_specs=[pl.BlockSpec(memory_space=pl.ANY)] * len(shapes),
+        grid=(tiles,),
+        in_specs=[pl.BlockSpec(memory_space=pltpu.SMEM)] + [spec(x.shape) for x in arrays],
+        out_specs=[spec(shape) for shape in shapes],
         out_shape=[jax.ShapeDtypeStruct(shape, jnp.bfloat16) for shape in shapes],
-        scratch_shapes=[pltpu.SemaphoreType.DMA((len(moves),))],
-        compiler_params=pltpu.CompilerParams(vmem_limit_bytes=VMEM),
-        cost_estimate=pl.CostEstimate(flops=1000, bytes_accessed=1000, transcendentals=0),
+        compiler_params=pltpu.CompilerParams(vmem_limit_bytes=VMEM),
+        cost_estimate=pl.CostEstimate(flops=1000, bytes_accessed=size, transcendentals=0),
     )(place, *arrays)
 
 
@@ -261,22 +279,18 @@
     scalars += [(quad * 2 + core) * pieces + p for p in range(pieces)]
     place = jnp.stack(scalars).astype(jnp.int32)
     near_at = lines + 2
-    near_given, kept, mine_first, sibling_first, *given = pack_call(
+    near_given, kept, value_given, mine_first, sibling_first, *given = pack_call(
         place,
         [key_weight, value_weight, caption[0]],
-        [(2 * rows + pieces * LIVE, half), (2 * rows, half)] + [(LIVE, wide)] * lines,
+        [(rows + pieces * LIVE, half), (2 * rows, half), (rows, half)] + [(LIVE, wide)] * lines,
         [
             (0, 0, (1,), rows, half, 0, 0, 0),
-            (1, 0, (1,), rows, half, 0, rows, 0),
-        ]
-        + [
-            (2, 0, (near_at + p,), LIVE, half, 0, 2 * rows + p * LIVE, 0) for p in range(pieces)
-        ]
-        + [
             (0, 0, (0,), rows, half, 1, 0, 0),
             (1, 0, (0,), rows, half, 1, rows, 0),
+            (1, 0, (1,), rows, half, 2, 0, 0),
         ]
-        + [(2, 0, (2 + s,), LIVE, wide, 2 + s, 0, 0) for s in range(lines)],
+        + [(2, 0, (near_at + p,), LIVE, half, 0, rows + p * LIVE, 0) for p in range(pieces)]
+        + [(2, 0, (2 + s,), LIVE, wide, 3 + s, 0, 0) for s in range(lines)],
     )
     near = over_dp(near_given, 2)
     beside = over_dp(kept, 1)
@@ -289,9 +303,10 @@
         [(2 * tokens, cols)] * n_seq,
         [
             (source, 0, (s,), tokens, cols, s, source * tokens, 0)
-            for s in [*range(2, n_seq), 1, 0]
+            for s in range(n_seq)
             for source in range(2)
         ],
+        size=8 * tokens * hid,
     )
     moved = [packed[0]] + [None] * (n_seq - 1)
     previous = ()
@@ -300,19 +315,26 @@
         previous = (moved[s],)
     moved[1] = over_seq(after(packed[1], beside), 1)
 
-    key_near, value_near, shared = pack_call(
+    value_near = over_dp(after(value_given, near, *arrived), 2)
+    key_near, shared, shared_given = pack_call(
         place,
         [near, *arrived],
-        [(rows, half), (rows, half), ((lines - 1) * LIVE, wide)],
-        [(0, 0, 0, rows, half, 0, 0, 0), (0, rows, 0, rows, half, 1, 0, 0)]
+        [(rows, half)] + [((lines - 1) * LIVE, wide)] * 2,
+        [(0, 0, 0, rows, half, 0, 0, 0)]
         + [
-            (0, 2 * rows + p * LIVE, 0, LIVE, half, 2, 0, p * half) for p in range(pieces)
+            (0, rows + p * LIVE, 0, LIVE, half, out, 0, p * half)
+            for p in range(pieces)
+            for out in (1, 2)
         ]
-        + [(s - 1, 0, 0, LIVE, wide, 2, (s - 1) * LIVE, 0) for s in range(2, lines)],
+        + [
+            (s - 1, 0, 0, LIVE, wide, out, (s - 1) * LIVE, 0)
+            for s in range(2, lines)
+            for out in (1, 2)
+        ],
     )
     key_far = over_dp(key_near, 1)
     value_far = over_dp(value_near, 1)
-    sibling = over_seq(shared, 1)
+    sibling = over_seq(shared_given, 1)
     key_quad = ((kept, rows, 0), (beside, rows, 0), (key_near, rows, 0), (key_far, rows, 0))
     value_quad = ((kept, rows, 1), (beside, rows, 1), (value_near, rows, 0), (value_far, rows, 0))
 
@@ -343,38 +365,39 @@
             jnp.concatenate([other, own], axis=1),
         )
 
-    def seq_sum(x):
+    def seq_sum(x, before=()):
         step = 1
         while step < n_seq:
             x = x + over_seq(x, step)
+            if step == 1:
+                x = after(x, *before)
             step *= 2
         return x
 
-    own = jnp.concatenate([mine_first, shared], axis=0)
-    other = jnp.concatenate([sibling_first, sibling], axis=0)
-    held = jnp.where(core == low, own, other)
-    other_columns = over_dp(col_block(held, 1 - side, rows), 1)
-    columns = jnp.concatenate([col_block(held, side, rows), other_columns], axis=0).T
+    own_columns, other_given = pick_call(places, mine_first, shared, sibling_first, sibling, rows)
+    other_columns = over_dp(other_given, 1)
+    columns = jnp.concatenate([own_columns, other_columns], axis=0).T
 
     key_sent = over_dp(product(key_quad, True), 4)
-    value_sent = over_dp(product(value_quad, True), 4)
-    key_total = reduced(product(key_quad, False) + after(key_sent, value_far))
+    value_product = product(value_quad, True)
+    value_sent = over_dp(value_product, 4)
+    key_total = reduced(product(key_quad, False) + after(key_sent, value_product))
     raw = joined(key_total)
     raw_wide = raw.astype(jnp.float32)
     squares = seq_sum(jnp.sum(raw_wide * raw_wide, axis=-1, keepdims=True))
     inv_rms = lax.rsqrt(squares / hid + 1e-06)
     gain = lax.dynamic_slice(key_gain, (lane * cols,), (cols,)).reshape(1, cols)
+    value_total = reduced(product(value_quad, False) + after(value_sent, inv_rms))
+    values = joined(value_total)
     attends, keys, value_grad = attend_call(
-        lengths, after(raw, columns), inv_rms, gain, moved, tokens
-    )
-    values = joined(reduced(product(value_quad, False) + after(value_sent, value_grad)))
-
-    value_given = after(value_grad, values)
-    value_near_parts = [over_dp(value_given, 2 * s) for s in range(1, lines)]
-    value_first = over_dp(value_given, 1)
+        lengths, after(raw, columns, value_total), inv_rms, gain, moved, tokens
+    )
+
+    value_near_parts = [over_dp(value_grad, 2 * s) for s in range(1, lines)]
+    value_first = over_dp(value_grad, 1)
     outs, scaled, inner = gradient_call(raw, keys, values, gain, moved, attends, tokens)
-    inner = after(inner, value_first, *value_near_parts)
-    inner_mean = seq_sum(jnp.sum(inner, axis=-1, keepdims=True)) / hid
+    inner = after(inner, value_first)
+    inner_mean = seq_sum(jnp.sum(inner, axis=-1, keepdims=True), value_near_parts) / hid
     raw_grad = (inv_rms * scaled - raw_wide * inv_rms**3 * inner_mean).astype(jnp.bfloat16)
     value_rest = over_dp(jnp.concatenate(value_near_parts, axis=0), 1)
     key_near_parts = [over_dp(raw_grad, 2 * s) for s in range(1, lines)]
@@ -405,7 +428,8 @@
         lanes,
         placed,
         [(tokens, hid)],
-        [(s, 0, 0, tokens, cols, 0, 0, (s,)) for s in range(n_seq)],
+        [(s, 0, 0, tokens // 2, cols, 0, 0, (s,)) for s in range(n_seq)],
+        2,
     )
     return query_grad[None], key_weight_grad, value_weight_grad
 

time: 662 us -> 238 us (0.36)
  Pallas kernels: 495 us -> 61.6 us
  waiting for transfers between devices: 103 us -> 117 us
    pallas_call x4 -> x5, Pallas kernels: 452 us -> 18.8 us  [the longest x4 16.1 us: pack_call(): pl.pallas_call(functools.partial(pack_kernel, moves, len(arrays)), grid=(...]
    ppermute x21 -> x22, waiting for transfers between devices: 96.3 us -> 112 us  [over_dp(): return lax.ppermute(x, 'dp', [(a, a ^ step) for a in range(n_dp)])]
    ppermute x21 -> x22, starting transfers between devices: 31.3 us -> 33.3 us  [over_dp(): return lax.ppermute(x, 'dp', [(a, a ^ step) for a in range(n_dp)])]
  transfers between devices with their start and end apart: 32 -> 33, of which waited for: 14 -> 15; matrix products, arithmetic and copies ran while one was open for 3% -> 5% of each run, Pallas kernels for 44% -> 18%
where the time goes in v5:
time: 238 us; the launch traced here: 237 us
  waiting for transfers between devices  117 us (49%)
  Pallas kernels  61.6 us (26%)
  starting transfers between devices  39.3 us (17%)
  local copies, waits for them, and re-layouts  10.7 us (4%)
  other arithmetic  7.25 us (3%)
    ppermute x22, waiting for transfers between devices, over_dp(): return lax.ppermute(x, 'dp', [(a, a ^ step) for a in range(n_dp)])  112 us
    ppermute x22, starting transfers between devices, over_dp(): return lax.ppermute(x, 'dp', [(a, a ^ step) for a in range(n_dp)])  33.3 us
    pallas_call x4, Pallas kernels, pack_call(): pl.pallas_call(functools.partial(pack_kernel, moves, len(arrays)), grid=(...  16.1 us
    pallas_call x4, Pallas kernels, product_call(): pl.pallas_call(functools.partial(product_kernel, videos), grid=(1,), in_s...  13.4 us
    pallas_call x1, Pallas kernels, gradient_call(): pl.pallas_call(functools.partial(gradient_kernel, parts), grid=(heads,),...  12.6 us
    pallas_call x1, Pallas kernels, attend_call(): pl.pallas_call(functools.partial(attend_kernel, parts), grid=(heads,), in...  11.3 us
    unnamed x48, local copies, waits for them, and re-layouts  6.01 us
    ppermute x11, starting transfers between devices, over_seq(): return lax.ppermute(x, 'seq', [(a, a ^ step) for a in range(n_seq)])  5.95 us
  transfers between devices with their start and end apart: 33, of which 15 were waited for; matrix products, arithmetic and copies ran while one was open for 5% of the time, Pallas kernels for 18%

profile of v5, /device:TPU:0, one launch (start us, length us, event | category | flops | bytes accessed | tf_op | source)
XLA Modules:
  0.0 237.1 jit_solution(8132689383450925091)
XLA Ops:
  1.3 4.2 %shard_map.94 = (bf16[768,512]{1,0:T(8,128)(2,1)}, bf16[1024,512]{1,0:T(8,128)(2,1)}, bf16[512,512]{1,0:T(8,128)(2,1)}, bf16[128,1024]{1,0:T(8,128)(2,1)}, bf16[...) custom-call(s32[8]{0:T(128)} %stack.72.place_ref, bf16[512,1024]{1,0:T(8,128)(2,1)} %refs_0_.1, ...), custom_call_target="tpu_custom_call" | custom-call | flops 1000 | bytes 1000 | tf_op jit(solution)/shard_map/pallas_call | solution.py:243
  5.5 3.0 %collective-permute-start = (bf16[768,512]{1,0:T(8,128)(2,1)}, bf16[768,512]{1,0:T(8,128)(2,1)S(1)}, u32[]{:S(2)}, u32[]{:S(2)}) collective-permute-start(bf16[768,512]{1,0:T(8,128)(2,1)} %get-tuple-element.47), channel_id=1, source_target_pairs={{0,8},{4,12},{8,0},{12,4},{16,24},{20,28},{24,16},{28,20},{1,9},{5... | collective-permute-start | bytes 2359304 | tf_op jit(solution)/shard_map/ppermute | solution.py:267
  9.1 6.1 %shard_map.101 = (bf16[768,1024]{1,0:T(8,128)(2,1)}, bf16[768,1024]{1,0:T(8,128)(2,1)}, bf16[768,1024]{1,0:T(8,128)(2,1)}, bf16[768,1024]{1,0:T(8,128)(2,1)}) custom-call(s32[4]{0:T(128)} %pad_add_fusion.place_ref, bf16[384,4096]{1,0:T(8,128)(2,1)} %bitcast.24, bf16[384,4096]{1,0:T(8,128)(2,1)} %bitcast.25), custom_call_target="tpu_custom_call" | custom-call | flops 1000 | bytes 12582912 | tf_op jit(solution)/shard_map/pallas_call | solution.py:243
  21.0 11.4 %collective-permute-done.1.refs_1_ = bf16[128,1024]{1,0:T(8,128)(2,1)S(1)} collective-permute-done((bf16[128,1024]{1,0:T(8,128)(2,1)}, bf16[128,1024]{1,0:T(8,128)(2,1)S(1)}, u32[]{:S(2)}, u32[]{:S(2)}) %collective-permute-start.1) | collective-permute-done | bytes 262176 | tf_op jit(solution)/shard_map/ppermute | solution.py:267
  32.5 7.3 %collective-permute-done.2.refs_2_ = bf16[128,1024]{1,0:T(8,128)(2,1)S(1)} collective-permute-done((bf16[128,1024]{1,0:T(8,128)(2,1)}, bf16[128,1024]{1,0:T(8,128)(2,1)S(1)}, u32[]{:S(2)}, u32[]{:S(2)}) %collective-permute-start.2) | collective-permute-done | bytes 262176 | tf_op jit(solution)/shard_map/ppermute | solution.py:267
  44.1 2.9 %collective-permute-start.7 = (bf16[512,512]{1,0:T(8,128)(2,1)}, bf16[512,512]{1,0:T(8,128)(2,1)}, u32[]{:S(2)}, u32[]{:S(2)}) collective-permute-start(bf16[512,512]{1,0:T(8,128)(2,1)} %get-tuple-element.56), channel_id=1, source_target_pairs={{0,8},{4,12},{8,0},{12,4},{16,24},{20,28},{24,16},{28,20},{1,9},{5... | collective-permute-start | bytes 1572872 | tf_op jit(solution)/shard_map/ppermute | solution.py:267
  49.2 10.7 %collective-permute-done.7.refs_6_ = bf16[512,512]{1,0:T(8,128)(2,1)} collective-permute-done((bf16[512,512]{1,0:T(8,128)(2,1)}, bf16[512,512]{1,0:T(8,128)(2,1)}, u32[]{:S(2)}, u32[]{:S(2)}) %collective-permute-start.7) | collective-permute-done | bytes 524320 | tf_op jit(solution)/shard_map/ppermute | solution.py:267
  62.4 3.3 %shard_map.97 = f32[256,512]{1,0:T(8,128)} custom-call(s32[4]{0:T(128)} %pad_add_fusion.1.place_ref, bf16[384,1024]{1,0:T(8,128)(2,1)} %get-tuple-element.50.refs_1_.refs_0_.mine_ref, bf16[384,1024]{1,0:T(8,128)(2,1)} %get-tuple-element.50.refs_1_.refs_0_.mine_ref, bf16[384,1024]{1,0:T(8,128)(2,1)} %copy-done, bf16[384,1024]{1,0:T(8,128)(2,1)} %copy-done, ...), custom_call_target="tpu_custom_call" | custom-call | flops 1000 | bytes 1000 | tf_op jit(solution)/shard_map/pallas_call | solution.py:181
  65.8 2.8 %collective-permute-start.6 = (f32[256,512]{1,0:T(8,128)}, f32[256,512]{1,0:T(8,128)S(1)}, u32[]{:S(2)}, u32[]{:S(2)}) collective-permute-start(f32[256,512]{1,0:T(8,128)} %shard_map.97), channel_id=1, source_target_pairs={{0,16},{4,20},{8,24},{12,28},{16,0},{20,4},{24,8},{28,12},{1,17},{... | collective-permute-start | bytes 1572872 | tf_op jit(solution)/shard_map/ppermute | solution.py:267
  69.2 3.3 %shard_map.96 = f32[256,512]{1,0:T(8,128)} custom-call(s32[4]{0:T(128)} %pad_add_fusion.1.place_ref, bf16[128,1024]{1,0:T(8,128)(2,1)} %get-tuple-element.46.refs_0_.first_ref, bf16[384,1024]{1,0:T(8,128)(2,1)} %get-tuple-element.50.refs_1_.refs_0_.mine_ref, bf16[128,1024]{1,0:T(8,128)(2,1)} %get-tuple-element.51.refs_2_.sibling_first_ref, ...), custom_call_target="tpu_custom_call" | custom-call | flops 1000 | bytes 1000 | tf_op jit(solution)/shard_map/pallas_call | solution.py:181
  74.0 3.4 %shard_map.98 = f32[256,512]{1,0:T(8,128)} custom-call(s32[4]{0:T(128)} %pad_add_fusion.1.place_ref, bf16[384,1024]{1,0:T(8,128)(2,1)} %get-tuple-element.50.refs_1_.refs_0_.mine_ref, bf16[384,1024]{1,0:T(8,128)(2,1)} %get-tuple-element.50.refs_1_.refs_0_.mine_ref, bf16[384,1024]{1,0:T(8,128)(2,1)} %copy-done, bf16[384,1024]{1,0:T(8,128)(2,1)} %copy-done, ...), custom_call_target="tpu_custom_call" | custom-call | flops 1000 | bytes 1000 | tf_op jit(solution)/shard_map/pallas_call | solution.py:181
  80.0 24.0 %collective-permute-done.6 = f32[256,512]{1,0:T(8,128)S(1)} collective-permute-done((f32[256,512]{1,0:T(8,128)}, f32[256,512]{1,0:T(8,128)S(1)}, u32[]{:S(2)}, u32[]{:S(2)}) %collective-permute-start.6) | collective-permute-done | bytes 524320 | tf_op jit(solution)/shard_map/ppermute | solution.py:267
  104.1 12.7 %collective-permute-done.9 = bf16[128,512]{1,0:T(8,128)(2,1)S(1)} collective-permute-done((bf16[128,512]{1,0:T(8,128)(2,1)S(1)}, bf16[128,512]{1,0:T(8,128)(2,1)S(1)}, u32[]{:S(2)}, u32[]{:S(2)}) %collective-permute-start.9) | collective-permute-done | bytes 131104 | tf_op jit(solution)/shard_map/ppermute | solution.py:267
  128.1 3.3 %shard_map.100 = f32[256,512]{1,0:T(8,128)} custom-call(s32[4]{0:T(128)} %pad_add_fusion.1.place_ref, bf16[128,1024]{1,0:T(8,128)(2,1)} %get-tuple-element.46.refs_0_.first_ref, bf16[384,1024]{1,0:T(8,128)(2,1)} %get-tuple-element.50.refs_1_.refs_0_.mine_ref, bf16[128,1024]{1,0:T(8,128)(2,1)} %get-tuple-element.51.refs_2_.sibling_first_ref, ...), custom_call_target="tpu_custom_call" | custom-call | flops 1000 | bytes 1000 | tf_op jit(solution)/shard_map/pallas_call | solution.py:181
  133.3 7.2 %collective-permute-done.10 = bf16[512,512]{0,1:T(8,128)(2,1)S(1)} collective-permute-done((bf16[512,512]{0,1:T(8,128)(2,1)S(1)}, bf16[512,512]{0,1:T(8,128)(2,1)S(1)}, u32[]{:S(2)}, u32[]{:S(2)}) %collective-permute-start.10) | collective-permute-done | bytes 524320 | tf_op jit(solution)/shard_map/ppermute | solution.py:267
  142.5 11.3 %shard_map.102 = (f32[8,128,384]{2,1,0:T(8,128)}, f32[8,128,384]{2,1,0:T(8,128)}, f32[8,128,384]{2,1,0:T(8,128)}, f32[8,128,384]{2,1,0:T(8,128)}, bf16[128,1024]{1,0:T(8,128)(2,1)}, /*index=5*/bf16[128,1024]{1,0:T(8,128)(2,1)}) custom-call(s32[1]{0:T(128)S(6)} %copy.22.length_ref, bf16[128,1024]{1,0:T(8,128)(2,1)} %get-tuple-element.61.raw_ref, ...), custom_call_target="tpu_custom_call" | custom-call | flops 3221225472 | bytes 25165824 | tf_op jit(solution)/shard_map/pallas_call | solution.py:81
  159.5 12.6 %shard_map.103 = (bf16[384,1024]{1,0:T(8,128)(2,1)}, bf16[384,1024]{1,0:T(8,128)(2,1)}, bf16[384,1024]{1,0:T(8,128)(2,1)}, bf16[384,1024]{1,0:T(8,128)(2,1)}, f32[128,1024]{1,0:T(8,128)}, /*index=5*/f32[128,128]{1,0:T(8,128)}) custom-call(bf16[128,1024]{1,0:T(8,128)(2,1)} %get-tuple-element.61.raw_ref, bf16[128,1024]{1,0:T(8,128)(2,1)} %get-tuple-element.69.keys_ref, ...), custom_call_target="tpu_custom_call" | custom-call | flops 4831838208 | bytes 25165824 | tf_op jit(solution)/shard_map/pallas_call | solution.py:110
  175.3 2.8 %collective-permute-done.19.refs_10_ = bf16[128,1024]{1,0:T(8,128)(2,1)S(1)} collective-permute-done((bf16[128,1024]{1,0:T(8,128)(2,1)}, bf16[128,1024]{1,0:T(8,128)(2,1)S(1)}, u32[]{:S(2)}, u32[]{:S(2)}) %collective-permute-start.19) | collective-permute-done | bytes 262176 | tf_op jit(solution)/shard_map/ppermute | solution.py:267
  189.4 6.7 %collective-permute-done.29.refs_3_ = bf16[128,1024]{1,0:T(8,128)(2,1)S(1)} collective-permute-done((bf16[128,1024]{1,0:T(8,128)(2,1)S(1)}, bf16[128,1024]{1,0:T(8,128)(2,1)S(1)}, u32[]{:S(2)}, u32[]{:S(2)}) %collective-permute-start.29) | collective-permute-done | bytes 262176 | tf_op jit(solution)/shard_map/ppermute | solution.py:267
  196.0 9.0 %collective-permute-done.28.refs_2_ = bf16[128,1024]{1,0:T(8,128)(2,1)S(1)} collective-permute-done((bf16[128,1024]{1,0:T(8,128)(2,1)S(1)}, bf16[128,1024]{1,0:T(8,128)(2,1)S(1)}, u32[]{:S(2)}, u32[]{:S(2)}) %collective-permute-start.28) | collective-permute-done | bytes 262176 | tf_op jit(solution)/shard_map/ppermute | solution.py:267
  208.2 11.8 %collective-permute-done.32.refs_6_.refs_7_ = bf16[256,1024]{1,0:T(8,128)(2,1)S(1)} collective-permute-done((bf16[256,1024]{1,0:T(8,128)(2,1)S(1)}, bf16[256,1024]{1,0:T(8,128)(2,1)S(1)}, u32[]{:S(2)}, u32[]{:S(2)}) %collective-permute-start.32) | collective-permute-done | bytes 524320 | tf_op jit(solution)/shard_map/ppermute | solution.py:267
  220.8 6.5 %collective-permute-done.31.refs_4_.refs_5_ = bf16[256,1024]{1,0:T(8,128)(2,1)} collective-permute-done((bf16[256,1024]{1,0:T(8,128)(2,1)S(1)}, bf16[256,1024]{1,0:T(8,128)(2,1)}, u32[]{:S(2)}, u32[]{:S(2)}) %collective-permute-start.31) | collective-permute-done | bytes 524320 | tf_op jit(solution)/shard_map/ppermute | solution.py:267
  227.3 5.5 %shard_map.105 = (f32[512,1024]{1,0:T(8,128)}, f32[512,1024]{1,0:T(8,128)}) custom-call(bf16[512,1024]{1,0:T(8,128)(2,1)} %maximum_bitcast_fusion.columns_ref, bf16[128,1024]{1,0:T(8,128)(2,1)} %copy-done.5, bf16[128,1024]{1,0:T(8,128)(2,1)} %copy-done.18, bf16[128,1024]{1,0:T(8,128)(2,1)} %copy-done.17, bf16[128,1024]{1,0:T(8,128)(2,1)} %copy-done.16, ...), custom_call_target="tpu_custom_call" | custom-call | flops 2147483648 | bytes 8388608 | tf_op jit(solution)/shard_map/pallas_call | solution.py:206
  234.0 3.1 %shard_map.104 = bf16[384,4096]{1,0:T(8,128)(2,1)} custom-call(s32[4]{0:T(128)} %pad_add_fusion.place_ref, bf16[384,1024]{1,0:T(8,128)(2,1)} %get-tuple-element.74.refs_0_, bf16[384,1024]{1,0:T(8,128)(2,1)} %copy-done.7, bf16[384,1024]{1,0:T(8,128)(2,1)} %copy-done.6, bf16[384,1024]{1,0:T(8,128)(2,1)} %copy-done.8), custom_call_target="tpu_custom_call" | custom-call | flops 1000 | bytes 1000 | tf_op jit(solution)/shard_map/pallas_call | solution.py:243
  (126 shorter events, 60.3 us)
Async XLA Ops:
  5.5 34.3 %collective-permute-start = (bf16[768,512]{1,0:T(8,128)(2,1)}, bf16[768,512]{1,0:T(8,128)(2,1)S(1)}, u32[]{:S(2)}, u32[]{:S(2)}) collective-permute-start(bf16[768,512]{1,0:T(8,128)(2,1)} %get-tuple-element.47), channel_id=1, source_target_pairs={{0,8},{4,12},{8,0},{12,4},{16,24},{20,28},{24,16},{28,20},{1,9},{5... | collective-permute-start | bytes 2359304 | tf_op jit(solution)/shard_map/ppermute | solution.py:267
  15.2 53.3 %collective-permute-start.15 = (bf16[768,1024]{1,0:T(8,128)(2,1)}, bf16[768,1024]{1,0:T(8,128)(2,1)S(1)}, u32[]{:S(2)}, u32[]{:S(2)}) collective-permute-start(bf16[768,1024]{1,0:T(8,128)(2,1)} %get-tuple-element.66), channel_id=1, source_target_pairs={{0,2},{1,3},{2,0},{3,1},{4,6},{5,7},{6,4},{7,5},{8,10},{9,11},{10,... | collective-permute-start | bytes 4718600 | tf_op jit(solution)/shard_map/ppermute | solution.py:270
  16.7 15.8 %collective-permute-start.1 = (bf16[128,1024]{1,0:T(8,128)(2,1)}, bf16[128,1024]{1,0:T(8,128)(2,1)S(1)}, u32[]{:S(2)}, u32[]{:S(2)}) collective-permute-start(bf16[128,1024]{1,0:T(8,128)(2,1)} %get-tuple-element.48), channel_id=1, source_target_pairs={{0,16},{4,20},{8,24},{12,28},{16,0},{20,4},{24,8},{28,12},{1,17},{... | collective-permute-start | bytes 786440 | tf_op jit(solution)/shard_map/ppermute | solution.py:267
  19.3 20.5 %collective-permute-start.2 = (bf16[128,1024]{1,0:T(8,128)(2,1)}, bf16[128,1024]{1,0:T(8,128)(2,1)S(1)}, u32[]{:S(2)}, u32[]{:S(2)}) collective-permute-start(bf16[128,1024]{1,0:T(8,128)(2,1)} %get-tuple-element.49), channel_id=1, source_target_pairs={{0,24},{4,28},{8,16},{12,20},{16,8},{20,12},{24,0},{28,4},{1,25},{... | collective-permute-start | bytes 786440 | tf_op jit(solution)/shard_map/ppermute | solution.py:267
  19.5 42.0 %collective-permute-start.4 = (bf16[1024,512]{1,0:T(8,128)(2,1)S(1)}, bf16[1024,512]{1,0:T(8,128)(2,1)}, u32[]{:S(2)}, u32[]{:S(2)}) collective-permute-start(bf16[1024,512]{1,0:T(8,128)(2,1)S(1)} %copy-done.2), channel_id=1, source_target_pairs={{0,4},{4,0},{8,12},{12,8},{16,20},{20,16},{24,28},{28,24},{1,5},{5... | collective-permute-start | bytes 3145736 | tf_op jit(solution)/shard_map/ppermute | solution.py:267
  44.1 17.4 %collective-permute-start.3 = (bf16[384,1024]{1,0:T(8,128)(2,1)}, bf16[384,1024]{1,0:T(8,128)(2,1)S(1)}, u32[]{:S(2)}, u32[]{:S(2)}) collective-permute-start(bf16[384,1024]{1,0:T(8,128)(2,1)} %get-tuple-element.52), channel_id=1, source_target_pairs={{0,1},{1,0},{2,3},{3,2},{4,5},{5,4},{6,7},{7,6},{8,9},{9,8},{10,11... | collective-permute-start | bytes 2359304 | tf_op jit(solution)/shard_map/ppermute | solution.py:270
  44.1 15.8 %collective-permute-start.7 = (bf16[512,512]{1,0:T(8,128)(2,1)}, bf16[512,512]{1,0:T(8,128)(2,1)}, u32[]{:S(2)}, u32[]{:S(2)}) collective-permute-start(bf16[512,512]{1,0:T(8,128)(2,1)} %get-tuple-element.56), channel_id=1, source_target_pairs={{0,8},{4,12},{8,0},{12,4},{16,24},{20,28},{24,16},{28,20},{1,9},{5... | collective-permute-start | bytes 1572872 | tf_op jit(solution)/shard_map/ppermute | solution.py:267
  47.0 14.4 %collective-permute-start.5 = (bf16[512,512]{1,0:T(8,128)(2,1)}, bf16[512,512]{1,0:T(8,128)(2,1)}, u32[]{:S(2)}, u32[]{:S(2)}) collective-permute-start(bf16[512,512]{1,0:T(8,128)(2,1)} %get-tuple-element.54.refs_6_), channel_id=1, source_target_pairs={{0,4},{4,0},{8,12},{12,8},{16,20},{20,16},{24,28},{28,24},{1,5},{5... | collective-permute-start | bytes 1572872 | tf_op jit(solution)/shard_map/ppermute | solution.py:267
  65.8 38.2 %collective-permute-start.6 = (f32[256,512]{1,0:T(8,128)}, f32[256,512]{1,0:T(8,128)S(1)}, u32[]{:S(2)}, u32[]{:S(2)}) collective-permute-start(f32[256,512]{1,0:T(8,128)} %shard_map.97), channel_id=1, source_target_pairs={{0,16},{4,20},{8,24},{12,28},{16,0},{20,4},{24,8},{28,12},{1,17},{... | collective-permute-start | bytes 1572872 | tf_op jit(solution)/shard_map/ppermute | solution.py:267
  68.5 74.0 %collective-permute-start.14 = (bf16[768,1024]{1,0:T(8,128)(2,1)}, bf16[768,1024]{1,0:T(8,128)(2,1)}, u32[]{:S(2)}, u32[]{:S(2)}) collective-permute-start(bf16[768,1024]{1,0:T(8,128)(2,1)} %get-tuple-element.65), channel_id=1, source_target_pairs={{0,1},{1,0},{2,3},{3,2},{4,5},{5,4},{6,7},{7,6},{8,9},{9,8},{10,11... | collective-permute-start | bytes 4718600 | tf_op jit(solution)/shard_map/ppermute | solution.py:270
  68.5 74.0 %collective-permute-start.16 = (bf16[768,1024]{1,0:T(8,128)(2,1)}, bf16[768,1024]{1,0:T(8,128)(2,1)}, u32[]{:S(2)}, u32[]{:S(2)}) collective-permute-start(bf16[768,1024]{1,0:T(8,128)(2,1)} %get-tuple-element.68), channel_id=1, source_target_pairs={{0,3},{1,2},{2,1},{3,0},{4,7},{5,6},{6,5},{7,4},{8,11},{9,10},{10,... | collective-permute-start | bytes 4718600 | tf_op jit(solution)/shard_map/ppermute | solution.py:270
  77.4 54.7 %collective-permute-start.11 = (f32[256,512]{1,0:T(8,128)}, f32[256,512]{1,0:T(8,128)S(1)}, u32[]{:S(2)}, u32[]{:S(2)}) collective-permute-start(f32[256,512]{1,0:T(8,128)} %shard_map.98), channel_id=1, source_target_pairs={{0,16},{4,20},{8,24},{12,28},{16,0},{20,4},{24,8},{28,12},{1,17},{... | collective-permute-start | bytes 1572872 | tf_op jit(solution)/shard_map/ppermute | solution.py:267
  153.8 18.3 %collective-permute-start.23 = (bf16[128,1024]{1,0:T(8,128)(2,1)}, bf16[128,1024]{1,0:T(8,128)(2,1)S(1)}, u32[]{:S(2)}, u32[]{:S(2)}) collective-permute-start(bf16[128,1024]{1,0:T(8,128)(2,1)} %get-tuple-element.76.refs_8_), channel_id=1, source_target_pairs={{0,4},{4,0},{8,12},{12,8},{16,20},{20,16},{24,28},{28,24},{1,5},{5... | collective-permute-start | bytes 786440 | tf_op jit(solution)/shard_map/ppermute | solution.py:267
  155.2 20.1 %collective-permute-start.20 = (bf16[128,1024]{1,0:T(8,128)(2,1)}, bf16[128,1024]{1,0:T(8,128)(2,1)S(1)}, u32[]{:S(2)}, u32[]{:S(2)}) collective-permute-start(bf16[128,1024]{1,0:T(8,128)(2,1)} %get-tuple-element.76.refs_8_), channel_id=1, source_target_pairs={{0,24},{4,28},{8,16},{12,20},{16,8},{20,12},{24,0},{28,4},{1,25},{... | collective-permute-start | bytes 786440 | tf_op jit(solution)/shard_map/ppermute | solution.py:267
  157.6 20.5 %collective-permute-start.19 = (bf16[128,1024]{1,0:T(8,128)(2,1)}, bf16[128,1024]{1,0:T(8,128)(2,1)S(1)}, u32[]{:S(2)}, u32[]{:S(2)}) collective-permute-start(bf16[128,1024]{1,0:T(8,128)(2,1)} %get-tuple-element.76.refs_8_), channel_id=1, source_target_pairs={{0,16},{4,20},{8,24},{12,28},{16,0},{20,4},{24,8},{28,12},{1,17},{... | collective-permute-start | bytes 786440 | tf_op jit(solution)/shard_map/ppermute | solution.py:267
  157.6 20.5 %collective-permute-start.18 = (bf16[128,1024]{1,0:T(8,128)(2,1)}, bf16[128,1024]{1,0:T(8,128)(2,1)S(1)}, u32[]{:S(2)}, u32[]{:S(2)}) collective-permute-start(bf16[128,1024]{1,0:T(8,128)(2,1)} %get-tuple-element.76.refs_8_), channel_id=1, source_target_pairs={{0,8},{4,12},{8,0},{12,4},{16,24},{20,28},{24,16},{28,20},{1,9},{5... | collective-permute-start | bytes 786440 | tf_op jit(solution)/shard_map/ppermute | solution.py:267
  179.8 26.2 %collective-permute-start.21 = (bf16[384,1024]{1,0:T(8,128)(2,1)S(1)}, bf16[384,1024]{1,0:T(8,128)(2,1)S(1)}, u32[]{:S(2)}, u32[]{:S(2)}) collective-permute-start(bf16[384,1024]{1,0:T(8,128)(2,1)S(1)} %pad_maximum_fusion), channel_id=1, source_target_pairs={{0,4},{4,0},{8,12},{12,8},{16,20},{20,16},{24,28},{28,24},{1,5},{5... | collective-permute-start | bytes 2359304 | tf_op jit(solution)/shard_map/ppermute | solution.py:267
  183.2 22.8 %collective-permute-start.26 = (bf16[384,1024]{1,0:T(8,128)(2,1)S(1)}, bf16[384,1024]{1,0:T(8,128)(2,1)S(1)}, u32[]{:S(2)}, u32[]{:S(2)}) collective-permute-start(bf16[384,1024]{1,0:T(8,128)(2,1)S(1)} %copy-done.20), channel_id=1, source_target_pairs={{0,2},{1,3},{2,0},{3,1},{4,6},{5,7},{6,4},{7,5},{8,10},{9,11},{10,... | collective-permute-start | bytes 2359304 | tf_op jit(solution)/shard_map/ppermute | solution.py:270
  187.5 17.5 %collective-permute-start.28 = (bf16[128,1024]{1,0:T(8,128)(2,1)S(1)}, bf16[128,1024]{1,0:T(8,128)(2,1)S(1)}, u32[]{:S(2)}, u32[]{:S(2)}) collective-permute-start(bf16[128,1024]{1,0:T(8,128)(2,1)S(1)} %fusion.3.refs_0_), channel_id=1, source_target_pairs={{0,16},{4,20},{8,24},{12,28},{16,0},{20,4},{24,8},{28,12},{1,17},{... | collective-permute-start | bytes 786440 | tf_op jit(solution)/shard_map/ppermute | solution.py:267
  187.5 18.5 %collective-permute-start.27 = (bf16[128,1024]{1,0:T(8,128)(2,1)S(1)}, bf16[128,1024]{1,0:T(8,128)(2,1)S(1)}, u32[]{:S(2)}, u32[]{:S(2)}) collective-permute-start(bf16[128,1024]{1,0:T(8,128)(2,1)S(1)} %fusion.3.refs_0_), channel_id=1, source_target_pairs={{0,8},{4,12},{8,0},{12,4},{16,24},{20,28},{24,16},{28,20},{1,9},{5... | collective-permute-start | bytes 786440 | tf_op jit(solution)/shard_map/ppermute | solution.py:267
  205.1 14.9 %collective-permute-start.32 = (bf16[256,1024]{1,0:T(8,128)(2,1)S(1)}, bf16[256,1024]{1,0:T(8,128)(2,1)S(1)}, u32[]{:S(2)}, u32[]{:S(2)}) collective-permute-start(bf16[256,1024]{1,0:T(8,128)(2,1)S(1)} %pad_maximum_fusion.2), channel_id=1, source_target_pairs={{0,4},{4,0},{8,12},{12,8},{16,20},{20,16},{24,28},{28,24},{1,5},{5... | collective-permute-start | bytes 1572872 | tf_op jit(solution)/shard_map/ppermute | solution.py:267
  206.0 26.9 %collective-permute-start.22 = (bf16[384,1024]{1,0:T(8,128)(2,1)}, bf16[384,1024]{1,0:T(8,128)(2,1)S(1)}, u32[]{:S(2)}, u32[]{:S(2)}) collective-permute-start(bf16[384,1024]{1,0:T(8,128)(2,1)} %get-tuple-element.77), channel_id=1, source_target_pairs={{0,1},{1,0},{2,3},{3,2},{4,5},{5,4},{6,7},{7,6},{8,9},{9,8},{10,11... | collective-permute-start | bytes 2359304 | tf_op jit(solution)/shard_map/ppermute | solution.py:270
  206.8 26.0 %collective-permute-start.30 = (bf16[384,1024]{1,0:T(8,128)(2,1)S(1)}, bf16[384,1024]{1,0:T(8,128)(2,1)S(1)}, u32[]{:S(2)}, u32[]{:S(2)}) collective-permute-start(bf16[384,1024]{1,0:T(8,128)(2,1)S(1)} %copy-done.19), channel_id=1, source_target_pairs={{0,3},{1,2},{2,1},{3,0},{4,7},{5,6},{6,5},{7,4},{8,11},{9,10},{10,... | collective-permute-start | bytes 2359304 | tf_op jit(solution)/shard_map/ppermute | solution.py:270
  206.9 20.4 %collective-permute-start.31 = (bf16[256,1024]{1,0:T(8,128)(2,1)S(1)}, bf16[256,1024]{1,0:T(8,128)(2,1)}, u32[]{:S(2)}, u32[]{:S(2)}) collective-permute-start(bf16[256,1024]{1,0:T(8,128)(2,1)S(1)} %pad_maximum_fusion.1), channel_id=1, source_target_pairs={{0,4},{4,0},{8,12},{12,8},{16,20},{20,16},{24,28},{28,24},{1,5},{5... | collective-permute-start | bytes 1572872 | tf_op jit(solution)/shard_map/ppermute | solution.py:267
  (33 other events, 426.6 us)

commit v6 on v5

--- a/solution.py
+++ b/solution.py
@@ -365,12 +365,10 @@
             jnp.concatenate([other, own], axis=1),
         )
 
-    def seq_sum(x, before=()):
+    def seq_sum(x):
         step = 1
         while step < n_seq:
             x = x + over_seq(x, step)
-            if step == 1:
-                x = after(x, *before)
             step *= 2
         return x
 
@@ -379,15 +377,16 @@
     columns = jnp.concatenate([own_columns, other_columns], axis=0).T
 
     key_sent = over_dp(product(key_quad, True), 4)
-    value_product = product(value_quad, True)
-    value_sent = over_dp(value_product, 4)
-    key_total = reduced(product(key_quad, False) + after(key_sent, value_product))
+    value_product, value_rest_product = product(value_quad, True), product(value_quad, False)
+    key_sent = after(key_sent, value_product, value_rest_product, other_columns)
+    value_sent = over_dp(after(value_product, key_sent), 4)
+    key_total = reduced(product(key_quad, False) + key_sent)
     raw = joined(key_total)
     raw_wide = raw.astype(jnp.float32)
     squares = seq_sum(jnp.sum(raw_wide * raw_wide, axis=-1, keepdims=True))
     inv_rms = lax.rsqrt(squares / hid + 1e-06)
     gain = lax.dynamic_slice(key_gain, (lane * cols,), (cols,)).reshape(1, cols)
-    value_total = reduced(product(value_quad, False) + after(value_sent, inv_rms))
+    value_total = reduced(value_rest_product + after(value_sent, inv_rms))
     values = joined(value_total)
     attends, keys, value_grad = attend_call(
         lengths, after(raw, columns, value_total), inv_rms, gain, moved, tokens
@@ -397,9 +396,10 @@
     value_first = over_dp(value_grad, 1)
     outs, scaled, inner = gradient_call(raw, keys, values, gain, moved, attends, tokens)
     inner = after(inner, value_first)
-    inner_mean = seq_sum(jnp.sum(inner, axis=-1, keepdims=True), value_near_parts) / hid
+    inner_mean = seq_sum(jnp.sum(inner, axis=-1, keepdims=True)) / hid
     raw_grad = (inv_rms * scaled - raw_wide * inv_rms**3 * inner_mean).astype(jnp.bfloat16)
     value_rest = over_dp(jnp.concatenate(value_near_parts, axis=0), 1)
+    raw_grad = after(raw_grad, *value_near_parts)
     key_near_parts = [over_dp(raw_grad, 2 * s) for s in range(1, lines)]
     placed = [outs[0]] + [None] * (n_seq - 1)
     previous = (inner_mean,)
@@ -408,10 +408,10 @@
         previous = (placed[s], value_rest, *key_near_parts)
     placed[1] = over_seq(after(outs[1], value_rest), 1)
     split = lines // 2
-    key_first = over_dp(
-        after(jnp.concatenate([raw_grad, *key_near_parts[: split - 1]], axis=0), value_rest), 1
-    )
-    key_rest = over_dp(jnp.concatenate(key_near_parts[split - 1 :], axis=0), 1)
+    key_early = jnp.concatenate([raw_grad, *key_near_parts[: split - 1]], axis=0)
+    key_first = over_dp(key_early, 1)
+    key_late = [after(x, key_first) for x in key_near_parts[split - 1 :]]
+    key_rest = over_dp(jnp.concatenate(key_late, axis=0), 1)
     key_parts = (
         [(x, LIVE, 0) for x in (raw_grad, *key_near_parts)]
         + [(key_first, LIVE, s) for s in range(split)]

time: 238 us -> 237 us (level)
  waiting for transfers between devices: 117 us -> 125 us
  starting transfers between devices: 39.3 us -> 31.6 us
  local copies, waits for them, and re-layouts: 10.7 us -> 7.31 us
    ppermute x22, waiting for transfers between devices: 112 us -> 122 us  [over_dp(): return lax.ppermute(x, 'dp', [(a, a ^ step) for a in range(n_dp)])]
    ppermute x22, starting transfers between devices: 33.3 us -> 24.5 us  [over_dp(): return lax.ppermute(x, 'dp', [(a, a ^ step) for a in range(n_dp)])]
  transfers between devices with their start and end apart: 33 -> 33, of which waited for: 15 -> 18; matrix products, arithmetic and copies ran while one was open for 5% -> 4% of each run, Pallas kernels for 18% -> 18%
where the time goes in v6:
time: 237 us; the launch traced here: 236 us
  waiting for transfers between devices  125 us (53%)
  Pallas kernels  61.9 us (26%)
  starting transfers between devices  31.6 us (13%)
  other arithmetic  8.27 us (3%)
  local copies, waits for them, and re-layouts  7.31 us (3%)
    ppermute x22, waiting for transfers between devices, over_dp(): return lax.ppermute(x, 'dp', [(a, a ^ step) for a in range(n_dp)])  122 us
    ppermute x22, starting transfers between devices, over_dp(): return lax.ppermute(x, 'dp', [(a, a ^ step) for a in range(n_dp)])  24.5 us
    pallas_call x4, Pallas kernels, pack_call(): pl.pallas_call(functools.partial(pack_kernel, moves, len(arrays)), grid=(...  16.2 us
    pallas_call x4, Pallas kernels, product_call(): pl.pallas_call(functools.partial(product_kernel, videos), grid=(1,), in_s...  13.5 us
    pallas_call x1, Pallas kernels, gradient_call(): pl.pallas_call(functools.partial(gradient_kernel, parts), grid=(heads,),...  12.7 us
    pallas_call x1, Pallas kernels, attend_call(): pl.pallas_call(functools.partial(attend_kernel, parts), grid=(heads,), in...  11.3 us
    ppermute x11, starting transfers between devices, over_seq(): return lax.ppermute(x, 'seq', [(a, a ^ step) for a in range(n_seq)])  7.17 us
    pallas_call x1, Pallas kernels, weights_call(): pl.pallas_call(functools.partial(weights_kernel, videos), grid=(cols // t...  5.55 us
  transfers between devices with their start and end apart: 33, of which 18 were waited for; matrix products, arithmetic and copies ran while one was open for 4% of the time, Pallas kernels for 18%

profile of v6, /device:TPU:0, one launch (start us, length us, event | category | flops | bytes accessed | tf_op | source)
XLA Modules:
  0.0 235.7 jit_solution(131538398793470294)
XLA Ops:
  1.3 4.3 %shard_map.94 = (bf16[768,512]{1,0:T(8,128)(2,1)}, bf16[1024,512]{1,0:T(8,128)(2,1)}, bf16[512,512]{1,0:T(8,128)(2,1)}, bf16[128,1024]{1,0:T(8,128)(2,1)}, bf16[...) custom-call(s32[8]{0:T(128)} %stack.72.place_ref, bf16[512,1024]{1,0:T(8,128)(2,1)} %refs_0_.1, ...), custom_call_target="tpu_custom_call" | custom-call | flops 1000 | bytes 1000 | tf_op jit(solution)/shard_map/pallas_call | solution.py:243
  5.6 3.0 %collective-permute-start = (bf16[768,512]{1,0:T(8,128)(2,1)}, bf16[768,512]{1,0:T(8,128)(2,1)S(1)}, u32[]{:S(2)}, u32[]{:S(2)}) collective-permute-start(bf16[768,512]{1,0:T(8,128)(2,1)} %get-tuple-element.49), channel_id=1, source_target_pairs={{0,8},{4,12},{8,0},{12,4},{16,24},{20,28},{24,16},{28,20},{1,9},{5... | collective-permute-start | bytes 2359304 | tf_op jit(solution)/shard_map/ppermute | solution.py:267
  11.8 6.1 %shard_map.101 = (bf16[768,1024]{1,0:T(8,128)(2,1)}, bf16[768,1024]{1,0:T(8,128)(2,1)}, bf16[768,1024]{1,0:T(8,128)(2,1)}, bf16[768,1024]{1,0:T(8,128)(2,1)}) custom-call(s32[4]{0:T(128)} %pad_add_fusion.place_ref, bf16[384,4096]{1,0:T(8,128)(2,1)} %bitcast.24, bf16[384,4096]{1,0:T(8,128)(2,1)} %bitcast.25), custom_call_target="tpu_custom_call" | custom-call | flops 1000 | bytes 12582912 | tf_op jit(solution)/shard_map/pallas_call | solution.py:243
  21.1 11.4 %collective-permute-done.1.refs_1_ = bf16[128,1024]{1,0:T(8,128)(2,1)} collective-permute-done((bf16[128,1024]{1,0:T(8,128)(2,1)}, bf16[128,1024]{1,0:T(8,128)(2,1)}, u32[]{:S(2)}, u32[]{:S(2)}) %collective-permute-start.1) | collective-permute-done | bytes 262176 | tf_op jit(solution)/shard_map/ppermute | solution.py:267
  32.5 7.4 %collective-permute-done.2.refs_2_ = bf16[128,1024]{1,0:T(8,128)(2,1)} collective-permute-done((bf16[128,1024]{1,0:T(8,128)(2,1)}, bf16[128,1024]{1,0:T(8,128)(2,1)}, u32[]{:S(2)}, u32[]{:S(2)}) %collective-permute-start.2) | collective-permute-done | bytes 262176 | tf_op jit(solution)/shard_map/ppermute | solution.py:267
  45.7 12.4 %collective-permute-done.7.refs_6_ = bf16[512,512]{1,0:T(8,128)(2,1)} collective-permute-done((bf16[512,512]{1,0:T(8,128)(2,1)}, bf16[512,512]{1,0:T(8,128)(2,1)}, u32[]{:S(2)}, u32[]{:S(2)}) %collective-permute-start.7) | collective-permute-done | bytes 524320 | tf_op jit(solution)/shard_map/ppermute | solution.py:267
  65.1 3.4 %shard_map.97 = f32[256,512]{1,0:T(8,128)} custom-call(s32[4]{0:T(128)} %pad_add_fusion.1.place_ref, bf16[384,1024]{1,0:T(8,128)(2,1)} %get-tuple-element.52.refs_1_.refs_0_.mine_ref, bf16[384,1024]{1,0:T(8,128)(2,1)} %get-tuple-element.52.refs_1_.refs_0_.mine_ref, bf16[384,1024]{1,0:T(8,128)(2,1)} %copy-done, bf16[384,1024]{1,0:T(8,128)(2,1)} %copy-done, ...), custom_call_target="tpu_custom_call" | custom-call | flops 1000 | bytes 1000 | tf_op jit(solution)/shard_map/pallas_call | solution.py:181
  70.4 3.4 %shard_map.96 = f32[256,512]{1,0:T(8,128)} custom-call(s32[4]{0:T(128)} %pad_add_fusion.1.place_ref, bf16[128,1024]{1,0:T(8,128)(2,1)} %get-tuple-element.48.refs_0_.first_ref, bf16[384,1024]{1,0:T(8,128)(2,1)} %get-tuple-element.52.refs_1_.refs_0_.mine_ref, bf16[128,1024]{1,0:T(8,128)(2,1)} %get-tuple-element.53.refs_2_.sibling_first_ref, ...), custom_call_target="tpu_custom_call" | custom-call | flops 1000 | bytes 1000 | tf_op jit(solution)/shard_map/pallas_call | solution.py:181
  73.8 3.3 %shard_map.99 = f32[256,512]{1,0:T(8,128)} custom-call(s32[4]{0:T(128)} %pad_add_fusion.1.place_ref, bf16[128,1024]{1,0:T(8,128)(2,1)} %get-tuple-element.48.refs_0_.first_ref, bf16[384,1024]{1,0:T(8,128)(2,1)} %get-tuple-element.52.refs_1_.refs_0_.mine_ref, bf16[128,1024]{1,0:T(8,128)(2,1)} %get-tuple-element.53.refs_2_.sibling_first_ref, ...), custom_call_target="tpu_custom_call" | custom-call | flops 1000 | bytes 1000 | tf_op jit(solution)/shard_map/pallas_call | solution.py:181
  77.1 3.4 %shard_map.98 = f32[256,512]{1,0:T(8,128)} custom-call(s32[4]{0:T(128)} %pad_add_fusion.1.place_ref, bf16[384,1024]{1,0:T(8,128)(2,1)} %get-tuple-element.52.refs_1_.refs_0_.mine_ref, bf16[384,1024]{1,0:T(8,128)(2,1)} %get-tuple-element.52.refs_1_.refs_0_.mine_ref, bf16[384,1024]{1,0:T(8,128)(2,1)} %copy-done, bf16[384,1024]{1,0:T(8,128)(2,1)} %copy-done, ...), custom_call_target="tpu_custom_call" | custom-call | flops 1000 | bytes 1000 | tf_op jit(solution)/shard_map/pallas_call | solution.py:181
  83.3 10.5 %collective-permute-done.6 = f32[256,512]{1,0:T(8,128)S(1)} collective-permute-done((f32[256,512]{1,0:T(8,128)}, f32[256,512]{1,0:T(8,128)S(1)}, u32[]{:S(2)}, u32[]{:S(2)}) %collective-permute-start.6) | collective-permute-done | bytes 524320 | tf_op jit(solution)/shard_map/ppermute | solution.py:267
  96.0 12.6 %collective-permute-done.10 = bf16[128,512]{1,0:T(8,128)(2,1)S(1)} collective-permute-done((bf16[128,512]{1,0:T(8,128)(2,1)S(1)}, bf16[128,512]{1,0:T(8,128)(2,1)S(1)}, u32[]{:S(2)}, u32[]{:S(2)}) %collective-permute-start.10) | collective-permute-done | bytes 131104 | tf_op jit(solution)/shard_map/ppermute | solution.py:267
  115.8 3.1 %collective-permute-done.11 = f32[256,512]{1,0:T(8,128)S(1)} collective-permute-done((f32[256,512]{1,0:T(8,128)}, f32[256,512]{1,0:T(8,128)S(1)}, u32[]{:S(2)}, u32[]{:S(2)}) %collective-permute-start.11) | collective-permute-done | bytes 524320 | tf_op jit(solution)/shard_map/ppermute | solution.py:267
  121.3 3.2 %collective-permute-done.17 = bf16[128,512]{1,0:T(8,128)(2,1)S(1)} collective-permute-done((bf16[128,512]{1,0:T(8,128)(2,1)S(1)}, bf16[128,512]{1,0:T(8,128)(2,1)S(1)}, u32[]{:S(2)}, u32[]{:S(2)}) %collective-permute-start.17) | collective-permute-done | bytes 131104 | tf_op jit(solution)/shard_map/ppermute | solution.py:267
  125.3 11.3 %shard_map.102 = (f32[8,128,384]{2,1,0:T(8,128)}, f32[8,128,384]{2,1,0:T(8,128)}, f32[8,128,384]{2,1,0:T(8,128)}, f32[8,128,384]{2,1,0:T(8,128)}, bf16[128,1024]{1,0:T(8,128)(2,1)}, /*index=5*/bf16[128,1024]{1,0:T(8,128)(2,1)}) custom-call(s32[1]{0:T(128)S(6)} %copy.22.length_ref, bf16[128,1024]{1,0:T(8,128)(2,1)} %get-tuple-element.64.raw_ref, ...), custom_call_target="tpu_custom_call" | custom-call | flops 3221225472 | bytes 25165824 | tf_op jit(solution)/shard_map/pallas_call | solution.py:81
  138.2 12.7 %shard_map.103 = (bf16[384,1024]{1,0:T(8,128)(2,1)}, bf16[384,1024]{1,0:T(8,128)(2,1)}, bf16[384,1024]{1,0:T(8,128)(2,1)}, bf16[384,1024]{1,0:T(8,128)(2,1)}, f32[128,1024]{1,0:T(8,128)}, /*index=5*/f32[128,128]{1,0:T(8,128)}) custom-call(bf16[128,1024]{1,0:T(8,128)(2,1)} %get-tuple-element.64.raw_ref, bf16[128,1024]{1,0:T(8,128)(2,1)} %get-tuple-element.72.keys_ref, ...), custom_call_target="tpu_custom_call" | custom-call | flops 4831838208 | bytes 25165824 | tf_op jit(solution)/shard_map/pallas_call | solution.py:110
  161.3 5.3 %collective-permute-done.20.refs_11_ = bf16[128,1024]{1,0:T(8,128)(2,1)S(1)} collective-permute-done((bf16[128,1024]{1,0:T(8,128)(2,1)S(1)}, bf16[128,1024]{1,0:T(8,128)(2,1)S(1)}, u32[]{:S(2)}, u32[]{:S(2)}) %collective-permute-start.20) | collective-permute-done | bytes 262176 | tf_op jit(solution)/shard_map/ppermute | solution.py:267
  166.6 13.6 %collective-permute-done.19.refs_10_ = bf16[128,1024]{1,0:T(8,128)(2,1)S(1)} collective-permute-done((bf16[128,1024]{1,0:T(8,128)(2,1)S(1)}, bf16[128,1024]{1,0:T(8,128)(2,1)S(1)}, u32[]{:S(2)}, u32[]{:S(2)}) %collective-permute-start.19) | collective-permute-done | bytes 262176 | tf_op jit(solution)/shard_map/ppermute | solution.py:267
  181.5 6.0 %collective-permute-done.27.refs_1_ = bf16[128,1024]{1,0:T(8,128)(2,1)S(1)} collective-permute-done((bf16[128,1024]{1,0:T(8,128)(2,1)S(1)}, bf16[128,1024]{1,0:T(8,128)(2,1)S(1)}, u32[]{:S(2)}, u32[]{:S(2)}) %collective-permute-start.27) | collective-permute-done | bytes 262176 | tf_op jit(solution)/shard_map/ppermute | solution.py:267
  190.5 10.4 %collective-permute-done.21.refs_13_.refs_14_.refs_15_ = bf16[384,1024]{1,0:T(8,128)(2,1)S(1)} collective-permute-done((bf16[384,1024]{1,0:T(8,128)(2,1)S(1)}, bf16[384,1024]{1,0:T(8,128)(2,1)S(1)}, u32[]{:S(2)}, u32[]{:S(2)}) %collective-permute-start.21) | collective-permute-done | bytes 786464 | tf_op jit(solution)/shard_map/ppermute | solution.py:267
  200.9 9.2 %collective-permute-done.31.refs_4_.refs_5_ = bf16[256,1024]{1,0:T(8,128)(2,1)S(1)} collective-permute-done((bf16[256,1024]{1,0:T(8,128)(2,1)S(1)}, bf16[256,1024]{1,0:T(8,128)(2,1)S(1)}, u32[]{:S(2)}, u32[]{:S(2)}) %collective-permute-start.31) | collective-permute-done | bytes 524320 | tf_op jit(solution)/shard_map/ppermute | solution.py:267
  212.8 13.0 %collective-permute-done.32.refs_6_.refs_7_ = bf16[256,1024]{1,0:T(8,128)(2,1)} collective-permute-done((bf16[256,1024]{1,0:T(8,128)(2,1)S(1)}, bf16[256,1024]{1,0:T(8,128)(2,1)}, u32[]{:S(2)}, u32[]{:S(2)}) %collective-permute-start.32) | collective-permute-done | bytes 524320 | tf_op jit(solution)/shard_map/ppermute | solution.py:267
  225.8 5.5 %shard_map.105 = (f32[512,1024]{1,0:T(8,128)}, f32[512,1024]{1,0:T(8,128)}) custom-call(bf16[512,1024]{1,0:T(8,128)(2,1)} %maximum_bitcast_fusion.columns_ref, bf16[128,1024]{1,0:T(8,128)(2,1)} %copy-done.6, bf16[128,1024]{1,0:T(8,128)(2,1)} %copy-done.15, bf16[128,1024]{1,0:T(8,128)(2,1)} %copy-done.17, bf16[128,1024]{1,0:T(8,128)(2,1)} %copy-done.16, ...), custom_call_target="tpu_custom_call" | custom-call | flops 2147483648 | bytes 8388608 | tf_op jit(solution)/shard_map/pallas_call | solution.py:206
  232.5 3.1 %shard_map.104 = bf16[384,4096]{1,0:T(8,128)(2,1)} custom-call(s32[4]{0:T(128)} %pad_add_fusion.place_ref, bf16[384,1024]{1,0:T(8,128)(2,1)} %get-tuple-element.77.refs_0_, bf16[384,1024]{1,0:T(8,128)(2,1)} %copy-done.8, bf16[384,1024]{1,0:T(8,128)(2,1)} %copy-done.7, bf16[384,1024]{1,0:T(8,128)(2,1)} %copy-done.9), custom_call_target="tpu_custom_call" | custom-call | flops 1000 | bytes 1000 | tf_op jit(solution)/shard_map/pallas_call | solution.py:243
  (126 shorter events, 56.3 us)
Async XLA Ops:
  5.6 34.3 %collective-permute-start = (bf16[768,512]{1,0:T(8,128)(2,1)}, bf16[768,512]{1,0:T(8,128)(2,1)S(1)}, u32[]{:S(2)}, u32[]{:S(2)}) collective-permute-start(bf16[768,512]{1,0:T(8,128)(2,1)} %get-tuple-element.49), channel_id=1, source_target_pairs={{0,8},{4,12},{8,0},{12,4},{16,24},{20,28},{24,16},{28,20},{1,9},{5... | collective-permute-start | bytes 2359304 | tf_op jit(solution)/shard_map/ppermute | solution.py:267
  8.6 23.9 %collective-permute-start.1 = (bf16[128,1024]{1,0:T(8,128)(2,1)}, bf16[128,1024]{1,0:T(8,128)(2,1)}, u32[]{:S(2)}, u32[]{:S(2)}) collective-permute-start(bf16[128,1024]{1,0:T(8,128)(2,1)} %get-tuple-element.50), channel_id=1, source_target_pairs={{0,16},{4,20},{8,24},{12,28},{16,0},{20,4},{24,8},{28,12},{1,17},{... | collective-permute-start | bytes 786440 | tf_op jit(solution)/shard_map/ppermute | solution.py:267
  11.2 28.7 %collective-permute-start.2 = (bf16[128,1024]{1,0:T(8,128)(2,1)}, bf16[128,1024]{1,0:T(8,128)(2,1)}, u32[]{:S(2)}, u32[]{:S(2)}) collective-permute-start(bf16[128,1024]{1,0:T(8,128)(2,1)} %get-tuple-element.51), channel_id=1, source_target_pairs={{0,24},{4,28},{8,16},{12,20},{16,8},{20,12},{24,0},{28,4},{1,25},{... | collective-permute-start | bytes 786440 | tf_op jit(solution)/shard_map/ppermute | solution.py:267
  17.9 50.8 %collective-permute-start.15 = (bf16[768,1024]{1,0:T(8,128)(2,1)}, bf16[768,1024]{1,0:T(8,128)(2,1)S(1)}, u32[]{:S(2)}, u32[]{:S(2)}) collective-permute-start(bf16[768,1024]{1,0:T(8,128)(2,1)} %get-tuple-element.69), channel_id=1, source_target_pairs={{0,2},{1,3},{2,0},{3,1},{4,6},{5,7},{6,4},{7,5},{8,10},{9,11},{10,... | collective-permute-start | bytes 4718600 | tf_op jit(solution)/shard_map/ppermute | solution.py:270
  19.6 45.5 %collective-permute-start.4 = (bf16[1024,512]{1,0:T(8,128)(2,1)S(1)}, bf16[1024,512]{1,0:T(8,128)(2,1)}, u32[]{:S(2)}, u32[]{:S(2)}) collective-permute-start(bf16[1024,512]{1,0:T(8,128)(2,1)S(1)} %copy-done.2), channel_id=1, source_target_pairs={{0,4},{4,0},{8,12},{12,8},{16,20},{20,16},{24,28},{28,24},{1,5},{5... | collective-permute-start | bytes 3145736 | tf_op jit(solution)/shard_map/ppermute | solution.py:267
  43.5 16.2 %collective-permute-start.3 = (bf16[384,1024]{1,0:T(8,128)(2,1)}, bf16[384,1024]{1,0:T(8,128)(2,1)S(1)}, u32[]{:S(2)}, u32[]{:S(2)}) collective-permute-start(bf16[384,1024]{1,0:T(8,128)(2,1)} %get-tuple-element.54), channel_id=1, source_target_pairs={{0,1},{1,0},{2,3},{3,2},{4,5},{5,4},{6,7},{7,6},{8,9},{9,8},{10,11... | collective-permute-start | bytes 2359304 | tf_op jit(solution)/shard_map/ppermute | solution.py:270
  43.5 14.7 %collective-permute-start.7 = (bf16[512,512]{1,0:T(8,128)(2,1)}, bf16[512,512]{1,0:T(8,128)(2,1)}, u32[]{:S(2)}, u32[]{:S(2)}) collective-permute-start(bf16[512,512]{1,0:T(8,128)(2,1)} %get-tuple-element.58), channel_id=1, source_target_pairs={{0,8},{4,12},{8,0},{12,4},{16,24},{20,28},{24,16},{28,20},{1,9},{5... | collective-permute-start | bytes 1572872 | tf_op jit(solution)/shard_map/ppermute | solution.py:267
  43.5 21.6 %collective-permute-start.5 = (bf16[512,512]{1,0:T(8,128)(2,1)}, bf16[512,512]{1,0:T(8,128)(2,1)}, u32[]{:S(2)}, u32[]{:S(2)}) collective-permute-start(bf16[512,512]{1,0:T(8,128)(2,1)} %get-tuple-element.56.refs_6_), channel_id=1, source_target_pairs={{0,4},{4,0},{8,12},{12,8},{16,20},{20,16},{24,28},{28,24},{1,5},{5... | collective-permute-start | bytes 1572872 | tf_op jit(solution)/shard_map/ppermute | solution.py:267
  58.2 15.6 %collective-permute-start.8 = (bf16[512,512]{1,0:T(8,128)(2,1)}, bf16[512,512]{1,0:T(8,128)(2,1)}, u32[]{:S(2)}, u32[]{:S(2)}) collective-permute-start(bf16[512,512]{1,0:T(8,128)(2,1)} %collective-permute-done.7.refs_6_), channel_id=1, source_target_pairs={{0,4},{4,0},{8,12},{12,8},{16,20},{20,16},{24,28},{28,24},{1,5},{5... | collective-permute-start | bytes 1572872 | tf_op jit(solution)/shard_map/ppermute | solution.py:267
  64.5 18.7 %collective-permute-start.9 = (bf16[512,512]{0,1:T(8,128)(2,1)S(1)}, bf16[512,512]{0,1:T(8,128)(2,1)}, u32[]{:S(2)}, u32[]{:S(2)}) collective-permute-start(bf16[512,512]{0,1:T(8,128)(2,1)S(1)} %copy.16), channel_id=1, source_target_pairs={{0,4},{4,0},{8,12},{12,8},{16,20},{20,16},{24,28},{28,24},{1,5},{5... | collective-permute-start | bytes 1572872 | tf_op jit(solution)/shard_map/ppermute | solution.py:267
  68.5 25.3 %collective-permute-start.6 = (f32[256,512]{1,0:T(8,128)}, f32[256,512]{1,0:T(8,128)S(1)}, u32[]{:S(2)}, u32[]{:S(2)}) collective-permute-start(f32[256,512]{1,0:T(8,128)} %shard_map.97), channel_id=1, source_target_pairs={{0,16},{4,20},{8,24},{12,28},{16,0},{20,4},{24,8},{28,12},{1,17},{... | collective-permute-start | bytes 1572872 | tf_op jit(solution)/shard_map/ppermute | solution.py:267
  68.7 56.6 %collective-permute-start.14 = (bf16[768,1024]{1,0:T(8,128)(2,1)}, bf16[768,1024]{1,0:T(8,128)(2,1)}, u32[]{:S(2)}, u32[]{:S(2)}) collective-permute-start(bf16[768,1024]{1,0:T(8,128)(2,1)} %get-tuple-element.68), channel_id=1, source_target_pairs={{0,1},{1,0},{2,3},{3,2},{4,5},{5,4},{6,7},{7,6},{8,9},{9,8},{10,11... | collective-permute-start | bytes 4718600 | tf_op jit(solution)/shard_map/ppermute | solution.py:270
  68.8 56.6 %collective-permute-start.16 = (bf16[768,1024]{1,0:T(8,128)(2,1)}, bf16[768,1024]{1,0:T(8,128)(2,1)}, u32[]{:S(2)}, u32[]{:S(2)}) collective-permute-start(bf16[768,1024]{1,0:T(8,128)(2,1)} %get-tuple-element.71), channel_id=1, source_target_pairs={{0,3},{1,2},{2,1},{3,0},{4,7},{5,6},{6,5},{7,4},{8,11},{9,10},{10,... | collective-permute-start | bytes 4718600 | tf_op jit(solution)/shard_map/ppermute | solution.py:270
  93.8 25.1 %collective-permute-start.11 = (f32[256,512]{1,0:T(8,128)}, f32[256,512]{1,0:T(8,128)S(1)}, u32[]{:S(2)}, u32[]{:S(2)}) collective-permute-start(f32[256,512]{1,0:T(8,128)} %shard_map.98), channel_id=1, source_target_pairs={{0,16},{4,20},{8,24},{12,28},{16,0},{20,4},{24,8},{28,12},{1,17},{... | collective-permute-start | bytes 1572872 | tf_op jit(solution)/shard_map/ppermute | solution.py:267
  93.9 14.7 %collective-permute-start.10 = (bf16[128,512]{1,0:T(8,128)(2,1)S(1)}, bf16[128,512]{1,0:T(8,128)(2,1)S(1)}, u32[]{:S(2)}, u32[]{:S(2)}) collective-permute-start(bf16[128,512]{1,0:T(8,128)(2,1)S(1)} %get-tuple-element.102), channel_id=1, source_target_pairs={{0,8},{4,12},{8,0},{12,4},{16,24},{20,28},{24,16},{28,20},{1,9},{5... | collective-permute-start | bytes 393224 | tf_op jit(solution)/shard_map/ppermute | solution.py:267
  157.9 22.3 %collective-permute-start.19 = (bf16[128,1024]{1,0:T(8,128)(2,1)S(1)}, bf16[128,1024]{1,0:T(8,128)(2,1)S(1)}, u32[]{:S(2)}, u32[]{:S(2)}) collective-permute-start(bf16[128,1024]{1,0:T(8,128)(2,1)S(1)} %copy-done.22), channel_id=1, source_target_pairs={{0,16},{4,20},{8,24},{12,28},{16,0},{20,4},{24,8},{28,12},{1,17},{... | collective-permute-start | bytes 786440 | tf_op jit(solution)/shard_map/ppermute | solution.py:267
  157.9 22.3 %collective-permute-start.18 = (bf16[128,1024]{1,0:T(8,128)(2,1)S(1)}, bf16[128,1024]{1,0:T(8,128)(2,1)S(1)}, u32[]{:S(2)}, u32[]{:S(2)}) collective-permute-start(bf16[128,1024]{1,0:T(8,128)(2,1)S(1)} %copy-done.22), channel_id=1, source_target_pairs={{0,8},{4,12},{8,0},{12,4},{16,24},{20,28},{24,16},{28,20},{1,9},{5... | collective-permute-start | bytes 786440 | tf_op jit(solution)/shard_map/ppermute | solution.py:267
  180.4 20.5 %collective-permute-start.21 = (bf16[384,1024]{1,0:T(8,128)(2,1)S(1)}, bf16[384,1024]{1,0:T(8,128)(2,1)S(1)}, u32[]{:S(2)}, u32[]{:S(2)}) collective-permute-start(bf16[384,1024]{1,0:T(8,128)(2,1)S(1)} %pad_maximum_fusion), channel_id=1, source_target_pairs={{0,4},{4,0},{8,12},{12,8},{16,20},{20,16},{24,28},{28,24},{1,5},{5... | collective-permute-start | bytes 2359304 | tf_op jit(solution)/shard_map/ppermute | solution.py:267
  180.9 30.1 %collective-permute-start.26 = (bf16[384,1024]{1,0:T(8,128)(2,1)S(1)}, bf16[384,1024]{1,0:T(8,128)(2,1)S(1)}, u32[]{:S(2)}, u32[]{:S(2)}) collective-permute-start(bf16[384,1024]{1,0:T(8,128)(2,1)S(1)} %copy-done.19), channel_id=1, source_target_pairs={{0,2},{1,3},{2,0},{3,1},{4,6},{5,7},{6,4},{7,5},{8,10},{9,11},{10,... | collective-permute-start | bytes 2359304 | tf_op jit(solution)/shard_map/ppermute | solution.py:270
  187.5 22.6 %collective-permute-start.31 = (bf16[256,1024]{1,0:T(8,128)(2,1)S(1)}, bf16[256,1024]{1,0:T(8,128)(2,1)S(1)}, u32[]{:S(2)}, u32[]{:S(2)}) collective-permute-start(bf16[256,1024]{1,0:T(8,128)(2,1)S(1)} %pad_maximum_fusion.1), channel_id=1, source_target_pairs={{0,4},{4,0},{8,12},{12,8},{16,20},{20,16},{24,28},{28,24},{1,5},{5... | collective-permute-start | bytes 1572872 | tf_op jit(solution)/shard_map/ppermute | solution.py:267
  190.5 20.5 %collective-permute-start.28 = (bf16[128,1024]{1,0:T(8,128)(2,1)S(1)}, bf16[128,1024]{1,0:T(8,128)(2,1)S(1)}, u32[]{:S(2)}, u32[]{:S(2)}) collective-permute-start(bf16[128,1024]{1,0:T(8,128)(2,1)S(1)} %fusion.3.refs_0_), channel_id=1, source_target_pairs={{0,16},{4,20},{8,24},{12,28},{16,0},{20,4},{24,8},{28,12},{1,17},{... | collective-permute-start | bytes 786440 | tf_op jit(solution)/shard_map/ppermute | solution.py:267
  200.9 30.5 %collective-permute-start.22 = (bf16[384,1024]{1,0:T(8,128)(2,1)}, bf16[384,1024]{1,0:T(8,128)(2,1)S(1)}, u32[]{:S(2)}, u32[]{:S(2)}) collective-permute-start(bf16[384,1024]{1,0:T(8,128)(2,1)} %get-tuple-element.80), channel_id=1, source_target_pairs={{0,1},{1,0},{2,3},{3,2},{4,5},{5,4},{6,7},{7,6},{8,9},{9,8},{10,11... | collective-permute-start | bytes 2359304 | tf_op jit(solution)/shard_map/ppermute | solution.py:270
  211.0 20.4 %collective-permute-start.30 = (bf16[384,1024]{1,0:T(8,128)(2,1)S(1)}, bf16[384,1024]{1,0:T(8,128)(2,1)S(1)}, u32[]{:S(2)}, u32[]{:S(2)}) collective-permute-start(bf16[384,1024]{1,0:T(8,128)(2,1)S(1)} %copy-done.18), channel_id=1, source_target_pairs={{0,3},{1,2},{2,1},{3,0},{4,7},{5,6},{6,5},{7,4},{8,11},{9,10},{10,... | collective-permute-start | bytes 2359304 | tf_op jit(solution)/shard_map/ppermute | solution.py:270
  211.2 14.6 %collective-permute-start.32 = (bf16[256,1024]{1,0:T(8,128)(2,1)S(1)}, bf16[256,1024]{1,0:T(8,128)(2,1)}, u32[]{:S(2)}, u32[]{:S(2)}) collective-permute-start(bf16[256,1024]{1,0:T(8,128)(2,1)S(1)} %pad_maximum_fusion.2), channel_id=1, source_target_pairs={{0,4},{4,0},{8,12},{12,8},{16,20},{20,16},{24,28},{28,24},{1,5},{5... | collective-permute-start | bytes 1572872 | tf_op jit(solution)/shard_map/ppermute | solution.py:267
  (33 other events, 543.0 us)

commit v7 on v5

--- a/solution.py
+++ b/solution.py
@@ -190,30 +190,28 @@
     )(place, *[part[0] for part in parts])
 
 
-def weights_kernel(videos, columns_ref, *refs):
-    part_refs, out_refs = refs[:-2], refs[-2:]
-    for index, out_ref in enumerate(out_refs):
-        parts = [ref[...] for ref in part_refs[index * videos : (index + 1) * videos]]
-        out_ref[...] = jnp.dot(
-            columns_ref[...], jnp.concatenate(parts, axis=0), preferred_element_type=jnp.float32
-        )
+def weights_kernel(columns_ref, *refs):
+    parts = [ref[...] for ref in refs[:-1]]
+    refs[-1][...] = jnp.dot(
+        columns_ref[...], jnp.concatenate(parts, axis=0), preferred_element_type=jnp.float32
+    )
 
 
 def weights_call(columns, parts):
-    rows, videos = columns.shape[0], len(parts) // 2
+    rows, depth = columns.shape
     cols = parts[0][0].shape[1]
-    tile = min(cols, 512)
+    tile = min(cols, 256)
     return pl.pallas_call(
-        functools.partial(weights_kernel, videos),
+        weights_kernel,
         grid=(cols // tile,),
         in_specs=[pl.BlockSpec(columns.shape, lambda n: (0, 0))]
         + [rows_spec(part, tile, True) for part in parts],
-        out_specs=[pl.BlockSpec((rows, tile), lambda n: (0, n))] * 2,
-        out_shape=[jax.ShapeDtypeStruct((rows, cols), jnp.float32)] * 2,
+        out_specs=pl.BlockSpec((rows, tile), lambda n: (0, n)),
+        out_shape=jax.ShapeDtypeStruct((rows, cols), jnp.float32),
         compiler_params=pltpu.CompilerParams(vmem_limit_bytes=VMEM),
         cost_estimate=pl.CostEstimate(
-            flops=4 * rows * cols * videos * LIVE,
-            bytes_accessed=8 * rows * cols + 4 * videos * LIVE * cols,
+            flops=2 * rows * cols * depth,
+            bytes_accessed=4 * rows * cols + 2 * depth * (rows + cols),
             transcendentals=0,
         ),
     )(columns, *[part[0] for part in parts])
@@ -374,27 +372,30 @@
             step *= 2
         return x
 
-    own_columns, other_given = pick_call(places, mine_first, shared, sibling_first, sibling, rows)
+    key_product = product(key_quad, True)
+    key_sent = over_dp(key_product, 4)
+    own_columns, other_given = pick_call(
+        after(places, key_product), mine_first, shared, sibling_first, sibling, rows
+    )
     other_columns = over_dp(other_given, 1)
     columns = jnp.concatenate([own_columns, other_columns], axis=0).T
-
-    key_sent = over_dp(product(key_quad, True), 4)
-    value_product = product(value_quad, True)
-    value_sent = over_dp(value_product, 4)
-    key_total = reduced(product(key_quad, False) + after(key_sent, value_product))
+    value_product, value_rest_product = product(value_quad, True), product(value_quad, False)
+    key_sent = after(key_sent, value_product, value_rest_product, other_columns)
+    key_total = reduced(product(key_quad, False) + key_sent)
     raw = joined(key_total)
+    value_sent = over_dp(after(value_product, raw), 4)
     raw_wide = raw.astype(jnp.float32)
     squares = seq_sum(jnp.sum(raw_wide * raw_wide, axis=-1, keepdims=True))
     inv_rms = lax.rsqrt(squares / hid + 1e-06)
     gain = lax.dynamic_slice(key_gain, (lane * cols,), (cols,)).reshape(1, cols)
-    value_total = reduced(product(value_quad, False) + after(value_sent, inv_rms))
-    values = joined(value_total)
     attends, keys, value_grad = attend_call(
-        lengths, after(raw, columns, value_total), inv_rms, gain, moved, tokens
-    )
-
-    value_near_parts = [over_dp(value_grad, 2 * s) for s in range(1, lines)]
-    value_first = over_dp(value_grad, 1)
+        lengths, after(raw, columns), inv_rms, gain, moved, tokens
+    )
+    values = joined(reduced(value_rest_product + after(value_sent, value_grad)))
+
+    value_given = after(value_grad, values)
+    value_near_parts = [over_dp(value_given, 2 * s) for s in range(1, lines)]
+    value_first = over_dp(value_given, 1)
     outs, scaled, inner = gradient_call(raw, keys, values, gain, moved, attends, tokens)
     inner = after(inner, value_first)
     inner_mean = seq_sum(jnp.sum(inner, axis=-1, keepdims=True), value_near_parts) / hid
@@ -407,22 +408,20 @@
         placed[s] = over_seq(after(outs[s], *previous), s)
         previous = (placed[s], value_rest, *key_near_parts)
     placed[1] = over_seq(after(outs[1], value_rest), 1)
-    split = lines // 2
-    key_first = over_dp(
-        after(jnp.concatenate([raw_grad, *key_near_parts[: split - 1]], axis=0), value_rest), 1
-    )
-    key_rest = over_dp(jnp.concatenate(key_near_parts[split - 1 :], axis=0), 1)
+    key_first = over_dp(raw_grad, 1)
+    key_rest = over_dp(jnp.concatenate(key_near_parts, axis=0), 1)
     key_parts = (
         [(x, LIVE, 0) for x in (raw_grad, *key_near_parts)]
-        + [(key_first, LIVE, s) for s in range(split)]
-        + [(key_rest, LIVE, s) for s in range(split)]
+        + [(key_first, LIVE, 0)]
+        + [(key_rest, LIVE, s) for s in range(lines - 1)]
     )
     value_parts = (
         [(x, LIVE, 0) for x in (value_grad, *value_near_parts)]
         + [(value_first, LIVE, 0)]
         + [(value_rest, LIVE, s) for s in range(lines - 1)]
     )
-    key_weight_grad, value_weight_grad = weights_call(columns, key_parts + value_parts)
+    value_weight_grad = weights_call(after(columns, key_first), value_parts)
+    key_weight_grad = weights_call(columns, key_parts)
 
     (query_grad,) = pack_call(
         lanes,

time: 238 us -> 231 us (0.971)
  waiting for transfers between devices: 117 us -> 108 us
  Pallas kernels: 61.6 us -> 66.5 us
    ppermute x22, waiting for transfers between devices: 112 us -> 101 us  [over_dp(): return lax.ppermute(x, 'dp', [(a, a ^ step) for a in range(n_dp)])]
    pallas_call x1 -> x2, Pallas kernels: 5.55 us -> 10.3 us  [weights_call(): pl.pallas_call(weights_kernel, grid=(cols // tile,), in_specs=[pl.BlockSp...]
    unnamed x48 -> x54, local copies, waits for them, and re-layouts: 6.01 us -> 5.28 us
  transfers between devices with their start and end apart: 33 -> 33, of which waited for: 15 -> 15; matrix products, arithmetic and copies ran while one was open for 5% -> 4% of each run, Pallas kernels for 18% -> 26%
where the time goes in v7:
time: 231 us; the launch traced here: 230 us
  waiting for transfers between devices  108 us (47%)
  Pallas kernels  66.5 us (29%)
  starting transfers between devices  37.8 us (16%)
  local copies, waits for them, and re-layouts  8.97 us (4%)
  other arithmetic  7.27 us (3%)
    ppermute x22, waiting for transfers between devices, over_dp(): return lax.ppermute(x, 'dp', [(a, a ^ step) for a in range(n_dp)])  101 us
    ppermute x22, starting transfers between devices, over_dp(): return lax.ppermute(x, 'dp', [(a, a ^ step) for a in range(n_dp)])  31.2 us
    pallas_call x4, Pallas kernels, pack_call(): pl.pallas_call(functools.partial(pack_kernel, moves, len(arrays)), grid=(...  16.1 us
    pallas_call x4, Pallas kernels, product_call(): pl.pallas_call(functools.partial(product_kernel, videos), grid=(1,), in_s...  13.4 us
    pallas_call x1, Pallas kernels, gradient_call(): pl.pallas_call(functools.partial(gradient_kernel, parts), grid=(heads,),...  12.6 us
    pallas_call x1, Pallas kernels, attend_call(): pl.pallas_call(functools.partial(attend_kernel, parts), grid=(heads,), in...  11.4 us
    pallas_call x2, Pallas kernels, weights_call(): pl.pallas_call(weights_kernel, grid=(cols // tile,), in_specs=[pl.BlockSp...  10.3 us
    ppermute x11, starting transfers between devices, over_seq(): return lax.ppermute(x, 'seq', [(a, a ^ step) for a in range(n_seq)])  6.57 us
  transfers between devices with their start and end apart: 33, of which 15 were waited for; matrix products, arithmetic and copies ran while one was open for 4% of the time, Pallas kernels for 26%

profile of v7, /device:TPU:0, one launch (start us, length us, event | category | flops | bytes accessed | tf_op | source)
XLA Modules:
  0.0 229.8 jit_solution(4637331327258461311)
XLA Ops:
  1.4 4.2 %shard_map.94 = (bf16[768,512]{1,0:T(8,128)(2,1)}, bf16[1024,512]{1,0:T(8,128)(2,1)}, bf16[512,512]{1,0:T(8,128)(2,1)}, bf16[128,1024]{1,0:T(8,128)(2,1)}, bf16[...) custom-call(s32[8]{0:T(128)} %stack.72.place_ref, bf16[512,1024]{1,0:T(8,128)(2,1)} %refs_0_.1, ...), custom_call_target="tpu_custom_call" | custom-call | flops 1000 | bytes 1000 | tf_op jit(solution)/shard_map/pallas_call | solution.py:241
  5.6 3.0 %collective-permute-start = (bf16[768,512]{1,0:T(8,128)(2,1)}, bf16[768,512]{1,0:T(8,128)(2,1)S(1)}, u32[]{:S(2)}, u32[]{:S(2)}) collective-permute-start(bf16[768,512]{1,0:T(8,128)(2,1)} %get-tuple-element.48), channel_id=1, source_target_pairs={{0,8},{4,12},{8,0},{12,4},{16,24},{20,28},{24,16},{28,20},{1,9},{5... | collective-permute-start | bytes 2359304 | tf_op jit(solution)/shard_map/ppermute | solution.py:265
  9.3 6.1 %shard_map.101 = (bf16[768,1024]{1,0:T(8,128)(2,1)}, bf16[768,1024]{1,0:T(8,128)(2,1)}, bf16[768,1024]{1,0:T(8,128)(2,1)}, bf16[768,1024]{1,0:T(8,128)(2,1)}) custom-call(s32[4]{0:T(128)} %pad_add_fusion.place_ref, bf16[384,4096]{1,0:T(8,128)(2,1)} %bitcast.24, bf16[384,4096]{1,0:T(8,128)(2,1)} %bitcast.25), custom_call_target="tpu_custom_call" | custom-call | flops 1000 | bytes 12582912 | tf_op jit(solution)/shard_map/pallas_call | solution.py:241
  21.2 11.4 %collective-permute-done.1.refs_1_ = bf16[128,1024]{1,0:T(8,128)(2,1)S(1)} collective-permute-done((bf16[128,1024]{1,0:T(8,128)(2,1)}, bf16[128,1024]{1,0:T(8,128)(2,1)S(1)}, u32[]{:S(2)}, u32[]{:S(2)}) %collective-permute-start.1) | collective-permute-done | bytes 262176 | tf_op jit(solution)/shard_map/ppermute | solution.py:265
  32.6 7.3 %collective-permute-done.2.refs_2_ = bf16[128,1024]{1,0:T(8,128)(2,1)S(1)} collective-permute-done((bf16[128,1024]{1,0:T(8,128)(2,1)}, bf16[128,1024]{1,0:T(8,128)(2,1)S(1)}, u32[]{:S(2)}, u32[]{:S(2)}) %collective-permute-start.2) | collective-permute-done | bytes 262176 | tf_op jit(solution)/shard_map/ppermute | solution.py:265
  49.3 10.8 %collective-permute-done.7.refs_6_ = bf16[512,512]{1,0:T(8,128)(2,1)} collective-permute-done((bf16[512,512]{1,0:T(8,128)(2,1)}, bf16[512,512]{1,0:T(8,128)(2,1)}, u32[]{:S(2)}, u32[]{:S(2)}) %collective-permute-start.7) | collective-permute-done | bytes 524320 | tf_op jit(solution)/shard_map/ppermute | solution.py:265
  62.6 3.3 %shard_map.97 = f32[256,512]{1,0:T(8,128)} custom-call(s32[4]{0:T(128)} %pad_add_fusion.1.place_ref, bf16[384,1024]{1,0:T(8,128)(2,1)} %get-tuple-element.51.refs_1_.refs_0_.mine_ref, bf16[384,1024]{1,0:T(8,128)(2,1)} %get-tuple-element.51.refs_1_.refs_0_.mine_ref, bf16[384,1024]{1,0:T(8,128)(2,1)} %copy-done, bf16[384,1024]{1,0:T(8,128)(2,1)} %copy-done, ...), custom_call_target="tpu_custom_call" | custom-call | flops 1000 | bytes 1000 | tf_op jit(solution)/shard_map/pallas_call | solution.py:181
  73.9 3.3 %shard_map.96 = f32[256,512]{1,0:T(8,128)} custom-call(s32[4]{0:T(128)} %pad_add_fusion.1.place_ref, bf16[128,1024]{1,0:T(8,128)(2,1)} %get-tuple-element.47.refs_0_.first_ref, bf16[384,1024]{1,0:T(8,128)(2,1)} %get-tuple-element.51.refs_1_.refs_0_.mine_ref, bf16[128,1024]{1,0:T(8,128)(2,1)} %get-tuple-element.52.refs_2_.sibling_first_ref, ...), custom_call_target="tpu_custom_call" | custom-call | flops 1000 | bytes 1000 | tf_op jit(solution)/shard_map/pallas_call | solution.py:181
  77.2 3.4 %shard_map.99 = f32[256,512]{1,0:T(8,128)} custom-call(s32[4]{0:T(128)} %pad_add_fusion.1.place_ref, bf16[128,1024]{1,0:T(8,128)(2,1)} %get-tuple-element.47.refs_0_.first_ref, bf16[384,1024]{1,0:T(8,128)(2,1)} %get-tuple-element.51.refs_1_.refs_0_.mine_ref, bf16[128,1024]{1,0:T(8,128)(2,1)} %get-tuple-element.52.refs_2_.sibling_first_ref, ...), custom_call_target="tpu_custom_call" | custom-call | flops 1000 | bytes 1000 | tf_op jit(solution)/shard_map/pallas_call | solution.py:181
  80.6 3.4 %shard_map.98 = f32[256,512]{1,0:T(8,128)} custom-call(s32[4]{0:T(128)} %pad_add_fusion.1.place_ref, bf16[384,1024]{1,0:T(8,128)(2,1)} %get-tuple-element.51.refs_1_.refs_0_.mine_ref, bf16[384,1024]{1,0:T(8,128)(2,1)} %get-tuple-element.51.refs_1_.refs_0_.mine_ref, bf16[384,1024]{1,0:T(8,128)(2,1)} %copy-done, bf16[384,1024]{1,0:T(8,128)(2,1)} %copy-done, ...), custom_call_target="tpu_custom_call" | custom-call | flops 1000 | bytes 1000 | tf_op jit(solution)/shard_map/pallas_call | solution.py:181
  85.3 11.2 %collective-permute-done.6 = f32[256,512]{1,0:T(8,128)S(1)} collective-permute-done((f32[256,512]{1,0:T(8,128)S(1)}, f32[256,512]{1,0:T(8,128)S(1)}, u32[]{:S(2)}, u32[]{:S(2)}) %collective-permute-start.6) | collective-permute-done | bytes 524320 | tf_op jit(solution)/shard_map/ppermute | solution.py:265
  96.7 5.1 %collective-permute-done.10 = bf16[128,512]{1,0:T(8,128)(2,1)S(1)} collective-permute-done((bf16[128,512]{1,0:T(8,128)(2,1)S(1)}, bf16[128,512]{1,0:T(8,128)(2,1)S(1)}, u32[]{:S(2)}, u32[]{:S(2)}) %collective-permute-start.10) | collective-permute-done | bytes 131104 | tf_op jit(solution)/shard_map/ppermute | solution.py:265
  108.0 3.6 %collective-permute-done.12 = f32[128,1]{1,0:T(8,128)S(1)} collective-permute-done((f32[128,1]{1,0:T(8,128)S(1)}, f32[128,1]{1,0:T(8,128)S(1)}, u32[]{:S(2)}, u32[]{:S(2)}) %collective-permute-start.12) | collective-permute-done | bytes 544 | tf_op jit(solution)/shard_map/ppermute | solution.py:268
  112.3 11.4 %shard_map.102 = (f32[8,128,384]{2,1,0:T(8,128)}, f32[8,128,384]{2,1,0:T(8,128)}, f32[8,128,384]{2,1,0:T(8,128)}, f32[8,128,384]{2,1,0:T(8,128)}, bf16[128,1024]{1,0:T(8,128)(2,1)}, /*index=5*/bf16[128,1024]{1,0:T(8,128)(2,1)}) custom-call(s32[1]{0:T(128)S(6)} %copy.22.length_ref, bf16[128,1024]{1,0:T(8,128)(2,1)} %get-tuple-element.62.raw_ref, ...), custom_call_target="tpu_custom_call" | custom-call | flops 3221225472 | bytes 25165824 | tf_op jit(solution)/shard_map/pallas_call | solution.py:81
  123.6 9.1 %collective-permute-done.16 = f32[256,512]{1,0:T(8,128)S(1)} collective-permute-done((f32[256,512]{1,0:T(8,128)S(1)}, f32[256,512]{1,0:T(8,128)S(1)}, u32[]{:S(2)}, u32[]{:S(2)}) %collective-permute-start.16) | collective-permute-done | bytes 524320 | tf_op jit(solution)/shard_map/ppermute | solution.py:265
  133.0 5.4 %collective-permute-done.17 = bf16[128,512]{1,0:T(8,128)(2,1)S(1)} collective-permute-done((bf16[128,512]{1,0:T(8,128)(2,1)S(1)}, bf16[128,512]{1,0:T(8,128)(2,1)S(1)}, u32[]{:S(2)}, u32[]{:S(2)}) %collective-permute-start.17) | collective-permute-done | bytes 131104 | tf_op jit(solution)/shard_map/ppermute | solution.py:265
  144.3 12.6 %shard_map.103 = (bf16[384,1024]{1,0:T(8,128)(2,1)}, bf16[384,1024]{1,0:T(8,128)(2,1)}, bf16[384,1024]{1,0:T(8,128)(2,1)}, bf16[384,1024]{1,0:T(8,128)(2,1)}, f32[128,1024]{1,0:T(8,128)}, /*index=5*/f32[128,128]{1,0:T(8,128)}) custom-call(bf16[128,1024]{1,0:T(8,128)(2,1)} %get-tuple-element.62.raw_ref, bf16[128,1024]{1,0:T(8,128)(2,1)} %get-tuple-element.70.keys_ref, ...), custom_call_target="tpu_custom_call" | custom-call | flops 4831838208 | bytes 25165824 | tf_op jit(solution)/shard_map/pallas_call | solution.py:110
  159.4 4.5 %collective-permute-done.19.refs_2_ = bf16[128,1024]{1,0:T(8,128)(2,1)S(1)} collective-permute-done((bf16[128,1024]{1,0:T(8,128)(2,1)S(1)}, bf16[128,1024]{1,0:T(8,128)(2,1)S(1)}, u32[]{:S(2)}, u32[]{:S(2)}) %collective-permute-start.19) | collective-permute-done | bytes 262176 | tf_op jit(solution)/shard_map/ppermute | solution.py:265
  174.6 6.7 %collective-permute-done.29.refs_3_ = bf16[128,1024]{1,0:T(8,128)(2,1)S(1)} collective-permute-done((bf16[128,1024]{1,0:T(8,128)(2,1)S(1)}, bf16[128,1024]{1,0:T(8,128)(2,1)S(1)}, u32[]{:S(2)}, u32[]{:S(2)}) %collective-permute-start.29) | collective-permute-done | bytes 262176 | tf_op jit(solution)/shard_map/ppermute | solution.py:265
  181.2 9.9 %collective-permute-done.28.refs_2_ = bf16[128,1024]{1,0:T(8,128)(2,1)S(1)} collective-permute-done((bf16[128,1024]{1,0:T(8,128)(2,1)S(1)}, bf16[128,1024]{1,0:T(8,128)(2,1)S(1)}, u32[]{:S(2)}, u32[]{:S(2)}) %collective-permute-start.28) | collective-permute-done | bytes 262176 | tf_op jit(solution)/shard_map/ppermute | solution.py:265
  195.8 18.7 %collective-permute-done.31.refs_4_ = bf16[128,1024]{1,0:T(8,128)(2,1)S(1)} collective-permute-done((bf16[128,1024]{1,0:T(8,128)(2,1)S(1)}, bf16[128,1024]{1,0:T(8,128)(2,1)S(1)}, u32[]{:S(2)}, u32[]{:S(2)}) %collective-permute-start.31) | collective-permute-done | bytes 262176 | tf_op jit(solution)/shard_map/ppermute | solution.py:265
  214.5 5.2 %shard_map.106 = f32[512,1024]{1,0:T(8,128)} custom-call(bf16[512,1024]{1,0:T(8,128)(2,1)} %maximum_bitcast_fusion.columns_ref, bf16[128,1024]{1,0:T(8,128)(2,1)} %get-tuple-element.80.refs_0_, bf16[128,1024]{1,0:T(8,128)(2,1)} %copy-done.11, bf16[128,1024]{1,0:T(8,128)(2,1)} %copy-done.10, bf16[128,1024]{1,0:T(8,128)(2,1)} %copy-done.9, ...), custom_call_target="tpu_custom_call" | custom-call | flops 1073741824 | bytes 5242880 | tf_op jit(solution)/shard_map/pallas_call | solution.py:204
  220.6 5.1 %shard_map.105 = f32[512,1024]{1,0:T(8,128)} custom-call(bf16[512,1024]{1,0:T(8,128)(2,1)} %maximum_bitcast_fusion.columns_ref, bf16[128,1024]{1,0:T(8,128)(2,1)} %copy-done.8, bf16[128,1024]{1,0:T(8,128)(2,1)} %copy-done.14, bf16[128,1024]{1,0:T(8,128)(2,1)} %copy-done.13, bf16[128,1024]{1,0:T(8,128)(2,1)} %copy-done.12, bf16[128,1024]{1,0:T(8,128)(2,1)} %copy-done.26, ...), custom_call_target="tpu_custom_call" | custom-call | flops 1073741824 | bytes 5242880 | tf_op jit(solution)/shard_map/pallas_call | solution.py:204
  226.6 3.1 %shard_map.104 = bf16[384,4096]{1,0:T(8,128)(2,1)} custom-call(s32[4]{0:T(128)} %pad_add_fusion.place_ref, bf16[384,1024]{1,0:T(8,128)(2,1)} %get-tuple-element.78.refs_0_, bf16[384,1024]{1,0:T(8,128)(2,1)} %copy-done.16, bf16[384,1024]{1,0:T(8,128)(2,1)} %copy-done.15, bf16[384,1024]{1,0:T(8,128)(2,1)} %collective-permute-done.30.refs_3_), custom_call_target="tpu_custom_call" | custom-call | flops 1000 | bytes 1000 | tf_op jit(solution)/shard_map/pallas_call | solution.py:241
  (132 shorter events, 60.3 us)
Async XLA Ops:
  5.6 34.3 %collective-permute-start = (bf16[768,512]{1,0:T(8,128)(2,1)}, bf16[768,512]{1,0:T(8,128)(2,1)S(1)}, u32[]{:S(2)}, u32[]{:S(2)}) collective-permute-start(bf16[768,512]{1,0:T(8,128)(2,1)} %get-tuple-element.48), channel_id=1, source_target_pairs={{0,8},{4,12},{8,0},{12,4},{16,24},{20,28},{24,16},{28,20},{1,9},{5... | collective-permute-start | bytes 2359304 | tf_op jit(solution)/shard_map/ppermute | solution.py:265
  15.4 57.9 %collective-permute-start.14 = (bf16[768,1024]{1,0:T(8,128)(2,1)}, bf16[768,1024]{1,0:T(8,128)(2,1)S(1)}, u32[]{:S(2)}, u32[]{:S(2)}) collective-permute-start(bf16[768,1024]{1,0:T(8,128)(2,1)} %get-tuple-element.67), channel_id=1, source_target_pairs={{0,2},{1,3},{2,0},{3,1},{4,6},{5,7},{6,4},{7,5},{8,10},{9,11},{10,... | collective-permute-start | bytes 4718600 | tf_op jit(solution)/shard_map/ppermute | solution.py:268
  16.9 15.7 %collective-permute-start.1 = (bf16[128,1024]{1,0:T(8,128)(2,1)}, bf16[128,1024]{1,0:T(8,128)(2,1)S(1)}, u32[]{:S(2)}, u32[]{:S(2)}) collective-permute-start(bf16[128,1024]{1,0:T(8,128)(2,1)} %get-tuple-element.49), channel_id=1, source_target_pairs={{0,16},{4,20},{8,24},{12,28},{16,0},{20,4},{24,8},{28,12},{1,17},{... | collective-permute-start | bytes 786440 | tf_op jit(solution)/shard_map/ppermute | solution.py:265
  19.4 20.5 %collective-permute-start.2 = (bf16[128,1024]{1,0:T(8,128)(2,1)}, bf16[128,1024]{1,0:T(8,128)(2,1)S(1)}, u32[]{:S(2)}, u32[]{:S(2)}) collective-permute-start(bf16[128,1024]{1,0:T(8,128)(2,1)} %get-tuple-element.50), channel_id=1, source_target_pairs={{0,24},{4,28},{8,16},{12,20},{16,8},{20,12},{24,0},{28,4},{1,25},{... | collective-permute-start | bytes 786440 | tf_op jit(solution)/shard_map/ppermute | solution.py:265
  19.7 42.0 %collective-permute-start.4 = (bf16[1024,512]{1,0:T(8,128)(2,1)S(1)}, bf16[1024,512]{1,0:T(8,128)(2,1)}, u32[]{:S(2)}, u32[]{:S(2)}) collective-permute-start(bf16[1024,512]{1,0:T(8,128)(2,1)S(1)} %copy-done.2), channel_id=1, source_target_pairs={{0,4},{4,0},{8,12},{12,8},{16,20},{20,16},{24,28},{28,24},{1,5},{5... | collective-permute-start | bytes 3145736 | tf_op jit(solution)/shard_map/ppermute | solution.py:265
  44.2 17.4 %collective-permute-start.3 = (bf16[384,1024]{1,0:T(8,128)(2,1)}, bf16[384,1024]{1,0:T(8,128)(2,1)S(1)}, u32[]{:S(2)}, u32[]{:S(2)}) collective-permute-start(bf16[384,1024]{1,0:T(8,128)(2,1)} %get-tuple-element.53), channel_id=1, source_target_pairs={{0,1},{1,0},{2,3},{3,2},{4,5},{5,4},{6,7},{7,6},{8,9},{9,8},{10,11... | collective-permute-start | bytes 2359304 | tf_op jit(solution)/shard_map/ppermute | solution.py:268
  44.2 15.9 %collective-permute-start.7 = (bf16[512,512]{1,0:T(8,128)(2,1)}, bf16[512,512]{1,0:T(8,128)(2,1)}, u32[]{:S(2)}, u32[]{:S(2)}) collective-permute-start(bf16[512,512]{1,0:T(8,128)(2,1)} %get-tuple-element.57), channel_id=1, source_target_pairs={{0,8},{4,12},{8,0},{12,4},{16,24},{20,28},{24,16},{28,20},{1,9},{5... | collective-permute-start | bytes 1572872 | tf_op jit(solution)/shard_map/ppermute | solution.py:265
  60.1 17.1 %collective-permute-start.8 = (bf16[512,512]{1,0:T(8,128)(2,1)}, bf16[512,512]{1,0:T(8,128)(2,1)}, u32[]{:S(2)}, u32[]{:S(2)}) collective-permute-start(bf16[512,512]{1,0:T(8,128)(2,1)} %collective-permute-done.7.refs_6_), channel_id=1, source_target_pairs={{0,4},{4,0},{8,12},{12,8},{16,20},{20,16},{24,28},{28,24},{1,5},{5... | collective-permute-start | bytes 1572872 | tf_op jit(solution)/shard_map/ppermute | solution.py:265
  71.4 25.1 %collective-permute-start.6 = (f32[256,512]{1,0:T(8,128)S(1)}, f32[256,512]{1,0:T(8,128)S(1)}, u32[]{:S(2)}, u32[]{:S(2)}) collective-permute-start(f32[256,512]{1,0:T(8,128)S(1)} %copy-done.21), channel_id=1, source_target_pairs={{0,16},{4,20},{8,24},{12,28},{16,0},{20,4},{24,8},{28,12},{1,17},{... | collective-permute-start | bytes 1572872 | tf_op jit(solution)/shard_map/ppermute | solution.py:265
  73.2 39.0 %collective-permute-start.13 = (bf16[768,1024]{1,0:T(8,128)(2,1)}, bf16[768,1024]{1,0:T(8,128)(2,1)}, u32[]{:S(2)}, u32[]{:S(2)}) collective-permute-start(bf16[768,1024]{1,0:T(8,128)(2,1)} %get-tuple-element.66), channel_id=1, source_target_pairs={{0,1},{1,0},{2,3},{3,2},{4,5},{5,4},{6,7},{7,6},{8,9},{9,8},{10,11... | collective-permute-start | bytes 4718600 | tf_op jit(solution)/shard_map/ppermute | solution.py:268
  73.2 39.0 %collective-permute-start.15 = (bf16[768,1024]{1,0:T(8,128)(2,1)}, bf16[768,1024]{1,0:T(8,128)(2,1)}, u32[]{:S(2)}, u32[]{:S(2)}) collective-permute-start(bf16[768,1024]{1,0:T(8,128)(2,1)} %get-tuple-element.69), channel_id=1, source_target_pairs={{0,3},{1,2},{2,1},{3,0},{4,7},{5,6},{6,5},{7,4},{8,11},{9,10},{10,... | collective-permute-start | bytes 4718600 | tf_op jit(solution)/shard_map/ppermute | solution.py:268
  106.7 26.0 %collective-permute-start.16 = (f32[256,512]{1,0:T(8,128)S(1)}, f32[256,512]{1,0:T(8,128)S(1)}, u32[]{:S(2)}, u32[]{:S(2)}) collective-permute-start(f32[256,512]{1,0:T(8,128)S(1)} %copy-done.20), channel_id=1, source_target_pairs={{0,16},{4,20},{8,24},{12,28},{16,0},{20,4},{24,8},{28,12},{1,17},{... | collective-permute-start | bytes 1572872 | tf_op jit(solution)/shard_map/ppermute | solution.py:265
  139.2 17.7 %collective-permute-start.23 = (bf16[128,1024]{1,0:T(8,128)(2,1)S(1)}, bf16[128,1024]{1,0:T(8,128)(2,1)S(1)}, u32[]{:S(2)}, u32[]{:S(2)}) collective-permute-start(bf16[128,1024]{1,0:T(8,128)(2,1)S(1)} %copy-done.24), channel_id=1, source_target_pairs={{0,4},{4,0},{8,12},{12,8},{16,20},{20,16},{24,28},{28,24},{1,5},{5... | collective-permute-start | bytes 786440 | tf_op jit(solution)/shard_map/ppermute | solution.py:265
  139.9 19.5 %collective-permute-start.20 = (bf16[128,1024]{1,0:T(8,128)(2,1)S(1)}, bf16[128,1024]{1,0:T(8,128)(2,1)S(1)}, u32[]{:S(2)}, u32[]{:S(2)}) collective-permute-start(bf16[128,1024]{1,0:T(8,128)(2,1)S(1)} %copy-done.24), channel_id=1, source_target_pairs={{0,24},{4,28},{8,16},{12,20},{16,8},{20,12},{24,0},{28,4},{1,25},{... | collective-permute-start | bytes 786440 | tf_op jit(solution)/shard_map/ppermute | solution.py:265
  142.0 21.9 %collective-permute-start.19 = (bf16[128,1024]{1,0:T(8,128)(2,1)S(1)}, bf16[128,1024]{1,0:T(8,128)(2,1)S(1)}, u32[]{:S(2)}, u32[]{:S(2)}) collective-permute-start(bf16[128,1024]{1,0:T(8,128)(2,1)S(1)} %copy-done.24), channel_id=1, source_target_pairs={{0,16},{4,20},{8,24},{12,28},{16,0},{20,4},{24,8},{28,12},{1,17},{... | collective-permute-start | bytes 786440 | tf_op jit(solution)/shard_map/ppermute | solution.py:265
  142.0 21.9 %collective-permute-start.18 = (bf16[128,1024]{1,0:T(8,128)(2,1)S(1)}, bf16[128,1024]{1,0:T(8,128)(2,1)S(1)}, u32[]{:S(2)}, u32[]{:S(2)}) collective-permute-start(bf16[128,1024]{1,0:T(8,128)(2,1)S(1)} %copy-done.24), channel_id=1, source_target_pairs={{0,8},{4,12},{8,0},{12,4},{16,24},{20,28},{24,16},{28,20},{1,9},{5... | collective-permute-start | bytes 786440 | tf_op jit(solution)/shard_map/ppermute | solution.py:265
  165.5 28.0 %collective-permute-start.21 = (bf16[384,1024]{1,0:T(8,128)(2,1)S(1)}, bf16[384,1024]{1,0:T(8,128)(2,1)S(1)}, u32[]{:S(2)}, u32[]{:S(2)}) collective-permute-start(bf16[384,1024]{1,0:T(8,128)(2,1)S(1)} %pad_maximum_fusion), channel_id=1, source_target_pairs={{0,4},{4,0},{8,12},{12,8},{16,20},{20,16},{24,28},{28,24},{1,5},{5... | collective-permute-start | bytes 2359304 | tf_op jit(solution)/shard_map/ppermute | solution.py:265
  168.3 25.2 %collective-permute-start.26 = (bf16[384,1024]{1,0:T(8,128)(2,1)}, bf16[384,1024]{1,0:T(8,128)(2,1)S(1)}, u32[]{:S(2)}, u32[]{:S(2)}) collective-permute-start(bf16[384,1024]{1,0:T(8,128)(2,1)} %get-tuple-element.86), channel_id=1, source_target_pairs={{0,2},{1,3},{2,0},{3,1},{4,6},{5,7},{6,4},{7,5},{8,10},{9,11},{10,... | collective-permute-start | bytes 2359304 | tf_op jit(solution)/shard_map/ppermute | solution.py:268
  172.2 18.9 %collective-permute-start.28 = (bf16[128,1024]{1,0:T(8,128)(2,1)S(1)}, bf16[128,1024]{1,0:T(8,128)(2,1)S(1)}, u32[]{:S(2)}, u32[]{:S(2)}) collective-permute-start(bf16[128,1024]{1,0:T(8,128)(2,1)S(1)} %fusion.3.refs_0_), channel_id=1, source_target_pairs={{0,16},{4,20},{8,24},{12,28},{16,0},{20,4},{24,8},{28,12},{1,17},{... | collective-permute-start | bytes 786440 | tf_op jit(solution)/shard_map/ppermute | solution.py:265
  172.3 18.9 %collective-permute-start.27 = (bf16[128,1024]{1,0:T(8,128)(2,1)S(1)}, bf16[128,1024]{1,0:T(8,128)(2,1)S(1)}, u32[]{:S(2)}, u32[]{:S(2)}) collective-permute-start(bf16[128,1024]{1,0:T(8,128)(2,1)S(1)} %fusion.3.refs_0_), channel_id=1, source_target_pairs={{0,8},{4,12},{8,0},{12,4},{16,24},{20,28},{24,16},{28,20},{1,9},{5... | collective-permute-start | bytes 786440 | tf_op jit(solution)/shard_map/ppermute | solution.py:265
  192.1 27.6 %collective-permute-start.32 = (bf16[384,1024]{1,0:T(8,128)(2,1)}, bf16[384,1024]{1,0:T(8,128)(2,1)S(1)}, u32[]{:S(2)}, u32[]{:S(2)}) collective-permute-start(bf16[384,1024]{1,0:T(8,128)(2,1)} %pad_maximum_fusion.1), channel_id=1, source_target_pairs={{0,4},{4,0},{8,12},{12,8},{16,20},{20,16},{24,28},{28,24},{1,5},{5... | collective-permute-start | bytes 2359304 | tf_op jit(solution)/shard_map/ppermute | solution.py:265
  193.5 32.2 %collective-permute-start.22 = (bf16[384,1024]{1,0:T(8,128)(2,1)}, bf16[384,1024]{1,0:T(8,128)(2,1)S(1)}, u32[]{:S(2)}, u32[]{:S(2)}) collective-permute-start(bf16[384,1024]{1,0:T(8,128)(2,1)} %get-tuple-element.81), channel_id=1, source_target_pairs={{0,1},{1,0},{2,3},{3,2},{4,5},{5,4},{6,7},{7,6},{8,9},{9,8},{10,11... | collective-permute-start | bytes 2359304 | tf_op jit(solution)/shard_map/ppermute | solution.py:268
  194.5 31.3 %collective-permute-start.30 = (bf16[384,1024]{1,0:T(8,128)(2,1)}, bf16[384,1024]{1,0:T(8,128)(2,1)}, u32[]{:S(2)}, u32[]{:S(2)}) collective-permute-start(bf16[384,1024]{1,0:T(8,128)(2,1)} %get-tuple-element.89), channel_id=1, source_target_pairs={{0,3},{1,2},{2,1},{3,0},{4,7},{5,6},{6,5},{7,4},{8,11},{9,10},{10,... | collective-permute-start | bytes 2359304 | tf_op jit(solution)/shard_map/ppermute | solution.py:268
  195.1 19.4 %collective-permute-start.31 = (bf16[128,1024]{1,0:T(8,128)(2,1)S(1)}, bf16[128,1024]{1,0:T(8,128)(2,1)S(1)}, u32[]{:S(2)}, u32[]{:S(2)}) collective-permute-start(bf16[128,1024]{1,0:T(8,128)(2,1)S(1)} %fusion.3.refs_0_), channel_id=1, source_target_pairs={{0,4},{4,0},{8,12},{12,8},{16,20},{20,16},{24,28},{28,24},{1,5},{5... | collective-permute-start | bytes 786440 | tf_op jit(solution)/shard_map/ppermute | solution.py:265
  (36 other events, 495.6 us)

commit v8 on v7

--- a/solution.py
+++ b/solution.py
@@ -38,21 +38,20 @@
     value_grad_ref[...] = value_grad.astype(jnp.bfloat16)
 
 
-def gradient_kernel(parts, raw_ref, keys_ref, value_ref, gain_ref, *refs):
+def gradient_kernel(parts, raw_ref, value_ref, gain_ref, *refs):
     query_refs, grad_refs = refs[:parts], refs[parts : 2 * parts]
-    attend_refs, out_refs = refs[2 * parts : 3 * parts], refs[3 * parts : 4 * parts]
+    attend_refs, score_refs = refs[2 * parts : 3 * parts], refs[3 * parts : 4 * parts]
     scaled_ref, inner_ref = refs[4 * parts :]
-    keys, values = keys_ref[...], value_ref[...]
+    values = value_ref[...]
     key_grad = jnp.zeros((LIVE, HD), jnp.float32)
-    for query_ref, grad_ref, attend_ref, out_ref in zip(
-        query_refs, grad_refs, attend_refs, out_refs
+    for query_ref, grad_ref, attend_ref, score_ref in zip(
+        query_refs, grad_refs, attend_refs, score_refs
     ):
         attend = attend_ref[0]
         dattend = lax.dot_general(values, grad_ref[...], ROWS, preferred_element_type=jnp.float32)
         delta = jnp.sum(attend * dattend, axis=0, keepdims=True)
         dscores = (attend * (dattend - delta)).astype(jnp.bfloat16)
-        out = lax.dot_general(dscores, keys, COLUMNS, preferred_element_type=jnp.float32)
-        out_ref[...] = (out * FACTOR).astype(jnp.bfloat16)
+        score_ref[0] = dscores
         key_grad += jnp.dot(dscores, query_ref[...], preferred_element_type=jnp.float32)
     scaled = key_grad * FACTOR * gain_ref[...]
     scaled_ref[...] = scaled
@@ -64,20 +63,29 @@
     inner_ref[...] += scaled * raw_ref[...].astype(jnp.float32)
 
 
+def query_kernel(parts, keys_ref, *refs):
+    for score_ref, out_ref in zip(refs[:parts], refs[parts:]):
+        out = lax.dot_general(
+            score_ref[0], keys_ref[...], COLUMNS, preferred_element_type=jnp.float32
+        )
+        out_ref[...] = (out * FACTOR).astype(jnp.bfloat16)
+
+
 def specs(tokens):
     head = pl.BlockSpec((LIVE, HD), lambda h: (0, h))
     block = pl.BlockSpec((tokens, HD), lambda h: (0, h))
-    lower = pl.BlockSpec((tokens, HD), lambda h: (1, h))
+    upper = pl.BlockSpec((None, tokens, HD), lambda h: (0, 0, h))
+    lower = pl.BlockSpec((None, tokens, HD), lambda h: (1, 0, h))
     weights = pl.BlockSpec((1, LIVE, tokens), lambda h: (h, 0, 0))
     gain = pl.BlockSpec((1, HD), lambda h: (0, h))
-    return head, block, lower, weights, gain
+    return head, block, upper, lower, weights, gain
 
 
 def attend_call(length, raw, inv, gain, moved, tokens):
     parts = len(moved)
-    cols = moved[0].shape[1]
+    cols = moved[0].shape[2]
     heads = cols // HD
-    head, block, lower, weights, gains = specs(tokens)
+    head, block, upper, lower, weights, gains = specs(tokens)
     outs = pl.pallas_call(
         functools.partial(attend_kernel, parts),
         grid=(heads,),
@@ -87,7 +95,7 @@
             pl.BlockSpec((LIVE, 1), lambda h: (0, 0)),
             gains,
         ]
-        + [block] * parts
+        + [upper] * parts
         + [lower] * parts,
         out_specs=[weights] * parts + [head, head],
         out_shape=[jax.ShapeDtypeStruct((heads, LIVE, tokens), jnp.float32)] * parts
@@ -102,29 +110,48 @@
     return outs[:parts], outs[parts], outs[parts + 1]
 
 
-def gradient_call(raw, keys, values, gain, moved, attends, tokens):
+def gradient_call(raw, values, gain, moved, attends, tokens):
     parts = len(moved)
-    cols = moved[0].shape[1]
+    cols = moved[0].shape[2]
     heads = cols // HD
-    head, block, lower, weights, gains = specs(tokens)
+    head, block, upper, lower, weights, gains = specs(tokens)
     outs = pl.pallas_call(
         functools.partial(gradient_kernel, parts),
         grid=(heads,),
-        in_specs=[head, head, head, gains] + [block] * parts + [lower] * parts + [weights] * parts,
-        out_specs=[block] * parts + [head, pl.BlockSpec((LIVE, HD), lambda h: (0, 0))],
-        out_shape=[jax.ShapeDtypeStruct((tokens, cols), jnp.bfloat16)] * parts
+        in_specs=[head, head, gains] + [upper] * parts + [lower] * parts + [weights] * parts,
+        out_specs=[weights] * parts + [head, pl.BlockSpec((LIVE, HD), lambda h: (0, 0))],
+        out_shape=[jax.ShapeDtypeStruct((heads, LIVE, tokens), jnp.bfloat16)] * parts
         + [
             jax.ShapeDtypeStruct((LIVE, cols), jnp.float32),
             jax.ShapeDtypeStruct((LIVE, HD), jnp.float32),
         ],
         compiler_params=pltpu.CompilerParams(vmem_limit_bytes=VMEM),
         cost_estimate=pl.CostEstimate(
-            flops=24 * parts * tokens * cols * LIVE,
+            flops=16 * parts * tokens * cols * LIVE,
             bytes_accessed=16 * parts * tokens * cols,
             transcendentals=0,
         ),
-    )(raw, keys, values, gain, *moved, *moved, *attends)
+    )(raw, values, gain, *moved, *moved, *attends)
     return outs[:parts], outs[parts], outs[parts + 1]
+
+
+def query_call(keys, scores):
+    parts = len(scores)
+    heads, _, tokens = scores[0].shape
+    head, block, _, _, weights, _ = specs(tokens)
+    return pl.pallas_call(
+        functools.partial(query_kernel, parts),
+        grid=(heads,),
+        in_specs=[head] + [weights] * parts,
+        out_specs=[block] * parts,
+        out_shape=[jax.ShapeDtypeStruct((tokens, keys.shape[1]), jnp.bfloat16)] * parts,
+        compiler_params=pltpu.CompilerParams(vmem_limit_bytes=VMEM),
+        cost_estimate=pl.CostEstimate(
+            flops=8 * parts * tokens * keys.shape[1] * LIVE,
+            bytes_accessed=8 * parts * tokens * keys.shape[1],
+            transcendentals=0,
+        ),
+    )(keys, *scores)
 
 
 def rows_spec(part, width, tiled=False):
@@ -200,7 +227,7 @@
 def weights_call(columns, parts):
     rows, depth = columns.shape
     cols = parts[0][0].shape[1]
-    tile = min(cols, 256)
+    tile = min(cols, 512)
     return pl.pallas_call(
         weights_kernel,
         grid=(cols // tile,),
@@ -219,6 +246,33 @@
 
 def after(x, *others):
     return lax.optimization_barrier((x, *others))[0]
+
+
+def blocks_kernel(lanes_ref, query_ref, grad_ref, *out_refs):
+    cols = out_refs[0].shape[2]
+    for index, out_ref in enumerate(out_refs):
+        at = pl.ds(pl.multiple_of(lanes_ref[index] * cols, cols), cols)
+        out_ref[0] = query_ref[:, at]
+        out_ref[1] = grad_ref[:, at]
+
+
+def blocks_call(lanes, query, grad):
+    parts = lanes.shape[0]
+    tokens, hid = query.shape
+    cols, tiles = hid // parts, 4
+    rows = tokens // tiles
+    return pl.pallas_call(
+        blocks_kernel,
+        grid=(tiles,),
+        in_specs=[pl.BlockSpec(memory_space=pltpu.SMEM)]
+        + [pl.BlockSpec((rows, hid), lambda n: (n, 0))] * 2,
+        out_specs=[pl.BlockSpec((2, rows, cols), lambda n: (0, n, 0))] * parts,
+        out_shape=[jax.ShapeDtypeStruct((2, tokens, cols), jnp.bfloat16)] * parts,
+        compiler_params=pltpu.CompilerParams(vmem_limit_bytes=VMEM),
+        cost_estimate=pl.CostEstimate(
+            flops=1000, bytes_accessed=8 * tokens * hid, transcendentals=0
+        ),
+    )(lanes, query, grad)
 
 
 def pack_kernel(moves, inputs, place_ref, *refs):
@@ -295,17 +349,7 @@
     arrived = [over_dp(x, 2 * s) for s, x in enumerate(given, 2)]
 
     lanes = jnp.stack([lane ^ s for s in range(n_seq)]).astype(jnp.int32)
-    packed = pack_call(
-        after(lanes, kept),
-        [query[0], out_grad[0]],
-        [(2 * tokens, cols)] * n_seq,
-        [
-            (source, 0, (s,), tokens, cols, s, source * tokens, 0)
-            for s in range(n_seq)
-            for source in range(2)
-        ],
-        size=8 * tokens * hid,
-    )
+    packed = blocks_call(after(lanes, kept), query[0], out_grad[0])
     moved = [packed[0]] + [None] * (n_seq - 1)
     previous = ()
     for s in range(2, n_seq):
@@ -313,7 +357,6 @@
         previous = (moved[s],)
     moved[1] = over_seq(after(packed[1], beside), 1)
 
-    value_near = over_dp(after(value_given, near, *arrived), 2)
     key_near, shared, shared_given = pack_call(
         place,
         [near, *arrived],
@@ -331,6 +374,7 @@
         ],
     )
     key_far = over_dp(key_near, 1)
+    value_near = over_dp(after(value_given, near, *arrived), 2)
     value_far = over_dp(value_near, 1)
     sibling = over_seq(shared_given, 1)
     key_quad = ((kept, rows, 0), (beside, rows, 0), (key_near, rows, 0), (key_far, rows, 0))
@@ -338,7 +382,7 @@
 
     places = jnp.stack([core ^ low, 1 - (core ^ low), side, 1 - side]).astype(jnp.int32)
 
-    def product(weights, other):
+    def product(places, weights, other):
         chosen = [s for s in range(lines) if bool(s & 2) == other]
         return product_call(
             places,
@@ -372,22 +416,22 @@
             step *= 2
         return x
 
-    key_product = product(key_quad, True)
+    gain = lax.dynamic_slice(key_gain, (lane * cols,), (cols,)).reshape(1, cols)
+    own_columns, other_given = pick_call(places, mine_first, shared, sibling_first, sibling, rows)
+    key_product = product(after(places, own_columns), key_quad, True)
     key_sent = over_dp(key_product, 4)
-    own_columns, other_given = pick_call(
-        after(places, key_product), mine_first, shared, sibling_first, sibling, rows
-    )
-    other_columns = over_dp(other_given, 1)
+    later = after(places, key_product)
+    other_columns = over_dp(after(other_given, key_product), 1)
     columns = jnp.concatenate([own_columns, other_columns], axis=0).T
-    value_product, value_rest_product = product(value_quad, True), product(value_quad, False)
-    key_sent = after(key_sent, value_product, value_rest_product, other_columns)
-    key_total = reduced(product(key_quad, False) + key_sent)
+    value_product = product(later, value_quad, True)
+    value_rest_product = product(later, value_quad, False)
+    key_sent = after(key_sent, value_product, value_rest_product, columns, gain)
+    key_total = reduced(product(later, key_quad, False) + key_sent)
     raw = joined(key_total)
     value_sent = over_dp(after(value_product, raw), 4)
     raw_wide = raw.astype(jnp.float32)
     squares = seq_sum(jnp.sum(raw_wide * raw_wide, axis=-1, keepdims=True))
     inv_rms = lax.rsqrt(squares / hid + 1e-06)
-    gain = lax.dynamic_slice(key_gain, (lane * cols,), (cols,)).reshape(1, cols)
     attends, keys, value_grad = attend_call(
         lengths, after(raw, columns), inv_rms, gain, moved, tokens
     )
@@ -396,7 +440,8 @@
     value_given = after(value_grad, values)
     value_near_parts = [over_dp(value_given, 2 * s) for s in range(1, lines)]
     value_first = over_dp(value_given, 1)
-    outs, scaled, inner = gradient_call(raw, keys, values, gain, moved, attends, tokens)
+    scores, scaled, inner = gradient_call(raw, values, gain, moved, attends, tokens)
+    outs = query_call(keys, scores)
     inner = after(inner, value_first)
     inner_mean = seq_sum(jnp.sum(inner, axis=-1, keepdims=True), value_near_parts) / hid
     raw_grad = (inv_rms * scaled - raw_wide * inv_rms**3 * inner_mean).astype(jnp.bfloat16)
@@ -406,10 +451,10 @@
     previous = (inner_mean,)
     for s in range(2, n_seq):
         placed[s] = over_seq(after(outs[s], *previous), s)
-        previous = (placed[s], value_rest, *key_near_parts)
+        previous = (placed[s], key_near_parts[0])
     placed[1] = over_seq(after(outs[1], value_rest), 1)
     key_first = over_dp(raw_grad, 1)
-    key_rest = over_dp(jnp.concatenate(key_near_parts, axis=0), 1)
+    key_rest = over_dp(after(jnp.concatenate(key_near_parts, axis=0), key_first), 1)
     key_parts = (
         [(x, LIVE, 0) for x in (raw_grad, *key_near_parts)]
         + [(key_first, LIVE, 0)]

time: 231 us -> 224 us (0.970)
  waiting for transfers between devices: 108 us -> 97.9 us
  Pallas kernels: 66.5 us -> 70.9 us
    pallas_call x0 -> x2, Pallas kernels: none -> 13 us  [the longest x1 7.01 us: query_call(): pl.pallas_call(functools.partial(query_kernel, parts), grid=(heads,), in_...]
    ppermute x22, waiting for transfers between devices: 101 us -> 92.1 us  [over_dp(): return lax.ppermute(x, 'dp', [(a, a ^ step) for a in range(n_dp)])]
    pallas_call x4 -> x3, Pallas kernels: 16.1 us -> 10.1 us  [pack_call(): pl.pallas_call(functools.partial(pack_kernel, moves, len(arrays)), grid=(...]
  transfers between devices with their start and end apart: 33 -> 33, of which waited for: 15 -> 14; matrix products, arithmetic and copies ran while one was open for 4% -> 5% of each run, Pallas kernels for 26% -> 28%
where the time goes in v8:
time: 224 us; the launch traced here: 223 us
  waiting for transfers between devices  97.9 us (44%)
  Pallas kernels  70.9 us (32%)
  starting transfers between devices  36.3 us (16%)
  other arithmetic  9.13 us (4%)
  local copies, waits for them, and re-layouts  7.01 us (3%)
    ppermute x22, waiting for transfers between devices, over_dp(): return lax.ppermute(x, 'dp', [(a, a ^ step) for a in range(n_dp)])  92.1 us
    ppermute x22, starting transfers between devices, over_dp(): return lax.ppermute(x, 'dp', [(a, a ^ step) for a in range(n_dp)])  29.6 us
    pallas_call x4, Pallas kernels, product_call(): pl.pallas_call(functools.partial(product_kernel, videos), grid=(1,), in_s...  13.6 us
    pallas_call x1, Pallas kernels, gradient_call(): pl.pallas_call(functools.partial(gradient_kernel, parts), grid=(heads,),...  11.7 us
    pallas_call x1, Pallas kernels, attend_call(): pl.pallas_call(functools.partial(attend_kernel, parts), grid=(heads,), in...  11.3 us
    pallas_call x3, Pallas kernels, pack_call(): pl.pallas_call(functools.partial(pack_kernel, moves, len(arrays)), grid=(...  10.1 us
    pallas_call x2, Pallas kernels, weights_call(): pl.pallas_call(weights_kernel, grid=(cols // tile,), in_specs=[pl.BlockSp...  8.52 us
    pallas_call x1, Pallas kernels, query_call(): pl.pallas_call(functools.partial(query_kernel, parts), grid=(heads,), in_...  7.01 us
  transfers between devices with their start and end apart: 33, of which 14 were waited for; matrix products, arithmetic and copies ran while one was open for 5% of the time, Pallas kernels for 28%

profile of v8, /device:TPU:0, one launch (start us, length us, event | category | flops | bytes accessed | tf_op | source)
XLA Modules:
  0.0 222.9 jit_solution(6307194856542327796)
XLA Ops:
  1.3 4.3 %shard_map.94 = (bf16[768,512]{1,0:T(8,128)(2,1)}, bf16[1024,512]{1,0:T(8,128)(2,1)}, bf16[512,512]{1,0:T(8,128)(2,1)}, bf16[128,1024]{1,0:T(8,128)(2,1)}, bf16[...) custom-call(s32[8]{0:T(128)} %stack.72.place_ref, bf16[512,1024]{1,0:T(8,128)(2,1)} %refs_0_.1, ...), custom_call_target="tpu_custom_call" | custom-call | flops 1000 | bytes 1000 | tf_op jit(solution)/shard_map/pallas_call | solution.py:295
  5.6 3.0 %collective-permute-start = (bf16[768,512]{1,0:T(8,128)(2,1)}, bf16[768,512]{1,0:T(8,128)(2,1)S(1)}, u32[]{:S(2)}, u32[]{:S(2)}) collective-permute-start(bf16[768,512]{1,0:T(8,128)(2,1)} %get-tuple-element.55), channel_id=1, source_target_pairs={{0,8},{4,12},{8,0},{12,4},{16,24},{20,28},{24,16},{28,20},{1,9},{5... | collective-permute-start | bytes 2359304 | tf_op jit(solution)/shard_map/ppermute | solution.py:319
  9.2 5.9 %shard_map.101 = (bf16[2,384,1024]{2,1,0:T(8,128)(2,1)}, bf16[2,384,1024]{2,1,0:T(8,128)(2,1)}, bf16[2,384,1024]{2,1,0:T(8,128)(2,1)}, bf16[2,384,1024]{2,1,0:T(8,128)(2,1)}) custom-call(s32[4]{0:T(128)} %pad_add_fusion.lanes_ref.place_ref, bf16[384,4096]{1,0:T(8,128)(2,1)} %bitcast.24, bf16[384,4096]{1,0:T(8,128)(2,1)} %bitcast.25), custom_call_target="tpu_custom_call" | custom-call | flops 1000 | bytes 12582912 | tf_op jit(solution)/shard_map/pallas_call | solution.py:264
  21.0 11.6 %collective-permute-done.1.refs_1_ = bf16[128,1024]{1,0:T(8,128)(2,1)S(1)} collective-permute-done((bf16[128,1024]{1,0:T(8,128)(2,1)}, bf16[128,1024]{1,0:T(8,128)(2,1)S(1)}, u32[]{:S(2)}, u32[]{:S(2)}) %collective-permute-start.1) | collective-permute-done | bytes 262176 | tf_op jit(solution)/shard_map/ppermute | solution.py:319
  32.5 7.3 %collective-permute-done.2.refs_2_ = bf16[128,1024]{1,0:T(8,128)(2,1)S(1)} collective-permute-done((bf16[128,1024]{1,0:T(8,128)(2,1)}, bf16[128,1024]{1,0:T(8,128)(2,1)S(1)}, u32[]{:S(2)}, u32[]{:S(2)}) %collective-permute-start.2) | collective-permute-done | bytes 262176 | tf_op jit(solution)/shard_map/ppermute | solution.py:319
  49.1 10.8 %collective-permute-done.7.refs_6_ = bf16[512,512]{1,0:T(8,128)(2,1)} collective-permute-done((bf16[512,512]{1,0:T(8,128)(2,1)}, bf16[512,512]{1,0:T(8,128)(2,1)}, u32[]{:S(2)}, u32[]{:S(2)}) %collective-permute-start.7) | collective-permute-done | bytes 524320 | tf_op jit(solution)/shard_map/ppermute | solution.py:319
  65.1 3.4 %shard_map.97 = f32[256,512]{1,0:T(8,128)} custom-call(s32[4]{0:T(128)} %pad_add_fusion.1.place_ref, bf16[384,1024]{1,0:T(8,128)(2,1)} %get-tuple-element.58.mine_ref.refs_0_.refs_1_, bf16[384,1024]{1,0:T(8,128)(2,1)} %get-tuple-element.58.mine_ref.refs_0_.refs_1_, bf16[384,1024]{1,0:T(8,128)(2,1)} %copy-done, bf16[384,1024]{1,0:T(8,128)(2,1)} %copy-done, ...), custom_call_target="tpu_custom_call" | custom-call | flops 1000 | bytes 1000 | tf_op jit(solution)/shard_map/pallas_call | solution.py:208
  73.9 3.4 %shard_map.98 = f32[256,512]{1,0:T(8,128)} custom-call(s32[4]{0:T(128)} %pad_add_fusion.1.place_ref, bf16[128,1024]{1,0:T(8,128)(2,1)} %get-tuple-element.54.first_ref.refs_0_, bf16[384,1024]{1,0:T(8,128)(2,1)} %get-tuple-element.58.mine_ref.refs_0_.refs_1_, bf16[128,1024]{1,0:T(8,128)(2,1)} %get-tuple-element.59.sibling_first_ref.refs_2_, ...), custom_call_target="tpu_custom_call" | custom-call | flops 1000 | bytes 1000 | tf_op jit(solution)/shard_map/pallas_call | solution.py:208
  77.6 3.4 %shard_map.100 = f32[256,512]{1,0:T(8,128)} custom-call(s32[4]{0:T(128)} %pad_add_fusion.1.place_ref, bf16[128,1024]{1,0:T(8,128)(2,1)} %get-tuple-element.54.first_ref.refs_0_, bf16[384,1024]{1,0:T(8,128)(2,1)} %get-tuple-element.58.mine_ref.refs_0_.refs_1_, bf16[128,1024]{1,0:T(8,128)(2,1)} %get-tuple-element.59.sibling_first_ref.refs_2_, ...), custom_call_target="tpu_custom_call" | custom-call | flops 1000 | bytes 1000 | tf_op jit(solution)/shard_map/pallas_call | solution.py:208
  81.0 3.4 %shard_map.99 = f32[256,512]{1,0:T(8,128)} custom-call(s32[4]{0:T(128)} %pad_add_fusion.1.place_ref, bf16[384,1024]{1,0:T(8,128)(2,1)} %get-tuple-element.58.mine_ref.refs_0_.refs_1_, bf16[384,1024]{1,0:T(8,128)(2,1)} %get-tuple-element.58.mine_ref.refs_0_.refs_1_, bf16[384,1024]{1,0:T(8,128)(2,1)} %copy-done, bf16[384,1024]{1,0:T(8,128)(2,1)} %copy-done, ...), custom_call_target="tpu_custom_call" | custom-call | flops 1000 | bytes 1000 | tf_op jit(solution)/shard_map/pallas_call | solution.py:208
  87.4 9.0 %collective-permute-done.6 = f32[256,512]{1,0:T(8,128)} collective-permute-done((f32[256,512]{1,0:T(8,128)}, f32[256,512]{1,0:T(8,128)}, u32[]{:S(2)}, u32[]{:S(2)}) %collective-permute-start.6) | collective-permute-done | bytes 524320 | tf_op jit(solution)/shard_map/ppermute | solution.py:319
  97.6 4.9 %collective-permute-done.10 = bf16[128,512]{1,0:T(8,128)(2,1)S(1)} collective-permute-done((bf16[128,512]{1,0:T(8,128)(2,1)S(1)}, bf16[128,512]{1,0:T(8,128)(2,1)S(1)}, u32[]{:S(2)}, u32[]{:S(2)}) %collective-permute-start.10) | collective-permute-done | bytes 131104 | tf_op jit(solution)/shard_map/ppermute | solution.py:319
  109.7 11.3 %shard_map.102 = (f32[8,128,384]{2,1,0:T(8,128)}, f32[8,128,384]{2,1,0:T(8,128)}, f32[8,128,384]{2,1,0:T(8,128)}, f32[8,128,384]{2,1,0:T(8,128)}, bf16[128,1024]{1,0:T(8,128)(2,1)}, /*index=5*/bf16[128,1024]{1,0:T(8,128)(2,1)}) custom-call(s32[1]{0:T(128)S(6)} %copy.22.length_ref, bf16[128,1024]{1,0:T(8,128)(2,1)} %get-tuple-element.71.raw_ref, ...), custom_call_target="tpu_custom_call" | custom-call | flops 3221225472 | bytes 25165824 | tf_op jit(solution)/shard_map/pallas_call | solution.py:89
  121.1 11.5 %collective-permute-done.16 = f32[256,512]{1,0:T(8,128)S(1)} collective-permute-done((f32[256,512]{1,0:T(8,128)S(1)}, f32[256,512]{1,0:T(8,128)S(1)}, u32[]{:S(2)}, u32[]{:S(2)}) %collective-permute-start.16) | collective-permute-done | bytes 524320 | tf_op jit(solution)/shard_map/ppermute | solution.py:319
  132.8 5.4 %collective-permute-done.17 = bf16[128,512]{1,0:T(8,128)(2,1)S(1)} collective-permute-done((bf16[128,512]{1,0:T(8,128)(2,1)S(1)}, bf16[128,512]{1,0:T(8,128)(2,1)S(1)}, u32[]{:S(2)}, u32[]{:S(2)}) %collective-permute-start.17) | collective-permute-done | bytes 131104 | tf_op jit(solution)/shard_map/ppermute | solution.py:319
  144.9 11.7 %shard_map.103 = (bf16[8,128,384]{2,1,0:T(8,128)(2,1)}, bf16[8,128,384]{2,1,0:T(8,128)(2,1)}, bf16[8,128,384]{2,1,0:T(8,128)(2,1)}, bf16[8,128,384]{2,1,0:T(8,12...) custom-call(bf16[128,1024]{1,0:T(8,128)(2,1)} %get-tuple-element.71.raw_ref, ...), custom_call_target="tpu_custom_call" | custom-call | flops 3221225472 | bytes 25165824 | tf_op jit(solution)/shard_map/pallas_call | solution.py:118
  157.9 7.0 %shard_map.104 = (bf16[384,1024]{1,0:T(8,128)(2,1)}, bf16[384,1024]{1,0:T(8,128)(2,1)}, bf16[384,1024]{1,0:T(8,128)(2,1)}, bf16[384,1024]{1,0:T(8,128)(2,1)}) custom-call(bf16[128,1024]{1,0:T(8,128)(2,1)} %get-tuple-element.79.keys_ref, bf16[8,128,384]{2,1,0:T(8,128)(2,1)} %get-tuple-element.87.refs_0_, bf16[8,128,384]{2,1,0:T(8,128)(2,1)} %get-tuple-element.88.refs_1_, ...), custom_call_target="tpu_custom_call" | custom-call | flops 1610612736 | bytes 12582912 | tf_op jit(solution)/shard_map/pallas_call | solution.py:142
  166.2 3.3 %collective-permute-done.25 = f32[128,1]{1,0:T(8,128)S(1)} collective-permute-done((f32[128,1]{1,0:T(8,128)S(1)}, f32[128,1]{1,0:T(8,128)S(1)}, u32[]{:S(2)}, u32[]{:S(2)}) %collective-permute-start.25) | collective-permute-done | bytes 544 | tf_op jit(solution)/shard_map/ppermute | solution.py:322
  174.9 6.8 %collective-permute-done.30.refs_3_ = bf16[128,1024]{1,0:T(8,128)(2,1)S(1)} collective-permute-done((bf16[128,1024]{1,0:T(8,128)(2,1)S(1)}, bf16[128,1024]{1,0:T(8,128)(2,1)S(1)}, u32[]{:S(2)}, u32[]{:S(2)}) %collective-permute-start.30) | collective-permute-done | bytes 262176 | tf_op jit(solution)/shard_map/ppermute | solution.py:319
  182.2 12.3 %collective-permute-done.29.refs_2_ = bf16[128,1024]{1,0:T(8,128)(2,1)S(1)} collective-permute-done((bf16[128,1024]{1,0:T(8,128)(2,1)S(1)}, bf16[128,1024]{1,0:T(8,128)(2,1)S(1)}, u32[]{:S(2)}, u32[]{:S(2)}) %collective-permute-start.29) | collective-permute-done | bytes 262176 | tf_op jit(solution)/shard_map/ppermute | solution.py:319
  197.6 4.3 %shard_map.107 = f32[512,1024]{1,0:T(8,128)} custom-call(bf16[512,1024]{1,0:T(8,128)(2,1)} %maximum_bitcast_fusion.columns_ref, bf16[128,1024]{1,0:T(8,128)(2,1)} %get-tuple-element.93.refs_0_, bf16[128,1024]{1,0:T(8,128)(2,1)} %copy-done.11, bf16[128,1024]{1,0:T(8,128)(2,1)} %copy-done.10, bf16[128,1024]{1,0:T(8,128)(2,1)} %copy-done.9, ...), custom_call_target="tpu_custom_call" | custom-call | flops 1073741824 | bytes 5242880 | tf_op jit(solution)/shard_map/pallas_call | solution.py:231
  201.9 11.7 %collective-permute-done.32.refs_5_.refs_6_.refs_7_ = bf16[384,1024]{1,0:T(8,128)(2,1)S(1)} collective-permute-done((bf16[384,1024]{1,0:T(8,128)(2,1)}, bf16[384,1024]{1,0:T(8,128)(2,1)S(1)}, u32[]{:S(2)}, u32[]{:S(2)}) %collective-permute-start.32) | collective-permute-done | bytes 786464 | tf_op jit(solution)/shard_map/ppermute | solution.py:319
  214.6 4.3 %shard_map.106 = f32[512,1024]{1,0:T(8,128)} custom-call(bf16[512,1024]{1,0:T(8,128)(2,1)} %maximum_bitcast_fusion.columns_ref, bf16[128,1024]{1,0:T(8,128)(2,1)} %copy-done.8, bf16[128,1024]{1,0:T(8,128)(2,1)} %copy-done.14, bf16[128,1024]{1,0:T(8,128)(2,1)} %copy-done.13, bf16[128,1024]{1,0:T(8,128)(2,1)} %copy-done.12, bf16[128,1024]{1,0:T(8,128)(2,1)} %copy-done.25, ...), custom_call_target="tpu_custom_call" | custom-call | flops 1073741824 | bytes 5242880 | tf_op jit(solution)/shard_map/pallas_call | solution.py:231
  219.7 3.1 %shard_map.105 = bf16[384,4096]{1,0:T(8,128)(2,1)} custom-call(s32[4]{0:T(128)} %pad_add_fusion.lanes_ref.place_ref, bf16[384,1024]{1,0:T(8,128)(2,1)} %get-tuple-element.91.refs_0_, bf16[384,1024]{1,0:T(8,128)(2,1)} %copy-done.15, bf16[384,1024]{1,0:T(8,128)(2,1)} %collective-permute-done.26.refs_2_, bf16[384,1024]{1,0:T(8,128)(2,1)} %collective-permute-done.28.refs_3_), custom_call_target="tpu_custom_call" | custom-call | flops 1000 | bytes 1000 | tf_op jit(solution)/shard_map/pallas_call | solution.py:295
  (133 shorter events, 58.0 us)
Async XLA Ops:
  5.6 34.3 %collective-permute-start = (bf16[768,512]{1,0:T(8,128)(2,1)}, bf16[768,512]{1,0:T(8,128)(2,1)S(1)}, u32[]{:S(2)}, u32[]{:S(2)}) collective-permute-start(bf16[768,512]{1,0:T(8,128)(2,1)} %get-tuple-element.55), channel_id=1, source_target_pairs={{0,8},{4,12},{8,0},{12,4},{16,24},{20,28},{24,16},{28,20},{1,9},{5... | collective-permute-start | bytes 2359304 | tf_op jit(solution)/shard_map/ppermute | solution.py:319
  15.1 54.1 %collective-permute-start.14 = (bf16[2,384,1024]{2,1,0:T(8,128)(2,1)}, bf16[2,384,1024]{2,1,0:T(8,128)(2,1)S(1)}, u32[]{:S(2)}, u32[]{:S(2)}) collective-permute-start(bf16[2,384,1024]{2,1,0:T(8,128)(2,1)} %get-tuple-element.76), channel_id=1, source_target_pairs={{0,2},{1,3},{2,0},{3,1},{4,6},{5,7},{6,4},{7,5},{8,10},{9,11},{10,... | collective-permute-start | bytes 4718600 | tf_op jit(solution)/shard_map/ppermute | solution.py:322
  16.6 15.9 %collective-permute-start.1 = (bf16[128,1024]{1,0:T(8,128)(2,1)}, bf16[128,1024]{1,0:T(8,128)(2,1)S(1)}, u32[]{:S(2)}, u32[]{:S(2)}) collective-permute-start(bf16[128,1024]{1,0:T(8,128)(2,1)} %get-tuple-element.56), channel_id=1, source_target_pairs={{0,16},{4,20},{8,24},{12,28},{16,0},{20,4},{24,8},{28,12},{1,17},{... | collective-permute-start | bytes 786440 | tf_op jit(solution)/shard_map/ppermute | solution.py:319
  19.2 20.7 %collective-permute-start.2 = (bf16[128,1024]{1,0:T(8,128)(2,1)}, bf16[128,1024]{1,0:T(8,128)(2,1)S(1)}, u32[]{:S(2)}, u32[]{:S(2)}) collective-permute-start(bf16[128,1024]{1,0:T(8,128)(2,1)} %get-tuple-element.57), channel_id=1, source_target_pairs={{0,24},{4,28},{8,16},{12,20},{16,8},{20,12},{24,0},{28,4},{1,25},{... | collective-permute-start | bytes 786440 | tf_op jit(solution)/shard_map/ppermute | solution.py:319
  19.4 45.6 %collective-permute-start.4 = (bf16[1024,512]{1,0:T(8,128)(2,1)S(1)}, bf16[1024,512]{1,0:T(8,128)(2,1)}, u32[]{:S(2)}, u32[]{:S(2)}) collective-permute-start(bf16[1024,512]{1,0:T(8,128)(2,1)S(1)} %copy-done.2), channel_id=1, source_target_pairs={{0,4},{4,0},{8,12},{12,8},{16,20},{20,16},{24,28},{28,24},{1,5},{5... | collective-permute-start | bytes 3145736 | tf_op jit(solution)/shard_map/ppermute | solution.py:319
  44.2 17.2 %collective-permute-start.3 = (bf16[384,1024]{1,0:T(8,128)(2,1)}, bf16[384,1024]{1,0:T(8,128)(2,1)S(1)}, u32[]{:S(2)}, u32[]{:S(2)}) collective-permute-start(bf16[384,1024]{1,0:T(8,128)(2,1)} %get-tuple-element.60), channel_id=1, source_target_pairs={{0,1},{1,0},{2,3},{3,2},{4,5},{5,4},{6,7},{7,6},{8,9},{9,8},{10,11... | collective-permute-start | bytes 2359304 | tf_op jit(solution)/shard_map/ppermute | solution.py:322
  47.0 18.1 %collective-permute-start.5 = (bf16[512,512]{1,0:T(8,128)(2,1)}, bf16[512,512]{1,0:T(8,128)(2,1)}, u32[]{:S(2)}, u32[]{:S(2)}) collective-permute-start(bf16[512,512]{1,0:T(8,128)(2,1)} %get-tuple-element.64.refs_6_), channel_id=1, source_target_pairs={{0,4},{4,0},{8,12},{12,8},{16,20},{20,16},{24,28},{28,24},{1,5},{5... | collective-permute-start | bytes 1572872 | tf_op jit(solution)/shard_map/ppermute | solution.py:319
  59.9 17.7 %collective-permute-start.8 = (bf16[512,512]{1,0:T(8,128)(2,1)}, bf16[512,512]{1,0:T(8,128)(2,1)}, u32[]{:S(2)}, u32[]{:S(2)}) collective-permute-start(bf16[512,512]{1,0:T(8,128)(2,1)} %collective-permute-done.7.refs_6_), channel_id=1, source_target_pairs={{0,4},{4,0},{8,12},{12,8},{16,20},{20,16},{24,28},{28,24},{1,5},{5... | collective-permute-start | bytes 1572872 | tf_op jit(solution)/shard_map/ppermute | solution.py:319
  68.7 16.5 %collective-permute-start.9 = (bf16[512,512]{0,1:T(8,128)(2,1)S(1)}, bf16[512,512]{0,1:T(8,128)(2,1)}, u32[]{:S(2)}, u32[]{:S(2)}) collective-permute-start(bf16[512,512]{0,1:T(8,128)(2,1)S(1)} %copy.16), channel_id=1, source_target_pairs={{0,4},{4,0},{8,12},{12,8},{16,20},{20,16},{24,28},{28,24},{1,5},{5... | collective-permute-start | bytes 1572872 | tf_op jit(solution)/shard_map/ppermute | solution.py:319
  69.2 40.5 %collective-permute-start.13 = (bf16[2,384,1024]{2,1,0:T(8,128)(2,1)}, bf16[2,384,1024]{2,1,0:T(8,128)(2,1)}, u32[]{:S(2)}, u32[]{:S(2)}) collective-permute-start(bf16[2,384,1024]{2,1,0:T(8,128)(2,1)} %get-tuple-element.75), channel_id=1, source_target_pairs={{0,1},{1,0},{2,3},{3,2},{4,5},{5,4},{6,7},{7,6},{8,9},{9,8},{10,11... | collective-permute-start | bytes 4718600 | tf_op jit(solution)/shard_map/ppermute | solution.py:322
  69.3 40.5 %collective-permute-start.15 = (bf16[2,384,1024]{2,1,0:T(8,128)(2,1)}, bf16[2,384,1024]{2,1,0:T(8,128)(2,1)}, u32[]{:S(2)}, u32[]{:S(2)}) collective-permute-start(bf16[2,384,1024]{2,1,0:T(8,128)(2,1)} %get-tuple-element.78), channel_id=1, source_target_pairs={{0,3},{1,2},{2,1},{3,0},{4,7},{5,6},{6,5},{7,4},{8,11},{9,10},{10,... | collective-permute-start | bytes 4718600 | tf_op jit(solution)/shard_map/ppermute | solution.py:322
  69.9 26.5 %collective-permute-start.6 = (f32[256,512]{1,0:T(8,128)}, f32[256,512]{1,0:T(8,128)}, u32[]{:S(2)}, u32[]{:S(2)}) collective-permute-start(f32[256,512]{1,0:T(8,128)} %shard_map.97), channel_id=1, source_target_pairs={{0,16},{4,20},{8,24},{12,28},{16,0},{20,4},{24,8},{28,12},{1,17},{... | collective-permute-start | bytes 1572872 | tf_op jit(solution)/shard_map/ppermute | solution.py:319
  107.0 25.6 %collective-permute-start.16 = (f32[256,512]{1,0:T(8,128)S(1)}, f32[256,512]{1,0:T(8,128)S(1)}, u32[]{:S(2)}, u32[]{:S(2)}) collective-permute-start(f32[256,512]{1,0:T(8,128)S(1)} %copy-done.20), channel_id=1, source_target_pairs={{0,16},{4,20},{8,24},{12,28},{16,0},{20,4},{24,8},{28,12},{1,17},{... | collective-permute-start | bytes 1572872 | tf_op jit(solution)/shard_map/ppermute | solution.py:319
  139.0 17.6 %collective-permute-start.23 = (bf16[128,1024]{1,0:T(8,128)(2,1)S(1)}, bf16[128,1024]{1,0:T(8,128)(2,1)S(1)}, u32[]{:S(2)}, u32[]{:S(2)}) collective-permute-start(bf16[128,1024]{1,0:T(8,128)(2,1)S(1)} %copy-done.23), channel_id=1, source_target_pairs={{0,4},{4,0},{8,12},{12,8},{16,20},{20,16},{24,28},{28,24},{1,5},{5... | collective-permute-start | bytes 786440 | tf_op jit(solution)/shard_map/ppermute | solution.py:319
  140.5 24.4 %collective-permute-start.20 = (bf16[128,1024]{1,0:T(8,128)(2,1)S(1)}, bf16[128,1024]{1,0:T(8,128)(2,1)S(1)}, u32[]{:S(2)}, u32[]{:S(2)}) collective-permute-start(bf16[128,1024]{1,0:T(8,128)(2,1)S(1)} %copy-done.23), channel_id=1, source_target_pairs={{0,24},{4,28},{8,16},{12,20},{16,8},{20,12},{24,0},{28,4},{1,25},{... | collective-permute-start | bytes 786440 | tf_op jit(solution)/shard_map/ppermute | solution.py:319
  142.6 22.4 %collective-permute-start.19 = (bf16[128,1024]{1,0:T(8,128)(2,1)S(1)}, bf16[128,1024]{1,0:T(8,128)(2,1)S(1)}, u32[]{:S(2)}, u32[]{:S(2)}) collective-permute-start(bf16[128,1024]{1,0:T(8,128)(2,1)S(1)} %copy-done.23), channel_id=1, source_target_pairs={{0,16},{4,20},{8,24},{12,28},{16,0},{20,4},{24,8},{28,12},{1,17},{... | collective-permute-start | bytes 786440 | tf_op jit(solution)/shard_map/ppermute | solution.py:319
  142.6 22.4 %collective-permute-start.18 = (bf16[128,1024]{1,0:T(8,128)(2,1)S(1)}, bf16[128,1024]{1,0:T(8,128)(2,1)S(1)}, u32[]{:S(2)}, u32[]{:S(2)}) collective-permute-start(bf16[128,1024]{1,0:T(8,128)(2,1)S(1)} %copy-done.23), channel_id=1, source_target_pairs={{0,8},{4,12},{8,0},{12,4},{16,24},{20,28},{24,16},{28,20},{1,9},{5... | collective-permute-start | bytes 786440 | tf_op jit(solution)/shard_map/ppermute | solution.py:319
  165.6 30.4 %collective-permute-start.21 = (bf16[384,1024]{1,0:T(8,128)(2,1)S(1)}, bf16[384,1024]{1,0:T(8,128)(2,1)S(1)}, u32[]{:S(2)}, u32[]{:S(2)}) collective-permute-start(bf16[384,1024]{1,0:T(8,128)(2,1)S(1)} %pad_maximum_fusion), channel_id=1, source_target_pairs={{0,4},{4,0},{8,12},{12,8},{16,20},{20,16},{24,28},{28,24},{1,5},{5... | collective-permute-start | bytes 2359304 | tf_op jit(solution)/shard_map/ppermute | solution.py:319
  169.7 26.4 %collective-permute-start.26 = (bf16[384,1024]{1,0:T(8,128)(2,1)S(1)}, bf16[384,1024]{1,0:T(8,128)(2,1)}, u32[]{:S(2)}, u32[]{:S(2)}) collective-permute-start(bf16[384,1024]{1,0:T(8,128)(2,1)S(1)} %copy-done.26), channel_id=1, source_target_pairs={{0,2},{1,3},{2,0},{3,1},{4,6},{5,7},{6,4},{7,5},{8,10},{9,11},{10,... | collective-permute-start | bytes 2359304 | tf_op jit(solution)/shard_map/ppermute | solution.py:322
  172.6 21.8 %collective-permute-start.29 = (bf16[128,1024]{1,0:T(8,128)(2,1)S(1)}, bf16[128,1024]{1,0:T(8,128)(2,1)S(1)}, u32[]{:S(2)}, u32[]{:S(2)}) collective-permute-start(bf16[128,1024]{1,0:T(8,128)(2,1)S(1)} %fusion.3.refs_0_), channel_id=1, source_target_pairs={{0,16},{4,20},{8,24},{12,28},{16,0},{20,4},{24,8},{28,12},{1,17},{... | collective-permute-start | bytes 786440 | tf_op jit(solution)/shard_map/ppermute | solution.py:319
  172.6 21.8 %collective-permute-start.27 = (bf16[128,1024]{1,0:T(8,128)(2,1)S(1)}, bf16[128,1024]{1,0:T(8,128)(2,1)S(1)}, u32[]{:S(2)}, u32[]{:S(2)}) collective-permute-start(bf16[128,1024]{1,0:T(8,128)(2,1)S(1)} %fusion.3.refs_0_), channel_id=1, source_target_pairs={{0,8},{4,12},{8,0},{12,4},{16,24},{20,28},{24,16},{28,20},{1,9},{5... | collective-permute-start | bytes 786440 | tf_op jit(solution)/shard_map/ppermute | solution.py:319
  195.4 18.2 %collective-permute-start.32 = (bf16[384,1024]{1,0:T(8,128)(2,1)}, bf16[384,1024]{1,0:T(8,128)(2,1)S(1)}, u32[]{:S(2)}, u32[]{:S(2)}) collective-permute-start(bf16[384,1024]{1,0:T(8,128)(2,1)} %pad_maximum_fusion.1), channel_id=1, source_target_pairs={{0,4},{4,0},{8,12},{12,8},{16,20},{20,16},{24,28},{28,24},{1,5},{5... | collective-permute-start | bytes 2359304 | tf_op jit(solution)/shard_map/ppermute | solution.py:319
  196.0 22.8 %collective-permute-start.22 = (bf16[384,1024]{1,0:T(8,128)(2,1)}, bf16[384,1024]{1,0:T(8,128)(2,1)S(1)}, u32[]{:S(2)}, u32[]{:S(2)}) collective-permute-start(bf16[384,1024]{1,0:T(8,128)(2,1)} %get-tuple-element.94), channel_id=1, source_target_pairs={{0,1},{1,0},{2,3},{3,2},{4,5},{5,4},{6,7},{7,6},{8,9},{9,8},{10,11... | collective-permute-start | bytes 2359304 | tf_op jit(solution)/shard_map/ppermute | solution.py:322
  196.0 22.8 %collective-permute-start.28 = (bf16[384,1024]{1,0:T(8,128)(2,1)}, bf16[384,1024]{1,0:T(8,128)(2,1)}, u32[]{:S(2)}, u32[]{:S(2)}) collective-permute-start(bf16[384,1024]{1,0:T(8,128)(2,1)} %get-tuple-element.102), channel_id=1, source_target_pairs={{0,3},{1,2},{2,1},{3,0},{4,7},{5,6},{6,5},{7,4},{8,11},{9,10},{10,... | collective-permute-start | bytes 2359304 | tf_op jit(solution)/shard_map/ppermute | solution.py:322
  (36 other events, 379.6 us)

commit v9 on v8

--- a/solution.py
+++ b/solution.py
@@ -21,74 +21,84 @@
     query_refs, grad_refs = refs[:parts], refs[parts : 2 * parts]
     attend_refs = refs[2 * parts : 3 * parts]
     keys_ref, value_grad_ref = refs[3 * parts :]
-    raw = raw_ref[...].astype(jnp.float32)
-    keys = (raw * inv_ref[...] * gain_ref[...]).astype(jnp.bfloat16)
+    keys = (raw_ref[...].astype(jnp.float32) * inv_ref[...] * gain_ref[...]).astype(jnp.bfloat16)
     keys_ref[...] = keys
     valid = lax.broadcasted_iota(jnp.int32, (LIVE, 1), 0) < length_ref[0]
-    value_grad = jnp.zeros((LIVE, HD), jnp.float32)
-    for query_ref, grad_ref, attend_ref in zip(query_refs, grad_refs, attend_refs):
-        scores = lax.dot_general(keys, query_ref[...], ROWS, preferred_element_type=jnp.float32)
-        scores = jnp.where(valid, scores * FACTOR, -jnp.inf)
-        powers = jnp.exp(scores - jnp.max(scores, axis=0, keepdims=True))
-        attend = powers * (1.0 / jnp.sum(powers, axis=0, keepdims=True))
-        attend_ref[0] = attend
-        value_grad += jnp.dot(
-            attend.astype(jnp.bfloat16), grad_ref[...], preferred_element_type=jnp.float32
-        )
-    value_grad_ref[...] = value_grad.astype(jnp.bfloat16)
+    for head in range(keys.shape[1] // HD):
+        at = slice(head * HD, (head + 1) * HD)
+        value_grad = jnp.zeros((LIVE, HD), jnp.float32)
+        for query_ref, grad_ref, attend_ref in zip(query_refs, grad_refs, attend_refs):
+            scores = lax.dot_general(
+                keys[:, at], query_ref[:, at], ROWS, preferred_element_type=jnp.float32
+            )
+            scores = jnp.where(valid, scores * FACTOR, -jnp.inf)
+            powers = jnp.exp(scores - jnp.max(scores, axis=0, keepdims=True))
+            attend = powers * (1.0 / jnp.sum(powers, axis=0, keepdims=True))
+            attend_ref[head] = attend
+            value_grad += jnp.dot(
+                attend.astype(jnp.bfloat16), grad_ref[:, at], preferred_element_type=jnp.float32
+            )
+        value_grad_ref[:, at] = value_grad.astype(jnp.bfloat16)
 
 
 def gradient_kernel(parts, raw_ref, value_ref, gain_ref, *refs):
     query_refs, grad_refs = refs[:parts], refs[parts : 2 * parts]
     attend_refs, score_refs = refs[2 * parts : 3 * parts], refs[3 * parts : 4 * parts]
     scaled_ref, inner_ref = refs[4 * parts :]
-    values = value_ref[...]
-    key_grad = jnp.zeros((LIVE, HD), jnp.float32)
-    for query_ref, grad_ref, attend_ref, score_ref in zip(
-        query_refs, grad_refs, attend_refs, score_refs
-    ):
-        attend = attend_ref[0]
-        dattend = lax.dot_general(values, grad_ref[...], ROWS, preferred_element_type=jnp.float32)
-        delta = jnp.sum(attend * dattend, axis=0, keepdims=True)
-        dscores = (attend * (dattend - delta)).astype(jnp.bfloat16)
-        score_ref[0] = dscores
-        key_grad += jnp.dot(dscores, query_ref[...], preferred_element_type=jnp.float32)
-    scaled = key_grad * FACTOR * gain_ref[...]
-    scaled_ref[...] = scaled
 
     @pl.when(pl.program_id(0) == 0)
     def _():
         inner_ref[...] = jnp.zeros_like(inner_ref)
 
-    inner_ref[...] += scaled * raw_ref[...].astype(jnp.float32)
+    for head in range(value_ref.shape[1] // HD):
+        at = slice(head * HD, (head + 1) * HD)
+        key_grad = jnp.zeros((LIVE, HD), jnp.float32)
+        for query_ref, grad_ref, attend_ref, score_ref in zip(
+            query_refs, grad_refs, attend_refs, score_refs
+        ):
+            attend = attend_ref[head]
+            dattend = lax.dot_general(
+                value_ref[:, at], grad_ref[:, at], ROWS, preferred_element_type=jnp.float32
+            )
+            delta = jnp.sum(attend * dattend, axis=0, keepdims=True)
+            dscores = (attend * (dattend - delta)).astype(jnp.bfloat16)
+            score_ref[head] = dscores
+            key_grad += jnp.dot(dscores, query_ref[:, at], preferred_element_type=jnp.float32)
+        scaled = key_grad * FACTOR * gain_ref[:, at]
+        scaled_ref[:, at] = scaled
+        inner_ref[...] += scaled * raw_ref[:, at].astype(jnp.float32)
 
 
 def query_kernel(parts, keys_ref, *refs):
-    for score_ref, out_ref in zip(refs[:parts], refs[parts:]):
-        out = lax.dot_general(
-            score_ref[0], keys_ref[...], COLUMNS, preferred_element_type=jnp.float32
-        )
-        out_ref[...] = (out * FACTOR).astype(jnp.bfloat16)
-
-
-def specs(tokens):
-    head = pl.BlockSpec((LIVE, HD), lambda h: (0, h))
-    block = pl.BlockSpec((tokens, HD), lambda h: (0, h))
-    upper = pl.BlockSpec((None, tokens, HD), lambda h: (0, 0, h))
-    lower = pl.BlockSpec((None, tokens, HD), lambda h: (1, 0, h))
-    weights = pl.BlockSpec((1, LIVE, tokens), lambda h: (h, 0, 0))
-    gain = pl.BlockSpec((1, HD), lambda h: (0, h))
-    return head, block, upper, lower, weights, gain
+    for head in range(keys_ref.shape[1] // HD):
+        at = slice(head * HD, (head + 1) * HD)
+        for score_ref, out_ref in zip(refs[:parts], refs[parts:]):
+            out = lax.dot_general(
+                score_ref[head], keys_ref[:, at], COLUMNS, preferred_element_type=jnp.float32
+            )
+            out_ref[:, at] = (out * FACTOR).astype(jnp.bfloat16)
+
+
+def specs(tokens, heads):
+    group = 2 - heads % 2
+    width = group * HD
+    head = pl.BlockSpec((LIVE, width), lambda h: (0, h))
+    block = pl.BlockSpec((tokens, width), lambda h: (0, h))
+    upper = pl.BlockSpec((None, tokens, width), lambda h: (0, 0, h))
+    lower = pl.BlockSpec((None, tokens, width), lambda h: (1, 0, h))
+    weights = pl.BlockSpec((group, LIVE, tokens), lambda h: (h, 0, 0))
+    gain = pl.BlockSpec((1, width), lambda h: (0, h))
+    return heads // group, head, block, upper, lower, weights, gain
 
 
 def attend_call(length, raw, inv, gain, moved, tokens):
     parts = len(moved)
     cols = moved[0].shape[2]
     heads = cols // HD
-    head, block, upper, lower, weights, gains = specs(tokens)
+    steps, head, block, upper, lower, weights, gains = specs(tokens, heads)
     outs = pl.pallas_call(
         functools.partial(attend_kernel, parts),
-        grid=(heads,),
+        grid=(steps,),
         in_specs=[
             pl.BlockSpec(memory_space=pltpu.SMEM),
             head,
@@ -114,10 +124,10 @@
     parts = len(moved)
     cols = moved[0].shape[2]
     heads = cols // HD
-    head, block, upper, lower, weights, gains = specs(tokens)
+    steps, head, block, upper, lower, weights, gains = specs(tokens, heads)
     outs = pl.pallas_call(
         functools.partial(gradient_kernel, parts),
-        grid=(heads,),
+        grid=(steps,),
         in_specs=[head, head, gains] + [upper] * parts + [lower] * parts + [weights] * parts,
         out_specs=[weights] * parts + [head, pl.BlockSpec((LIVE, HD), lambda h: (0, 0))],
         out_shape=[jax.ShapeDtypeStruct((heads, LIVE, tokens), jnp.bfloat16)] * parts
@@ -138,10 +148,10 @@
 def query_call(keys, scores):
     parts = len(scores)
     heads, _, tokens = scores[0].shape
-    head, block, _, _, weights, _ = specs(tokens)
+    steps, head, block, _, _, weights, _ = specs(tokens, heads)
     return pl.pallas_call(
         functools.partial(query_kernel, parts),
-        grid=(heads,),
+        grid=(steps,),
         in_specs=[head] + [weights] * parts,
         out_specs=[block] * parts,
         out_shape=[jax.ShapeDtypeStruct((tokens, keys.shape[1]), jnp.bfloat16)] * parts,
@@ -399,23 +409,19 @@
             step *= 2
         return lax.reduce_precision(total, 8, 7).astype(jnp.bfloat16)
 
-    def joined(total):
-        own, other = total[:LIVE], over_dp(total[LIVE:], 2)
+    def joined(own, other):
         return jnp.where(
             low == 0,
             jnp.concatenate([own, other], axis=1),
             jnp.concatenate([other, own], axis=1),
         )
 
-    def seq_sum(x, before=()):
-        step = 1
-        while step < n_seq:
+    def seq_sum(x):
+        for step in steps:
             x = x + over_seq(x, step)
-            if step == 1:
-                x = after(x, *before)
-            step *= 2
         return x
 
+    steps = [1 << k for k in reversed(range(n_seq.bit_length() - 1))]
     gain = lax.dynamic_slice(key_gain, (lane * cols,), (cols,)).reshape(1, cols)
     own_columns, other_given = pick_call(places, mine_first, shared, sibling_first, sibling, rows)
     key_product = product(after(places, own_columns), key_quad, True)
@@ -426,29 +432,34 @@
     value_product = product(later, value_quad, True)
     value_rest_product = product(later, value_quad, False)
     key_sent = after(key_sent, value_product, value_rest_product, columns, gain)
+    value_sent = over_dp(after(value_product, key_sent), 4)
     key_total = reduced(product(later, key_quad, False) + key_sent)
-    raw = joined(key_total)
-    value_sent = over_dp(after(value_product, raw), 4)
+    raw = joined(key_total[:LIVE], over_dp(key_total[LIVE:], 2))
     raw_wide = raw.astype(jnp.float32)
     squares = seq_sum(jnp.sum(raw_wide * raw_wide, axis=-1, keepdims=True))
     inv_rms = lax.rsqrt(squares / hid + 1e-06)
+    value_total = reduced(value_rest_product + after(value_sent, inv_rms))
+    value_other = over_dp(value_total[LIVE:], 2)
     attends, keys, value_grad = attend_call(
-        lengths, after(raw, columns), inv_rms, gain, moved, tokens
-    )
-    values = joined(reduced(value_rest_product + after(value_sent, value_grad)))
-
-    value_given = after(value_grad, values)
-    value_near_parts = [over_dp(value_given, 2 * s) for s in range(1, lines)]
-    value_first = over_dp(value_given, 1)
+        lengths, after(raw, columns, value_total), inv_rms, gain, moved, tokens
+    )
+
+    values = joined(value_total[:LIVE], after(value_other, value_grad))
+
+    value_near_parts = [over_dp(value_grad, 2 * s) for s in range(1, lines)]
+    value_first = over_dp(value_grad, 1)
     scores, scaled, inner = gradient_call(raw, values, gain, moved, attends, tokens)
     outs = query_call(keys, scores)
-    inner = after(inner, value_first)
-    inner_mean = seq_sum(jnp.sum(inner, axis=-1, keepdims=True), value_near_parts) / hid
+    inner = jnp.sum(after(inner, value_first), axis=-1, keepdims=True)
+    for step in steps[:-1]:
+        inner = inner + over_seq(inner, step)
+    far_sum = after(inner, *value_near_parts)
+    inner_mean = (far_sum + over_seq(far_sum, 1)) / hid
     raw_grad = (inv_rms * scaled - raw_wide * inv_rms**3 * inner_mean).astype(jnp.bfloat16)
     value_rest = over_dp(jnp.concatenate(value_near_parts, axis=0), 1)
     key_near_parts = [over_dp(raw_grad, 2 * s) for s in range(1, lines)]
     placed = [outs[0]] + [None] * (n_seq - 1)
-    previous = (inner_mean,)
+    previous = (inner,)
     for s in range(2, n_seq):
         placed[s] = over_seq(after(outs[s], *previous), s)
         previous = (placed[s], key_near_parts[0])
@@ -466,8 +477,6 @@
         + [(value_rest, LIVE, s) for s in range(lines - 1)]
     )
     value_weight_grad = weights_call(after(columns, key_first), value_parts)
-    key_weight_grad = weights_call(columns, key_parts)
-
     (query_grad,) = pack_call(
         lanes,
         placed,
@@ -475,6 +484,7 @@
         [(s, 0, 0, tokens // 2, cols, 0, 0, (s,)) for s in range(n_seq)],
         2,
     )
+    key_weight_grad = weights_call(after(columns, query_grad), key_parts)
     return query_grad[None], key_weight_grad, value_weight_grad
 
 

time: 224 us -> 211 us (0.942)
  Pallas kernels: 70.9 us -> 63.9 us
  waiting for transfers between devices: 97.9 us -> 93.9 us
    ppermute x22, waiting for transfers between devices: 92.1 us -> 77.6 us  [over_dp(): return lax.ppermute(x, 'dp', [(a, a ^ step) for a in range(n_dp)])]
    ppermute x11, waiting for transfers between devices: 5.73 us -> 16.2 us  [over_seq(): return lax.ppermute(x, 'seq', [(a, a ^ step) for a in range(n_seq)])]
    pallas_call x3, Pallas kernels: 30.1 us -> 23.1 us  [the longest x1 9.04 us: gradient_call(): pl.pallas_call(functools.partial(gradient_kernel, parts), grid=(steps,),...]
    ppermute x11, starting transfers between devices: 6.61 us -> 9.05 us  [over_seq(): return lax.ppermute(x, 'seq', [(a, a ^ step) for a in range(n_seq)])]
    ppermute x22, starting transfers between devices: 29.6 us -> 27.3 us  [over_dp(): return lax.ppermute(x, 'dp', [(a, a ^ step) for a in range(n_dp)])]
  transfers between devices with their start and end apart: 33 -> 33, of which waited for: 14 -> 13; matrix products, arithmetic and copies ran while one was open for 5% -> 5% of each run, Pallas kernels for 28% -> 26%
where the time goes in v9:
time: 211 us; the launch traced here: 210 us
  waiting for transfers between devices  93.9 us (45%)
  Pallas kernels  63.9 us (30%)
  starting transfers between devices  36.4 us (17%)
  other arithmetic  8.18 us (4%)
  local copies, waits for them, and re-layouts  6.43 us (3%)
    ppermute x22, waiting for transfers between devices, over_dp(): return lax.ppermute(x, 'dp', [(a, a ^ step) for a in range(n_dp)])  77.6 us
    ppermute x22, starting transfers between devices, over_dp(): return lax.ppermute(x, 'dp', [(a, a ^ step) for a in range(n_dp)])  27.3 us
    ppermute x11, waiting for transfers between devices, over_seq(): return lax.ppermute(x, 'seq', [(a, a ^ step) for a in range(n_seq)])  16.2 us
    pallas_call x4, Pallas kernels, product_call(): pl.pallas_call(functools.partial(product_kernel, videos), grid=(1,), in_s...  13.5 us
    pallas_call x3, Pallas kernels, pack_call(): pl.pallas_call(functools.partial(pack_kernel, moves, len(arrays)), grid=(...  10.2 us
    ppermute x11, starting transfers between devices, over_seq(): return lax.ppermute(x, 'seq', [(a, a ^ step) for a in range(n_seq)])  9.05 us
    pallas_call x1, Pallas kernels, gradient_call(): pl.pallas_call(functools.partial(gradient_kernel, parts), grid=(steps,),...  9.04 us
    pallas_call x1, Pallas kernels, attend_call(): pl.pallas_call(functools.partial(attend_kernel, parts), grid=(steps,), in...  8.96 us
  transfers between devices with their start and end apart: 33, of which 13 were waited for; matrix products, arithmetic and copies ran while one was open for 5% of the time, Pallas kernels for 26%

profile of v9, /device:TPU:0, one launch (start us, length us, event | category | flops | bytes accessed | tf_op | source)
XLA Modules:
  0.0 210.5 jit_solution(2044409508552307234)
XLA Ops:
  1.3 4.3 %shard_map.94 = (bf16[768,512]{1,0:T(8,128)(2,1)}, bf16[1024,512]{1,0:T(8,128)(2,1)}, bf16[512,512]{1,0:T(8,128)(2,1)}, bf16[128,1024]{1,0:T(8,128)(2,1)}, bf16[...) custom-call(s32[8]{0:T(128)} %stack.72.place_ref, bf16[512,1024]{1,0:T(8,128)(2,1)} %refs_0_.1, ...), custom_call_target="tpu_custom_call" | custom-call | flops 1000 | bytes 1000 | tf_op jit(solution)/shard_map/pallas_call | solution.py:305
  5.6 3.0 %collective-permute-start = (bf16[768,512]{1,0:T(8,128)(2,1)}, bf16[768,512]{1,0:T(8,128)(2,1)S(1)}, u32[]{:S(2)}, u32[]{:S(2)}) collective-permute-start(bf16[768,512]{1,0:T(8,128)(2,1)} %get-tuple-element.56), channel_id=1, source_target_pairs={{0,8},{4,12},{8,0},{12,4},{16,24},{20,28},{24,16},{28,20},{1,9},{5... | collective-permute-start | bytes 2359304 | tf_op jit(solution)/shard_map/ppermute | solution.py:329
  11.8 6.0 %shard_map.101 = (bf16[2,384,1024]{2,1,0:T(8,128)(2,1)}, bf16[2,384,1024]{2,1,0:T(8,128)(2,1)}, bf16[2,384,1024]{2,1,0:T(8,128)(2,1)}, bf16[2,384,1024]{2,1,0:T(8,128)(2,1)}) custom-call(s32[4]{0:T(128)} %pad_add_fusion.lanes_ref.place_ref, bf16[384,4096]{1,0:T(8,128)(2,1)} %bitcast.24, bf16[384,4096]{1,0:T(8,128)(2,1)} %bitcast.25), custom_call_target="tpu_custom_call" | custom-call | flops 1000 | bytes 12582912 | tf_op jit(solution)/shard_map/pallas_call | solution.py:274
  21.0 11.5 %collective-permute-done.1.refs_1_ = bf16[128,1024]{1,0:T(8,128)(2,1)} collective-permute-done((bf16[128,1024]{1,0:T(8,128)(2,1)}, bf16[128,1024]{1,0:T(8,128)(2,1)}, u32[]{:S(2)}, u32[]{:S(2)}) %collective-permute-start.1) | collective-permute-done | bytes 262176 | tf_op jit(solution)/shard_map/ppermute | solution.py:329
  32.5 7.4 %collective-permute-done.2.refs_2_ = bf16[128,1024]{1,0:T(8,128)(2,1)} collective-permute-done((bf16[128,1024]{1,0:T(8,128)(2,1)}, bf16[128,1024]{1,0:T(8,128)(2,1)}, u32[]{:S(2)}, u32[]{:S(2)}) %collective-permute-start.2) | collective-permute-done | bytes 262176 | tf_op jit(solution)/shard_map/ppermute | solution.py:329
  45.7 12.5 %collective-permute-done.7.refs_6_ = bf16[512,512]{1,0:T(8,128)(2,1)} collective-permute-done((bf16[512,512]{1,0:T(8,128)(2,1)}, bf16[512,512]{1,0:T(8,128)(2,1)}, u32[]{:S(2)}, u32[]{:S(2)}) %collective-permute-start.7) | collective-permute-done | bytes 524320 | tf_op jit(solution)/shard_map/ppermute | solution.py:329
  63.3 3.4 %shard_map.97 = f32[256,512]{1,0:T(8,128)} custom-call(s32[4]{0:T(128)} %pad_add_fusion.1.place_ref, bf16[384,1024]{1,0:T(8,128)(2,1)} %get-tuple-element.59.mine_ref.refs_0_.refs_1_, bf16[384,1024]{1,0:T(8,128)(2,1)} %get-tuple-element.59.mine_ref.refs_0_.refs_1_, bf16[384,1024]{1,0:T(8,128)(2,1)} %copy-done, bf16[384,1024]{1,0:T(8,128)(2,1)} %copy-done, ...), custom_call_target="tpu_custom_call" | custom-call | flops 1000 | bytes 1000 | tf_op jit(solution)/shard_map/pallas_call | solution.py:218
  70.7 3.4 %shard_map.98 = f32[256,512]{1,0:T(8,128)} custom-call(s32[4]{0:T(128)} %pad_add_fusion.1.place_ref, bf16[128,1024]{1,0:T(8,128)(2,1)} %get-tuple-element.55.first_ref.refs_0_, bf16[384,1024]{1,0:T(8,128)(2,1)} %get-tuple-element.59.mine_ref.refs_0_.refs_1_, bf16[128,1024]{1,0:T(8,128)(2,1)} %get-tuple-element.60.sibling_first_ref.refs_2_, ...), custom_call_target="tpu_custom_call" | custom-call | flops 1000 | bytes 1000 | tf_op jit(solution)/shard_map/pallas_call | solution.py:218
  75.3 3.4 %shard_map.100 = f32[256,512]{1,0:T(8,128)} custom-call(s32[4]{0:T(128)} %pad_add_fusion.1.place_ref, bf16[128,1024]{1,0:T(8,128)(2,1)} %get-tuple-element.55.first_ref.refs_0_, bf16[384,1024]{1,0:T(8,128)(2,1)} %get-tuple-element.59.mine_ref.refs_0_.refs_1_, bf16[128,1024]{1,0:T(8,128)(2,1)} %get-tuple-element.60.sibling_first_ref.refs_2_, ...), custom_call_target="tpu_custom_call" | custom-call | flops 1000 | bytes 1000 | tf_op jit(solution)/shard_map/pallas_call | solution.py:218
  78.7 3.4 %shard_map.99 = f32[256,512]{1,0:T(8,128)} custom-call(s32[4]{0:T(128)} %pad_add_fusion.1.place_ref, bf16[384,1024]{1,0:T(8,128)(2,1)} %get-tuple-element.59.mine_ref.refs_0_.refs_1_, bf16[384,1024]{1,0:T(8,128)(2,1)} %get-tuple-element.59.mine_ref.refs_0_.refs_1_, bf16[384,1024]{1,0:T(8,128)(2,1)} %copy-done, bf16[384,1024]{1,0:T(8,128)(2,1)} %copy-done, ...), custom_call_target="tpu_custom_call" | custom-call | flops 1000 | bytes 1000 | tf_op jit(solution)/shard_map/pallas_call | solution.py:218
  85.5 7.3 %collective-permute-done.6 = f32[256,512]{1,0:T(8,128)S(1)} collective-permute-done((f32[256,512]{1,0:T(8,128)}, f32[256,512]{1,0:T(8,128)S(1)}, u32[]{:S(2)}, u32[]{:S(2)}) %collective-permute-start.6) | collective-permute-done | bytes 524320 | tf_op jit(solution)/shard_map/ppermute | solution.py:329
  95.0 12.5 %collective-permute-done.10 = bf16[128,512]{1,0:T(8,128)(2,1)S(1)} collective-permute-done((bf16[128,512]{1,0:T(8,128)(2,1)S(1)}, bf16[128,512]{1,0:T(8,128)(2,1)S(1)}, u32[]{:S(2)}, u32[]{:S(2)}) %collective-permute-start.10) | collective-permute-done | bytes 131104 | tf_op jit(solution)/shard_map/ppermute | solution.py:329
  109.9 2.8 %collective-permute-done.12 = f32[128,1]{1,0:T(8,128)S(1)} collective-permute-done((f32[128,1]{1,0:T(8,128)S(1)}, f32[128,1]{1,0:T(8,128)S(1)}, u32[]{:S(2)}, u32[]{:S(2)}) %collective-permute-start.12) | collective-permute-done | bytes 544 | tf_op jit(solution)/shard_map/ppermute | solution.py:332
  114.7 3.1 %collective-permute-done.11 = f32[256,512]{1,0:T(8,128)S(1)} collective-permute-done((f32[256,512]{1,0:T(8,128)}, f32[256,512]{1,0:T(8,128)S(1)}, u32[]{:S(2)}, u32[]{:S(2)}) %collective-permute-start.11) | collective-permute-done | bytes 524320 | tf_op jit(solution)/shard_map/ppermute | solution.py:329
  118.0 9.0 %shard_map.102 = (f32[8,128,384]{2,1,0:T(8,128)}, f32[8,128,384]{2,1,0:T(8,128)}, f32[8,128,384]{2,1,0:T(8,128)}, f32[8,128,384]{2,1,0:T(8,128)}, bf16[128,1024]{1,0:T(8,128)(2,1)}, /*index=5*/bf16[128,1024]{1,0:T(8,128)(2,1)}) custom-call(s32[1]{0:T(128)S(6)} %copy.22.length_ref, bf16[128,1024]{1,0:T(8,128)(2,1)} %get-tuple-element.74.raw_ref, ...), custom_call_target="tpu_custom_call" | custom-call | flops 3221225472 | bytes 25165824 | tf_op jit(solution)/shard_map/pallas_call | solution.py:99
  133.8 9.0 %shard_map.103 = (bf16[8,128,384]{2,1,0:T(8,128)(2,1)}, bf16[8,128,384]{2,1,0:T(8,128)(2,1)}, bf16[8,128,384]{2,1,0:T(8,128)(2,1)}, bf16[8,128,384]{2,1,0:T(8,12...) custom-call(bf16[128,1024]{1,0:T(8,128)(2,1)} %get-tuple-element.74.raw_ref, ...), custom_call_target="tpu_custom_call" | custom-call | flops 3221225472 | bytes 25165824 | tf_op jit(solution)/shard_map/pallas_call | solution.py:128
  145.5 5.1 %shard_map.104 = (bf16[384,1024]{1,0:T(8,128)(2,1)}, bf16[384,1024]{1,0:T(8,128)(2,1)}, bf16[384,1024]{1,0:T(8,128)(2,1)}, bf16[384,1024]{1,0:T(8,128)(2,1)}) custom-call(bf16[128,1024]{1,0:T(8,128)(2,1)} %get-tuple-element.82.keys_ref, bf16[8,128,384]{2,1,0:T(8,128)(2,1)} %get-tuple-element.89.refs_0_, bf16[8,128,384]{2,1,0:T(8,128)(2,1)} %get-tuple-element.90.refs_1_, ...), custom_call_target="tpu_custom_call" | custom-call | flops 1610612736 | bytes 12582912 | tf_op jit(solution)/shard_map/pallas_call | solution.py:152
  150.7 4.0 %collective-permute-done.19.refs_2_ = bf16[128,1024]{1,0:T(8,128)(2,1)S(1)} collective-permute-done((bf16[128,1024]{1,0:T(8,128)(2,1)}, bf16[128,1024]{1,0:T(8,128)(2,1)S(1)}, u32[]{:S(2)}, u32[]{:S(2)}) %collective-permute-start.19) | collective-permute-done | bytes 262176 | tf_op jit(solution)/shard_map/ppermute | solution.py:329
  161.7 6.7 %collective-permute-done.30.refs_3_ = bf16[128,1024]{1,0:T(8,128)(2,1)S(1)} collective-permute-done((bf16[128,1024]{1,0:T(8,128)(2,1)S(1)}, bf16[128,1024]{1,0:T(8,128)(2,1)S(1)}, u32[]{:S(2)}, u32[]{:S(2)}) %collective-permute-start.30) | collective-permute-done | bytes 262176 | tf_op jit(solution)/shard_map/ppermute | solution.py:329
  169.9 11.4 %collective-permute-done.29.refs_2_ = bf16[128,1024]{1,0:T(8,128)(2,1)S(1)} collective-permute-done((bf16[128,1024]{1,0:T(8,128)(2,1)S(1)}, bf16[128,1024]{1,0:T(8,128)(2,1)S(1)}, u32[]{:S(2)}, u32[]{:S(2)}) %collective-permute-start.29) | collective-permute-done | bytes 262176 | tf_op jit(solution)/shard_map/ppermute | solution.py:329
  185.0 4.3 %shard_map.107 = f32[512,1024]{1,0:T(8,128)} custom-call(bf16[512,1024]{1,0:T(8,128)(2,1)} %maximum_bitcast_fusion.columns_ref, bf16[128,1024]{1,0:T(8,128)(2,1)} %get-tuple-element.83.refs_0_, bf16[128,1024]{1,0:T(8,128)(2,1)} %copy-done.11, bf16[128,1024]{1,0:T(8,128)(2,1)} %copy-done.10, bf16[128,1024]{1,0:T(8,128)(2,1)} %copy-done.9, ...), custom_call_target="tpu_custom_call" | custom-call | flops 1073741824 | bytes 5242880 | tf_op jit(solution)/shard_map/pallas_call | solution.py:241
  189.3 12.9 %collective-permute-done.28.refs_3_ = bf16[384,1024]{1,0:T(8,128)(2,1)} collective-permute-done((bf16[384,1024]{1,0:T(8,128)(2,1)}, bf16[384,1024]{1,0:T(8,128)(2,1)}, u32[]{:S(2)}, u32[]{:S(2)}) %collective-permute-start.28) | collective-permute-done | bytes 786464 | tf_op jit(solution)/shard_map/ppermute | solution.py:332
  202.2 3.1 %shard_map.105 = bf16[384,4096]{1,0:T(8,128)(2,1)} custom-call(s32[4]{0:T(128)} %pad_add_fusion.lanes_ref.place_ref, bf16[384,1024]{1,0:T(8,128)(2,1)} %get-tuple-element.93.refs_0_, bf16[384,1024]{1,0:T(8,128)(2,1)} %copy-done.16, bf16[384,1024]{1,0:T(8,128)(2,1)} %copy-done.15, bf16[384,1024]{1,0:T(8,128)(2,1)} %collective-permute-done.28.refs_3_), custom_call_target="tpu_custom_call" | custom-call | flops 1000 | bytes 1000 | tf_op jit(solution)/shard_map/pallas_call | solution.py:305
  206.2 4.3 %shard_map.106 = f32[512,1024]{1,0:T(8,128)} custom-call(bf16[512,1024]{1,0:T(8,128)(2,1)} %maximum_bitcast_fusion.columns_ref, bf16[128,1024]{1,0:T(8,128)(2,1)} %copy-done.8, bf16[128,1024]{1,0:T(8,128)(2,1)} %copy-done.14, bf16[128,1024]{1,0:T(8,128)(2,1)} %copy-done.13, bf16[128,1024]{1,0:T(8,128)(2,1)} %copy-done.12, bf16[128,1024]{1,0:T(8,128)(2,1)} %copy-done.21, ...), custom_call_target="tpu_custom_call" | custom-call | flops 1073741824 | bytes 5242880 | tf_op jit(solution)/shard_map/pallas_call | solution.py:241
  (125 shorter events, 55.2 us)
Async XLA Ops:
  5.6 34.3 %collective-permute-start = (bf16[768,512]{1,0:T(8,128)(2,1)}, bf16[768,512]{1,0:T(8,128)(2,1)S(1)}, u32[]{:S(2)}, u32[]{:S(2)}) collective-permute-start(bf16[768,512]{1,0:T(8,128)(2,1)} %get-tuple-element.56), channel_id=1, source_target_pairs={{0,8},{4,12},{8,0},{12,4},{16,24},{20,28},{24,16},{28,20},{1,9},{5... | collective-permute-start | bytes 2359304 | tf_op jit(solution)/shard_map/ppermute | solution.py:329
  8.6 23.9 %collective-permute-start.1 = (bf16[128,1024]{1,0:T(8,128)(2,1)}, bf16[128,1024]{1,0:T(8,128)(2,1)}, u32[]{:S(2)}, u32[]{:S(2)}) collective-permute-start(bf16[128,1024]{1,0:T(8,128)(2,1)} %get-tuple-element.57), channel_id=1, source_target_pairs={{0,16},{4,20},{8,24},{12,28},{16,0},{20,4},{24,8},{28,12},{1,17},{... | collective-permute-start | bytes 786440 | tf_op jit(solution)/shard_map/ppermute | solution.py:329
  11.2 28.7 %collective-permute-start.2 = (bf16[128,1024]{1,0:T(8,128)(2,1)}, bf16[128,1024]{1,0:T(8,128)(2,1)}, u32[]{:S(2)}, u32[]{:S(2)}) collective-permute-start(bf16[128,1024]{1,0:T(8,128)(2,1)} %get-tuple-element.58), channel_id=1, source_target_pairs={{0,24},{4,28},{8,16},{12,20},{16,8},{20,12},{24,0},{28,4},{1,25},{... | collective-permute-start | bytes 786440 | tf_op jit(solution)/shard_map/ppermute | solution.py:329
  17.8 51.3 %collective-permute-start.15 = (bf16[2,384,1024]{2,1,0:T(8,128)(2,1)}, bf16[2,384,1024]{2,1,0:T(8,128)(2,1)S(1)}, u32[]{:S(2)}, u32[]{:S(2)}) collective-permute-start(bf16[2,384,1024]{2,1,0:T(8,128)(2,1)} %get-tuple-element.79), channel_id=1, source_target_pairs={{0,2},{1,3},{2,0},{3,1},{4,6},{5,7},{6,4},{7,5},{8,10},{9,11},{10,... | collective-permute-start | bytes 4718600 | tf_op jit(solution)/shard_map/ppermute | solution.py:332
  19.5 43.8 %collective-permute-start.4 = (bf16[1024,512]{1,0:T(8,128)(2,1)S(1)}, bf16[1024,512]{1,0:T(8,128)(2,1)}, u32[]{:S(2)}, u32[]{:S(2)}) collective-permute-start(bf16[1024,512]{1,0:T(8,128)(2,1)S(1)} %copy-done.2), channel_id=1, source_target_pairs={{0,4},{4,0},{8,12},{12,8},{16,20},{20,16},{24,28},{28,24},{1,5},{5... | collective-permute-start | bytes 3145736 | tf_op jit(solution)/shard_map/ppermute | solution.py:329
  43.5 16.2 %collective-permute-start.3 = (bf16[384,1024]{1,0:T(8,128)(2,1)}, bf16[384,1024]{1,0:T(8,128)(2,1)S(1)}, u32[]{:S(2)}, u32[]{:S(2)}) collective-permute-start(bf16[384,1024]{1,0:T(8,128)(2,1)} %get-tuple-element.61), channel_id=1, source_target_pairs={{0,1},{1,0},{2,3},{3,2},{4,5},{5,4},{6,7},{7,6},{8,9},{9,8},{10,11... | collective-permute-start | bytes 2359304 | tf_op jit(solution)/shard_map/ppermute | solution.py:332
  43.5 19.8 %collective-permute-start.5 = (bf16[512,512]{1,0:T(8,128)(2,1)}, bf16[512,512]{1,0:T(8,128)(2,1)}, u32[]{:S(2)}, u32[]{:S(2)}) collective-permute-start(bf16[512,512]{1,0:T(8,128)(2,1)} %get-tuple-element.65.refs_6_), channel_id=1, source_target_pairs={{0,4},{4,0},{8,12},{12,8},{16,20},{20,16},{24,28},{28,24},{1,5},{5... | collective-permute-start | bytes 1572872 | tf_op jit(solution)/shard_map/ppermute | solution.py:329
  58.2 17.2 %collective-permute-start.8 = (bf16[512,512]{1,0:T(8,128)(2,1)}, bf16[512,512]{1,0:T(8,128)(2,1)}, u32[]{:S(2)}, u32[]{:S(2)}) collective-permute-start(bf16[512,512]{1,0:T(8,128)(2,1)} %collective-permute-done.7.refs_6_), channel_id=1, source_target_pairs={{0,4},{4,0},{8,12},{12,8},{16,20},{20,16},{24,28},{28,24},{1,5},{5... | collective-permute-start | bytes 1572872 | tf_op jit(solution)/shard_map/ppermute | solution.py:329
  67.0 16.3 %collective-permute-start.9 = (bf16[512,512]{0,1:T(8,128)(2,1)S(1)}, bf16[512,512]{0,1:T(8,128)(2,1)}, u32[]{:S(2)}, u32[]{:S(2)}) collective-permute-start(bf16[512,512]{0,1:T(8,128)(2,1)S(1)} %copy.16), channel_id=1, source_target_pairs={{0,4},{4,0},{8,12},{12,8},{16,20},{20,16},{24,28},{28,24},{1,5},{5... | collective-permute-start | bytes 1572872 | tf_op jit(solution)/shard_map/ppermute | solution.py:329
  67.5 25.3 %collective-permute-start.6 = (f32[256,512]{1,0:T(8,128)}, f32[256,512]{1,0:T(8,128)S(1)}, u32[]{:S(2)}, u32[]{:S(2)}) collective-permute-start(f32[256,512]{1,0:T(8,128)} %shard_map.97), channel_id=1, source_target_pairs={{0,16},{4,20},{8,24},{12,28},{16,0},{20,4},{24,8},{28,12},{1,17},{... | collective-permute-start | bytes 1572872 | tf_op jit(solution)/shard_map/ppermute | solution.py:329
  69.1 48.9 %collective-permute-start.14 = (bf16[2,384,1024]{2,1,0:T(8,128)(2,1)}, bf16[2,384,1024]{2,1,0:T(8,128)(2,1)}, u32[]{:S(2)}, u32[]{:S(2)}) collective-permute-start(bf16[2,384,1024]{2,1,0:T(8,128)(2,1)} %get-tuple-element.78), channel_id=1, source_target_pairs={{0,1},{1,0},{2,3},{3,2},{4,5},{5,4},{6,7},{7,6},{8,9},{9,8},{10,11... | collective-permute-start | bytes 4718600 | tf_op jit(solution)/shard_map/ppermute | solution.py:332
  69.1 48.9 %collective-permute-start.16 = (bf16[2,384,1024]{2,1,0:T(8,128)(2,1)}, bf16[2,384,1024]{2,1,0:T(8,128)(2,1)}, u32[]{:S(2)}, u32[]{:S(2)}) collective-permute-start(bf16[2,384,1024]{2,1,0:T(8,128)(2,1)} %get-tuple-element.81), channel_id=1, source_target_pairs={{0,3},{1,2},{2,1},{3,0},{4,7},{5,6},{6,5},{7,4},{8,11},{9,10},{10,... | collective-permute-start | bytes 4718600 | tf_op jit(solution)/shard_map/ppermute | solution.py:332
  92.8 25.0 %collective-permute-start.11 = (f32[256,512]{1,0:T(8,128)}, f32[256,512]{1,0:T(8,128)S(1)}, u32[]{:S(2)}, u32[]{:S(2)}) collective-permute-start(f32[256,512]{1,0:T(8,128)} %shard_map.99), channel_id=1, source_target_pairs={{0,16},{4,20},{8,24},{12,28},{16,0},{20,4},{24,8},{28,12},{1,17},{... | collective-permute-start | bytes 1572872 | tf_op jit(solution)/shard_map/ppermute | solution.py:329
  117.9 15.0 %collective-permute-start.17 = (bf16[128,512]{1,0:T(8,128)(2,1)S(1)}, bf16[128,512]{1,0:T(8,128)(2,1)S(1)}, u32[]{:S(2)}, u32[]{:S(2)}) collective-permute-start(bf16[128,512]{1,0:T(8,128)(2,1)S(1)} %get-tuple-element.113), channel_id=1, source_target_pairs={{0,8},{4,12},{8,0},{12,4},{16,24},{20,28},{24,16},{28,20},{1,9},{5... | collective-permute-start | bytes 393224 | tf_op jit(solution)/shard_map/ppermute | solution.py:329
  127.0 15.8 %collective-permute-start.23 = (bf16[128,1024]{1,0:T(8,128)(2,1)}, bf16[128,1024]{1,0:T(8,128)(2,1)S(1)}, u32[]{:S(2)}, u32[]{:S(2)}) collective-permute-start(bf16[128,1024]{1,0:T(8,128)(2,1)} %get-tuple-element.83.refs_0_), channel_id=1, source_target_pairs={{0,4},{4,0},{8,12},{12,8},{16,20},{20,16},{24,28},{28,24},{1,5},{5... | collective-permute-start | bytes 786440 | tf_op jit(solution)/shard_map/ppermute | solution.py:329
  128.6 22.1 %collective-permute-start.20 = (bf16[128,1024]{1,0:T(8,128)(2,1)}, bf16[128,1024]{1,0:T(8,128)(2,1)S(1)}, u32[]{:S(2)}, u32[]{:S(2)}) collective-permute-start(bf16[128,1024]{1,0:T(8,128)(2,1)} %get-tuple-element.83.refs_0_), channel_id=1, source_target_pairs={{0,24},{4,28},{8,16},{12,20},{16,8},{20,12},{24,0},{28,4},{1,25},{... | collective-permute-start | bytes 786440 | tf_op jit(solution)/shard_map/ppermute | solution.py:329
  130.9 23.8 %collective-permute-start.19 = (bf16[128,1024]{1,0:T(8,128)(2,1)}, bf16[128,1024]{1,0:T(8,128)(2,1)S(1)}, u32[]{:S(2)}, u32[]{:S(2)}) collective-permute-start(bf16[128,1024]{1,0:T(8,128)(2,1)} %get-tuple-element.83.refs_0_), channel_id=1, source_target_pairs={{0,16},{4,20},{8,24},{12,28},{16,0},{20,4},{24,8},{28,12},{1,17},{... | collective-permute-start | bytes 786440 | tf_op jit(solution)/shard_map/ppermute | solution.py:329
  132.0 22.7 %collective-permute-start.18 = (bf16[128,1024]{1,0:T(8,128)(2,1)}, bf16[128,1024]{1,0:T(8,128)(2,1)S(1)}, u32[]{:S(2)}, u32[]{:S(2)}) collective-permute-start(bf16[128,1024]{1,0:T(8,128)(2,1)} %get-tuple-element.83.refs_0_), channel_id=1, source_target_pairs={{0,8},{4,12},{8,0},{12,4},{16,24},{20,28},{24,16},{28,20},{1,9},{5... | collective-permute-start | bytes 786440 | tf_op jit(solution)/shard_map/ppermute | solution.py:329
  154.9 27.5 %collective-permute-start.21 = (bf16[384,1024]{1,0:T(8,128)(2,1)S(1)}, bf16[384,1024]{1,0:T(8,128)(2,1)S(1)}, u32[]{:S(2)}, u32[]{:S(2)}) collective-permute-start(bf16[384,1024]{1,0:T(8,128)(2,1)S(1)} %pad_maximum_fusion), channel_id=1, source_target_pairs={{0,4},{4,0},{8,12},{12,8},{16,20},{20,16},{24,28},{28,24},{1,5},{5... | collective-permute-start | bytes 2359304 | tf_op jit(solution)/shard_map/ppermute | solution.py:329
  155.5 27.0 %collective-permute-start.25 = (bf16[384,1024]{1,0:T(8,128)(2,1)S(1)}, bf16[384,1024]{1,0:T(8,128)(2,1)S(1)}, u32[]{:S(2)}, u32[]{:S(2)}) collective-permute-start(bf16[384,1024]{1,0:T(8,128)(2,1)S(1)} %copy-done.22), channel_id=1, source_target_pairs={{0,2},{1,3},{2,0},{3,1},{4,6},{5,7},{6,4},{7,5},{8,10},{9,11},{10,... | collective-permute-start | bytes 2359304 | tf_op jit(solution)/shard_map/ppermute | solution.py:332
  159.7 21.7 %collective-permute-start.29 = (bf16[128,1024]{1,0:T(8,128)(2,1)S(1)}, bf16[128,1024]{1,0:T(8,128)(2,1)S(1)}, u32[]{:S(2)}, u32[]{:S(2)}) collective-permute-start(bf16[128,1024]{1,0:T(8,128)(2,1)S(1)} %fusion.3.refs_0_), channel_id=1, source_target_pairs={{0,16},{4,20},{8,24},{12,28},{16,0},{20,4},{24,8},{28,12},{1,17},{... | collective-permute-start | bytes 786440 | tf_op jit(solution)/shard_map/ppermute | solution.py:329
  159.7 21.7 %collective-permute-start.27 = (bf16[128,1024]{1,0:T(8,128)(2,1)S(1)}, bf16[128,1024]{1,0:T(8,128)(2,1)S(1)}, u32[]{:S(2)}, u32[]{:S(2)}) collective-permute-start(bf16[128,1024]{1,0:T(8,128)(2,1)S(1)} %fusion.3.refs_0_), channel_id=1, source_target_pairs={{0,8},{4,12},{8,0},{12,4},{16,24},{20,28},{24,16},{28,20},{1,9},{5... | collective-permute-start | bytes 786440 | tf_op jit(solution)/shard_map/ppermute | solution.py:329
  182.5 19.7 %collective-permute-start.28 = (bf16[384,1024]{1,0:T(8,128)(2,1)}, bf16[384,1024]{1,0:T(8,128)(2,1)}, u32[]{:S(2)}, u32[]{:S(2)}) collective-permute-start(bf16[384,1024]{1,0:T(8,128)(2,1)} %get-tuple-element.103), channel_id=1, source_target_pairs={{0,3},{1,2},{2,1},{3,0},{4,7},{5,6},{6,5},{7,4},{8,11},{9,10},{10,... | collective-permute-start | bytes 2359304 | tf_op jit(solution)/shard_map/ppermute | solution.py:332
  183.5 21.8 %collective-permute-start.32 = (bf16[384,1024]{1,0:T(8,128)(2,1)}, bf16[384,1024]{1,0:T(8,128)(2,1)S(1)}, u32[]{:S(2)}, u32[]{:S(2)}) collective-permute-start(bf16[384,1024]{1,0:T(8,128)(2,1)} %pad_maximum_fusion.1), channel_id=1, source_target_pairs={{0,4},{4,0},{8,12},{12,8},{16,20},{20,16},{24,28},{28,24},{1,5},{5... | collective-permute-start | bytes 2359304 | tf_op jit(solution)/shard_map/ppermute | solution.py:329
  (32 other events, 341.9 us)

commit v10 on v9

--- a/solution.py
+++ b/solution.py
@@ -237,7 +237,7 @@
 def weights_call(columns, parts):
     rows, depth = columns.shape
     cols = parts[0][0].shape[1]
-    tile = min(cols, 512)
+    tile = min(cols, 1024)
     return pl.pallas_call(
         weights_kernel,
         grid=(cols // tile,),
@@ -322,7 +322,9 @@
     tokens = query.shape[1]
     me = lax.axis_index("dp")
     lane = lax.axis_index("seq")
-    quad, low, side = me // 4, me // 2 % 2, me % 2
+    line, side = me // 2, me % 2
+    top = lines // 2
+    low, base = line // top, line % top
     core = lane % 2
 
     def over_dp(x, step):
@@ -335,10 +337,9 @@
         return lax.dynamic_slice(x, (0, index * width), (x.shape[0], width))
 
     pieces = wide // half
-    quads = lines // 2
-    scalars = [low, 1 - low, quad * 2 + core, quad * 2 + 1 - core]
-    scalars += [(quad ^ (s // 2)) * 2 + core for s in range(2, lines)]
-    scalars += [(quad * 2 + core) * pieces + p for p in range(pieces)]
+    scalars = [low, 1 - low, base + core * top, base + (1 - core) * top]
+    scalars += [(line ^ s) % top + core * top for s in range(1, lines) if s != top]
+    scalars += [(base + core * top) * pieces + p for p in range(pieces)]
     place = jnp.stack(scalars).astype(jnp.int32)
     near_at = lines + 2
     near_given, kept, value_given, mine_first, sibling_first, *given = pack_call(
@@ -354,9 +355,10 @@
         + [(2, 0, (near_at + p,), LIVE, half, 0, rows + p * LIVE, 0) for p in range(pieces)]
         + [(2, 0, (2 + s,), LIVE, wide, 3 + s, 0, 0) for s in range(lines)],
     )
-    near = over_dp(near_given, 2)
+    near = over_dp(near_given, 2 * top)
     beside = over_dp(kept, 1)
-    arrived = [over_dp(x, 2 * s) for s, x in enumerate(given, 2)]
+    direct = [s for s in range(1, lines) if s != top]
+    arrived = [over_dp(x, 2 * s) for s, x in zip(direct, given)]
 
     lanes = jnp.stack([lane ^ s for s in range(n_seq)]).astype(jnp.int32)
     packed = blocks_call(after(lanes, kept), query[0], out_grad[0])
@@ -365,6 +367,7 @@
     for s in range(2, n_seq):
         moved[s] = over_seq(after(packed[s], *previous), s)
         previous = (moved[s],)
+    previous = moved[2 : n_seq // 2 + 1]
     moved[1] = over_seq(after(packed[1], beside), 1)
 
     key_near, shared, shared_given = pack_call(
@@ -373,18 +376,18 @@
         [(rows, half)] + [((lines - 1) * LIVE, wide)] * 2,
         [(0, 0, 0, rows, half, 0, 0, 0)]
         + [
-            (0, rows + p * LIVE, 0, LIVE, half, out, 0, p * half)
+            (0, rows + p * LIVE, 0, LIVE, half, out, (top - 1) * LIVE, p * half)
             for p in range(pieces)
             for out in (1, 2)
         ]
         + [
-            (s - 1, 0, 0, LIVE, wide, out, (s - 1) * LIVE, 0)
-            for s in range(2, lines)
+            (at, 0, 0, LIVE, wide, out, (s - 1) * LIVE, 0)
+            for at, s in enumerate(direct, 1)
             for out in (1, 2)
         ],
     )
     key_far = over_dp(key_near, 1)
-    value_near = over_dp(after(value_given, near, *arrived), 2)
+    value_near = over_dp(after(value_given, near, *arrived), 2 * top)
     value_far = over_dp(value_near, 1)
     sibling = over_seq(shared_given, 1)
     key_quad = ((kept, rows, 0), (beside, rows, 0), (key_near, rows, 0), (key_far, rows, 0))
@@ -392,8 +395,11 @@
 
     places = jnp.stack([core ^ low, 1 - (core ^ low), side, 1 - side]).astype(jnp.int32)
 
+    bits = lines.bit_length() - 1
+    kept_videos = sorted(range(0, lines, 2), key=lambda s: [s >> k & 1 for k in range(1, bits)])
+
     def product(places, weights, other):
-        chosen = [s for s in range(lines) if bool(s & 2) == other]
+        chosen = [s | 1 for s in kept_videos] if other else kept_videos
         return product_call(
             places,
             [(shared, LIVE, s - 1) if s else (mine_first, LIVE, 0) for s in chosen],
@@ -402,8 +408,8 @@
         )
 
     def reduced(total):
-        step = 8
-        while step < n_dp:
+        step = 4
+        while step < 2 * top:
             count = total.shape[0] // 2
             total = total[:count] + over_dp(total[count:], step)
             step *= 2
@@ -423,46 +429,48 @@
 
     steps = [1 << k for k in reversed(range(n_seq.bit_length() - 1))]
     gain = lax.dynamic_slice(key_gain, (lane * cols,), (cols,)).reshape(1, cols)
-    own_columns, other_given = pick_call(places, mine_first, shared, sibling_first, sibling, rows)
+    own_columns, other_given = pick_call(after(places, *previous[:1]), mine_first, shared, sibling_first, sibling, rows)
     key_product = product(after(places, own_columns), key_quad, True)
-    key_sent = over_dp(key_product, 4)
+    key_sent = over_dp(key_product, 2)
     later = after(places, key_product)
     other_columns = over_dp(after(other_given, key_product), 1)
     columns = jnp.concatenate([own_columns, other_columns], axis=0).T
     value_product = product(later, value_quad, True)
     value_rest_product = product(later, value_quad, False)
     key_sent = after(key_sent, value_product, value_rest_product, columns, gain)
-    value_sent = over_dp(after(value_product, key_sent), 4)
+    value_sent = over_dp(after(value_product, key_sent), 2)
     key_total = reduced(product(later, key_quad, False) + key_sent)
-    raw = joined(key_total[:LIVE], over_dp(key_total[LIVE:], 2))
+    raw = joined(key_total[:LIVE], over_dp(key_total[LIVE:], 2 * top))
     raw_wide = raw.astype(jnp.float32)
     squares = seq_sum(jnp.sum(raw_wide * raw_wide, axis=-1, keepdims=True))
     inv_rms = lax.rsqrt(squares / hid + 1e-06)
     value_total = reduced(value_rest_product + after(value_sent, inv_rms))
-    value_other = over_dp(value_total[LIVE:], 2)
+    value_own, value_sent = value_total[:LIVE], value_total[LIVE:]
+    value_other = over_dp(value_sent, 2 * top)
     attends, keys, value_grad = attend_call(
-        lengths, after(raw, columns, value_total), inv_rms, gain, moved, tokens
-    )
-
-    values = joined(value_total[:LIVE], after(value_other, value_grad))
+        lengths, after(raw, columns, value_own, value_sent), inv_rms, gain, moved, tokens
+    )
+
+    values = joined(value_own, after(value_other, value_grad))
 
     value_near_parts = [over_dp(value_grad, 2 * s) for s in range(1, lines)]
-    value_first = over_dp(value_grad, 1)
     scores, scaled, inner = gradient_call(raw, values, gain, moved, attends, tokens)
     outs = query_call(keys, scores)
-    inner = jnp.sum(after(inner, value_first), axis=-1, keepdims=True)
+    inner = jnp.sum(inner, axis=-1, keepdims=True)
     for step in steps[:-1]:
         inner = inner + over_seq(inner, step)
-    far_sum = after(inner, *value_near_parts)
+    far_sum = after(inner, value_near_parts[-1])
     inner_mean = (far_sum + over_seq(far_sum, 1)) / hid
     raw_grad = (inv_rms * scaled - raw_wide * inv_rms**3 * inner_mean).astype(jnp.bfloat16)
-    value_rest = over_dp(jnp.concatenate(value_near_parts, axis=0), 1)
+    value_parts = lax.optimization_barrier((value_grad, *value_near_parts, inner))[:-1]
+    value_rest = over_dp(jnp.concatenate(value_parts, axis=0), 1)
+    raw_grad = after(raw_grad, *value_near_parts)
     key_near_parts = [over_dp(raw_grad, 2 * s) for s in range(1, lines)]
     placed = [outs[0]] + [None] * (n_seq - 1)
     previous = (inner,)
     for s in range(2, n_seq):
         placed[s] = over_seq(after(outs[s], *previous), s)
-        previous = (placed[s], key_near_parts[0])
+        previous = (placed[s], key_near_parts[-1])
     placed[1] = over_seq(after(outs[1], value_rest), 1)
     key_first = over_dp(raw_grad, 1)
     key_rest = over_dp(after(jnp.concatenate(key_near_parts, axis=0), key_first), 1)
@@ -473,8 +481,7 @@
     )
     value_parts = (
         [(x, LIVE, 0) for x in (value_grad, *value_near_parts)]
-        + [(value_first, LIVE, 0)]
-        + [(value_rest, LIVE, s) for s in range(lines - 1)]
+        + [(value_rest, LIVE, s) for s in range(lines)]
     )
     value_weight_grad = weights_call(after(columns, key_first), value_parts)
     (query_grad,) = pack_call(

time: 211 us -> 237 us (1.12); the launches traced: 210 us -> 233 us
  waiting for transfers between devices: 93.9 us -> 112 us
  starting transfers between devices: 36.4 us -> 40.5 us
    ppermute x22 -> x21, waiting for transfers between devices: 77.6 us -> 89.3 us  [over_dp(): return lax.ppermute(x, 'dp', [(a, a ^ step) for a in range(n_dp)])]
    ppermute x11, waiting for transfers between devices: 16.2 us -> 22.8 us  [over_seq(): return lax.ppermute(x, 'seq', [(a, a ^ step) for a in range(n_seq)])]
    ppermute x22 -> x21, starting transfers between devices: 27.3 us -> 32.9 us  [over_dp(): return lax.ppermute(x, 'dp', [(a, a ^ step) for a in range(n_dp)])]
  transfers between devices with their start and end apart: 33 -> 32, of which waited for: 13 -> 14; matrix products, arithmetic and copies ran while one was open for 5% -> 5% of each run, Pallas kernels for 26% -> 24%
where the time goes in v10:
time: 237 us; the launch traced here: 233 us
  waiting for transfers between devices  112 us (47%)
  Pallas kernels  64.2 us (27%)
  starting transfers between devices  40.5 us (17%)
  other arithmetic  8.14 us (3%)
  local copies, waits for them, and re-layouts  6.2 us (3%)
    ppermute x21, waiting for transfers between devices, over_dp(): return lax.ppermute(x, 'dp', [(a, a ^ step) for a in range(n_dp)])  89.3 us
    ppermute x21, starting transfers between devices, over_dp(): return lax.ppermute(x, 'dp', [(a, a ^ step) for a in range(n_dp)])  32.9 us
    ppermute x11, waiting for transfers between devices, over_seq(): return lax.ppermute(x, 'seq', [(a, a ^ step) for a in range(n_seq)])  22.8 us
    pallas_call x4, Pallas kernels, product_call(): pl.pallas_call(functools.partial(product_kernel, videos), grid=(1,), in_s...  13.5 us
    pallas_call x3, Pallas kernels, pack_call(): pl.pallas_call(functools.partial(pack_kernel, moves, len(arrays)), grid=(...  10.1 us
    pallas_call x1, Pallas kernels, gradient_call(): pl.pallas_call(functools.partial(gradient_kernel, parts), grid=(steps,),...  9.07 us
    pallas_call x1, Pallas kernels, attend_call(): pl.pallas_call(functools.partial(attend_kernel, parts), grid=(steps,), in...  8.96 us
    pallas_call x2, Pallas kernels, weights_call(): pl.pallas_call(weights_kernel, grid=(cols // tile,), in_specs=[pl.BlockSp...  8.78 us
  transfers between devices with their start and end apart: 32, of which 14 were waited for; matrix products, arithmetic and copies ran while one was open for 5% of the time, Pallas kernels for 24%

profile of v10, /device:TPU:0, one launch (start us, length us, event | category | flops | bytes accessed | tf_op | source)
XLA Modules:
  0.0 232.8 jit_solution(11754748016852793112)
XLA Ops:
  1.3 4.3 %shard_map.94 = (bf16[768,512]{1,0:T(8,128)(2,1)}, bf16[1024,512]{1,0:T(8,128)(2,1)}, bf16[512,512]{1,0:T(8,128)(2,1)}, bf16[128,1024]{1,0:T(8,128)(2,1)}, bf16[...) custom-call(s32[8]{0:T(128)} %stack.75.place_ref, bf16[512,1024]{1,0:T(8,128)(2,1)} %refs_0_.1, ...), custom_call_target="tpu_custom_call" | custom-call | flops 1000 | bytes 1000 | tf_op jit(solution)/shard_map/pallas_call | solution.py:305
  5.6 4.0 %collective-permute-start.1 = (bf16[768,512]{1,0:T(8,128)(2,1)}, bf16[768,512]{1,0:T(8,128)(2,1)S(1)}, u32[]{:S(2)}, u32[]{:S(2)}) collective-permute-start(bf16[768,512]{1,0:T(8,128)(2,1)} %get-tuple-element.65), channel_id=1, source_target_pairs={{0,16},{4,20},{8,24},{12,28},{16,0},{20,4},{24,8},{28,12},{1,17},{... | collective-permute-start | bytes 2359304 | tf_op jit(solution)/shard_map/ppermute | solution.py:331
  10.2 5.9 %shard_map.95 = (bf16[2,384,1024]{2,1,0:T(8,128)(2,1)}, bf16[2,384,1024]{2,1,0:T(8,128)(2,1)}, bf16[2,384,1024]{2,1,0:T(8,128)(2,1)}, bf16[2,384,1024]{2,1,0:T(8,128)(2,1)}) custom-call(s32[4]{0:T(128)} %pad_add_fusion.lanes_ref.place_ref, bf16[384,4096]{1,0:T(8,128)(2,1)} %bitcast.25, bf16[384,4096]{1,0:T(8,128)(2,1)} %bitcast.26), custom_call_target="tpu_custom_call" | custom-call | flops 1000 | bytes 12582912 | tf_op jit(solution)/shard_map/pallas_call | solution.py:274
  21.0 12.6 %collective-permute-done.2.refs_1_ = bf16[128,1024]{1,0:T(8,128)(2,1)S(1)} collective-permute-done((bf16[128,1024]{1,0:T(8,128)(2,1)}, bf16[128,1024]{1,0:T(8,128)(2,1)S(1)}, u32[]{:S(2)}, u32[]{:S(2)}) %collective-permute-start.2) | collective-permute-done | bytes 262176 | tf_op jit(solution)/shard_map/ppermute | solution.py:331
  33.6 6.3 %collective-permute-done.3.refs_2_ = bf16[128,1024]{1,0:T(8,128)(2,1)S(1)} collective-permute-done((bf16[128,1024]{1,0:T(8,128)(2,1)}, bf16[128,1024]{1,0:T(8,128)(2,1)S(1)}, u32[]{:S(2)}, u32[]{:S(2)}) %collective-permute-start.3) | collective-permute-done | bytes 262176 | tf_op jit(solution)/shard_map/ppermute | solution.py:331
  39.8 10.8 %collective-permute-done.1.refs_0_ = bf16[768,512]{1,0:T(8,128)(2,1)S(1)} collective-permute-done((bf16[768,512]{1,0:T(8,128)(2,1)}, bf16[768,512]{1,0:T(8,128)(2,1)S(1)}, u32[]{:S(2)}, u32[]{:S(2)}) %collective-permute-start.1) | collective-permute-done | bytes 786464 | tf_op jit(solution)/shard_map/ppermute | solution.py:331
  54.3 8.2 %collective-permute-start.8 = (bf16[512,512]{1,0:T(8,128)(2,1)}, bf16[512,512]{1,0:T(8,128)(2,1)}, u32[]{:S(2)}, u32[]{:S(2)}) collective-permute-start(bf16[512,512]{1,0:T(8,128)(2,1)} %get-tuple-element.76), channel_id=1, source_target_pairs={{0,16},{4,20},{8,24},{12,28},{16,0},{20,4},{24,8},{28,12},{1,17},{... | collective-permute-start | bytes 1572872 | tf_op jit(solution)/shard_map/ppermute | solution.py:331
  64.6 22.0 %collective-permute-done.8.refs_6_ = bf16[512,512]{1,0:T(8,128)(2,1)} collective-permute-done((bf16[512,512]{1,0:T(8,128)(2,1)}, bf16[512,512]{1,0:T(8,128)(2,1)}, u32[]{:S(2)}, u32[]{:S(2)}) %collective-permute-start.8) | collective-permute-done | bytes 524320 | tf_op jit(solution)/shard_map/ppermute | solution.py:331
  91.7 3.4 %shard_map.98 = f32[256,512]{1,0:T(8,128)} custom-call(s32[4]{0:T(128)} %pad_add_fusion.1.place_ref, bf16[384,1024]{1,0:T(8,128)(2,1)} %get-tuple-element.68.mine_ref.refs_0_.refs_1_, bf16[384,1024]{1,0:T(8,128)(2,1)} %get-tuple-element.68.mine_ref.refs_0_.refs_1_, bf16[384,1024]{1,0:T(8,128)(2,1)} %copy-done, bf16[384,1024]{1,0:T(8,128)(2,1)} %copy-done, ...), custom_call_target="tpu_custom_call" | custom-call | flops 1000 | bytes 1000 | tf_op jit(solution)/shard_map/pallas_call | solution.py:218
  99.6 3.4 %shard_map.99 = f32[256,512]{1,0:T(8,128)} custom-call(s32[4]{0:T(128)} %pad_add_fusion.1.place_ref, bf16[128,1024]{1,0:T(8,128)(2,1)} %get-tuple-element.64.first_ref.refs_0_, bf16[384,1024]{1,0:T(8,128)(2,1)} %get-tuple-element.68.mine_ref.refs_0_.refs_1_, bf16[128,1024]{1,0:T(8,128)(2,1)} %get-tuple-element.69.sibling_first_ref.refs_2_, ...), custom_call_target="tpu_custom_call" | custom-call | flops 1000 | bytes 1000 | tf_op jit(solution)/shard_map/pallas_call | solution.py:218
  103.2 3.3 %shard_map.101 = f32[256,512]{1,0:T(8,128)} custom-call(s32[4]{0:T(128)} %pad_add_fusion.1.place_ref, bf16[128,1024]{1,0:T(8,128)(2,1)} %get-tuple-element.64.first_ref.refs_0_, bf16[384,1024]{1,0:T(8,128)(2,1)} %get-tuple-element.68.mine_ref.refs_0_.refs_1_, bf16[128,1024]{1,0:T(8,128)(2,1)} %get-tuple-element.69.sibling_first_ref.refs_2_, ...), custom_call_target="tpu_custom_call" | custom-call | flops 1000 | bytes 1000 | tf_op jit(solution)/shard_map/pallas_call | solution.py:218
  106.5 3.4 %shard_map.100 = f32[256,512]{1,0:T(8,128)} custom-call(s32[4]{0:T(128)} %pad_add_fusion.1.place_ref, bf16[384,1024]{1,0:T(8,128)(2,1)} %get-tuple-element.68.mine_ref.refs_0_.refs_1_, bf16[384,1024]{1,0:T(8,128)(2,1)} %get-tuple-element.68.mine_ref.refs_0_.refs_1_, bf16[384,1024]{1,0:T(8,128)(2,1)} %copy-done, bf16[384,1024]{1,0:T(8,128)(2,1)} %copy-done, ...), custom_call_target="tpu_custom_call" | custom-call | flops 1000 | bytes 1000 | tf_op jit(solution)/shard_map/pallas_call | solution.py:218
  115.4 13.0 %collective-permute-done.11 = bf16[128,512]{1,0:T(8,128)(2,1)S(1)} collective-permute-done((bf16[128,512]{1,0:T(8,128)(2,1)S(1)}, bf16[128,512]{1,0:T(8,128)(2,1)S(1)}, u32[]{:S(2)}, u32[]{:S(2)}) %collective-permute-start.11) | collective-permute-done | bytes 131104 | tf_op jit(solution)/shard_map/ppermute | solution.py:331
  130.0 6.2 %collective-permute-done.13 = f32[128,1]{1,0:T(8,128)S(1)} collective-permute-done((f32[128,1]{1,0:T(8,128)S(1)}, f32[128,1]{1,0:T(8,128)S(1)}, u32[]{:S(2)}, u32[]{:S(2)}) %collective-permute-start.13) | collective-permute-done | bytes 544 | tf_op jit(solution)/shard_map/ppermute | solution.py:334
  139.5 9.0 %shard_map.102 = (f32[8,128,384]{2,1,0:T(8,128)}, f32[8,128,384]{2,1,0:T(8,128)}, f32[8,128,384]{2,1,0:T(8,128)}, f32[8,128,384]{2,1,0:T(8,128)}, bf16[128,1024]{1,0:T(8,128)(2,1)}, /*index=5*/bf16[128,1024]{1,0:T(8,128)(2,1)}) custom-call(s32[1]{0:T(128)S(6)} %copy.22.length_ref, bf16[128,1024]{1,0:T(8,128)(2,1)} %get-tuple-element.82.raw_ref, ...), custom_call_target="tpu_custom_call" | custom-call | flops 3221225472 | bytes 25165824 | tf_op jit(solution)/shard_map/pallas_call | solution.py:99
  148.5 3.3 %collective-permute-start.20 = (bf16[128,1024]{1,0:T(8,128)(2,1)}, bf16[128,1024]{1,0:T(8,128)(2,1)S(1)}, u32[]{:S(2)}, u32[]{:S(2)}) collective-permute-start(bf16[128,1024]{1,0:T(8,128)(2,1)} %get-tuple-element.102.refs_0_), channel_id=1, source_target_pairs={{0,24},{4,28},{8,16},{12,20},{16,8},{20,12},{24,0},{28,4},{1,25},{... | collective-permute-start | bytes 786440 | tf_op jit(solution)/shard_map/ppermute | solution.py:331
  153.7 9.1 %shard_map.103 = (bf16[8,128,384]{2,1,0:T(8,128)(2,1)}, bf16[8,128,384]{2,1,0:T(8,128)(2,1)}, bf16[8,128,384]{2,1,0:T(8,128)(2,1)}, bf16[8,128,384]{2,1,0:T(8,12...) custom-call(bf16[128,1024]{1,0:T(8,128)(2,1)} %get-tuple-element.82.raw_ref, ...), custom_call_target="tpu_custom_call" | custom-call | flops 3221225472 | bytes 25165824 | tf_op jit(solution)/shard_map/pallas_call | solution.py:128
  168.2 6.2 %collective-permute-done.19.refs_2_ = bf16[128,1024]{1,0:T(8,128)(2,1)S(1)} collective-permute-done((bf16[128,1024]{1,0:T(8,128)(2,1)}, bf16[128,1024]{1,0:T(8,128)(2,1)S(1)}, u32[]{:S(2)}, u32[]{:S(2)}) %collective-permute-start.19) | collective-permute-done | bytes 262176 | tf_op jit(solution)/shard_map/ppermute | solution.py:331
  176.1 5.2 %shard_map.104 = (bf16[384,1024]{1,0:T(8,128)(2,1)}, bf16[384,1024]{1,0:T(8,128)(2,1)}, bf16[384,1024]{1,0:T(8,128)(2,1)}, bf16[384,1024]{1,0:T(8,128)(2,1)}) custom-call(bf16[128,1024]{1,0:T(8,128)(2,1)} %get-tuple-element.88.keys_ref, bf16[8,128,384]{2,1,0:T(8,128)(2,1)} %get-tuple-element.95.refs_0_, bf16[8,128,384]{2,1,0:T(8,128)(2,1)} %get-tuple-element.96.refs_1_, ...), custom_call_target="tpu_custom_call" | custom-call | flops 1610612736 | bytes 12582912 | tf_op jit(solution)/shard_map/pallas_call | solution.py:152
  187.6 10.5 %collective-permute-done.29.refs_2_ = bf16[128,1024]{1,0:T(8,128)(2,1)S(1)} collective-permute-done((bf16[128,1024]{1,0:T(8,128)(2,1)S(1)}, bf16[128,1024]{1,0:T(8,128)(2,1)S(1)}, u32[]{:S(2)}, u32[]{:S(2)}) %collective-permute-start.29) | collective-permute-done | bytes 262176 | tf_op jit(solution)/shard_map/ppermute | solution.py:331
  198.6 4.9 %collective-permute-done.28.refs_1_ = bf16[128,1024]{1,0:T(8,128)(2,1)S(1)} collective-permute-done((bf16[128,1024]{1,0:T(8,128)(2,1)S(1)}, bf16[128,1024]{1,0:T(8,128)(2,1)S(1)}, u32[]{:S(2)}, u32[]{:S(2)}) %collective-permute-start.28) | collective-permute-done | bytes 262176 | tf_op jit(solution)/shard_map/ppermute | solution.py:331
  206.7 4.4 %shard_map.107 = f32[512,1024]{1,0:T(8,128)} custom-call(bf16[512,1024]{1,0:T(8,128)(2,1)} %maximum_bitcast_fusion.columns_ref, bf16[128,1024]{1,0:T(8,128)(2,1)} %get-tuple-element.102.refs_0_, bf16[128,1024]{1,0:T(8,128)(2,1)} %copy-done.11, bf16[128,1024]{1,0:T(8,128)(2,1)} %copy-done.10, bf16[128,1024]{1,0:T(8,128)(2,1)} %copy-done.9, ...), custom_call_target="tpu_custom_call" | custom-call | flops 1073741824 | bytes 5242880 | tf_op jit(solution)/shard_map/pallas_call | solution.py:241
  211.1 13.2 %collective-permute-done.27.refs_3_ = bf16[384,1024]{1,0:T(8,128)(2,1)} collective-permute-done((bf16[384,1024]{1,0:T(8,128)(2,1)}, bf16[384,1024]{1,0:T(8,128)(2,1)}, u32[]{:S(2)}, u32[]{:S(2)}) %collective-permute-start.27) | collective-permute-done | bytes 786464 | tf_op jit(solution)/shard_map/ppermute | solution.py:334
  228.4 4.4 %shard_map.106 = f32[512,1024]{1,0:T(8,128)} custom-call(bf16[512,1024]{1,0:T(8,128)(2,1)} %maximum_bitcast_fusion.columns_ref, bf16[128,1024]{1,0:T(8,128)(2,1)} %copy-done.12, bf16[128,1024]{1,0:T(8,128)(2,1)} %copy-done.14, bf16[128,1024]{1,0:T(8,128)(2,1)} %copy-done.13, bf16[128,1024]{1,0:T(8,128)(2,1)} %copy-done.15, bf16[128,1024]{1,0:T(8,128)(2,1)} %copy-done.24, ...), custom_call_target="tpu_custom_call" | custom-call | flops 1073741824 | bytes 5242880 | tf_op jit(solution)/shard_map/pallas_call | solution.py:241
  (127 shorter events, 54.2 us)
Async XLA Ops:
  5.6 45.1 %collective-permute-start.1 = (bf16[768,512]{1,0:T(8,128)(2,1)}, bf16[768,512]{1,0:T(8,128)(2,1)S(1)}, u32[]{:S(2)}, u32[]{:S(2)}) collective-permute-start(bf16[768,512]{1,0:T(8,128)(2,1)} %get-tuple-element.65), channel_id=1, source_target_pairs={{0,16},{4,20},{8,24},{12,28},{16,0},{20,4},{24,8},{28,12},{1,17},{... | collective-permute-start | bytes 2359304 | tf_op jit(solution)/shard_map/ppermute | solution.py:331
  16.2 71.9 %collective-permute-start = (bf16[2,384,1024]{2,1,0:T(8,128)(2,1)}, bf16[2,384,1024]{2,1,0:T(8,128)(2,1)S(1)}, u32[]{:S(2)}, u32[]{:S(2)}) collective-permute-start(bf16[2,384,1024]{2,1,0:T(8,128)(2,1)} %get-tuple-element.62), channel_id=1, source_target_pairs={{0,2},{1,3},{2,0},{3,1},{4,6},{5,7},{6,4},{7,5},{8,10},{9,11},{10,... | collective-permute-start | bytes 4718600 | tf_op jit(solution)/shard_map/ppermute | solution.py:334
  17.7 15.9 %collective-permute-start.2 = (bf16[128,1024]{1,0:T(8,128)(2,1)}, bf16[128,1024]{1,0:T(8,128)(2,1)S(1)}, u32[]{:S(2)}, u32[]{:S(2)}) collective-permute-start(bf16[128,1024]{1,0:T(8,128)(2,1)} %get-tuple-element.66), channel_id=1, source_target_pairs={{0,8},{4,12},{8,0},{12,4},{16,24},{20,28},{24,16},{28,20},{1,9},{5... | collective-permute-start | bytes 786440 | tf_op jit(solution)/shard_map/ppermute | solution.py:331
  19.3 20.6 %collective-permute-start.3 = (bf16[128,1024]{1,0:T(8,128)(2,1)}, bf16[128,1024]{1,0:T(8,128)(2,1)S(1)}, u32[]{:S(2)}, u32[]{:S(2)}) collective-permute-start(bf16[128,1024]{1,0:T(8,128)(2,1)} %get-tuple-element.67), channel_id=1, source_target_pairs={{0,24},{4,28},{8,16},{12,20},{16,8},{20,12},{24,0},{28,4},{1,25},{... | collective-permute-start | bytes 786440 | tf_op jit(solution)/shard_map/ppermute | solution.py:331
  19.5 72.2 %collective-permute-start.5 = (bf16[1024,512]{1,0:T(8,128)(2,1)S(1)}, bf16[1024,512]{1,0:T(8,128)(2,1)}, u32[]{:S(2)}, u32[]{:S(2)}) collective-permute-start(bf16[1024,512]{1,0:T(8,128)(2,1)S(1)} %copy-done.2), channel_id=1, source_target_pairs={{0,4},{4,0},{8,12},{12,8},{16,20},{20,16},{24,28},{28,24},{1,5},{5... | collective-permute-start | bytes 3145736 | tf_op jit(solution)/shard_map/ppermute | solution.py:331
  54.3 33.8 %collective-permute-start.4 = (bf16[384,1024]{1,0:T(8,128)(2,1)}, bf16[384,1024]{1,0:T(8,128)(2,1)S(1)}, u32[]{:S(2)}, u32[]{:S(2)}) collective-permute-start(bf16[384,1024]{1,0:T(8,128)(2,1)} %get-tuple-element.70), channel_id=1, source_target_pairs={{0,1},{1,0},{2,3},{3,2},{4,5},{5,4},{6,7},{7,6},{8,9},{9,8},{10,11... | collective-permute-start | bytes 2359304 | tf_op jit(solution)/shard_map/ppermute | solution.py:334
  54.3 32.3 %collective-permute-start.8 = (bf16[512,512]{1,0:T(8,128)(2,1)}, bf16[512,512]{1,0:T(8,128)(2,1)}, u32[]{:S(2)}, u32[]{:S(2)}) collective-permute-start(bf16[512,512]{1,0:T(8,128)(2,1)} %get-tuple-element.76), channel_id=1, source_target_pairs={{0,16},{4,20},{8,24},{12,28},{16,0},{20,4},{24,8},{28,12},{1,17},{... | collective-permute-start | bytes 1572872 | tf_op jit(solution)/shard_map/ppermute | solution.py:331
  62.4 29.3 %collective-permute-start.6 = (bf16[512,512]{1,0:T(8,128)(2,1)}, bf16[512,512]{1,0:T(8,128)(2,1)}, u32[]{:S(2)}, u32[]{:S(2)}) collective-permute-start(bf16[512,512]{1,0:T(8,128)(2,1)} %get-tuple-element.73.refs_6_), channel_id=1, source_target_pairs={{0,4},{4,0},{8,12},{12,8},{16,20},{20,16},{24,28},{28,24},{1,5},{5... | collective-permute-start | bytes 1572872 | tf_op jit(solution)/shard_map/ppermute | solution.py:331
  86.6 16.6 %collective-permute-start.9 = (bf16[512,512]{1,0:T(8,128)(2,1)}, bf16[512,512]{1,0:T(8,128)(2,1)}, u32[]{:S(2)}, u32[]{:S(2)}) collective-permute-start(bf16[512,512]{1,0:T(8,128)(2,1)} %collective-permute-done.8.refs_6_), channel_id=1, source_target_pairs={{0,4},{4,0},{8,12},{12,8},{16,20},{20,16},{24,28},{28,24},{1,5},{5... | collective-permute-start | bytes 1572872 | tf_op jit(solution)/shard_map/ppermute | solution.py:331
  96.2 15.7 %collective-permute-start.10 = (bf16[512,512]{0,1:T(8,128)(2,1)}, bf16[512,512]{0,1:T(8,128)(2,1)}, u32[]{:S(2)}, u32[]{:S(2)}) collective-permute-start(bf16[512,512]{0,1:T(8,128)(2,1)} %copy.16), channel_id=1, source_target_pairs={{0,4},{4,0},{8,12},{12,8},{16,20},{20,16},{24,28},{28,24},{1,5},{5... | collective-permute-start | bytes 1572872 | tf_op jit(solution)/shard_map/ppermute | solution.py:331
  96.7 17.4 %collective-permute-start.7 = (f32[256,512]{1,0:T(8,128)}, f32[256,512]{1,0:T(8,128)S(1)}, u32[]{:S(2)}, u32[]{:S(2)}) collective-permute-start(f32[256,512]{1,0:T(8,128)} %shard_map.98), channel_id=1, source_target_pairs={{0,8},{4,12},{8,0},{12,4},{16,24},{20,28},{24,16},{28,20},{1,9},{5... | collective-permute-start | bytes 1572872 | tf_op jit(solution)/shard_map/ppermute | solution.py:331
  97.9 41.6 %collective-permute-start.15 = (bf16[2,384,1024]{2,1,0:T(8,128)(2,1)}, bf16[2,384,1024]{2,1,0:T(8,128)(2,1)}, u32[]{:S(2)}, u32[]{:S(2)}) collective-permute-start(bf16[2,384,1024]{2,1,0:T(8,128)(2,1)} %get-tuple-element.85), channel_id=1, source_target_pairs={{0,1},{1,0},{2,3},{3,2},{4,5},{5,4},{6,7},{7,6},{8,9},{9,8},{10,11... | collective-permute-start | bytes 4718600 | tf_op jit(solution)/shard_map/ppermute | solution.py:334
  97.9 41.6 %collective-permute-start.16 = (bf16[2,384,1024]{2,1,0:T(8,128)(2,1)}, bf16[2,384,1024]{2,1,0:T(8,128)(2,1)}, u32[]{:S(2)}, u32[]{:S(2)}) collective-permute-start(bf16[2,384,1024]{2,1,0:T(8,128)(2,1)} %get-tuple-element.87), channel_id=1, source_target_pairs={{0,3},{1,2},{2,1},{3,0},{4,7},{5,6},{6,5},{7,4},{8,11},{9,10},{10,... | collective-permute-start | bytes 4718600 | tf_op jit(solution)/shard_map/ppermute | solution.py:334
  114.1 24.1 %collective-permute-start.12 = (f32[256,512]{1,0:T(8,128)S(1)}, f32[256,512]{1,0:T(8,128)S(1)}, u32[]{:S(2)}, u32[]{:S(2)}) collective-permute-start(f32[256,512]{1,0:T(8,128)S(1)} %copy-done.21), channel_id=1, source_target_pairs={{0,8},{4,12},{8,0},{12,4},{16,24},{20,28},{24,16},{28,20},{1,9},{5... | collective-permute-start | bytes 1572872 | tf_op jit(solution)/shard_map/ppermute | solution.py:331
  148.5 19.7 %collective-permute-start.20 = (bf16[128,1024]{1,0:T(8,128)(2,1)}, bf16[128,1024]{1,0:T(8,128)(2,1)S(1)}, u32[]{:S(2)}, u32[]{:S(2)}) collective-permute-start(bf16[128,1024]{1,0:T(8,128)(2,1)} %get-tuple-element.102.refs_0_), channel_id=1, source_target_pairs={{0,24},{4,28},{8,16},{12,20},{16,8},{20,12},{24,0},{28,4},{1,25},{... | collective-permute-start | bytes 786440 | tf_op jit(solution)/shard_map/ppermute | solution.py:331
  151.8 22.6 %collective-permute-start.19 = (bf16[128,1024]{1,0:T(8,128)(2,1)}, bf16[128,1024]{1,0:T(8,128)(2,1)S(1)}, u32[]{:S(2)}, u32[]{:S(2)}) collective-permute-start(bf16[128,1024]{1,0:T(8,128)(2,1)} %get-tuple-element.102.refs_0_), channel_id=1, source_target_pairs={{0,16},{4,20},{8,24},{12,28},{16,0},{20,4},{24,8},{28,12},{1,17},{... | collective-permute-start | bytes 786440 | tf_op jit(solution)/shard_map/ppermute | solution.py:331
  151.8 22.6 %collective-permute-start.18 = (bf16[128,1024]{1,0:T(8,128)(2,1)}, bf16[128,1024]{1,0:T(8,128)(2,1)S(1)}, u32[]{:S(2)}, u32[]{:S(2)}) collective-permute-start(bf16[128,1024]{1,0:T(8,128)(2,1)} %get-tuple-element.102.refs_0_), channel_id=1, source_target_pairs={{0,8},{4,12},{8,0},{12,4},{16,24},{20,28},{24,16},{28,20},{1,9},{5... | collective-permute-start | bytes 786440 | tf_op jit(solution)/shard_map/ppermute | solution.py:331
  174.5 30.0 %collective-permute-start.22 = (bf16[512,1024]{1,0:T(8,128)(2,1)S(1)}, bf16[512,1024]{1,0:T(8,128)(2,1)S(1)}, u32[]{:S(2)}, u32[]{:S(2)}) collective-permute-start(bf16[512,1024]{1,0:T(8,128)(2,1)S(1)} %pad_maximum_fusion), channel_id=1, source_target_pairs={{0,4},{4,0},{8,12},{12,8},{16,20},{20,16},{24,28},{28,24},{1,5},{5... | collective-permute-start | bytes 3145736 | tf_op jit(solution)/shard_map/ppermute | solution.py:331
  181.3 23.2 %collective-permute-start.24 = (bf16[384,1024]{1,0:T(8,128)(2,1)}, bf16[384,1024]{1,0:T(8,128)(2,1)S(1)}, u32[]{:S(2)}, u32[]{:S(2)}) collective-permute-start(bf16[384,1024]{1,0:T(8,128)(2,1)} %get-tuple-element.108), channel_id=1, source_target_pairs={{0,2},{1,3},{2,0},{3,1},{4,6},{5,7},{6,4},{7,5},{8,10},{9,11},{10,... | collective-permute-start | bytes 2359304 | tf_op jit(solution)/shard_map/ppermute | solution.py:334
  183.3 20.2 %collective-permute-start.28 = (bf16[128,1024]{1,0:T(8,128)(2,1)S(1)}, bf16[128,1024]{1,0:T(8,128)(2,1)S(1)}, u32[]{:S(2)}, u32[]{:S(2)}) collective-permute-start(bf16[128,1024]{1,0:T(8,128)(2,1)S(1)} %fusion.3.refs_0_), channel_id=1, source_target_pairs={{0,8},{4,12},{8,0},{12,4},{16,24},{20,28},{24,16},{28,20},{1,9},{5... | collective-permute-start | bytes 786440 | tf_op jit(solution)/shard_map/ppermute | solution.py:331
  185.8 17.7 %collective-permute-start.26 = (bf16[128,1024]{1,0:T(8,128)(2,1)S(1)}, bf16[128,1024]{1,0:T(8,128)(2,1)S(1)}, u32[]{:S(2)}, u32[]{:S(2)}) collective-permute-start(bf16[128,1024]{1,0:T(8,128)(2,1)S(1)} %fusion.3.refs_0_), channel_id=1, source_target_pairs={{0,24},{4,28},{8,16},{12,20},{16,8},{20,12},{24,0},{28,4},{1,25},{... | collective-permute-start | bytes 786440 | tf_op jit(solution)/shard_map/ppermute | solution.py:331
  204.5 19.8 %collective-permute-start.27 = (bf16[384,1024]{1,0:T(8,128)(2,1)}, bf16[384,1024]{1,0:T(8,128)(2,1)}, u32[]{:S(2)}, u32[]{:S(2)}) collective-permute-start(bf16[384,1024]{1,0:T(8,128)(2,1)} %get-tuple-element.113), channel_id=1, source_target_pairs={{0,3},{1,2},{2,1},{3,0},{4,7},{5,6},{6,5},{7,4},{8,11},{9,10},{10,... | collective-permute-start | bytes 2359304 | tf_op jit(solution)/shard_map/ppermute | solution.py:334
  204.5 19.8 %collective-permute-start.23 = (bf16[384,1024]{1,0:T(8,128)(2,1)}, bf16[384,1024]{1,0:T(8,128)(2,1)}, u32[]{:S(2)}, u32[]{:S(2)}) collective-permute-start(bf16[384,1024]{1,0:T(8,128)(2,1)} %get-tuple-element.106), channel_id=1, source_target_pairs={{0,1},{1,0},{2,3},{3,2},{4,5},{5,4},{6,7},{7,6},{8,9},{9,8},{10,11... | collective-permute-start | bytes 2359304 | tf_op jit(solution)/shard_map/ppermute | solution.py:334
  206.2 21.3 %collective-permute-start.31 = (bf16[384,1024]{1,0:T(8,128)(2,1)}, bf16[384,1024]{1,0:T(8,128)(2,1)S(1)}, u32[]{:S(2)}, u32[]{:S(2)}) collective-permute-start(bf16[384,1024]{1,0:T(8,128)(2,1)} %pad_maximum_fusion.1), channel_id=1, source_target_pairs={{0,4},{4,0},{8,12},{12,8},{16,20},{20,16},{24,28},{28,24},{1,5},{5... | collective-permute-start | bytes 2359304 | tf_op jit(solution)/shard_map/ppermute | solution.py:331
  (33 other events, 297.4 us)

commit v11 on v10

--- a/solution.py
+++ b/solution.py
@@ -80,7 +80,7 @@
 
 
 def specs(tokens, heads):
-    group = 2 - heads % 2
+    group = next(g for g in (4, 2, 1) if heads % g == 0)
     width = group * HD
     head = pl.BlockSpec((LIVE, width), lambda h: (0, h))
     block = pl.BlockSpec((tokens, width), lambda h: (0, h))
@@ -388,10 +388,8 @@
     )
     key_far = over_dp(key_near, 1)
     value_near = over_dp(after(value_given, near, *arrived), 2 * top)
-    value_far = over_dp(value_near, 1)
     sibling = over_seq(shared_given, 1)
     key_quad = ((kept, rows, 0), (beside, rows, 0), (key_near, rows, 0), (key_far, rows, 0))
-    value_quad = ((kept, rows, 1), (beside, rows, 1), (value_near, rows, 0), (value_far, rows, 0))
 
     places = jnp.stack([core ^ low, 1 - (core ^ low), side, 1 - side]).astype(jnp.int32)
 
@@ -433,38 +431,37 @@
     key_product = product(after(places, own_columns), key_quad, True)
     key_sent = over_dp(key_product, 2)
     later = after(places, key_product)
+    value_far = over_dp(after(value_near, key_product), 1)
+    value_quad = ((kept, rows, 1), (beside, rows, 1), (value_near, rows, 0), (value_far, rows, 0))
     other_columns = over_dp(after(other_given, key_product), 1)
     columns = jnp.concatenate([own_columns, other_columns], axis=0).T
     value_product = product(later, value_quad, True)
     value_rest_product = product(later, value_quad, False)
-    key_sent = after(key_sent, value_product, value_rest_product, columns, gain)
+    key_sent = after(key_sent, columns, gain)
     value_sent = over_dp(after(value_product, key_sent), 2)
     key_total = reduced(product(later, key_quad, False) + key_sent)
     raw = joined(key_total[:LIVE], over_dp(key_total[LIVE:], 2 * top))
     raw_wide = raw.astype(jnp.float32)
     squares = seq_sum(jnp.sum(raw_wide * raw_wide, axis=-1, keepdims=True))
     inv_rms = lax.rsqrt(squares / hid + 1e-06)
-    value_total = reduced(value_rest_product + after(value_sent, inv_rms))
-    value_own, value_sent = value_total[:LIVE], value_total[LIVE:]
-    value_other = over_dp(value_sent, 2 * top)
     attends, keys, value_grad = attend_call(
-        lengths, after(raw, columns, value_own, value_sent), inv_rms, gain, moved, tokens
-    )
-
-    values = joined(value_own, after(value_other, value_grad))
-
-    value_near_parts = [over_dp(value_grad, 2 * s) for s in range(1, lines)]
+        lengths, after(raw, columns, value_rest_product), inv_rms, gain, moved, tokens
+    )
+    value_total = reduced(value_rest_product + after(value_sent, value_grad))
+    values = joined(value_total[:LIVE], over_dp(value_total[LIVE:], 2 * top))
+
+    value_given = after(value_grad, values)
+    value_near_parts = [over_dp(value_given, 2 * s) for s in range(1, lines)]
     scores, scaled, inner = gradient_call(raw, values, gain, moved, attends, tokens)
     outs = query_call(keys, scores)
     inner = jnp.sum(inner, axis=-1, keepdims=True)
     for step in steps[:-1]:
         inner = inner + over_seq(inner, step)
-    far_sum = after(inner, value_near_parts[-1])
+    far_sum = after(inner, *value_near_parts)
     inner_mean = (far_sum + over_seq(far_sum, 1)) / hid
     raw_grad = (inv_rms * scaled - raw_wide * inv_rms**3 * inner_mean).astype(jnp.bfloat16)
-    value_parts = lax.optimization_barrier((value_grad, *value_near_parts, inner))[:-1]
+    value_parts = lax.optimization_barrier((value_grad, *value_near_parts, inner, outs[0]))[:-2]
     value_rest = over_dp(jnp.concatenate(value_parts, axis=0), 1)
-    raw_grad = after(raw_grad, *value_near_parts)
     key_near_parts = [over_dp(raw_grad, 2 * s) for s in range(1, lines)]
     placed = [outs[0]] + [None] * (n_seq - 1)
     previous = (inner,)

time: 237 us -> 228 us (0.962)
  waiting for transfers between devices: 112 us -> 89.4 us
  starting transfers between devices: 40.5 us -> 53.6 us
  Pallas kernels: 64.2 us -> 61.3 us
  local copies, waits for them, and re-layouts: 6.2 us -> 8.98 us
    ppermute x21, starting transfers between devices: 32.9 us -> 45.5 us  [over_dp(): return lax.ppermute(x, 'dp', [(a, a ^ step) for a in range(n_dp)])]
    ppermute x21, waiting for transfers between devices: 89.3 us -> 77.6 us  [over_dp(): return lax.ppermute(x, 'dp', [(a, a ^ step) for a in range(n_dp)])]
    ppermute x11, waiting for transfers between devices: 22.8 us -> 11.8 us  [over_seq(): return lax.ppermute(x, 'seq', [(a, a ^ step) for a in range(n_seq)])]
  transfers between devices with their start and end apart: 32 -> 32, of which waited for: 14 -> 16; matrix products, arithmetic and copies ran while one was open for 5% -> 5% of each run, Pallas kernels for 24% -> 23%
where the time goes in v11:
time: 228 us; the launch traced here: 224 us
  waiting for transfers between devices  89.4 us (39%)
  Pallas kernels  61.3 us (27%)
  starting transfers between devices  53.6 us (24%)
  other arithmetic  9.15 us (4%)
  local copies, waits for them, and re-layouts  8.98 us (4%)
    ppermute x21, waiting for transfers between devices, over_dp(): return lax.ppermute(x, 'dp', [(a, a ^ step) for a in range(n_dp)])  77.6 us
    ppermute x21, starting transfers between devices, over_dp(): return lax.ppermute(x, 'dp', [(a, a ^ step) for a in range(n_dp)])  45.5 us
    pallas_call x4, Pallas kernels, product_call(): pl.pallas_call(functools.partial(product_kernel, videos), grid=(1,), in_s...  13.3 us
    ppermute x11, waiting for transfers between devices, over_seq(): return lax.ppermute(x, 'seq', [(a, a ^ step) for a in range(n_seq)])  11.8 us
    pallas_call x3, Pallas kernels, pack_call(): pl.pallas_call(functools.partial(pack_kernel, moves, len(arrays)), grid=(...  10.1 us
    pallas_call x2, Pallas kernels, weights_call(): pl.pallas_call(weights_kernel, grid=(cols // tile,), in_specs=[pl.BlockSp...  8.78 us
    pallas_call x1, Pallas kernels, attend_call(): pl.pallas_call(functools.partial(attend_kernel, parts), grid=(steps,), in...  8.65 us
    pallas_call x1, Pallas kernels, gradient_call(): pl.pallas_call(functools.partial(gradient_kernel, parts), grid=(steps,),...  8.11 us
  transfers between devices with their start and end apart: 32, of which 16 were waited for; matrix products, arithmetic and copies ran while one was open for 5% of the time, Pallas kernels for 23%

profile of v11, /device:TPU:0, one launch (start us, length us, event | category | flops | bytes accessed | tf_op | source)
XLA Modules:
  0.0 224.1 jit_solution(12152238313730673164)
XLA Ops:
  1.4 4.3 %shard_map.94 = (bf16[768,512]{1,0:T(8,128)(2,1)}, bf16[1024,512]{1,0:T(8,128)(2,1)}, bf16[512,512]{1,0:T(8,128)(2,1)}, bf16[128,1024]{1,0:T(8,128)(2,1)}, bf16[...) custom-call(s32[8]{0:T(128)} %stack.75.place_ref, bf16[512,1024]{1,0:T(8,128)(2,1)} %refs_0_.1, ...), custom_call_target="tpu_custom_call" | custom-call | flops 1000 | bytes 1000 | tf_op jit(solution)/shard_map/pallas_call | solution.py:305
  5.7 4.0 %collective-permute-start.1 = (bf16[768,512]{1,0:T(8,128)(2,1)}, bf16[768,512]{1,0:T(8,128)(2,1)S(1)}, u32[]{:S(2)}, u32[]{:S(2)}) collective-permute-start(bf16[768,512]{1,0:T(8,128)(2,1)} %get-tuple-element.65), channel_id=1, source_target_pairs={{0,16},{4,20},{8,24},{12,28},{16,0},{20,4},{24,8},{28,12},{1,17},{... | collective-permute-start | bytes 2359304 | tf_op jit(solution)/shard_map/ppermute | solution.py:331
  10.3 6.0 %shard_map.95 = (bf16[2,384,1024]{2,1,0:T(8,128)(2,1)}, bf16[2,384,1024]{2,1,0:T(8,128)(2,1)}, bf16[2,384,1024]{2,1,0:T(8,128)(2,1)}, bf16[2,384,1024]{2,1,0:T(8,128)(2,1)}) custom-call(s32[4]{0:T(128)} %pad_add_fusion.lanes_ref.place_ref, bf16[384,4096]{1,0:T(8,128)(2,1)} %bitcast.25, bf16[384,4096]{1,0:T(8,128)(2,1)} %bitcast.26), custom_call_target="tpu_custom_call" | custom-call | flops 1000 | bytes 12582912 | tf_op jit(solution)/shard_map/pallas_call | solution.py:274
  21.0 12.6 %collective-permute-done.2.refs_1_ = bf16[128,1024]{1,0:T(8,128)(2,1)S(1)} collective-permute-done((bf16[128,1024]{1,0:T(8,128)(2,1)}, bf16[128,1024]{1,0:T(8,128)(2,1)S(1)}, u32[]{:S(2)}, u32[]{:S(2)}) %collective-permute-start.2) | collective-permute-done | bytes 262176 | tf_op jit(solution)/shard_map/ppermute | solution.py:331
  33.6 6.3 %collective-permute-done.3.refs_2_ = bf16[128,1024]{1,0:T(8,128)(2,1)S(1)} collective-permute-done((bf16[128,1024]{1,0:T(8,128)(2,1)}, bf16[128,1024]{1,0:T(8,128)(2,1)S(1)}, u32[]{:S(2)}, u32[]{:S(2)}) %collective-permute-start.3) | collective-permute-done | bytes 262176 | tf_op jit(solution)/shard_map/ppermute | solution.py:331
  39.9 10.8 %collective-permute-done.1.refs_0_ = bf16[768,512]{1,0:T(8,128)(2,1)S(1)} collective-permute-done((bf16[768,512]{1,0:T(8,128)(2,1)}, bf16[768,512]{1,0:T(8,128)(2,1)S(1)}, u32[]{:S(2)}, u32[]{:S(2)}) %collective-permute-start.1) | collective-permute-done | bytes 786464 | tf_op jit(solution)/shard_map/ppermute | solution.py:331
  56.9 7.8 %collective-permute-start.10 = (bf16[512,512]{1,0:T(8,128)(2,1)}, bf16[512,512]{1,0:T(8,128)(2,1)}, u32[]{:S(2)}, u32[]{:S(2)}) collective-permute-start(bf16[512,512]{1,0:T(8,128)(2,1)} %get-tuple-element.79), channel_id=1, source_target_pairs={{0,16},{4,20},{8,24},{12,28},{16,0},{20,4},{24,8},{28,12},{1,17},{... | collective-permute-start | bytes 1572872 | tf_op jit(solution)/shard_map/ppermute | solution.py:331
  76.8 6.0 %collective-permute-start.7 = (f32[256,512]{1,0:T(8,128)}, f32[256,512]{1,0:T(8,128)}, u32[]{:S(2)}, u32[]{:S(2)}) collective-permute-start(f32[256,512]{1,0:T(8,128)} %shard_map.98), channel_id=1, source_target_pairs={{0,8},{4,12},{8,0},{12,4},{16,24},{20,28},{24,16},{28,20},{1,9},{5... | collective-permute-start | bytes 1572872 | tf_op jit(solution)/shard_map/ppermute | solution.py:331
  84.1 4.5 %collective-permute-done.10.refs_6_ = bf16[512,512]{1,0:T(8,128)(2,1)} collective-permute-done((bf16[512,512]{1,0:T(8,128)(2,1)}, bf16[512,512]{1,0:T(8,128)(2,1)}, u32[]{:S(2)}, u32[]{:S(2)}) %collective-permute-start.10) | collective-permute-done | bytes 524320 | tf_op jit(solution)/shard_map/ppermute | solution.py:331
  96.0 3.8 %collective-permute-done.7 = f32[256,512]{1,0:T(8,128)} collective-permute-done((f32[256,512]{1,0:T(8,128)}, f32[256,512]{1,0:T(8,128)}, u32[]{:S(2)}, u32[]{:S(2)}) %collective-permute-start.7) | collective-permute-done | bytes 524320 | tf_op jit(solution)/shard_map/ppermute | solution.py:331
  101.0 8.1 %collective-permute-done.9 = bf16[128,512]{1,0:T(8,128)(2,1)S(1)} collective-permute-done((bf16[128,512]{1,0:T(8,128)(2,1)S(1)}, bf16[128,512]{1,0:T(8,128)(2,1)S(1)}, u32[]{:S(2)}, u32[]{:S(2)}) %collective-permute-start.9) | collective-permute-done | bytes 131104 | tf_op jit(solution)/shard_map/ppermute | solution.py:331
  119.2 5.2 %collective-permute-start.16 = (f32[256,512]{1,0:T(8,128)}, f32[256,512]{1,0:T(8,128)S(1)}, u32[]{:S(2)}, u32[]{:S(2)}) collective-permute-start(f32[256,512]{1,0:T(8,128)} %shard_map.102), channel_id=1, source_target_pairs={{0,8},{4,12},{8,0},{12,4},{16,24},{20,28},{24,16},{28,20},{1,9},{5... | collective-permute-start | bytes 1572872 | tf_op jit(solution)/shard_map/ppermute | solution.py:331
  124.4 3.3 %shard_map.100 = f32[256,512]{1,0:T(8,128)} custom-call(s32[4]{0:T(128)} %pad_add_fusion.1.place_ref, bf16[128,1024]{1,0:T(8,128)(2,1)} %get-tuple-element.64.first_ref.refs_0_, bf16[384,1024]{1,0:T(8,128)(2,1)} %get-tuple-element.68.mine_ref.refs_0_.refs_1_, bf16[128,1024]{1,0:T(8,128)(2,1)} %get-tuple-element.69.sibling_first_ref.refs_2_, ...), custom_call_target="tpu_custom_call" | custom-call | flops 1000 | bytes 1000 | tf_op jit(solution)/shard_map/pallas_call | solution.py:218
  128.4 8.7 %shard_map.101 = (f32[8,128,384]{2,1,0:T(8,128)}, f32[8,128,384]{2,1,0:T(8,128)}, f32[8,128,384]{2,1,0:T(8,128)}, f32[8,128,384]{2,1,0:T(8,128)}, bf16[128,1024]{1,0:T(8,128)(2,1)}, /*index=5*/bf16[128,1024]{1,0:T(8,128)(2,1)}) custom-call(s32[1]{0:T(128)S(6)} %copy.22.length_ref, bf16[128,1024]{1,0:T(8,128)(2,1)} %get-tuple-element.81.raw_ref, ...), custom_call_target="tpu_custom_call" | custom-call | flops 3221225472 | bytes 25165824 | tf_op jit(solution)/shard_map/pallas_call | solution.py:99
  137.3 3.6 %collective-permute-start.17 = (bf16[128,512]{1,0:T(8,128)(2,1)S(1)}, bf16[128,512]{1,0:T(8,128)(2,1)S(1)}, u32[]{:S(2)}, u32[]{:S(2)}) collective-permute-start(bf16[128,512]{1,0:T(8,128)(2,1)S(1)} %get-tuple-element.123), channel_id=1, source_target_pairs={{0,16},{4,20},{8,24},{12,28},{16,0},{20,4},{24,8},{28,12},{1,17},{... | collective-permute-start | bytes 393224 | tf_op jit(solution)/shard_map/ppermute | solution.py:331
  140.9 6.2 %collective-permute-done.17 = bf16[128,512]{1,0:T(8,128)(2,1)S(1)} collective-permute-done((bf16[128,512]{1,0:T(8,128)(2,1)S(1)}, bf16[128,512]{1,0:T(8,128)(2,1)S(1)}, u32[]{:S(2)}, u32[]{:S(2)}) %collective-permute-start.17) | collective-permute-done | bytes 131104 | tf_op jit(solution)/shard_map/ppermute | solution.py:331
  152.3 8.1 %shard_map.103 = (bf16[8,128,384]{2,1,0:T(8,128)(2,1)}, bf16[8,128,384]{2,1,0:T(8,128)(2,1)}, bf16[8,128,384]{2,1,0:T(8,128)(2,1)}, bf16[8,128,384]{2,1,0:T(8,12...) custom-call(bf16[128,1024]{1,0:T(8,128)(2,1)} %get-tuple-element.81.raw_ref, ...), custom_call_target="tpu_custom_call" | custom-call | flops 3221225472 | bytes 25165824 | tf_op jit(solution)/shard_map/pallas_call | solution.py:128
  163.0 3.8 %shard_map.104 = (bf16[384,1024]{1,0:T(8,128)(2,1)}, bf16[384,1024]{1,0:T(8,128)(2,1)}, bf16[384,1024]{1,0:T(8,128)(2,1)}, bf16[384,1024]{1,0:T(8,128)(2,1)}) custom-call(bf16[128,1024]{1,0:T(8,128)(2,1)} %get-tuple-element.87.keys_ref, bf16[8,128,384]{2,1,0:T(8,128)(2,1)} %get-tuple-element.95.refs_0_, bf16[8,128,384]{2,1,0:T(8,128)(2,1)} %get-tuple-element.96.refs_1_, ...), custom_call_target="tpu_custom_call" | custom-call | flops 1610612736 | bytes 12582912 | tf_op jit(solution)/shard_map/pallas_call | solution.py:152
  166.8 4.8 %collective-permute-done.19.refs_2_ = bf16[128,1024]{1,0:T(8,128)(2,1)S(1)} collective-permute-done((bf16[128,1024]{1,0:T(8,128)(2,1)S(1)}, bf16[128,1024]{1,0:T(8,128)(2,1)S(1)}, u32[]{:S(2)}, u32[]{:S(2)}) %collective-permute-start.19) | collective-permute-done | bytes 262176 | tf_op jit(solution)/shard_map/ppermute | solution.py:331
  178.6 10.0 %collective-permute-done.29.refs_2_ = bf16[128,1024]{1,0:T(8,128)(2,1)S(1)} collective-permute-done((bf16[128,1024]{1,0:T(8,128)(2,1)S(1)}, bf16[128,1024]{1,0:T(8,128)(2,1)S(1)}, u32[]{:S(2)}, u32[]{:S(2)}) %collective-permute-start.29) | collective-permute-done | bytes 262176 | tf_op jit(solution)/shard_map/ppermute | solution.py:331
  190.1 3.9 %collective-permute-done.28.refs_1_ = bf16[128,1024]{1,0:T(8,128)(2,1)S(1)} collective-permute-done((bf16[128,1024]{1,0:T(8,128)(2,1)S(1)}, bf16[128,1024]{1,0:T(8,128)(2,1)S(1)}, u32[]{:S(2)}, u32[]{:S(2)}) %collective-permute-start.28) | collective-permute-done | bytes 262176 | tf_op jit(solution)/shard_map/ppermute | solution.py:331
  201.4 4.4 %shard_map.107 = f32[512,1024]{1,0:T(8,128)} custom-call(bf16[512,1024]{1,0:T(8,128)(2,1)} %maximum_bitcast_fusion.columns_ref, bf16[128,1024]{1,0:T(8,128)(2,1)} %get-tuple-element.103.refs_0_, bf16[128,1024]{1,0:T(8,128)(2,1)} %copy-done.12, bf16[128,1024]{1,0:T(8,128)(2,1)} %copy-done.11, bf16[128,1024]{1,0:T(8,128)(2,1)} %copy-done.10, ...), custom_call_target="tpu_custom_call" | custom-call | flops 1073741824 | bytes 5242880 | tf_op jit(solution)/shard_map/pallas_call | solution.py:241
  205.8 9.0 %collective-permute-done.27.refs_3_ = bf16[384,1024]{1,0:T(8,128)(2,1)S(1)} collective-permute-done((bf16[384,1024]{1,0:T(8,128)(2,1)}, bf16[384,1024]{1,0:T(8,128)(2,1)S(1)}, u32[]{:S(2)}, u32[]{:S(2)}) %collective-permute-start.27) | collective-permute-done | bytes 786464 | tf_op jit(solution)/shard_map/ppermute | solution.py:334
  219.7 4.4 %shard_map.106 = f32[512,1024]{1,0:T(8,128)} custom-call(bf16[512,1024]{1,0:T(8,128)(2,1)} %maximum_bitcast_fusion.columns_ref, bf16[128,1024]{1,0:T(8,128)(2,1)} %copy-done.13, bf16[128,1024]{1,0:T(8,128)(2,1)} %copy-done.15, bf16[128,1024]{1,0:T(8,128)(2,1)} %copy-done.14, bf16[128,1024]{1,0:T(8,128)(2,1)} %copy-done.16, bf16[128,1024]{1,0:T(8,128)(2,1)} %copy-done.24, ...), custom_call_target="tpu_custom_call" | custom-call | flops 1073741824 | bytes 5242880 | tf_op jit(solution)/shard_map/pallas_call | solution.py:241
  (129 shorter events, 73.0 us)
Async XLA Ops:
  5.7 45.1 %collective-permute-start.1 = (bf16[768,512]{1,0:T(8,128)(2,1)}, bf16[768,512]{1,0:T(8,128)(2,1)S(1)}, u32[]{:S(2)}, u32[]{:S(2)}) collective-permute-start(bf16[768,512]{1,0:T(8,128)(2,1)} %get-tuple-element.65), channel_id=1, source_target_pairs={{0,16},{4,20},{8,24},{12,28},{16,0},{20,4},{24,8},{28,12},{1,17},{... | collective-permute-start | bytes 2359304 | tf_op jit(solution)/shard_map/ppermute | solution.py:331
  16.2 48.4 %collective-permute-start = (bf16[2,384,1024]{2,1,0:T(8,128)(2,1)}, bf16[2,384,1024]{2,1,0:T(8,128)(2,1)S(1)}, u32[]{:S(2)}, u32[]{:S(2)}) collective-permute-start(bf16[2,384,1024]{2,1,0:T(8,128)(2,1)} %get-tuple-element.62), channel_id=1, source_target_pairs={{0,2},{1,3},{2,0},{3,1},{4,6},{5,7},{6,4},{7,5},{8,10},{9,11},{10,... | collective-permute-start | bytes 4718600 | tf_op jit(solution)/shard_map/ppermute | solution.py:334
  17.7 15.9 %collective-permute-start.2 = (bf16[128,1024]{1,0:T(8,128)(2,1)}, bf16[128,1024]{1,0:T(8,128)(2,1)S(1)}, u32[]{:S(2)}, u32[]{:S(2)}) collective-permute-start(bf16[128,1024]{1,0:T(8,128)(2,1)} %get-tuple-element.66), channel_id=1, source_target_pairs={{0,8},{4,12},{8,0},{12,4},{16,24},{20,28},{24,16},{28,20},{1,9},{5... | collective-permute-start | bytes 786440 | tf_op jit(solution)/shard_map/ppermute | solution.py:331
  19.3 20.6 %collective-permute-start.3 = (bf16[128,1024]{1,0:T(8,128)(2,1)}, bf16[128,1024]{1,0:T(8,128)(2,1)S(1)}, u32[]{:S(2)}, u32[]{:S(2)}) collective-permute-start(bf16[128,1024]{1,0:T(8,128)(2,1)} %get-tuple-element.67), channel_id=1, source_target_pairs={{0,24},{4,28},{8,16},{12,20},{16,8},{20,12},{24,0},{28,4},{1,25},{... | collective-permute-start | bytes 786440 | tf_op jit(solution)/shard_map/ppermute | solution.py:331
  19.5 48.7 %collective-permute-start.5 = (bf16[1024,512]{1,0:T(8,128)(2,1)S(1)}, bf16[1024,512]{1,0:T(8,128)(2,1)}, u32[]{:S(2)}, u32[]{:S(2)}) collective-permute-start(bf16[1024,512]{1,0:T(8,128)(2,1)S(1)} %copy-done.2), channel_id=1, source_target_pairs={{0,4},{4,0},{8,12},{12,8},{16,20},{20,16},{24,28},{28,24},{1,5},{5... | collective-permute-start | bytes 3145736 | tf_op jit(solution)/shard_map/ppermute | solution.py:331
  54.3 14.8 %collective-permute-start.6 = (bf16[512,512]{1,0:T(8,128)(2,1)}, bf16[512,512]{1,0:T(8,128)(2,1)}, u32[]{:S(2)}, u32[]{:S(2)}) collective-permute-start(bf16[512,512]{1,0:T(8,128)(2,1)} %get-tuple-element.73.refs_6_), channel_id=1, source_target_pairs={{0,4},{4,0},{8,12},{12,8},{16,20},{20,16},{24,28},{28,24},{1,5},{5... | collective-permute-start | bytes 1572872 | tf_op jit(solution)/shard_map/ppermute | solution.py:331
  56.9 31.8 %collective-permute-start.10 = (bf16[512,512]{1,0:T(8,128)(2,1)}, bf16[512,512]{1,0:T(8,128)(2,1)}, u32[]{:S(2)}, u32[]{:S(2)}) collective-permute-start(bf16[512,512]{1,0:T(8,128)(2,1)} %get-tuple-element.79), channel_id=1, source_target_pairs={{0,16},{4,20},{8,24},{12,28},{16,0},{20,4},{24,8},{28,12},{1,17},{... | collective-permute-start | bytes 1572872 | tf_op jit(solution)/shard_map/ppermute | solution.py:331
  73.5 20.3 %collective-permute-start.8 = (bf16[512,512]{0,1:T(8,128)(2,1)}, bf16[512,512]{0,1:T(8,128)(2,1)}, u32[]{:S(2)}, u32[]{:S(2)}) collective-permute-start(bf16[512,512]{0,1:T(8,128)(2,1)} %copy.16), channel_id=1, source_target_pairs={{0,4},{4,0},{8,12},{12,8},{16,20},{20,16},{24,28},{28,24},{1,5},{5... | collective-permute-start | bytes 1572872 | tf_op jit(solution)/shard_map/ppermute | solution.py:331
  75.2 53.2 %collective-permute-start.14 = (bf16[2,384,1024]{2,1,0:T(8,128)(2,1)}, bf16[2,384,1024]{2,1,0:T(8,128)(2,1)}, u32[]{:S(2)}, u32[]{:S(2)}) collective-permute-start(bf16[2,384,1024]{2,1,0:T(8,128)(2,1)} %get-tuple-element.84), channel_id=1, source_target_pairs={{0,1},{1,0},{2,3},{3,2},{4,5},{5,4},{6,7},{7,6},{8,9},{9,8},{10,11... | collective-permute-start | bytes 4718600 | tf_op jit(solution)/shard_map/ppermute | solution.py:334
  75.2 53.2 %collective-permute-start.15 = (bf16[2,384,1024]{2,1,0:T(8,128)(2,1)}, bf16[2,384,1024]{2,1,0:T(8,128)(2,1)}, u32[]{:S(2)}, u32[]{:S(2)}) collective-permute-start(bf16[2,384,1024]{2,1,0:T(8,128)(2,1)} %get-tuple-element.86), channel_id=1, source_target_pairs={{0,3},{1,2},{2,1},{3,0},{4,7},{5,6},{6,5},{7,4},{8,11},{9,10},{10,... | collective-permute-start | bytes 4718600 | tf_op jit(solution)/shard_map/ppermute | solution.py:334
  76.8 22.9 %collective-permute-start.7 = (f32[256,512]{1,0:T(8,128)}, f32[256,512]{1,0:T(8,128)}, u32[]{:S(2)}, u32[]{:S(2)}) collective-permute-start(f32[256,512]{1,0:T(8,128)} %shard_map.98), channel_id=1, source_target_pairs={{0,8},{4,12},{8,0},{12,4},{16,24},{20,28},{24,16},{28,20},{1,9},{5... | collective-permute-start | bytes 1572872 | tf_op jit(solution)/shard_map/ppermute | solution.py:331
  88.6 26.5 %collective-permute-start.11 = (bf16[512,512]{1,0:T(8,128)(2,1)}, bf16[512,512]{1,0:T(8,128)(2,1)S(1)}, u32[]{:S(2)}, u32[]{:S(2)}) collective-permute-start(bf16[512,512]{1,0:T(8,128)(2,1)} %collective-permute-done.10.refs_6_), channel_id=1, source_target_pairs={{0,4},{4,0},{8,12},{12,8},{16,20},{20,16},{24,28},{28,24},{1,5},{5... | collective-permute-start | bytes 1572872 | tf_op jit(solution)/shard_map/ppermute | solution.py:331
  119.2 18.0 %collective-permute-start.16 = (f32[256,512]{1,0:T(8,128)}, f32[256,512]{1,0:T(8,128)S(1)}, u32[]{:S(2)}, u32[]{:S(2)}) collective-permute-start(f32[256,512]{1,0:T(8,128)} %shard_map.102), channel_id=1, source_target_pairs={{0,8},{4,12},{8,0},{12,4},{16,24},{20,28},{24,16},{28,20},{1,9},{5... | collective-permute-start | bytes 1572872 | tf_op jit(solution)/shard_map/ppermute | solution.py:331
  147.9 18.9 %collective-permute-start.20 = (bf16[128,1024]{1,0:T(8,128)(2,1)S(1)}, bf16[128,1024]{1,0:T(8,128)(2,1)S(1)}, u32[]{:S(2)}, u32[]{:S(2)}) collective-permute-start(bf16[128,1024]{1,0:T(8,128)(2,1)S(1)} %copy-done.9), channel_id=1, source_target_pairs={{0,24},{4,28},{8,16},{12,20},{16,8},{20,12},{24,0},{28,4},{1,25},{... | collective-permute-start | bytes 786440 | tf_op jit(solution)/shard_map/ppermute | solution.py:331
  150.6 21.0 %collective-permute-start.19 = (bf16[128,1024]{1,0:T(8,128)(2,1)S(1)}, bf16[128,1024]{1,0:T(8,128)(2,1)S(1)}, u32[]{:S(2)}, u32[]{:S(2)}) collective-permute-start(bf16[128,1024]{1,0:T(8,128)(2,1)S(1)} %copy-done.9), channel_id=1, source_target_pairs={{0,16},{4,20},{8,24},{12,28},{16,0},{20,4},{24,8},{28,12},{1,17},{... | collective-permute-start | bytes 786440 | tf_op jit(solution)/shard_map/ppermute | solution.py:331
  150.7 21.0 %collective-permute-start.18 = (bf16[128,1024]{1,0:T(8,128)(2,1)S(1)}, bf16[128,1024]{1,0:T(8,128)(2,1)S(1)}, u32[]{:S(2)}, u32[]{:S(2)}) collective-permute-start(bf16[128,1024]{1,0:T(8,128)(2,1)S(1)} %copy-done.9), channel_id=1, source_target_pairs={{0,8},{4,12},{8,0},{12,4},{16,24},{20,28},{24,16},{28,20},{1,9},{5... | collective-permute-start | bytes 786440 | tf_op jit(solution)/shard_map/ppermute | solution.py:331
  171.7 26.2 %collective-permute-start.22 = (bf16[512,1024]{1,0:T(8,128)(2,1)S(1)}, bf16[512,1024]{1,0:T(8,128)(2,1)S(1)}, u32[]{:S(2)}, u32[]{:S(2)}) collective-permute-start(bf16[512,1024]{1,0:T(8,128)(2,1)S(1)} %pad_maximum_fusion), channel_id=1, source_target_pairs={{0,4},{4,0},{8,12},{12,8},{16,20},{20,16},{24,28},{28,24},{1,5},{5... | collective-permute-start | bytes 3145736 | tf_op jit(solution)/shard_map/ppermute | solution.py:331
  172.3 22.7 %collective-permute-start.24 = (bf16[384,1024]{1,0:T(8,128)(2,1)S(1)}, bf16[384,1024]{1,0:T(8,128)(2,1)S(1)}, u32[]{:S(2)}, u32[]{:S(2)}) collective-permute-start(bf16[384,1024]{1,0:T(8,128)(2,1)S(1)} %copy-done.25), channel_id=1, source_target_pairs={{0,2},{1,3},{2,0},{3,1},{4,6},{5,7},{6,4},{7,5},{8,10},{9,11},{10,... | collective-permute-start | bytes 2359304 | tf_op jit(solution)/shard_map/ppermute | solution.py:334
  174.1 14.4 %collective-permute-start.29 = (bf16[128,1024]{1,0:T(8,128)(2,1)S(1)}, bf16[128,1024]{1,0:T(8,128)(2,1)S(1)}, u32[]{:S(2)}, u32[]{:S(2)}) collective-permute-start(bf16[128,1024]{1,0:T(8,128)(2,1)S(1)} %fusion.3.refs_0_), channel_id=1, source_target_pairs={{0,16},{4,20},{8,24},{12,28},{16,0},{20,4},{24,8},{28,12},{1,17},{... | collective-permute-start | bytes 786440 | tf_op jit(solution)/shard_map/ppermute | solution.py:331
  174.2 19.7 %collective-permute-start.28 = (bf16[128,1024]{1,0:T(8,128)(2,1)S(1)}, bf16[128,1024]{1,0:T(8,128)(2,1)S(1)}, u32[]{:S(2)}, u32[]{:S(2)}) collective-permute-start(bf16[128,1024]{1,0:T(8,128)(2,1)S(1)} %fusion.3.refs_0_), channel_id=1, source_target_pairs={{0,8},{4,12},{8,0},{12,4},{16,24},{20,28},{24,16},{28,20},{1,9},{5... | collective-permute-start | bytes 786440 | tf_op jit(solution)/shard_map/ppermute | solution.py:331
  176.3 17.7 %collective-permute-start.26 = (bf16[128,1024]{1,0:T(8,128)(2,1)S(1)}, bf16[128,1024]{1,0:T(8,128)(2,1)S(1)}, u32[]{:S(2)}, u32[]{:S(2)}) collective-permute-start(bf16[128,1024]{1,0:T(8,128)(2,1)S(1)} %fusion.3.refs_0_), channel_id=1, source_target_pairs={{0,24},{4,28},{8,16},{12,20},{16,8},{20,12},{24,0},{28,4},{1,25},{... | collective-permute-start | bytes 786440 | tf_op jit(solution)/shard_map/ppermute | solution.py:331
  195.0 19.8 %collective-permute-start.27 = (bf16[384,1024]{1,0:T(8,128)(2,1)}, bf16[384,1024]{1,0:T(8,128)(2,1)S(1)}, u32[]{:S(2)}, u32[]{:S(2)}) collective-permute-start(bf16[384,1024]{1,0:T(8,128)(2,1)} %get-tuple-element.113), channel_id=1, source_target_pairs={{0,3},{1,2},{2,1},{3,0},{4,7},{5,6},{6,5},{7,4},{8,11},{9,10},{10,... | collective-permute-start | bytes 2359304 | tf_op jit(solution)/shard_map/ppermute | solution.py:334
  197.9 16.9 %collective-permute-start.23 = (bf16[384,1024]{1,0:T(8,128)(2,1)}, bf16[384,1024]{1,0:T(8,128)(2,1)}, u32[]{:S(2)}, u32[]{:S(2)}) collective-permute-start(bf16[384,1024]{1,0:T(8,128)(2,1)} %get-tuple-element.107), channel_id=1, source_target_pairs={{0,1},{1,0},{2,3},{3,2},{4,5},{5,4},{6,7},{7,6},{8,9},{9,8},{10,11... | collective-permute-start | bytes 2359304 | tf_op jit(solution)/shard_map/ppermute | solution.py:334
  200.8 18.0 %collective-permute-start.31 = (bf16[384,1024]{1,0:T(8,128)(2,1)}, bf16[384,1024]{1,0:T(8,128)(2,1)S(1)}, u32[]{:S(2)}, u32[]{:S(2)}) collective-permute-start(bf16[384,1024]{1,0:T(8,128)(2,1)} %pad_maximum_fusion.1), channel_id=1, source_target_pairs={{0,4},{4,0},{8,12},{12,8},{16,20},{20,16},{24,28},{28,24},{1,5},{5... | collective-permute-start | bytes 2359304 | tf_op jit(solution)/shard_map/ppermute | solution.py:331
  (34 other events, 344.2 us)

commit v12 on v9

--- a/solution.py
+++ b/solution.py
@@ -80,7 +80,7 @@
 
 
 def specs(tokens, heads):
-    group = 2 - heads % 2
+    group = next(g for g in (4, 2, 1) if heads % g == 0)
     width = group * HD
     head = pl.BlockSpec((LIVE, width), lambda h: (0, h))
     block = pl.BlockSpec((tokens, width), lambda h: (0, h))
@@ -385,10 +385,8 @@
     )
     key_far = over_dp(key_near, 1)
     value_near = over_dp(after(value_given, near, *arrived), 2)
-    value_far = over_dp(value_near, 1)
     sibling = over_seq(shared_given, 1)
     key_quad = ((kept, rows, 0), (beside, rows, 0), (key_near, rows, 0), (key_far, rows, 0))
-    value_quad = ((kept, rows, 1), (beside, rows, 1), (value_near, rows, 0), (value_far, rows, 0))
 
     places = jnp.stack([core ^ low, 1 - (core ^ low), side, 1 - side]).astype(jnp.int32)
 
@@ -427,6 +425,8 @@
     key_product = product(after(places, own_columns), key_quad, True)
     key_sent = over_dp(key_product, 4)
     later = after(places, key_product)
+    value_far = over_dp(after(value_near, key_product), 1)
+    value_quad = ((kept, rows, 1), (beside, rows, 1), (value_near, rows, 0), (value_far, rows, 0))
     other_columns = over_dp(after(other_given, key_product), 1)
     columns = jnp.concatenate([own_columns, other_columns], axis=0).T
     value_product = product(later, value_quad, True)
@@ -447,22 +447,22 @@
     values = joined(value_total[:LIVE], after(value_other, value_grad))
 
     value_near_parts = [over_dp(value_grad, 2 * s) for s in range(1, lines)]
-    value_first = over_dp(value_grad, 1)
     scores, scaled, inner = gradient_call(raw, values, gain, moved, attends, tokens)
     outs = query_call(keys, scores)
-    inner = jnp.sum(after(inner, value_first), axis=-1, keepdims=True)
+    inner = jnp.sum(inner, axis=-1, keepdims=True)
     for step in steps[:-1]:
         inner = inner + over_seq(inner, step)
     far_sum = after(inner, *value_near_parts)
     inner_mean = (far_sum + over_seq(far_sum, 1)) / hid
     raw_grad = (inv_rms * scaled - raw_wide * inv_rms**3 * inner_mean).astype(jnp.bfloat16)
-    value_rest = over_dp(jnp.concatenate(value_near_parts, axis=0), 1)
+    value_parts = lax.optimization_barrier((value_grad, *value_near_parts, inner, outs[0]))[:-2]
+    value_rest = over_dp(jnp.concatenate(value_parts, axis=0), 1)
     key_near_parts = [over_dp(raw_grad, 2 * s) for s in range(1, lines)]
     placed = [outs[0]] + [None] * (n_seq - 1)
     previous = (inner,)
     for s in range(2, n_seq):
         placed[s] = over_seq(after(outs[s], *previous), s)
-        previous = (placed[s], key_near_parts[0])
+        previous = (placed[s], key_near_parts[-1])
     placed[1] = over_seq(after(outs[1], value_rest), 1)
     key_first = over_dp(raw_grad, 1)
     key_rest = over_dp(after(jnp.concatenate(key_near_parts, axis=0), key_first), 1)
@@ -473,8 +473,7 @@
     )
     value_parts = (
         [(x, LIVE, 0) for x in (value_grad, *value_near_parts)]
-        + [(value_first, LIVE, 0)]
-        + [(value_rest, LIVE, s) for s in range(lines - 1)]
+        + [(value_rest, LIVE, s) for s in range(lines)]
     )
     value_weight_grad = weights_call(after(columns, key_first), value_parts)
     (query_grad,) = pack_call(
@@ -484,7 +483,7 @@
         [(s, 0, 0, tokens // 2, cols, 0, 0, (s,)) for s in range(n_seq)],
         2,
     )
-    key_weight_grad = weights_call(after(columns, query_grad), key_parts)
+    key_weight_grad = weights_call(columns, key_parts)
     return query_grad[None], key_weight_grad, value_weight_grad
 
 

time: 211 us -> 208 us (0.986)
  local copies, waits for them, and re-layouts: 6.43 us -> 9.98 us
  Pallas kernels: 63.9 us -> 61 us
  waiting for transfers between devices: 93.9 us -> 91.3 us
    ppermute x11, waiting for transfers between devices: 16.2 us -> 3.69 us  [over_seq(): return lax.ppermute(x, 'seq', [(a, a ^ step) for a in range(n_seq)])]
    ppermute x22 -> x21, waiting for transfers between devices: 77.6 us -> 87.6 us  [over_dp(): return lax.ppermute(x, 'dp', [(a, a ^ step) for a in range(n_dp)])]
    unnamed x46 -> x50, local copies, waits for them, and re-layouts: 2.81 us -> 5.5 us
    ppermute x22 -> x21, starting transfers between devices: 27.3 us -> 26.3 us  [over_dp(): return lax.ppermute(x, 'dp', [(a, a ^ step) for a in range(n_dp)])]
  transfers between devices with their start and end apart: 33 -> 32, of which waited for: 13 -> 15; matrix products, arithmetic and copies ran while one was open for 5% -> 6% of each run, Pallas kernels for 26% -> 26%
where the time goes in v12:
time: 208 us; the launch traced here: 207 us
  waiting for transfers between devices  91.3 us (44%)
  Pallas kernels  61 us (29%)
  starting transfers between devices  34.9 us (17%)
  local copies, waits for them, and re-layouts  9.98 us (5%)
  other arithmetic  8.23 us (4%)
    ppermute x21, waiting for transfers between devices, over_dp(): return lax.ppermute(x, 'dp', [(a, a ^ step) for a in range(n_dp)])  87.6 us
    ppermute x21, starting transfers between devices, over_dp(): return lax.ppermute(x, 'dp', [(a, a ^ step) for a in range(n_dp)])  26.3 us
    pallas_call x4, Pallas kernels, product_call(): pl.pallas_call(functools.partial(product_kernel, videos), grid=(1,), in_s...  13.4 us
    pallas_call x3, Pallas kernels, pack_call(): pl.pallas_call(functools.partial(pack_kernel, moves, len(arrays)), grid=(...  10 us
    pallas_call x1, Pallas kernels, attend_call(): pl.pallas_call(functools.partial(attend_kernel, parts), grid=(steps,), in...  8.62 us
    ppermute x11, starting transfers between devices, over_seq(): return lax.ppermute(x, 'seq', [(a, a ^ step) for a in range(n_seq)])  8.6 us
    pallas_call x2, Pallas kernels, weights_call(): pl.pallas_call(weights_kernel, grid=(cols // tile,), in_specs=[pl.BlockSp...  8.51 us
    pallas_call x1, Pallas kernels, gradient_call(): pl.pallas_call(functools.partial(gradient_kernel, parts), grid=(steps,),...  8.11 us
  transfers between devices with their start and end apart: 32, of which 15 were waited for; matrix products, arithmetic and copies ran while one was open for 6% of the time, Pallas kernels for 26%

profile of v12, /device:TPU:0, one launch (start us, length us, event | category | flops | bytes accessed | tf_op | source)
XLA Modules:
  0.0 207.1 jit_solution(17304056237078091505)
XLA Ops:
  1.4 4.2 %shard_map.94 = (bf16[768,512]{1,0:T(8,128)(2,1)}, bf16[1024,512]{1,0:T(8,128)(2,1)}, bf16[512,512]{1,0:T(8,128)(2,1)}, bf16[128,1024]{1,0:T(8,128)(2,1)}, bf16[...) custom-call(s32[8]{0:T(128)} %stack.72.place_ref, bf16[512,1024]{1,0:T(8,128)(2,1)} %refs_0_.1, ...), custom_call_target="tpu_custom_call" | custom-call | flops 1000 | bytes 1000 | tf_op jit(solution)/shard_map/pallas_call | solution.py:305
  5.6 3.0 %collective-permute-start = (bf16[768,512]{1,0:T(8,128)(2,1)}, bf16[768,512]{1,0:T(8,128)(2,1)S(1)}, u32[]{:S(2)}, u32[]{:S(2)}) collective-permute-start(bf16[768,512]{1,0:T(8,128)(2,1)} %get-tuple-element.59), channel_id=1, source_target_pairs={{0,8},{4,12},{8,0},{12,4},{16,24},{20,28},{24,16},{28,20},{1,9},{5... | collective-permute-start | bytes 2359304 | tf_op jit(solution)/shard_map/ppermute | solution.py:329
  13.5 5.8 %shard_map.101 = (bf16[2,384,1024]{2,1,0:T(8,128)(2,1)}, bf16[2,384,1024]{2,1,0:T(8,128)(2,1)}, bf16[2,384,1024]{2,1,0:T(8,128)(2,1)}, bf16[2,384,1024]{2,1,0:T(8,128)(2,1)}) custom-call(s32[4]{0:T(128)} %pad_add_fusion.lanes_ref.place_ref, bf16[384,4096]{1,0:T(8,128)(2,1)} %bitcast.24, bf16[384,4096]{1,0:T(8,128)(2,1)} %bitcast.25), custom_call_target="tpu_custom_call" | custom-call | flops 1000 | bytes 12582912 | tf_op jit(solution)/shard_map/pallas_call | solution.py:274
  20.9 11.6 %collective-permute-done.1.refs_1_ = bf16[128,1024]{1,0:T(8,128)(2,1)} collective-permute-done((bf16[128,1024]{1,0:T(8,128)(2,1)}, bf16[128,1024]{1,0:T(8,128)(2,1)}, u32[]{:S(2)}, u32[]{:S(2)}) %collective-permute-start.1) | collective-permute-done | bytes 262176 | tf_op jit(solution)/shard_map/ppermute | solution.py:329
  32.5 7.4 %collective-permute-done.2.refs_2_ = bf16[128,1024]{1,0:T(8,128)(2,1)} collective-permute-done((bf16[128,1024]{1,0:T(8,128)(2,1)}, bf16[128,1024]{1,0:T(8,128)(2,1)}, u32[]{:S(2)}, u32[]{:S(2)}) %collective-permute-start.2) | collective-permute-done | bytes 262176 | tf_op jit(solution)/shard_map/ppermute | solution.py:329
  49.6 8.5 %collective-permute-done.5.refs_7_ = bf16[512,512]{1,0:T(8,128)(2,1)} collective-permute-done((bf16[512,512]{1,0:T(8,128)(2,1)}, bf16[512,512]{1,0:T(8,128)(2,1)}, u32[]{:S(2)}, u32[]{:S(2)}) %collective-permute-start.5) | collective-permute-done | bytes 524320 | tf_op jit(solution)/shard_map/ppermute | solution.py:329
  58.1 3.4 %shard_map.97 = f32[256,512]{1,0:T(8,128)} custom-call(s32[4]{0:T(128)} %pad_add_fusion.1.place_ref, bf16[384,1024]{1,0:T(8,128)(2,1)} %get-tuple-element.62.mine_ref.refs_0_.refs_1_, bf16[384,1024]{1,0:T(8,128)(2,1)} %get-tuple-element.62.mine_ref.refs_0_.refs_1_, bf16[384,1024]{1,0:T(8,128)(2,1)} %copy-done, bf16[384,1024]{1,0:T(8,128)(2,1)} %copy-done, ...), custom_call_target="tpu_custom_call" | custom-call | flops 1000 | bytes 1000 | tf_op jit(solution)/shard_map/pallas_call | solution.py:218
  67.4 3.4 %shard_map.98 = f32[256,512]{1,0:T(8,128)} custom-call(s32[4]{0:T(128)} %pad_add_fusion.1.place_ref, bf16[128,1024]{1,0:T(8,128)(2,1)} %get-tuple-element.58.first_ref.refs_0_, bf16[384,1024]{1,0:T(8,128)(2,1)} %get-tuple-element.62.mine_ref.refs_0_.refs_1_, bf16[128,1024]{1,0:T(8,128)(2,1)} %get-tuple-element.63.sibling_first_ref.refs_2_, ...), custom_call_target="tpu_custom_call" | custom-call | flops 1000 | bytes 1000 | tf_op jit(solution)/shard_map/pallas_call | solution.py:218
  72.0 4.5 %collective-permute-done.8.refs_7_ = bf16[512,512]{1,0:T(8,128)(2,1)S(1)} collective-permute-done((bf16[512,512]{1,0:T(8,128)(2,1)}, bf16[512,512]{1,0:T(8,128)(2,1)S(1)}, u32[]{:S(2)}, u32[]{:S(2)}) %collective-permute-start.8) | collective-permute-done | bytes 524320 | tf_op jit(solution)/shard_map/ppermute | solution.py:329
  77.4 3.3 %shard_map.100 = f32[256,512]{1,0:T(8,128)} custom-call(s32[4]{0:T(128)} %pad_add_fusion.1.place_ref, bf16[128,1024]{1,0:T(8,128)(2,1)} %get-tuple-element.58.first_ref.refs_0_, bf16[384,1024]{1,0:T(8,128)(2,1)} %get-tuple-element.62.mine_ref.refs_0_.refs_1_, bf16[128,1024]{1,0:T(8,128)(2,1)} %get-tuple-element.63.sibling_first_ref.refs_2_, ...), custom_call_target="tpu_custom_call" | custom-call | flops 1000 | bytes 1000 | tf_op jit(solution)/shard_map/pallas_call | solution.py:218
  80.7 3.3 %shard_map.99 = f32[256,512]{1,0:T(8,128)} custom-call(s32[4]{0:T(128)} %pad_add_fusion.1.place_ref, bf16[384,1024]{1,0:T(8,128)(2,1)} %get-tuple-element.62.mine_ref.refs_0_.refs_1_, bf16[384,1024]{1,0:T(8,128)(2,1)} %get-tuple-element.62.mine_ref.refs_0_.refs_1_, bf16[384,1024]{1,0:T(8,128)(2,1)} %copy-done, bf16[384,1024]{1,0:T(8,128)(2,1)} %copy-done, ...), custom_call_target="tpu_custom_call" | custom-call | flops 1000 | bytes 1000 | tf_op jit(solution)/shard_map/pallas_call | solution.py:218
  91.8 11.4 %collective-permute-done.10 = bf16[128,512]{1,0:T(8,128)(2,1)S(1)} collective-permute-done((bf16[128,512]{1,0:T(8,128)(2,1)S(1)}, bf16[128,512]{1,0:T(8,128)(2,1)S(1)}, u32[]{:S(2)}, u32[]{:S(2)}) %collective-permute-start.10) | collective-permute-done | bytes 131104 | tf_op jit(solution)/shard_map/ppermute | solution.py:329
  110.4 4.0 %collective-permute-done.11 = f32[256,512]{1,0:T(8,128)S(1)} collective-permute-done((f32[256,512]{1,0:T(8,128)S(1)}, f32[256,512]{1,0:T(8,128)S(1)}, u32[]{:S(2)}, u32[]{:S(2)}) %collective-permute-start.11) | collective-permute-done | bytes 524320 | tf_op jit(solution)/shard_map/ppermute | solution.py:329
  114.6 8.6 %shard_map.102 = (f32[8,128,384]{2,1,0:T(8,128)}, f32[8,128,384]{2,1,0:T(8,128)}, f32[8,128,384]{2,1,0:T(8,128)}, f32[8,128,384]{2,1,0:T(8,128)}, bf16[128,1024]{1,0:T(8,128)(2,1)}, /*index=5*/bf16[128,1024]{1,0:T(8,128)(2,1)}) custom-call(s32[1]{0:T(128)S(6)} %copy.22.length_ref, bf16[128,1024]{1,0:T(8,128)(2,1)} %get-tuple-element.78.raw_ref, ...), custom_call_target="tpu_custom_call" | custom-call | flops 3221225472 | bytes 25165824 | tf_op jit(solution)/shard_map/pallas_call | solution.py:99
  128.5 8.1 %shard_map.103 = (bf16[8,128,384]{2,1,0:T(8,128)(2,1)}, bf16[8,128,384]{2,1,0:T(8,128)(2,1)}, bf16[8,128,384]{2,1,0:T(8,128)(2,1)}, bf16[8,128,384]{2,1,0:T(8,12...) custom-call(bf16[128,1024]{1,0:T(8,128)(2,1)} %get-tuple-element.78.raw_ref, ...), custom_call_target="tpu_custom_call" | custom-call | flops 3221225472 | bytes 25165824 | tf_op jit(solution)/shard_map/pallas_call | solution.py:128
  139.2 3.8 %shard_map.104 = (bf16[384,1024]{1,0:T(8,128)(2,1)}, bf16[384,1024]{1,0:T(8,128)(2,1)}, bf16[384,1024]{1,0:T(8,128)(2,1)}, bf16[384,1024]{1,0:T(8,128)(2,1)}) custom-call(bf16[128,1024]{1,0:T(8,128)(2,1)} %get-tuple-element.86.keys_ref, bf16[8,128,384]{2,1,0:T(8,128)(2,1)} %get-tuple-element.93.refs_0_, bf16[8,128,384]{2,1,0:T(8,128)(2,1)} %get-tuple-element.94.refs_1_, ...), custom_call_target="tpu_custom_call" | custom-call | flops 1610612736 | bytes 12582912 | tf_op jit(solution)/shard_map/pallas_call | solution.py:152
  143.1 6.6 %collective-permute-done.19.refs_2_ = bf16[128,1024]{1,0:T(8,128)(2,1)S(1)} collective-permute-done((bf16[128,1024]{1,0:T(8,128)(2,1)}, bf16[128,1024]{1,0:T(8,128)(2,1)S(1)}, u32[]{:S(2)}, u32[]{:S(2)}) %collective-permute-start.19) | collective-permute-done | bytes 262176 | tf_op jit(solution)/shard_map/ppermute | solution.py:329
  157.7 9.9 %collective-permute-done.29.refs_2_ = bf16[128,1024]{1,0:T(8,128)(2,1)S(1)} collective-permute-done((bf16[128,1024]{1,0:T(8,128)(2,1)S(1)}, bf16[128,1024]{1,0:T(8,128)(2,1)S(1)}, u32[]{:S(2)}, u32[]{:S(2)}) %collective-permute-start.29) | collective-permute-done | bytes 262176 | tf_op jit(solution)/shard_map/ppermute | solution.py:329
  168.1 4.9 %collective-permute-done.28.refs_1_ = bf16[128,1024]{1,0:T(8,128)(2,1)S(1)} collective-permute-done((bf16[128,1024]{1,0:T(8,128)(2,1)S(1)}, bf16[128,1024]{1,0:T(8,128)(2,1)S(1)}, u32[]{:S(2)}, u32[]{:S(2)}) %collective-permute-start.28) | collective-permute-done | bytes 262176 | tf_op jit(solution)/shard_map/ppermute | solution.py:329
  174.1 5.8 %collective-permute-done.30.refs_4_ = bf16[128,1024]{1,0:T(8,128)(2,1)S(1)} collective-permute-done((bf16[128,1024]{1,0:T(8,128)(2,1)S(1)}, bf16[128,1024]{1,0:T(8,128)(2,1)S(1)}, u32[]{:S(2)}, u32[]{:S(2)}) %collective-permute-start.30) | collective-permute-done | bytes 262176 | tf_op jit(solution)/shard_map/ppermute | solution.py:329
  183.2 4.3 %shard_map.107 = f32[512,1024]{1,0:T(8,128)} custom-call(bf16[512,1024]{1,0:T(8,128)(2,1)} %maximum_bitcast_fusion.columns_ref, bf16[128,1024]{1,0:T(8,128)(2,1)} %get-tuple-element.100.refs_0_, bf16[128,1024]{1,0:T(8,128)(2,1)} %copy-done.12, bf16[128,1024]{1,0:T(8,128)(2,1)} %copy-done.11, bf16[128,1024]{1,0:T(8,128)(2,1)} %copy-done.10, ...), custom_call_target="tpu_custom_call" | custom-call | flops 1073741824 | bytes 5242880 | tf_op jit(solution)/shard_map/pallas_call | solution.py:241
  187.5 10.4 %collective-permute-done.31.refs_5_.refs_6_.refs_7_ = bf16[384,1024]{1,0:T(8,128)(2,1)S(1)} collective-permute-done((bf16[384,1024]{1,0:T(8,128)(2,1)}, bf16[384,1024]{1,0:T(8,128)(2,1)S(1)}, u32[]{:S(2)}, u32[]{:S(2)}) %collective-permute-start.31) | collective-permute-done | bytes 786464 | tf_op jit(solution)/shard_map/ppermute | solution.py:329
  198.8 4.3 %shard_map.106 = f32[512,1024]{1,0:T(8,128)} custom-call(bf16[512,1024]{1,0:T(8,128)(2,1)} %maximum_bitcast_fusion.columns_ref, bf16[128,1024]{1,0:T(8,128)(2,1)} %copy-done.13, bf16[128,1024]{1,0:T(8,128)(2,1)} %copy-done.15, bf16[128,1024]{1,0:T(8,128)(2,1)} %copy-done.14, bf16[128,1024]{1,0:T(8,128)(2,1)} %copy-done.16, bf16[128,1024]{1,0:T(8,128)(2,1)} %copy-done.23, ...), custom_call_target="tpu_custom_call" | custom-call | flops 1073741824 | bytes 5242880 | tf_op jit(solution)/shard_map/pallas_call | solution.py:241
  204.0 3.1 %shard_map.105 = bf16[384,4096]{1,0:T(8,128)(2,1)} custom-call(s32[4]{0:T(128)} %pad_add_fusion.lanes_ref.place_ref, bf16[384,1024]{1,0:T(8,128)(2,1)} %get-tuple-element.97.refs_0_, bf16[384,1024]{1,0:T(8,128)(2,1)} %collective-permute-done.23.refs_1_, bf16[384,1024]{1,0:T(8,128)(2,1)} %copy-done.17, bf16[384,1024]{1,0:T(8,128)(2,1)} %copy-done.18), custom_call_target="tpu_custom_call" | custom-call | flops 1000 | bytes 1000 | tf_op jit(solution)/shard_map/pallas_call | solution.py:305
  (127 shorter events, 61.7 us)
Async XLA Ops:
  5.6 34.3 %collective-permute-start = (bf16[768,512]{1,0:T(8,128)(2,1)}, bf16[768,512]{1,0:T(8,128)(2,1)S(1)}, u32[]{:S(2)}, u32[]{:S(2)}) collective-permute-start(bf16[768,512]{1,0:T(8,128)(2,1)} %get-tuple-element.59), channel_id=1, source_target_pairs={{0,8},{4,12},{8,0},{12,4},{16,24},{20,28},{24,16},{28,20},{1,9},{5... | collective-permute-start | bytes 2359304 | tf_op jit(solution)/shard_map/ppermute | solution.py:329
  8.6 23.9 %collective-permute-start.1 = (bf16[128,1024]{1,0:T(8,128)(2,1)}, bf16[128,1024]{1,0:T(8,128)(2,1)}, u32[]{:S(2)}, u32[]{:S(2)}) collective-permute-start(bf16[128,1024]{1,0:T(8,128)(2,1)} %get-tuple-element.60), channel_id=1, source_target_pairs={{0,16},{4,20},{8,24},{12,28},{16,0},{20,4},{24,8},{28,12},{1,17},{... | collective-permute-start | bytes 786440 | tf_op jit(solution)/shard_map/ppermute | solution.py:329
  11.2 28.7 %collective-permute-start.2 = (bf16[128,1024]{1,0:T(8,128)(2,1)}, bf16[128,1024]{1,0:T(8,128)(2,1)}, u32[]{:S(2)}, u32[]{:S(2)}) collective-permute-start(bf16[128,1024]{1,0:T(8,128)(2,1)} %get-tuple-element.61), channel_id=1, source_target_pairs={{0,24},{4,28},{8,16},{12,20},{16,8},{20,12},{24,0},{28,4},{1,25},{... | collective-permute-start | bytes 786440 | tf_op jit(solution)/shard_map/ppermute | solution.py:329
  11.2 38.4 %collective-permute-start.4 = (bf16[1024,512]{1,0:T(8,128)(2,1)}, bf16[1024,512]{1,0:T(8,128)(2,1)S(1)}, u32[]{:S(2)}, u32[]{:S(2)}) collective-permute-start(bf16[1024,512]{1,0:T(8,128)(2,1)} %get-tuple-element.67.refs_4_), channel_id=1, source_target_pairs={{0,4},{4,0},{8,12},{12,8},{16,20},{20,16},{24,28},{28,24},{1,5},{5... | collective-permute-start | bytes 3145736 | tf_op jit(solution)/shard_map/ppermute | solution.py:329
  19.4 46.4 %collective-permute-start.15 = (bf16[2,384,1024]{2,1,0:T(8,128)(2,1)}, bf16[2,384,1024]{2,1,0:T(8,128)(2,1)S(1)}, u32[]{:S(2)}, u32[]{:S(2)}) collective-permute-start(bf16[2,384,1024]{2,1,0:T(8,128)(2,1)} %get-tuple-element.83), channel_id=1, source_target_pairs={{0,2},{1,3},{2,0},{3,1},{4,6},{5,7},{6,4},{7,5},{8,10},{9,11},{10,... | collective-permute-start | bytes 4718600 | tf_op jit(solution)/shard_map/ppermute | solution.py:332
  43.5 14.7 %collective-permute-start.5 = (bf16[512,512]{1,0:T(8,128)(2,1)}, bf16[512,512]{1,0:T(8,128)(2,1)}, u32[]{:S(2)}, u32[]{:S(2)}) collective-permute-start(bf16[512,512]{1,0:T(8,128)(2,1)} %get-tuple-element.68.refs_6_), channel_id=1, source_target_pairs={{0,4},{4,0},{8,12},{12,8},{16,20},{20,16},{24,28},{28,24},{1,5},{5... | collective-permute-start | bytes 1572872 | tf_op jit(solution)/shard_map/ppermute | solution.py:329
  45.0 16.5 %collective-permute-start.7 = (bf16[512,512]{1,0:T(8,128)(2,1)}, bf16[512,512]{1,0:T(8,128)(2,1)}, u32[]{:S(2)}, u32[]{:S(2)}) collective-permute-start(bf16[512,512]{1,0:T(8,128)(2,1)} %get-tuple-element.71), channel_id=1, source_target_pairs={{0,8},{4,12},{8,0},{12,4},{16,24},{20,28},{24,16},{28,20},{1,9},{5... | collective-permute-start | bytes 1572872 | tf_op jit(solution)/shard_map/ppermute | solution.py:329
  61.5 15.0 %collective-permute-start.8 = (bf16[512,512]{1,0:T(8,128)(2,1)}, bf16[512,512]{1,0:T(8,128)(2,1)S(1)}, u32[]{:S(2)}, u32[]{:S(2)}) collective-permute-start(bf16[512,512]{1,0:T(8,128)(2,1)} %collective-permute-done.7.refs_6_), channel_id=1, source_target_pairs={{0,4},{4,0},{8,12},{12,8},{16,20},{20,16},{24,28},{28,24},{1,5},{5... | collective-permute-start | bytes 1572872 | tf_op jit(solution)/shard_map/ppermute | solution.py:329
  64.0 22.6 %collective-permute-start.9 = (bf16[512,512]{0,1:T(8,128)(2,1)}, bf16[512,512]{0,1:T(8,128)(2,1)}, u32[]{:S(2)}, u32[]{:S(2)}) collective-permute-start(bf16[512,512]{0,1:T(8,128)(2,1)} %copy.16), channel_id=1, source_target_pairs={{0,4},{4,0},{8,12},{12,8},{16,20},{20,16},{24,28},{28,24},{1,5},{5... | collective-permute-start | bytes 1572872 | tf_op jit(solution)/shard_map/ppermute | solution.py:329
  64.5 24.3 %collective-permute-start.6 = (f32[256,512]{1,0:T(8,128)}, f32[256,512]{1,0:T(8,128)S(1)}, u32[]{:S(2)}, u32[]{:S(2)}) collective-permute-start(f32[256,512]{1,0:T(8,128)} %shard_map.97), channel_id=1, source_target_pairs={{0,16},{4,20},{8,24},{12,28},{16,0},{20,4},{24,8},{28,12},{1,17},{... | collective-permute-start | bytes 1572872 | tf_op jit(solution)/shard_map/ppermute | solution.py:329
  65.8 48.8 %collective-permute-start.14 = (bf16[2,384,1024]{2,1,0:T(8,128)(2,1)}, bf16[2,384,1024]{2,1,0:T(8,128)(2,1)}, u32[]{:S(2)}, u32[]{:S(2)}) collective-permute-start(bf16[2,384,1024]{2,1,0:T(8,128)(2,1)} %get-tuple-element.82), channel_id=1, source_target_pairs={{0,1},{1,0},{2,3},{3,2},{4,5},{5,4},{6,7},{7,6},{8,9},{9,8},{10,11... | collective-permute-start | bytes 4718600 | tf_op jit(solution)/shard_map/ppermute | solution.py:332
  65.8 48.8 %collective-permute-start.16 = (bf16[2,384,1024]{2,1,0:T(8,128)(2,1)}, bf16[2,384,1024]{2,1,0:T(8,128)(2,1)}, u32[]{:S(2)}, u32[]{:S(2)}) collective-permute-start(bf16[2,384,1024]{2,1,0:T(8,128)(2,1)} %get-tuple-element.85), channel_id=1, source_target_pairs={{0,3},{1,2},{2,1},{3,0},{4,7},{5,6},{6,5},{7,4},{8,11},{9,10},{10,... | collective-permute-start | bytes 4718600 | tf_op jit(solution)/shard_map/ppermute | solution.py:332
  88.8 25.6 %collective-permute-start.11 = (f32[256,512]{1,0:T(8,128)S(1)}, f32[256,512]{1,0:T(8,128)S(1)}, u32[]{:S(2)}, u32[]{:S(2)}) collective-permute-start(f32[256,512]{1,0:T(8,128)S(1)} %copy-done.22), channel_id=1, source_target_pairs={{0,16},{4,20},{8,24},{12,28},{16,0},{20,4},{24,8},{28,12},{1,17},{... | collective-permute-start | bytes 1572872 | tf_op jit(solution)/shard_map/ppermute | solution.py:329
  123.2 19.8 %collective-permute-start.20 = (bf16[128,1024]{1,0:T(8,128)(2,1)}, bf16[128,1024]{1,0:T(8,128)(2,1)S(1)}, u32[]{:S(2)}, u32[]{:S(2)}) collective-permute-start(bf16[128,1024]{1,0:T(8,128)(2,1)} %get-tuple-element.100.refs_0_), channel_id=1, source_target_pairs={{0,24},{4,28},{8,16},{12,20},{16,8},{20,12},{24,0},{28,4},{1,25},{... | collective-permute-start | bytes 786440 | tf_op jit(solution)/shard_map/ppermute | solution.py:329
  124.8 25.0 %collective-permute-start.19 = (bf16[128,1024]{1,0:T(8,128)(2,1)}, bf16[128,1024]{1,0:T(8,128)(2,1)S(1)}, u32[]{:S(2)}, u32[]{:S(2)}) collective-permute-start(bf16[128,1024]{1,0:T(8,128)(2,1)} %get-tuple-element.100.refs_0_), channel_id=1, source_target_pairs={{0,16},{4,20},{8,24},{12,28},{16,0},{20,4},{24,8},{28,12},{1,17},{... | collective-permute-start | bytes 786440 | tf_op jit(solution)/shard_map/ppermute | solution.py:329
  126.7 23.0 %collective-permute-start.18 = (bf16[128,1024]{1,0:T(8,128)(2,1)}, bf16[128,1024]{1,0:T(8,128)(2,1)S(1)}, u32[]{:S(2)}, u32[]{:S(2)}) collective-permute-start(bf16[128,1024]{1,0:T(8,128)(2,1)} %get-tuple-element.100.refs_0_), channel_id=1, source_target_pairs={{0,8},{4,12},{8,0},{12,4},{16,24},{20,28},{24,16},{28,20},{1,9},{5... | collective-permute-start | bytes 786440 | tf_op jit(solution)/shard_map/ppermute | solution.py:329
  149.8 31.6 %collective-permute-start.22 = (bf16[512,1024]{1,0:T(8,128)(2,1)S(1)}, bf16[512,1024]{1,0:T(8,128)(2,1)S(1)}, u32[]{:S(2)}, u32[]{:S(2)}) collective-permute-start(bf16[512,1024]{1,0:T(8,128)(2,1)S(1)} %pad_maximum_fusion), channel_id=1, source_target_pairs={{0,4},{4,0},{8,12},{12,8},{16,20},{20,16},{24,28},{28,24},{1,5},{5... | collective-permute-start | bytes 3145736 | tf_op jit(solution)/shard_map/ppermute | solution.py:329
  151.4 30.0 %collective-permute-start.24 = (bf16[384,1024]{1,0:T(8,128)(2,1)S(1)}, bf16[384,1024]{1,0:T(8,128)(2,1)S(1)}, u32[]{:S(2)}, u32[]{:S(2)}) collective-permute-start(bf16[384,1024]{1,0:T(8,128)(2,1)S(1)} %copy-done.24), channel_id=1, source_target_pairs={{0,2},{1,3},{2,0},{3,1},{4,6},{5,7},{6,4},{7,5},{8,10},{9,11},{10,... | collective-permute-start | bytes 2359304 | tf_op jit(solution)/shard_map/ppermute | solution.py:332
  153.2 14.4 %collective-permute-start.29 = (bf16[128,1024]{1,0:T(8,128)(2,1)S(1)}, bf16[128,1024]{1,0:T(8,128)(2,1)S(1)}, u32[]{:S(2)}, u32[]{:S(2)}) collective-permute-start(bf16[128,1024]{1,0:T(8,128)(2,1)S(1)} %fusion.3.refs_0_), channel_id=1, source_target_pairs={{0,16},{4,20},{8,24},{12,28},{16,0},{20,4},{24,8},{28,12},{1,17},{... | collective-permute-start | bytes 786440 | tf_op jit(solution)/shard_map/ppermute | solution.py:329
  153.3 19.7 %collective-permute-start.28 = (bf16[128,1024]{1,0:T(8,128)(2,1)S(1)}, bf16[128,1024]{1,0:T(8,128)(2,1)S(1)}, u32[]{:S(2)}, u32[]{:S(2)}) collective-permute-start(bf16[128,1024]{1,0:T(8,128)(2,1)S(1)} %fusion.3.refs_0_), channel_id=1, source_target_pairs={{0,8},{4,12},{8,0},{12,4},{16,24},{20,28},{24,16},{28,20},{1,9},{5... | collective-permute-start | bytes 786440 | tf_op jit(solution)/shard_map/ppermute | solution.py:329
  155.3 17.7 %collective-permute-start.26 = (bf16[128,1024]{1,0:T(8,128)(2,1)S(1)}, bf16[128,1024]{1,0:T(8,128)(2,1)S(1)}, u32[]{:S(2)}, u32[]{:S(2)}) collective-permute-start(bf16[128,1024]{1,0:T(8,128)(2,1)S(1)} %fusion.3.refs_0_), channel_id=1, source_target_pairs={{0,24},{4,28},{8,16},{12,20},{16,8},{20,12},{24,0},{28,4},{1,25},{... | collective-permute-start | bytes 786440 | tf_op jit(solution)/shard_map/ppermute | solution.py:329
  179.9 18.0 %collective-permute-start.31 = (bf16[384,1024]{1,0:T(8,128)(2,1)}, bf16[384,1024]{1,0:T(8,128)(2,1)S(1)}, u32[]{:S(2)}, u32[]{:S(2)}) collective-permute-start(bf16[384,1024]{1,0:T(8,128)(2,1)} %pad_maximum_fusion.1), channel_id=1, source_target_pairs={{0,4},{4,0},{8,12},{12,8},{16,20},{20,16},{24,28},{28,24},{1,5},{5... | collective-permute-start | bytes 2359304 | tf_op jit(solution)/shard_map/ppermute | solution.py:329
  181.4 21.7 %collective-permute-start.27 = (bf16[384,1024]{1,0:T(8,128)(2,1)}, bf16[384,1024]{1,0:T(8,128)(2,1)S(1)}, u32[]{:S(2)}, u32[]{:S(2)}) collective-permute-start(bf16[384,1024]{1,0:T(8,128)(2,1)} %get-tuple-element.110), channel_id=1, source_target_pairs={{0,3},{1,2},{2,1},{3,0},{4,7},{5,6},{6,5},{7,4},{8,11},{9,10},{10,... | collective-permute-start | bytes 2359304 | tf_op jit(solution)/shard_map/ppermute | solution.py:332
  182.3 20.8 %collective-permute-start.23 = (bf16[384,1024]{1,0:T(8,128)(2,1)}, bf16[384,1024]{1,0:T(8,128)(2,1)}, u32[]{:S(2)}, u32[]{:S(2)}) collective-permute-start(bf16[384,1024]{1,0:T(8,128)(2,1)} %get-tuple-element.104), channel_id=1, source_target_pairs={{0,1},{1,0},{2,3},{3,2},{4,5},{5,4},{6,7},{7,6},{8,9},{9,8},{10,11... | collective-permute-start | bytes 2359304 | tf_op jit(solution)/shard_map/ppermute | solution.py:332
  (33 other events, 347.6 us)

commit v13 on v12

--- a/solution.py
+++ b/solution.py
@@ -311,6 +311,32 @@
         compiler_params=pltpu.CompilerParams(vmem_limit_bytes=VMEM),
         cost_estimate=pl.CostEstimate(flops=1000, bytes_accessed=size, transcendentals=0),
     )(place, *arrays)
+
+
+def insert_kernel(index_ref, whole_ref, block_ref, out_ref):
+    out_ref[...] = block_ref[...]
+
+
+def insert_call(index, whole, block):
+    tokens, cols = block.shape
+    return pl.pallas_call(
+        insert_kernel,
+        grid_spec=pltpu.PrefetchScalarGridSpec(
+            num_scalar_prefetch=1,
+            grid=(1,),
+            in_specs=[
+                pl.BlockSpec(memory_space=pl.ANY),
+                pl.BlockSpec((tokens, cols), lambda n, at: (0, 0)),
+            ],
+            out_specs=pl.BlockSpec((tokens, cols), lambda n, at: (0, at[0])),
+        ),
+        out_shape=jax.ShapeDtypeStruct(whole.shape, whole.dtype),
+        input_output_aliases={1: 0},
+        compiler_params=pltpu.CompilerParams(vmem_limit_bytes=VMEM),
+        cost_estimate=pl.CostEstimate(
+            flops=1000, bytes_accessed=4 * tokens * cols, transcendentals=0
+        ),
+    )(index, whole, block)
 
 
 def shards(n_dp, n_seq, query, caption, key_weight, value_weight, key_gain, lengths, out_grad):
@@ -449,13 +475,14 @@
     value_near_parts = [over_dp(value_grad, 2 * s) for s in range(1, lines)]
     scores, scaled, inner = gradient_call(raw, values, gain, moved, attends, tokens)
     outs = query_call(keys, scores)
-    inner = jnp.sum(inner, axis=-1, keepdims=True)
+    value_first = over_dp(value_grad, 1)
+    inner = jnp.sum(after(inner, value_first), axis=-1, keepdims=True)
     for step in steps[:-1]:
         inner = inner + over_seq(inner, step)
     far_sum = after(inner, *value_near_parts)
     inner_mean = (far_sum + over_seq(far_sum, 1)) / hid
     raw_grad = (inv_rms * scaled - raw_wide * inv_rms**3 * inner_mean).astype(jnp.bfloat16)
-    value_parts = lax.optimization_barrier((value_grad, *value_near_parts, inner, outs[0]))[:-2]
+    value_parts = lax.optimization_barrier((*value_near_parts, inner, outs[0]))[:-2]
     value_rest = over_dp(jnp.concatenate(value_parts, axis=0), 1)
     key_near_parts = [over_dp(raw_grad, 2 * s) for s in range(1, lines)]
     placed = [outs[0]] + [None] * (n_seq - 1)
@@ -473,16 +500,18 @@
     )
     value_parts = (
         [(x, LIVE, 0) for x in (value_grad, *value_near_parts)]
-        + [(value_rest, LIVE, s) for s in range(lines)]
+        + [(value_first, LIVE, 0)]
+        + [(value_rest, LIVE, s) for s in range(lines - 1)]
     )
     value_weight_grad = weights_call(after(columns, key_first), value_parts)
-    (query_grad,) = pack_call(
+    (assembled,) = pack_call(
         lanes,
-        placed,
+        placed[:-1],
         [(tokens, hid)],
-        [(s, 0, 0, tokens // 2, cols, 0, 0, (s,)) for s in range(n_seq)],
+        [(s, 0, 0, tokens // 2, cols, 0, 0, (s,)) for s in range(n_seq - 1)],
         2,
     )
+    query_grad = insert_call(lanes[-1:], assembled, placed[-1])
     key_weight_grad = weights_call(columns, key_parts)
     return query_grad[None], key_weight_grad, value_weight_grad
 

time: 208 us -> 208 us (level)
  waiting for transfers between devices: 91.3 us -> 88.1 us
    ppermute x21 -> x22, waiting for transfers between devices: 87.6 us -> 84.4 us  [over_dp(): return lax.ppermute(x, 'dp', [(a, a ^ step) for a in range(n_dp)])]
    ppermute x21 -> x22, starting transfers between devices: 26.3 us -> 27.1 us  [over_dp(): return lax.ppermute(x, 'dp', [(a, a ^ step) for a in range(n_dp)])]
  transfers between devices with their start and end apart: 32 -> 33, of which waited for: 15 -> 15; matrix products, arithmetic and copies ran while one was open for 6% -> 6% of each run, Pallas kernels for 26% -> 27%
where the time goes in v13:
time: 208 us; the launch traced here: 207 us
  waiting for transfers between devices  88.1 us (42%)
  Pallas kernels  62.9 us (30%)
  starting transfers between devices  36.3 us (17%)
  local copies, waits for them, and re-layouts  9.91 us (5%)
  other arithmetic  8.28 us (4%)
    ppermute x22, waiting for transfers between devices, over_dp(): return lax.ppermute(x, 'dp', [(a, a ^ step) for a in range(n_dp)])  84.4 us
    ppermute x22, starting transfers between devices, over_dp(): return lax.ppermute(x, 'dp', [(a, a ^ step) for a in range(n_dp)])  27.1 us
    pallas_call x4, Pallas kernels, product_call(): pl.pallas_call(functools.partial(product_kernel, videos), grid=(1,), in_s...  13.5 us
    pallas_call x3, Pallas kernels, pack_call(): pl.pallas_call(functools.partial(pack_kernel, moves, len(arrays)), grid=(...  9.89 us
    ppermute x11, starting transfers between devices, over_seq(): return lax.ppermute(x, 'seq', [(a, a ^ step) for a in range(n_seq)])  9.17 us
    pallas_call x1, Pallas kernels, attend_call(): pl.pallas_call(functools.partial(attend_kernel, parts), grid=(steps,), in...  8.6 us
    pallas_call x2, Pallas kernels, weights_call(): pl.pallas_call(weights_kernel, grid=(cols // tile,), in_specs=[pl.BlockSp...  8.52 us
    pallas_call x1, Pallas kernels, gradient_call(): pl.pallas_call(functools.partial(gradient_kernel, parts), grid=(steps,),...  8.1 us
  transfers between devices with their start and end apart: 33, of which 15 were waited for; matrix products, arithmetic and copies ran while one was open for 6% of the time, Pallas kernels for 27%

profile of v13, /device:TPU:0, one launch (start us, length us, event | category | flops | bytes accessed | tf_op | source)
XLA Modules:
  0.0 207.2 jit_solution(13426521332787719194)
XLA Ops:
  1.3 4.2 %shard_map.94 = (bf16[768,512]{1,0:T(8,128)(2,1)}, bf16[1024,512]{1,0:T(8,128)(2,1)}, bf16[512,512]{1,0:T(8,128)(2,1)}, bf16[128,1024]{1,0:T(8,128)(2,1)}, bf16[...) custom-call(s32[8]{0:T(128)} %stack.72.place_ref, bf16[512,1024]{1,0:T(8,128)(2,1)} %refs_0_.1, ...), custom_call_target="tpu_custom_call" | custom-call | flops 1000 | bytes 1000 | tf_op jit(solution)/shard_map/pallas_call | solution.py:305
  5.6 3.0 %collective-permute-start = (bf16[768,512]{1,0:T(8,128)(2,1)}, bf16[768,512]{1,0:T(8,128)(2,1)S(1)}, u32[]{:S(2)}, u32[]{:S(2)}) collective-permute-start(bf16[768,512]{1,0:T(8,128)(2,1)} %get-tuple-element.59), channel_id=1, source_target_pairs={{0,8},{4,12},{8,0},{12,4},{16,24},{20,28},{24,16},{28,20},{1,9},{5... | collective-permute-start | bytes 2359304 | tf_op jit(solution)/shard_map/ppermute | solution.py:355
  13.6 5.9 %shard_map.101 = (bf16[2,384,1024]{2,1,0:T(8,128)(2,1)}, bf16[2,384,1024]{2,1,0:T(8,128)(2,1)}, bf16[2,384,1024]{2,1,0:T(8,128)(2,1)}, bf16[2,384,1024]{2,1,0:T(8,128)(2,1)}) custom-call(s32[4]{0:T(128)} %pad_add_fusion.lanes_ref.place_ref, bf16[384,4096]{1,0:T(8,128)(2,1)} %bitcast.25, bf16[384,4096]{1,0:T(8,128)(2,1)} %bitcast.26), custom_call_target="tpu_custom_call" | custom-call | flops 1000 | bytes 12582912 | tf_op jit(solution)/shard_map/pallas_call | solution.py:274
  20.9 11.5 %collective-permute-done.1.refs_1_ = bf16[128,1024]{1,0:T(8,128)(2,1)} collective-permute-done((bf16[128,1024]{1,0:T(8,128)(2,1)}, bf16[128,1024]{1,0:T(8,128)(2,1)}, u32[]{:S(2)}, u32[]{:S(2)}) %collective-permute-start.1) | collective-permute-done | bytes 262176 | tf_op jit(solution)/shard_map/ppermute | solution.py:355
  32.5 7.4 %collective-permute-done.2.refs_2_ = bf16[128,1024]{1,0:T(8,128)(2,1)} collective-permute-done((bf16[128,1024]{1,0:T(8,128)(2,1)}, bf16[128,1024]{1,0:T(8,128)(2,1)}, u32[]{:S(2)}, u32[]{:S(2)}) %collective-permute-start.2) | collective-permute-done | bytes 262176 | tf_op jit(solution)/shard_map/ppermute | solution.py:355
  49.6 8.5 %collective-permute-done.5.refs_7_ = bf16[512,512]{1,0:T(8,128)(2,1)} collective-permute-done((bf16[512,512]{1,0:T(8,128)(2,1)}, bf16[512,512]{1,0:T(8,128)(2,1)}, u32[]{:S(2)}, u32[]{:S(2)}) %collective-permute-start.5) | collective-permute-done | bytes 524320 | tf_op jit(solution)/shard_map/ppermute | solution.py:355
  58.1 3.4 %shard_map.97 = f32[256,512]{1,0:T(8,128)} custom-call(s32[4]{0:T(128)} %pad_add_fusion.1.place_ref, bf16[384,1024]{1,0:T(8,128)(2,1)} %get-tuple-element.62.mine_ref.refs_0_.refs_1_, bf16[384,1024]{1,0:T(8,128)(2,1)} %get-tuple-element.62.mine_ref.refs_0_.refs_1_, bf16[384,1024]{1,0:T(8,128)(2,1)} %copy-done, bf16[384,1024]{1,0:T(8,128)(2,1)} %copy-done, ...), custom_call_target="tpu_custom_call" | custom-call | flops 1000 | bytes 1000 | tf_op jit(solution)/shard_map/pallas_call | solution.py:218
  67.4 3.4 %shard_map.98 = f32[256,512]{1,0:T(8,128)} custom-call(s32[4]{0:T(128)} %pad_add_fusion.1.place_ref, bf16[128,1024]{1,0:T(8,128)(2,1)} %get-tuple-element.58.first_ref.refs_0_, bf16[384,1024]{1,0:T(8,128)(2,1)} %get-tuple-element.62.mine_ref.refs_0_.refs_1_, bf16[128,1024]{1,0:T(8,128)(2,1)} %get-tuple-element.63.sibling_first_ref.refs_2_, ...), custom_call_target="tpu_custom_call" | custom-call | flops 1000 | bytes 1000 | tf_op jit(solution)/shard_map/pallas_call | solution.py:218
  72.1 4.5 %collective-permute-done.8.refs_7_ = bf16[512,512]{1,0:T(8,128)(2,1)S(1)} collective-permute-done((bf16[512,512]{1,0:T(8,128)(2,1)}, bf16[512,512]{1,0:T(8,128)(2,1)S(1)}, u32[]{:S(2)}, u32[]{:S(2)}) %collective-permute-start.8) | collective-permute-done | bytes 524320 | tf_op jit(solution)/shard_map/ppermute | solution.py:355
  77.4 3.4 %shard_map.100 = f32[256,512]{1,0:T(8,128)} custom-call(s32[4]{0:T(128)} %pad_add_fusion.1.place_ref, bf16[128,1024]{1,0:T(8,128)(2,1)} %get-tuple-element.58.first_ref.refs_0_, bf16[384,1024]{1,0:T(8,128)(2,1)} %get-tuple-element.62.mine_ref.refs_0_.refs_1_, bf16[128,1024]{1,0:T(8,128)(2,1)} %get-tuple-element.63.sibling_first_ref.refs_2_, ...), custom_call_target="tpu_custom_call" | custom-call | flops 1000 | bytes 1000 | tf_op jit(solution)/shard_map/pallas_call | solution.py:218
  80.7 3.4 %shard_map.99 = f32[256,512]{1,0:T(8,128)} custom-call(s32[4]{0:T(128)} %pad_add_fusion.1.place_ref, bf16[384,1024]{1,0:T(8,128)(2,1)} %get-tuple-element.62.mine_ref.refs_0_.refs_1_, bf16[384,1024]{1,0:T(8,128)(2,1)} %get-tuple-element.62.mine_ref.refs_0_.refs_1_, bf16[384,1024]{1,0:T(8,128)(2,1)} %copy-done, bf16[384,1024]{1,0:T(8,128)(2,1)} %copy-done, ...), custom_call_target="tpu_custom_call" | custom-call | flops 1000 | bytes 1000 | tf_op jit(solution)/shard_map/pallas_call | solution.py:218
  89.0 2.8 %collective-permute-start.10 = (bf16[128,512]{1,0:T(8,128)(2,1)S(1)}, bf16[128,512]{1,0:T(8,128)(2,1)S(1)}, u32[]{:S(2)}, u32[]{:S(2)}) collective-permute-start(bf16[128,512]{1,0:T(8,128)(2,1)S(1)} %get-tuple-element.120), channel_id=1, source_target_pairs={{0,8},{4,12},{8,0},{12,4},{16,24},{20,28},{24,16},{28,20},{1,9},{5... | collective-permute-start | bytes 393224 | tf_op jit(solution)/shard_map/ppermute | solution.py:355
  91.8 11.4 %collective-permute-done.10 = bf16[128,512]{1,0:T(8,128)(2,1)S(1)} collective-permute-done((bf16[128,512]{1,0:T(8,128)(2,1)S(1)}, bf16[128,512]{1,0:T(8,128)(2,1)S(1)}, u32[]{:S(2)}, u32[]{:S(2)}) %collective-permute-start.10) | collective-permute-done | bytes 131104 | tf_op jit(solution)/shard_map/ppermute | solution.py:355
  110.4 4.0 %collective-permute-done.11 = f32[256,512]{1,0:T(8,128)S(1)} collective-permute-done((f32[256,512]{1,0:T(8,128)S(1)}, f32[256,512]{1,0:T(8,128)S(1)}, u32[]{:S(2)}, u32[]{:S(2)}) %collective-permute-start.11) | collective-permute-done | bytes 524320 | tf_op jit(solution)/shard_map/ppermute | solution.py:355
  114.6 8.6 %shard_map.102 = (f32[8,128,384]{2,1,0:T(8,128)}, f32[8,128,384]{2,1,0:T(8,128)}, f32[8,128,384]{2,1,0:T(8,128)}, f32[8,128,384]{2,1,0:T(8,128)}, bf16[128,1024]{1,0:T(8,128)(2,1)}, /*index=5*/bf16[128,1024]{1,0:T(8,128)(2,1)}) custom-call(s32[1]{0:T(128)S(6)} %copy.24.length_ref, bf16[128,1024]{1,0:T(8,128)(2,1)} %get-tuple-element.78.raw_ref, ...), custom_call_target="tpu_custom_call" | custom-call | flops 3221225472 | bytes 25165824 | tf_op jit(solution)/shard_map/pallas_call | solution.py:99
  130.0 8.1 %shard_map.103 = (bf16[8,128,384]{2,1,0:T(8,128)(2,1)}, bf16[8,128,384]{2,1,0:T(8,128)(2,1)}, bf16[8,128,384]{2,1,0:T(8,128)(2,1)}, bf16[8,128,384]{2,1,0:T(8,12...) custom-call(bf16[128,1024]{1,0:T(8,128)(2,1)} %get-tuple-element.78.raw_ref, ...), custom_call_target="tpu_custom_call" | custom-call | flops 3221225472 | bytes 25165824 | tf_op jit(solution)/shard_map/pallas_call | solution.py:128
  140.8 3.7 %shard_map.104 = (bf16[384,1024]{1,0:T(8,128)(2,1)}, bf16[384,1024]{1,0:T(8,128)(2,1)}, bf16[384,1024]{1,0:T(8,128)(2,1)}, bf16[384,1024]{1,0:T(8,128)(2,1)}) custom-call(bf16[128,1024]{1,0:T(8,128)(2,1)} %get-tuple-element.86.keys_ref, bf16[8,128,384]{2,1,0:T(8,128)(2,1)} %get-tuple-element.93.refs_0_, bf16[8,128,384]{2,1,0:T(8,128)(2,1)} %get-tuple-element.94.refs_1_, ...), custom_call_target="tpu_custom_call" | custom-call | flops 1610612736 | bytes 12582912 | tf_op jit(solution)/shard_map/pallas_call | solution.py:152
  144.6 6.3 %collective-permute-done.19.refs_2_ = bf16[128,1024]{1,0:T(8,128)(2,1)S(1)} collective-permute-done((bf16[128,1024]{1,0:T(8,128)(2,1)}, bf16[128,1024]{1,0:T(8,128)(2,1)S(1)}, u32[]{:S(2)}, u32[]{:S(2)}) %collective-permute-start.19) | collective-permute-done | bytes 262176 | tf_op jit(solution)/shard_map/ppermute | solution.py:355
  158.0 10.0 %collective-permute-done.30.refs_2_ = bf16[128,1024]{1,0:T(8,128)(2,1)S(1)} collective-permute-done((bf16[128,1024]{1,0:T(8,128)(2,1)S(1)}, bf16[128,1024]{1,0:T(8,128)(2,1)S(1)}, u32[]{:S(2)}, u32[]{:S(2)}) %collective-permute-start.30) | collective-permute-done | bytes 262176 | tf_op jit(solution)/shard_map/ppermute | solution.py:355
  169.4 3.6 %collective-permute-done.29.refs_1_ = bf16[128,1024]{1,0:T(8,128)(2,1)S(1)} collective-permute-done((bf16[128,1024]{1,0:T(8,128)(2,1)S(1)}, bf16[128,1024]{1,0:T(8,128)(2,1)S(1)}, u32[]{:S(2)}, u32[]{:S(2)}) %collective-permute-start.29) | collective-permute-done | bytes 262176 | tf_op jit(solution)/shard_map/ppermute | solution.py:355
  179.7 4.3 %shard_map.108 = f32[512,1024]{1,0:T(8,128)} custom-call(bf16[512,1024]{1,0:T(8,128)(2,1)} %maximum_bitcast_fusion.columns_ref, bf16[128,1024]{1,0:T(8,128)(2,1)} %get-tuple-element.87.refs_0_, bf16[128,1024]{1,0:T(8,128)(2,1)} %copy-done.12, bf16[128,1024]{1,0:T(8,128)(2,1)} %copy-done.11, bf16[128,1024]{1,0:T(8,128)(2,1)} %copy-done.10, ...), custom_call_target="tpu_custom_call" | custom-call | flops 1073741824 | bytes 5242880 | tf_op jit(solution)/shard_map/pallas_call | solution.py:241
  184.0 12.1 %collective-permute-done.32.refs_5_.refs_6_.refs_7_ = bf16[384,1024]{1,0:T(8,128)(2,1)S(1)} collective-permute-done((bf16[384,1024]{1,0:T(8,128)(2,1)}, bf16[384,1024]{1,0:T(8,128)(2,1)S(1)}, u32[]{:S(2)}, u32[]{:S(2)}) %collective-permute-start.32) | collective-permute-done | bytes 786464 | tf_op jit(solution)/shard_map/ppermute | solution.py:355
  197.0 4.3 %shard_map.107 = f32[512,1024]{1,0:T(8,128)} custom-call(bf16[512,1024]{1,0:T(8,128)(2,1)} %maximum_bitcast_fusion.columns_ref, bf16[128,1024]{1,0:T(8,128)(2,1)} %copy-done.9, bf16[128,1024]{1,0:T(8,128)(2,1)} %copy-done.14, bf16[128,1024]{1,0:T(8,128)(2,1)} %copy-done.13, bf16[128,1024]{1,0:T(8,128)(2,1)} %copy-done.15, bf16[128,1024]{1,0:T(8,128)(2,1)} %copy-done.23, ...), custom_call_target="tpu_custom_call" | custom-call | flops 1073741824 | bytes 5242880 | tf_op jit(solution)/shard_map/pallas_call | solution.py:241
  201.2 3.0 %shard_map.105.whole_ref = bf16[384,4096]{1,0:T(8,128)(2,1)} custom-call(s32[4]{0:T(128)} %pad_add_fusion.lanes_ref.place_ref, bf16[384,1024]{1,0:T(8,128)(2,1)} %get-tuple-element.97.refs_0_, bf16[384,1024]{1,0:T(8,128)(2,1)} %collective-permute-done.24.refs_1_, bf16[384,1024]{1,0:T(8,128)(2,1)} %copy-done.18), custom_call_target="tpu_custom_call" | custom-call | flops 1000 | bytes 1000 | tf_op jit(solution)/shard_map/pallas_call | solution.py:305
  (130 shorter events, 65.0 us)
Async XLA Ops:
  5.6 34.3 %collective-permute-start = (bf16[768,512]{1,0:T(8,128)(2,1)}, bf16[768,512]{1,0:T(8,128)(2,1)S(1)}, u32[]{:S(2)}, u32[]{:S(2)}) collective-permute-start(bf16[768,512]{1,0:T(8,128)(2,1)} %get-tuple-element.59), channel_id=1, source_target_pairs={{0,8},{4,12},{8,0},{12,4},{16,24},{20,28},{24,16},{28,20},{1,9},{5... | collective-permute-start | bytes 2359304 | tf_op jit(solution)/shard_map/ppermute | solution.py:355
  8.6 23.9 %collective-permute-start.1 = (bf16[128,1024]{1,0:T(8,128)(2,1)}, bf16[128,1024]{1,0:T(8,128)(2,1)}, u32[]{:S(2)}, u32[]{:S(2)}) collective-permute-start(bf16[128,1024]{1,0:T(8,128)(2,1)} %get-tuple-element.60), channel_id=1, source_target_pairs={{0,16},{4,20},{8,24},{12,28},{16,0},{20,4},{24,8},{28,12},{1,17},{... | collective-permute-start | bytes 786440 | tf_op jit(solution)/shard_map/ppermute | solution.py:355
  11.2 28.7 %collective-permute-start.2 = (bf16[128,1024]{1,0:T(8,128)(2,1)}, bf16[128,1024]{1,0:T(8,128)(2,1)}, u32[]{:S(2)}, u32[]{:S(2)}) collective-permute-start(bf16[128,1024]{1,0:T(8,128)(2,1)} %get-tuple-element.61), channel_id=1, source_target_pairs={{0,24},{4,28},{8,16},{12,20},{16,8},{20,12},{24,0},{28,4},{1,25},{... | collective-permute-start | bytes 786440 | tf_op jit(solution)/shard_map/ppermute | solution.py:355
  11.2 38.4 %collective-permute-start.4 = (bf16[1024,512]{1,0:T(8,128)(2,1)}, bf16[1024,512]{1,0:T(8,128)(2,1)S(1)}, u32[]{:S(2)}, u32[]{:S(2)}) collective-permute-start(bf16[1024,512]{1,0:T(8,128)(2,1)} %get-tuple-element.67.refs_4_), channel_id=1, source_target_pairs={{0,4},{4,0},{8,12},{12,8},{16,20},{20,16},{24,28},{28,24},{1,5},{5... | collective-permute-start | bytes 3145736 | tf_op jit(solution)/shard_map/ppermute | solution.py:355
  19.4 46.4 %collective-permute-start.15 = (bf16[2,384,1024]{2,1,0:T(8,128)(2,1)}, bf16[2,384,1024]{2,1,0:T(8,128)(2,1)S(1)}, u32[]{:S(2)}, u32[]{:S(2)}) collective-permute-start(bf16[2,384,1024]{2,1,0:T(8,128)(2,1)} %get-tuple-element.83), channel_id=1, source_target_pairs={{0,2},{1,3},{2,0},{3,1},{4,6},{5,7},{6,4},{7,5},{8,10},{9,11},{10,... | collective-permute-start | bytes 4718600 | tf_op jit(solution)/shard_map/ppermute | solution.py:358
  45.0 16.5 %collective-permute-start.7 = (bf16[512,512]{1,0:T(8,128)(2,1)}, bf16[512,512]{1,0:T(8,128)(2,1)}, u32[]{:S(2)}, u32[]{:S(2)}) collective-permute-start(bf16[512,512]{1,0:T(8,128)(2,1)} %get-tuple-element.71), channel_id=1, source_target_pairs={{0,8},{4,12},{8,0},{12,4},{16,24},{20,28},{24,16},{28,20},{1,9},{5... | collective-permute-start | bytes 1572872 | tf_op jit(solution)/shard_map/ppermute | solution.py:355
  61.5 15.0 %collective-permute-start.8 = (bf16[512,512]{1,0:T(8,128)(2,1)}, bf16[512,512]{1,0:T(8,128)(2,1)S(1)}, u32[]{:S(2)}, u32[]{:S(2)}) collective-permute-start(bf16[512,512]{1,0:T(8,128)(2,1)} %collective-permute-done.7.refs_6_), channel_id=1, source_target_pairs={{0,4},{4,0},{8,12},{12,8},{16,20},{20,16},{24,28},{28,24},{1,5},{5... | collective-permute-start | bytes 1572872 | tf_op jit(solution)/shard_map/ppermute | solution.py:355
  64.0 22.6 %collective-permute-start.9 = (bf16[512,512]{0,1:T(8,128)(2,1)}, bf16[512,512]{0,1:T(8,128)(2,1)}, u32[]{:S(2)}, u32[]{:S(2)}) collective-permute-start(bf16[512,512]{0,1:T(8,128)(2,1)} %copy.17), channel_id=1, source_target_pairs={{0,4},{4,0},{8,12},{12,8},{16,20},{20,16},{24,28},{28,24},{1,5},{5... | collective-permute-start | bytes 1572872 | tf_op jit(solution)/shard_map/ppermute | solution.py:355
  64.5 24.3 %collective-permute-start.6 = (f32[256,512]{1,0:T(8,128)}, f32[256,512]{1,0:T(8,128)S(1)}, u32[]{:S(2)}, u32[]{:S(2)}) collective-permute-start(f32[256,512]{1,0:T(8,128)} %shard_map.97), channel_id=1, source_target_pairs={{0,16},{4,20},{8,24},{12,28},{16,0},{20,4},{24,8},{28,12},{1,17},{... | collective-permute-start | bytes 1572872 | tf_op jit(solution)/shard_map/ppermute | solution.py:355
  65.8 48.8 %collective-permute-start.14 = (bf16[2,384,1024]{2,1,0:T(8,128)(2,1)}, bf16[2,384,1024]{2,1,0:T(8,128)(2,1)}, u32[]{:S(2)}, u32[]{:S(2)}) collective-permute-start(bf16[2,384,1024]{2,1,0:T(8,128)(2,1)} %get-tuple-element.82), channel_id=1, source_target_pairs={{0,1},{1,0},{2,3},{3,2},{4,5},{5,4},{6,7},{7,6},{8,9},{9,8},{10,11... | collective-permute-start | bytes 4718600 | tf_op jit(solution)/shard_map/ppermute | solution.py:358
  65.8 48.8 %collective-permute-start.16 = (bf16[2,384,1024]{2,1,0:T(8,128)(2,1)}, bf16[2,384,1024]{2,1,0:T(8,128)(2,1)}, u32[]{:S(2)}, u32[]{:S(2)}) collective-permute-start(bf16[2,384,1024]{2,1,0:T(8,128)(2,1)} %get-tuple-element.85), channel_id=1, source_target_pairs={{0,3},{1,2},{2,1},{3,0},{4,7},{5,6},{6,5},{7,4},{8,11},{9,10},{10,... | collective-permute-start | bytes 4718600 | tf_op jit(solution)/shard_map/ppermute | solution.py:358
  88.8 25.6 %collective-permute-start.11 = (f32[256,512]{1,0:T(8,128)S(1)}, f32[256,512]{1,0:T(8,128)S(1)}, u32[]{:S(2)}, u32[]{:S(2)}) collective-permute-start(f32[256,512]{1,0:T(8,128)S(1)} %copy-done.21), channel_id=1, source_target_pairs={{0,16},{4,20},{8,24},{12,28},{16,0},{20,4},{24,8},{28,12},{1,17},{... | collective-permute-start | bytes 1572872 | tf_op jit(solution)/shard_map/ppermute | solution.py:355
  114.5 14.7 %collective-permute-start.17 = (bf16[128,512]{1,0:T(8,128)(2,1)S(1)}, bf16[128,512]{1,0:T(8,128)(2,1)S(1)}, u32[]{:S(2)}, u32[]{:S(2)}) collective-permute-start(bf16[128,512]{1,0:T(8,128)(2,1)S(1)} %get-tuple-element.119), channel_id=1, source_target_pairs={{0,8},{4,12},{8,0},{12,4},{16,24},{20,28},{24,16},{28,20},{1,9},{5... | collective-permute-start | bytes 393224 | tf_op jit(solution)/shard_map/ppermute | solution.py:355
  123.2 14.9 %collective-permute-start.21 = (bf16[128,1024]{1,0:T(8,128)(2,1)}, bf16[128,1024]{1,0:T(8,128)(2,1)S(1)}, u32[]{:S(2)}, u32[]{:S(2)}) collective-permute-start(bf16[128,1024]{1,0:T(8,128)(2,1)} %get-tuple-element.87.refs_0_), channel_id=1, source_target_pairs={{0,4},{4,0},{8,12},{12,8},{16,20},{20,16},{24,28},{28,24},{1,5},{5... | collective-permute-start | bytes 786440 | tf_op jit(solution)/shard_map/ppermute | solution.py:355
  124.8 19.8 %collective-permute-start.20 = (bf16[128,1024]{1,0:T(8,128)(2,1)}, bf16[128,1024]{1,0:T(8,128)(2,1)S(1)}, u32[]{:S(2)}, u32[]{:S(2)}) collective-permute-start(bf16[128,1024]{1,0:T(8,128)(2,1)} %get-tuple-element.87.refs_0_), channel_id=1, source_target_pairs={{0,24},{4,28},{8,16},{12,20},{16,8},{20,12},{24,0},{28,4},{1,25},{... | collective-permute-start | bytes 786440 | tf_op jit(solution)/shard_map/ppermute | solution.py:355
  126.3 24.7 %collective-permute-start.19 = (bf16[128,1024]{1,0:T(8,128)(2,1)}, bf16[128,1024]{1,0:T(8,128)(2,1)S(1)}, u32[]{:S(2)}, u32[]{:S(2)}) collective-permute-start(bf16[128,1024]{1,0:T(8,128)(2,1)} %get-tuple-element.87.refs_0_), channel_id=1, source_target_pairs={{0,16},{4,20},{8,24},{12,28},{16,0},{20,4},{24,8},{28,12},{1,17},{... | collective-permute-start | bytes 786440 | tf_op jit(solution)/shard_map/ppermute | solution.py:355
  128.3 22.7 %collective-permute-start.18 = (bf16[128,1024]{1,0:T(8,128)(2,1)}, bf16[128,1024]{1,0:T(8,128)(2,1)S(1)}, u32[]{:S(2)}, u32[]{:S(2)}) collective-permute-start(bf16[128,1024]{1,0:T(8,128)(2,1)} %get-tuple-element.87.refs_0_), channel_id=1, source_target_pairs={{0,8},{4,12},{8,0},{12,4},{16,24},{20,28},{24,16},{28,20},{1,9},{5... | collective-permute-start | bytes 786440 | tf_op jit(solution)/shard_map/ppermute | solution.py:355
  151.1 26.4 %collective-permute-start.23 = (bf16[384,1024]{1,0:T(8,128)(2,1)S(1)}, bf16[384,1024]{1,0:T(8,128)(2,1)S(1)}, u32[]{:S(2)}, u32[]{:S(2)}) collective-permute-start(bf16[384,1024]{1,0:T(8,128)(2,1)S(1)} %pad_maximum_fusion), channel_id=1, source_target_pairs={{0,4},{4,0},{8,12},{12,8},{16,20},{20,16},{24,28},{28,24},{1,5},{5... | collective-permute-start | bytes 2359304 | tf_op jit(solution)/shard_map/ppermute | solution.py:355
  151.7 25.8 %collective-permute-start.25 = (bf16[384,1024]{1,0:T(8,128)(2,1)S(1)}, bf16[384,1024]{1,0:T(8,128)(2,1)S(1)}, u32[]{:S(2)}, u32[]{:S(2)}) collective-permute-start(bf16[384,1024]{1,0:T(8,128)(2,1)S(1)} %copy-done.24), channel_id=1, source_target_pairs={{0,2},{1,3},{2,0},{3,1},{4,6},{5,7},{6,4},{7,5},{8,10},{9,11},{10,... | collective-permute-start | bytes 2359304 | tf_op jit(solution)/shard_map/ppermute | solution.py:358
  153.6 19.4 %collective-permute-start.29 = (bf16[128,1024]{1,0:T(8,128)(2,1)S(1)}, bf16[128,1024]{1,0:T(8,128)(2,1)S(1)}, u32[]{:S(2)}, u32[]{:S(2)}) collective-permute-start(bf16[128,1024]{1,0:T(8,128)(2,1)S(1)} %fusion.3.refs_0_), channel_id=1, source_target_pairs={{0,8},{4,12},{8,0},{12,4},{16,24},{20,28},{24,16},{28,20},{1,9},{5... | collective-permute-start | bytes 786440 | tf_op jit(solution)/shard_map/ppermute | solution.py:355
  155.6 17.4 %collective-permute-start.27 = (bf16[128,1024]{1,0:T(8,128)(2,1)S(1)}, bf16[128,1024]{1,0:T(8,128)(2,1)S(1)}, u32[]{:S(2)}, u32[]{:S(2)}) collective-permute-start(bf16[128,1024]{1,0:T(8,128)(2,1)S(1)} %fusion.3.refs_0_), channel_id=1, source_target_pairs={{0,24},{4,28},{8,16},{12,20},{16,8},{20,12},{24,0},{28,4},{1,25},{... | collective-permute-start | bytes 786440 | tf_op jit(solution)/shard_map/ppermute | solution.py:355
  176.7 19.4 %collective-permute-start.32 = (bf16[384,1024]{1,0:T(8,128)(2,1)}, bf16[384,1024]{1,0:T(8,128)(2,1)S(1)}, u32[]{:S(2)}, u32[]{:S(2)}) collective-permute-start(bf16[384,1024]{1,0:T(8,128)(2,1)} %pad_maximum_fusion.1), channel_id=1, source_target_pairs={{0,4},{4,0},{8,12},{12,8},{16,20},{20,16},{24,28},{28,24},{1,5},{5... | collective-permute-start | bytes 2359304 | tf_op jit(solution)/shard_map/ppermute | solution.py:355
  177.5 23.8 %collective-permute-start.24 = (bf16[384,1024]{1,0:T(8,128)(2,1)}, bf16[384,1024]{1,0:T(8,128)(2,1)}, u32[]{:S(2)}, u32[]{:S(2)}) collective-permute-start(bf16[384,1024]{1,0:T(8,128)(2,1)} %get-tuple-element.104), channel_id=1, source_target_pairs={{0,1},{1,0},{2,3},{3,2},{4,5},{5,4},{6,7},{7,6},{8,9},{9,8},{10,11... | collective-permute-start | bytes 2359304 | tf_op jit(solution)/shard_map/ppermute | solution.py:358
  178.4 25.8 %collective-permute-start.28 = (bf16[384,1024]{1,0:T(8,128)(2,1)}, bf16[384,1024]{1,0:T(8,128)(2,1)S(1)}, u32[]{:S(2)}, u32[]{:S(2)}) collective-permute-start(bf16[384,1024]{1,0:T(8,128)(2,1)} %get-tuple-element.110), channel_id=1, source_target_pairs={{0,3},{1,2},{2,1},{3,0},{4,7},{5,6},{6,5},{7,4},{8,11},{9,10},{10,... | collective-permute-start | bytes 2359304 | tf_op jit(solution)/shard_map/ppermute | solution.py:358
  (34 other events, 331.9 us)
